TPU v7x, 32 devices: a whole 2x2x4 slice. The times are simulated.
32 devices in a mesh: parts: 1, dp: 2 (over core), expert: 16 (over z, y, x).
Axes of the slice: x: 2, y: 2, z: 4, core: 2. Of those that a mesh axis runs over, the one named last changes fastest.
Arguments:
- tokens: bfloat16 [2048, 2048], P(('parts', 'dp', 'expert')), may hold values from -6 to 6
- routes: int32 [2048, 8], P(('parts', 'dp', 'expert')), may hold values from 0 to 15, all different within a row; in each aligned block of 64 rows (0 to 63, 64 to 127, ...) at most 36 rows name the same one
- combine: bfloat16 [2048, 8], P(('parts', 'dp', 'expert')), may hold values from 0.099609375 to 1
- upstream: bfloat16 [2048, 2048], P(('parts', 'dp', 'expert')), may hold values from -6 to 6
- w_gate: bfloat16 [16, 2048, 768], P('expert', None, 'dp'), may hold values from -0.125 to 0.125
- w_up: bfloat16 [16, 2048, 768], P('expert', None, 'dp'), may hold values from -0.125 to 0.125
- w_down: bfloat16 [16, 768, 2048], P('expert', 'dp'), may hold values from -0.21875 to 0.21875
Outputs:
- grad_tokens: bfloat16 [2048, 2048], P(('parts', 'dp', 'expert'))
- grad_combine: bfloat16 [2048, 8], P(('parts', 'dp', 'expert'))
- grad_gate: bfloat16 [16, 2048, 768], P(('parts', 'expert'), None, 'dp')
- grad_up: bfloat16 [16, 2048, 768], P(('parts', 'expert'), None, 'dp')
- grad_down: bfloat16 [16, 768, 2048], P(('parts', 'expert'), 'dp')
Inputs may be any that keep to these rules, and one draw needn't show every extreme that they name: `routes`: each row names 8 different experts. Among the rows of one device no expert is named by more than 36 rows, a bound that some block reaches.
All inputs are finite; a program needn't handle non-finite values.
Results may differ from a plain program's by a relative error of at most 0.008.
Values may be sent and summed in bfloat16 or wider, within the bound.
No kernel may reach another device: no remote copies, remote signals or barrier semaphores. Data moves between devices by JAX's collectives and lax.ppermute only.
A program may use at most 128 MiB of HBM per device.

v0:
```python
import jax
import jax.numpy as jnp
from jax import lax
from jax.sharding import PartitionSpec as P


def expert_math(x_rows, d_rows, c_rows, gate_mat, up_mat, down_mat):
    gate_pre = jnp.dot(x_rows, gate_mat, preferred_element_type=jnp.float32)
    up_pre = jnp.dot(x_rows, up_mat, preferred_element_type=jnp.float32)
    logistic = jax.nn.sigmoid(gate_pre)
    hidden = (gate_pre * logistic * up_pre).astype(jnp.bfloat16)
    grad_hidden = jnp.dot(d_rows, down_mat.T, preferred_element_type=jnp.float32)
    comb_part = jnp.sum(hidden.astype(jnp.float32) * grad_hidden, axis=1)
    scale_col = c_rows.astype(jnp.float32)[:, None]
    scaled = (scale_col * d_rows.astype(jnp.float32)).astype(jnp.bfloat16)
    grad_mixed = scale_col * grad_hidden
    grad_gpre = (grad_mixed * up_pre * logistic * (1.0 + gate_pre * (1.0 - logistic))).astype(
        jnp.bfloat16
    )
    grad_upre = (grad_mixed * gate_pre * logistic).astype(jnp.bfloat16)
    grad_downw = jnp.dot(hidden.T, scaled, preferred_element_type=jnp.float32)
    grad_gatew = jnp.dot(x_rows.T, grad_gpre, preferred_element_type=jnp.float32)
    grad_upw = jnp.dot(x_rows.T, grad_upre, preferred_element_type=jnp.float32)
    row_part = jnp.dot(grad_gpre, gate_mat.T, preferred_element_type=jnp.float32)
    row_part = row_part + jnp.dot(grad_upre, up_mat.T, preferred_element_type=jnp.float32)
    return (grad_gatew, grad_upw, grad_downw, row_part, comb_part)


def on_device(tokens, routes, combine, upstream, w_gate, w_up, w_down):
    tok_count, top_count = routes.shape
    width = tokens.shape[1]
    peer_count = lax.axis_size("expert")
    mean_load = tok_count * top_count // peer_count
    capacity = min(tok_count, max(2, mean_load + tok_count * top_count // (8 * peer_count)))
    route_count = tok_count * top_count
    flat_ids = routes.reshape(-1)
    onehot = (flat_ids[:, None] == jnp.arange(peer_count, dtype=jnp.int32)[None, :]).astype(
        jnp.int32
    )
    earlier = jnp.cumsum(onehot, axis=0) - onehot
    position = jnp.sum(earlier * onehot, axis=1)
    slot_index = flat_ids * capacity + position
    owners = jnp.full((peer_count * capacity,), route_count, jnp.int32)
    owners = owners.at[slot_index].set(jnp.arange(route_count, dtype=jnp.int32))
    filled = owners < route_count
    safe_ids = jnp.where(filled, owners, 0)
    token_ids = safe_ids // top_count
    zero_half = jnp.zeros((), jnp.bfloat16)
    x_send = jnp.where(filled[:, None], tokens[token_ids], zero_half).reshape(
        peer_count, capacity, width
    )
    d_send = jnp.where(filled[:, None], upstream[token_ids], zero_half).reshape(
        peer_count, capacity, width
    )
    c_send = jnp.where(filled, combine.reshape(-1)[safe_ids], zero_half).reshape(
        peer_count, capacity
    )
    x_recv, d_recv, c_recv = (
        lax.all_to_all(x_send, "expert", split_axis=0, concat_axis=0, tiled=True),
        lax.all_to_all(d_send, "expert", split_axis=0, concat_axis=0, tiled=True),
        lax.all_to_all(c_send, "expert", split_axis=0, concat_axis=0, tiled=True),
    )
    row_count = peer_count * capacity
    gate_full, up_full = (
        lax.all_gather(w_gate, "dp", axis=2, tiled=True),
        lax.all_gather(w_up, "dp", axis=2, tiled=True),
    )
    down_full = lax.all_gather(w_down, "dp", axis=1, tiled=True)
    grad_gatew, grad_upw, grad_downw, row_part, comb_part = expert_math(
        x_recv.reshape(row_count, width),
        d_recv.reshape(row_count, width),
        c_recv.reshape(row_count),
        gate_full[0],
        up_full[0],
        down_full[0],
    )
    grad_gate, grad_up = (
        lax.psum_scatter(grad_gatew[None], "dp", scatter_dimension=2, tiled=True),
        lax.psum_scatter(grad_upw[None], "dp", scatter_dimension=2, tiled=True),
    )
    grad_down = lax.psum_scatter(grad_downw[None], "dp", scatter_dimension=1, tiled=True)
    back_rows = row_part.astype(jnp.bfloat16)
    back_comb = comb_part.astype(jnp.bfloat16)
    rows_home, comb_home = (
        lax.all_to_all(
            back_rows.reshape(peer_count, capacity, width),
            "expert",
            split_axis=0,
            concat_axis=0,
            tiled=True,
        ),
        lax.all_to_all(
            back_comb.reshape(peer_count, capacity),
            "expert",
            split_axis=0,
            concat_axis=0,
            tiled=True,
        ),
    )
    picked = rows_home.reshape(row_count, width)[slot_index]
    grad_tokens = jnp.sum(
        picked.reshape(tok_count, top_count, width).astype(jnp.float32), axis=1
    ).astype(jnp.bfloat16)
    grad_combine = comb_home.reshape(-1)[slot_index].reshape(tok_count, top_count)
    return (
        grad_tokens,
        grad_combine,
        grad_gate.astype(jnp.bfloat16),
        grad_up.astype(jnp.bfloat16),
        grad_down.astype(jnp.bfloat16),
    )


def solution(mesh):
    in_specs = (
        P(("parts", "dp", "expert"), None),
        P(("parts", "dp", "expert"), None),
        P(("parts", "dp", "expert"), None),
        P(("parts", "dp", "expert"), None),
        P("expert", None, "dp"),
        P("expert", None, "dp"),
        P("expert", "dp", None),
    )
    out_specs = (
        P(("parts", "dp", "expert"), None),
        P(("parts", "dp", "expert"), None),
        P(("parts", "expert"), None, "dp"),
        P(("parts", "expert"), None, "dp"),
        P(("parts", "expert"), "dp", None),
    )
    return jax.shard_map(
        on_device, mesh=mesh, in_specs=in_specs, out_specs=out_specs, check_vma=False
    )
```

profile of v0, /device:TPU:12, one launch (start us, length us, event | category | flops | bytes accessed | tf_op | source)
XLA Modules:
  0.0 320.1 jit_solution(11690840229439822200)
XLA Ops:
  14.0 3.9 %gather_fusion = bf16[576]{0:T(1024)(128)(2,1)S(1)} fusion(bf16[512]{0:T(512)(128)(2,1)S(1)} %reshape.124, s32[1024]{0:T(1024)S(1)} %pad_clamp_fusion.2), kind=kCustom, calls=%fused_computation | custom fusion | bytes 4608 | tf_op jit(solution)/shard_map/gather | solution.py:55
  18.6 7.2 %all-to-all-start = ((bf16[16,1,36]{2,1,0:T(2,128)(2,1)}), bf16[16,1,36]{2,1,0:T(2,128)(2,1)S(1)}, u32[]{:S(2)}, u32[]{:S(2)}) async-start(bf16[16,1,36]{2,1,0:T(2,128)(2,1)} %all_to_all.25), calls=%async_computation | async-start | bytes 16384 | tf_op jit(solution)/shard_map/all_to_all | solution.py:61
  25.9 4.0 %gather_fusion.1 = bf16[576,2048]{1,0:T(8,128)(2,1)} fusion(bf16[64,2048]{1,0:T(8,128)(2,1)S(1)} %copy-done, s32[1024]{0:T(1024)S(1)} %pad_clamp_fusion.1), kind=kCustom, calls=%fused_computation.1 | custom fusion | bytes 4720896 | tf_op jit(solution)/shard_map/gather | solution.py:52
  32.5 4.0 %gather_fusion.2 = bf16[576,2048]{1,0:T(8,128)(2,1)} fusion(bf16[64,2048]{1,0:T(8,128)(2,1)S(1)} %copy-done.2, s32[1024]{0:T(1024)S(1)} %pad_clamp_fusion.1), kind=kCustom, calls=%fused_computation.2 | custom fusion | bytes 4720896 | tf_op jit(solution)/shard_map/gather | solution.py:49
  36.6 4.1 %gather.23 = bf16[16,36,2048]{2,1,0:T(8,128)(2,1)} reshape(bf16[576,2048]{1,0:T(8,128)(2,1)} %gather_fusion.2) | data formatting | bytes 4718592 | tf_op jit(solution)/shard_map/gather | solution.py:49
  40.6 4.4 %broadcast_select_fusion.1 = (bf16[16,36,2048]{2,1,0:T(8,128)(2,1)}, bf16[16,36,2048]{2,1,0:T(8,128)(2,1)}) fusion(bf16[16,36,2048]{2,1,0:T(8,128)(2,1)S(1)} %gather.21, pred[16,36]{1,0:T(8,128)(4,1)S(1)} %broadcast_in_dim.52, bf16[16,36,2048]{2,1,0:T(8,128)(2,1)} %gather.23), kind=kLoop, calls=%fused_computation.22 | loop fusion | flops 2359296 | bytes 9437760 | tf_op jit(solution)/shard_map/jit(_where)/select_n | solution.py:52
  45.1 6.9 %all-to-all-start.2 = ((bf16[16,36,2048]{2,1,0:T(8,128)(2,1)}), bf16[16,36,2048]{2,1,0:T(8,128)(2,1)S(1)}, u32[]{:S(2)}, u32[]{:S(2)}) async-start(bf16[16,36,2048]{2,1,0:T(8,128)(2,1)} %get-tuple-element.22), calls=%async_computation.2 | async-start | bytes 5242880 | tf_op jit(solution)/shard_map/all_to_all | solution.py:59
  53.5 57.4 %all-to-all-done.2 = bf16[16,36,2048]{2,1,0:T(8,128)(2,1)S(1)} async-done(((bf16[16,36,2048]{2,1,0:T(8,128)(2,1)}), bf16[16,36,2048]{2,1,0:T(8,128)(2,1)S(1)}, u32[]{:S(2)}, u32[]{:S(2)}) %all-to-all-start.2) | async-done | bytes 2359328 | tf_op jit(solution)/shard_map/all_to_all | solution.py:59
  110.9 4.8 %all-to-all-start.1 = ((bf16[16,36,2048]{2,1,0:T(8,128)(2,1)}), bf16[16,36,2048]{2,1,0:T(8,128)(2,1)}, u32[]{:S(2)}, u32[]{:S(2)}) async-start(bf16[16,36,2048]{2,1,0:T(8,128)(2,1)} %get-tuple-element.21), calls=%async_computation.1 | async-start | bytes 5242880 | tf_op jit(solution)/shard_map/all_to_all | solution.py:60
  118.9 55.4 %all-to-all-done.1 = bf16[16,36,2048]{2,1,0:T(8,128)(2,1)} async-done(((bf16[16,36,2048]{2,1,0:T(8,128)(2,1)}), bf16[16,36,2048]{2,1,0:T(8,128)(2,1)}, u32[]{:S(2)}, u32[]{:S(2)}) %all-to-all-start.1) | async-done | bytes 2359328 | tf_op jit(solution)/shard_map/all_to_all | solution.py:60
  177.1 5.8 %fusion.6 = f32[576,768]{1,0:T(8,128)} fusion(bf16[576,2048]{1,0:T(8,128)(2,1)} %reshape.126, bf16[1,2048,768]{2,1,0:T(8,128)(2,1)} %all-gather.6.cloned.1.call-done), kind=kOutput, calls=%fused_computation.17 | convolution fusion | flops 1811939328 | bytes 7274496 | tf_op jit(solution)/shard_map/dot_general | solution.py:9
  182.9 5.8 %fusion.2 = f32[576,768]{1,0:T(8,128)} fusion(bf16[576,2048]{1,0:T(8,128)(2,1)} %reshape.126, bf16[1,2048,768]{2,1,0:T(8,128)(2,1)} %all-gather.8.cloned.1.call-done), kind=kOutput, calls=%fused_computation.13 | convolution fusion | flops 1811939328 | bytes 7274496 | tf_op jit(solution)/shard_map/dot_general | solution.py:8
  188.7 7.0 %multiply_reduce_fusion = (bf16[576]{0:T(1024)(128)(2,1)S(1)}, bf16[576,768]{1,0:T(8,128)(2,1)}, bf16[576,768]{1,0:T(8,128)(2,1)S(1)}, bf16[576,768]{1,0:T(8,128)(2,1)}) fusion(f32[576,768]{1,0:T(8,128)} %fusion.6, f32[576,768]{1,0:T(8,128)} %fusion.2, f32[576]{0:T(1024)S(1)} %reshape.132, bf16[576,2048]{1,0:T(8,128)(2,1)S(1)} %reshape.125, ...), kind=kOutput, calls=%fused_computation.25 | convolution fusion | flops 1820786176 | bytes 11701632 | tf_op jit(solution)/shard_map/dot_general | solution.py:12
  196.7 4.6 %convolution_bitcast_fusion.2 = f32[1,2048,768]{2,1,0:T(8,128)} fusion(bf16[576,2048]{1,0:T(8,128)(2,1)S(1)} %copy-done.3, bf16[576,768]{1,0:T(8,128)(2,1)S(1)} %get-tuple-element.19), kind=kOutput, calls=%fused_computation.10 | convolution fusion | flops 1811939328 | bytes 9535488 | tf_op jit(solution)/shard_map/dot_general | solution.py:22
  201.3 7.8 %convolution_bitcast_fusion.1 = f32[1,2048,768]{2,1,0:T(8,128)} fusion(bf16[576,2048]{1,0:T(8,128)(2,1)} %reshape.126, bf16[576,768]{1,0:T(8,128)(2,1)} %get-tuple-element.20), kind=kOutput, calls=%fused_computation.9 | convolution fusion | flops 1811939328 | bytes 9535488 | tf_op jit(solution)/shard_map/dot_general | solution.py:23
  209.2 6.1 %convolution_bitcast_fusion = f32[1,768,2048]{2,1,0:T(8,128)} fusion(bf16[576,768]{1,0:T(8,128)(2,1)} %get-tuple-element.16, bf16[576,2048]{1,0:T(8,128)(2,1)S(1)} %reshape.125, f32[576]{0:T(1024)S(1)} %reshape.132), kind=kOutput, calls=%fused_computation.8 | convolution fusion | flops 1815478272 | bytes 9537792 | tf_op jit(solution)/shard_map/dot_general | solution.py:21
  216.0 5.0 %all-to-all-start.4 = ((bf16[16,1,36]{2,1,0:T(2,128)(2,1)}), bf16[16,1,36]{2,1,0:T(2,128)(2,1)S(1)}, u32[]{:S(2)}, u32[]{:S(2)}) async-start(bf16[16,1,36]{2,1,0:T(2,128)(2,1)} %convert_element_type.80), calls=%async_computation.4 | async-start | bytes 16384 | tf_op jit(solution)/shard_map/all_to_all | solution.py:92
  221.0 4.1 %fusion = f32[576,2048]{1,0:T(8,128)S(1)} fusion(bf16[576,768]{1,0:T(8,128)(2,1)S(1)} %copy-done.7, bf16[1,2048,768]{2,1,0:T(8,128)(2,1)} %all-gather.8.cloned.1.call-done), kind=kOutput, calls=%fused_computation.11 | convolution fusion | flops 1811939328 | bytes 8749056 | tf_op jit(solution)/shard_map/dot_general | solution.py:24
  229.4 6.9 %all-to-all-start.3 = ((bf16[16,36,2048]{2,1,0:T(8,128)(2,1)}), bf16[16,36,2048]{2,1,0:T(8,128)(2,1)}, u32[]{:S(2)}, u32[]{:S(2)}) async-start(bf16[16,36,2048]{2,1,0:T(8,128)(2,1)} %reshape.127), calls=%async_computation.3 | async-start | bytes 5242880 | tf_op jit(solution)/shard_map/all_to_all | solution.py:85
  236.5 3.5 %gather_fusion.4 = bf16[512]{0:T(512)(128)(2,1)S(1)} fusion(bf16[576]{0:T(1024)(128)(2,1)S(1)} %reshape.130, s32[1024]{0:T(1024)S(1)} %pad_clamp_fusion), kind=kCustom, calls=%fused_computation.4 | custom fusion | bytes 4096 | tf_op jit(solution)/shard_map/gather | solution.py:104
  240.7 53.1 %all-to-all-done.3 = bf16[16,36,2048]{2,1,0:T(8,128)(2,1)} async-done(((bf16[16,36,2048]{2,1,0:T(8,128)(2,1)}), bf16[16,36,2048]{2,1,0:T(8,128)(2,1)}, u32[]{:S(2)}, u32[]{:S(2)}) %all-to-all-start.3) | async-done | bytes 2359328 | tf_op jit(solution)/shard_map/all_to_all | solution.py:85
  296.5 3.3 %gather_fusion.3 = bf16[512,2048]{1,0:T(8,128)(2,1)} fusion(bf16[576,2048]{1,0:T(8,128)(2,1)S(1)} %reshape.128, s32[1024]{0:T(1024)S(1)} %pad_clamp_fusion), kind=kCustom, calls=%fused_computation.3 | custom fusion | bytes 4196352 | tf_op jit(solution)/shard_map/gather | solution.py:100
  299.8 3.7 %bitcast_reduce_fusion = bf16[64,2048]{1,0:T(8,128)(2,1)} fusion(bf16[512,2048]{1,0:T(8,128)(2,1)} %gather_fusion.3), kind=kLoop, calls=%fused_computation.24 | loop fusion | flops 917504 | bytes 2359296 | tf_op jit(solution)/shard_map/reduce_sum | solution.py:101
  310.0 3.3 %convert_element_type.78 = bf16[1,384,2048]{2,1,0:T(8,128)(2,1)} convert(f32[1,384,2048]{2,1,0:T(8,128)} %reduce-scatter.8.cloned.1.call-done) | non-fusion elementwise | flops 786432 | bytes 4718592 | tf_op jit(solution)/shard_map/convert_element_type | solution.py:110
  (76 shorter events, 33.6 us)
Async XLA Ops:
  7.2 18.8 %copy-start = (bf16[64,2048]{1,0:T(8,128)(2,1)S(1)}, bf16[64,2048]{1,0:T(8,128)(2,1)}, u32[]{:S(2)}) copy-start(bf16[64,2048]{1,0:T(8,128)(2,1)} %param.10) | copy-start | bytes 786436
  18.6 26.5 %all-to-all-start = ((bf16[16,1,36]{2,1,0:T(2,128)(2,1)}), bf16[16,1,36]{2,1,0:T(2,128)(2,1)S(1)}, u32[]{:S(2)}, u32[]{:S(2)}) async-start(bf16[16,1,36]{2,1,0:T(2,128)(2,1)} %all_to_all.25), calls=%async_computation | async-start | bytes 16384 | tf_op jit(solution)/shard_map/all_to_all | solution.py:61
  29.9 2.6 copy-start.2
  45.1 65.8 %all-to-all-start.2 = ((bf16[16,36,2048]{2,1,0:T(8,128)(2,1)}), bf16[16,36,2048]{2,1,0:T(8,128)(2,1)S(1)}, u32[]{:S(2)}, u32[]{:S(2)}) async-start(bf16[16,36,2048]{2,1,0:T(8,128)(2,1)} %get-tuple-element.22), calls=%async_computation.2 | async-start | bytes 5242880 | tf_op jit(solution)/shard_map/all_to_all | solution.py:59
  52.0 125.1 %all-gather.6.cloned.1.call-start = ((), (), s32[]{:S(2)}) async-start(), calls=%async_computation.9 | async-start | bytes 4718592 | tf_op jit(solution)/shard_map/all_gather | solution.py:66
  52.7 130.2 %all-gather.8.cloned.1.call-start = ((), (), s32[]{:S(2)}) async-start(), calls=%async_computation.10 | async-start | bytes 4718592 | tf_op jit(solution)/shard_map/all_gather | solution.py:65
  110.9 63.5 %all-to-all-start.1 = ((bf16[16,36,2048]{2,1,0:T(8,128)(2,1)}), bf16[16,36,2048]{2,1,0:T(8,128)(2,1)}, u32[]{:S(2)}, u32[]{:S(2)}) async-start(bf16[16,36,2048]{2,1,0:T(8,128)(2,1)} %get-tuple-element.21), calls=%async_computation.1 | async-start | bytes 5242880 | tf_op jit(solution)/shard_map/all_to_all | solution.py:60
  115.7 73.1 %all-gather.4.cloned.1.call-start = ((), (), s32[]{:S(2)}) async-start(), calls=%async_computation.8 | async-start | bytes 4718592 | tf_op jit(solution)/shard_map/all_gather | solution.py:68
  116.4 187.1 %reduce-scatter.4.cloned.1.call-start = ((), (), s32[]{:S(2)}) async-start(), calls=%async_computation.11 | async-start | bytes 9437184 | tf_op jit(solution)/shard_map/reduce_scatter | solution.py:78
  188.7 7.9 %copy-start.3 = (bf16[576,2048]{1,0:T(8,128)(2,1)S(1)}, bf16[576,2048]{1,0:T(8,128)(2,1)}, u32[]{:S(2)}) copy-start(bf16[576,2048]{1,0:T(8,128)(2,1)} %reshape.126) | copy-start | bytes 7077892
  195.8 0.9 copy-start.6
  201.2 105.5 %reduce-scatter.6.cloned.1.call-start = ((), (), s32[]{:S(2)}) async-start(), calls=%async_computation.12 | async-start | bytes 9437184 | tf_op jit(solution)/shard_map/reduce_scatter | solution.py:79
  209.1 100.8 %reduce-scatter.8.cloned.1.call-start = ((), (), s32[]{:S(2)}) async-start(), calls=%async_computation.13 | async-start | bytes 9437184 | tf_op jit(solution)/shard_map/reduce_scatter | solution.py:81
  215.3 5.7 %copy-start.7 = (bf16[576,768]{1,0:T(8,128)(2,1)S(1)}, bf16[576,768]{1,0:T(8,128)(2,1)}, u32[]{:S(2)}) copy-start(bf16[576,768]{1,0:T(8,128)(2,1)} %copy-done.6) | copy-start | bytes 2654212
  216.0 13.4 %all-to-all-start.4 = ((bf16[16,1,36]{2,1,0:T(2,128)(2,1)}), bf16[16,1,36]{2,1,0:T(2,128)(2,1)S(1)}, u32[]{:S(2)}, u32[]{:S(2)}) async-start(bf16[16,1,36]{2,1,0:T(2,128)(2,1)} %convert_element_type.80), calls=%async_computation.4 | async-start | bytes 16384 | tf_op jit(solution)/shard_map/all_to_all | solution.py:92
  221.0 4.1 %copy-start.4 = (bf16[1,2048,768]{2,1,0:T(8,128)(2,1)S(1)}, bf16[1,2048,768]{2,1,0:T(8,128)(2,1)}, u32[]{:S(2)}) copy-start(bf16[1,2048,768]{2,1,0:T(8,128)(2,1)} %all-gather.6.cloned.1.call-done) | copy-start | bytes 9437188
  221.0 4.1 %copy-start.5 = (bf16[576,768]{1,0:T(8,128)(2,1)S(1)}, bf16[576,768]{1,0:T(8,128)(2,1)}, u32[]{:S(2)}) copy-start(bf16[576,768]{1,0:T(8,128)(2,1)} %get-tuple-element.20) | copy-start | bytes 2654212
  229.4 64.4 %all-to-all-start.3 = ((bf16[16,36,2048]{2,1,0:T(8,128)(2,1)}), bf16[16,36,2048]{2,1,0:T(8,128)(2,1)}, u32[]{:S(2)}, u32[]{:S(2)}) async-start(bf16[16,36,2048]{2,1,0:T(8,128)(2,1)} %reshape.127), calls=%async_computation.3 | async-start | bytes 5242880 | tf_op jit(solution)/shard_map/all_to_all | solution.py:85
  306.7 6.5 %copy-start.1 = (bf16[64,2048]{1,0:T(8,128)(2,1)S(1)}, bf16[64,2048]{1,0:T(8,128)(2,1)}, u32[]{:S(2)}) copy-start(bf16[64,2048]{1,0:T(8,128)(2,1)} %param.10) | copy-start | bytes 786436
Sparse Core Ops, SparseCore 0:
  54.4 13.1 all-gather.5
  69.1 13.1 all-gather.7
  118.0 13.2 all-gather.3
  201.4 13.4 reduce-scatter.3
  217.1 15.6 reduce-scatter.5
  235.0 15.6 reduce-scatter.7
where the time goes:
time: 321 us; the launch traced here: 320 us
  waiting for transfers between devices  168 us (52%)
  local copies, waits for them, and re-layouts  43.2 us (13%)
  matrix products  43.2 us (13%)
  starting transfers between devices  31.2 us (10%)
  other arithmetic  20 us (6%)
  between operations  14.3 us (4%)
    all_to_all x1, waiting for transfers between devices, on_device(): lax.all_to_all(x_send, 'expert', split_axis=0, concat_axis=0, tiled=True)  57.4 us
    all_to_all x1, waiting for transfers between devices, on_device(): lax.all_to_all(d_send, 'expert', split_axis=0, concat_axis=0, tiled=True)  55.4 us
    all_to_all x1, waiting for transfers between devices, on_device(): lax.all_to_all(back_rows.reshape(peer_count, capacity, width), 'expert',...  53.1 us
    gather x2, local copies, waits for them, and re-layouts, on_device(): tokens[token_ids]  8.08 us
    dot_general x1, matrix products, expert_math(): grad_upw = jnp.dot(x_rows.T, grad_upre, preferred_element_type=jnp.float32)  7.79 us
    all_to_all x1, starting transfers between devices, on_device(): lax.all_to_all(c_send, 'expert', split_axis=0, concat_axis=0, tiled=True)  7.17 us
    dot_general x1, matrix products, expert_math(): jnp.dot(d_rows, down_mat.T, preferred_element_type=jnp.float32)  7.02 us
    all_to_all x1, starting transfers between devices, on_device(): lax.all_to_all(x_send, 'expert', split_axis=0, concat_axis=0, tiled=True)  6.92 us
  transfers between devices with their start and end apart: 11, of which 3 were waited for; matrix products, arithmetic and copies ran while one was open for 25% of the time, Pallas kernels for 0%

commit v1 on v0

v1 whole, which is shorter than its diff:
```python
import functools

import jax
import jax.numpy as jnp
import numpy as np
from jax import lax
from jax.experimental import pallas as pl
from jax.experimental.pallas import tpu as pltpu
from jax.sharding import PartitionSpec as P

BF = jnp.bfloat16
F32 = jnp.float32
LANES = 128
HALF = 64
STRIDE = 1024
NOWHERE = -(1 << 20)
ANY = pl.BlockSpec(memory_space=pl.ANY)
VMEM = pl.BlockSpec(memory_space=pltpu.VMEM)
SMEM = pl.BlockSpec(memory_space=pltpu.SMEM)
TN = (((0,), (0,)), ((), ()))
NT = (((1,), (1,)), ((), ()))


def params(megabytes):
    return pltpu.CompilerParams(vmem_limit_bytes=megabytes << 20)


def cost(flops, moved):
    return pl.CostEstimate(flops=int(flops), bytes_accessed=int(moved), transcendentals=0)


class Plan:
    def __init__(self, experts, tok, top, width, hidden):
        self.experts, self.tok, self.top = experts, tok, top
        self.width, self.hidden = width, hidden
        outer = 1
        while outer * outer < experts:
            outer *= 2
        self.outer, self.inner = outer, experts // outer
        mean = tok * top // experts
        self.cap = min(tok, max(2, mean + tok * top // (8 * experts)))
        total = -(-self.outer * self.cap // 16) * 16
        first = self.outer // 2 * self.cap // 16 * 16
        self.chunks = ((0, first), (first, total))
        self.rows = tuple(b - a for a, b in self.chunks)
        self.cands = 2 * self.outer - 1
        self.use = (self.used(self.outer // 2), list(range(self.cands)))
        self.keys = [
            np.array(
                [[d * STRIDE + q for d in range(self.inner) for q in range(a, b)]], np.int32
            )
            for a, b in self.chunks
        ]

    def order(self, z):
        return sorted(range(self.outer), key=lambda s: abs(s - z))

    def cand(self, z, source):
        if source == z:
            return 0
        return z - source if source < z else self.outer - 1 + source - z

    def used(self, slots):
        return sorted({self.cand(z, s) for z in range(self.outer) for s in self.order(z)[:slots]})

    def partner(self, p, d):
        return p ^ d if self.inner & (self.inner - 1) == 0 else (d - p) % self.inner

    def table(self):
        rows = []
        for e in range(self.experts):
            z, p = divmod(e, self.inner)
            offs = [NOWHERE] * self.cands
            for slot, source in enumerate(self.order(z)):
                offs[self.cand(z, source)] = slot * self.cap
            rows.append(offs + [z * self.inner + self.partner(p, d) for d in range(self.inner)])
        return np.array(rows, np.int32)

    def line(self, step):
        return [
            (z * self.inner + p, (z + step) * self.inner + p)
            for z in range(self.outer)
            for p in range(self.inner)
            if 0 <= z + step < self.outer
        ]

    def across(self, d):
        return [
            (z * self.inner + p, z * self.inner + self.partner(p, d))
            for z in range(self.outer)
            for p in range(self.inner)
        ]

    def shift(self, r):
        return [
            (z * self.inner + p, (z + r) % self.outer * self.inner + p)
            for z in range(self.outer)
            for p in range(self.inner)
        ]


def pack_kernel(plan, tok_ref, up_ref, routes_ref, comb_ref, out_ref):
    tok, width = plan.tok, plan.width
    out_ref[:, :width] = tok_ref[...]
    out_ref[:, width : 2 * width] = up_ref[...]
    lane = lax.broadcasted_iota(jnp.int32, (tok, LANES), 1)
    weight = jnp.zeros((tok, LANES), F32)
    named = jnp.zeros((tok, LANES), F32)
    comb = comb_ref[...].astype(F32)
    for k in range(plan.top):
        e = routes_ref[:, k : k + 1]
        weight = jnp.where(lane == e, comb[:, k : k + 1], weight)
        named = jnp.where(lane == e + HALF, 1.0, named)
    row = lax.broadcasted_iota(jnp.int32, (tok, tok), 0)
    col = lax.broadcasted_iota(jnp.int32, (tok, tok), 1)
    upto = jnp.where(col <= row, 1.0, 0.0).astype(BF)
    count = jnp.dot(upto, named.astype(BF), preferred_element_type=F32)
    out_ref[:, 2 * width :] = (weight + count * named).astype(BF)


def picks(plan, meta, off, experts, key, scaled):
    tok = meta.shape[0]
    lane = lax.broadcasted_iota(jnp.int32, (tok, LANES), 1)
    one = jnp.zeros((tok, key.shape[1]), F32)
    two = jnp.zeros((tok, key.shape[1]), F32)
    for d, e in enumerate(experts):
        place = jnp.sum(jnp.where(lane == e + HALF, meta, 0.0), axis=1, keepdims=True)
        place = place.astype(jnp.int32)
        spot = jnp.where(place > 0, place - 1 + off + d * STRIDE, -1)
        hit = spot == key
        one = jnp.where(hit, 1.0, one)
        if scaled:
            weight = jnp.sum(jnp.where(lane == e, meta, 0.0), axis=1, keepdims=True)
            two = jnp.where(hit, weight, two)
    return one, two


def compact_kernel(plan, chunk, *refs):
    use, rows = plan.use[chunk], plan.rows[chunk]
    n, width, tok, inner = len(use), plan.width, plan.tok, plan.inner
    info, key_ref = refs[:2]
    blocks, outs = refs[2 : 2 + n], refs[2 + n : 2 + n + inner]
    held, one_s, two_s, sems = refs[2 + n + inner :]
    copies = [
        pltpu.make_async_copy(b, held.at[pl.ds(i * tok, tok)], sems.at[i])
        for i, b in enumerate(blocks)
    ]
    for c in copies:
        c.start()
    experts = [info[plan.cands + d] for d in range(inner)]
    for i, c in enumerate(copies):
        c.wait()
        meta = held[i * tok : (i + 1) * tok, 2 * width :].astype(F32)
        one, two = picks(plan, meta, info[use[i]], experts, key_ref[...], True)
        one_s[i * tok : (i + 1) * tok, :] = one.astype(BF)
        two_s[i * tok : (i + 1) * tok, :] = two.astype(BF)
    tile = 512
    for part, source in ((0, one_s), (1, two_s)):

        @pl.loop(0, width // tile)
        def _(j):
            at = pl.multiple_of(j * tile, tile)
            got = lax.dot_general(
                source[...],
                held[:, pl.ds(pl.multiple_of(part * width + at, tile), tile)],
                TN,
                preferred_element_type=F32,
            ).astype(BF)
            for d in range(inner):
                outs[d][part * rows : (part + 1) * rows, pl.ds(at, tile)] = got[
                    d * rows : (d + 1) * rows
                ]


def expert_kernel(plan, chunk, *refs):
    inner, rows, width, hidden = plan.inner, plan.rows[chunk], plan.width, plan.hidden
    part, count = hidden // 2, plan.inner * plan.rows[chunk]
    info = refs[0]
    got, weights = refs[1 : 1 + inner], refs[1 + inner : 7 + inner]
    hid_o, gate_o, up_o = refs[7 + inner : 10 + inner]
    backs = refs[10 + inner : 10 + 2 * inner]
    x_s, d_s, wg_s, wu_s, wd_s, comb_s, sems = refs[10 + 2 * inner :]
    x_copies = [
        pltpu.make_async_copy(g.at[pl.ds(0, rows)], x_s.at[pl.ds(d * rows, rows)], sems.at[d])
        for d, g in enumerate(got)
    ]
    d_copies = [
        pltpu.make_async_copy(
            g.at[pl.ds(rows, rows)], d_s.at[pl.ds(d * rows, rows)], sems.at[inner + d]
        )
        for d, g in enumerate(got)
    ]
    w_copies = []
    for i in range(6):
        half, where = pl.ds(i % 2 * part, part), (wg_s, wu_s, wd_s)[i // 2]
        to = where.at[half] if i >= 4 else where.at[:, half]
        w_copies.append(pltpu.make_async_copy(weights[i].at[0], to, sems.at[2 * inner + i]))
    for c in x_copies + w_copies[:4] + d_copies + w_copies[4:]:
        c.start()
    for c in x_copies + w_copies[:4] + d_copies + w_copies[4:]:
        c.wait()
    tile = 256
    comb_s[...] = jnp.zeros_like(comb_s)

    @pl.loop(0, hidden // tile)
    def _(n):
        at = pl.ds(pl.multiple_of(n * tile, tile), tile)
        gate = jnp.dot(x_s[...], wg_s[:, at], preferred_element_type=F32)
        up = jnp.dot(x_s[...], wu_s[:, at], preferred_element_type=F32)
        mixed = lax.dot_general(d_s[...], wd_s[at, :], NT, preferred_element_type=F32)
        logistic = jax.nn.sigmoid(gate)
        silu = gate * logistic
        hid = (silu * up).astype(BF)
        hid_o[:, at] = hid
        comb_s[...] += jnp.sum(hid.astype(F32) * mixed, axis=1, keepdims=True)
        gate_o[:, at] = (mixed * up * logistic * (1.0 + gate * (1.0 - logistic))).astype(BF)
        up_o[:, at] = (mixed * silu).astype(BF)

    wide = 256

    @pl.loop(0, width // wide)
    def _(j):
        at = pl.ds(pl.multiple_of(j * wide, wide), wide)
        back = lax.dot_general(gate_o[...], wg_s[at, :], NT, preferred_element_type=F32)
        back += lax.dot_general(up_o[...], wu_s[at, :], NT, preferred_element_type=F32)
        back = back.astype(BF)
        for d in range(inner):
            backs[d][:, at] = back[d * rows : (d + 1) * rows]

    lane = lax.broadcasted_iota(jnp.int32, (count, LANES), 1)
    comb = jnp.where(lane == info[plan.cands], comb_s[...], 0.0).astype(BF)
    for d in range(inner):
        backs[d][:, width:] = comb[d * rows : (d + 1) * rows]


def weight_kernel(plan, own, *refs):
    inner, width, hidden = plan.inner, plan.width, plan.hidden
    part, counts = hidden // 2, [inner * r for r in plan.rows]
    got = refs[: 2 * inner]
    mids = refs[2 * inner : 2 * inner + 6]
    at = 2 * inner + 6
    theirs = refs[at : at + 3] if own else None
    at += 3 if own else 0
    g_o, u_o, d_o = refs[at : at + 3]
    x_s, d_s, h_s, gu_s, sems = refs[at + 3 :]
    x_copies, d_copies = [], []
    start = 0
    for c in range(2):
        rows = plan.rows[c]
        for d in range(inner):
            g, to = got[c * inner + d], pl.ds(start, rows)
            i = c * inner + d
            x_copies.append(pltpu.make_async_copy(g.at[pl.ds(0, rows)], x_s.at[to], sems.at[i]))
            d_copies.append(
                pltpu.make_async_copy(g.at[pl.ds(rows, rows)], d_s.at[to], sems.at[2 * inner + i])
            )
            start += rows
    m_copies = []
    half = pl.ds(0 if own else part, part)
    for c in range(2):
        to = pl.ds(0 if c == 0 else counts[0], counts[c])
        hid, gate, up = mids[3 * c : 3 * c + 3]
        spots = (h_s.at[to], gu_s.at[to, pl.ds(0, part)], gu_s.at[to, pl.ds(part, part)])
        for i, (m, s) in enumerate(zip((hid, gate, up), spots)):
            m_copies.append(
                pltpu.make_async_copy(m.at[:, half], s, sems.at[4 * inner + 3 * c + i])
            )
    everything = x_copies + m_copies + d_copies
    for c in everything:
        c.start()
    for c in everything:
        c.wait()
    tile = 256

    @pl.loop(0, width // tile)
    def _(j):
        to = pl.ds(pl.multiple_of(j * tile, tile), tile)
        both = lax.dot_general(x_s[:, to], gu_s[...], TN, preferred_element_type=F32)
        first, second = both[:, :part], both[:, part:]
        if own:
            first += theirs[0][0, to, :].astype(F32)
            second += theirs[1][0, to, :].astype(F32)
        g_o[0, to, :] = first.astype(BF)
        u_o[0, to, :] = second.astype(BF)

    @pl.loop(0, width // tile)
    def _(j):
        to = pl.ds(pl.multiple_of(j * tile, tile), tile)
        down = lax.dot_general(h_s[...], d_s[:, to], TN, preferred_element_type=F32)
        if own:
            down += theirs[2][0, :, to].astype(F32)
        d_o[0, :, to] = down.astype(BF)


def spread_kernel(plan, *refs):
    inner, outer, tok, width = plan.inner, plan.outer, plan.tok, plan.width
    info, key_ref = refs[:2]
    blocks = refs[2 : 2 + plan.cands]
    backs = refs[2 + plan.cands : 2 + plan.cands + 2 * inner]
    outs = refs[2 + plan.cands + 2 * inner :][:outer]
    held, metas, pick_s, sems, meta_sems = refs[2 + plan.cands + 2 * inner + outer :]
    copies, start = [], 0
    for i, b in enumerate(blocks):
        copies.append(
            pltpu.make_async_copy(b.at[:, pl.ds(2 * width, LANES)], metas.at[i], meta_sems.at[i])
        )
    later = []
    for i, b in enumerate(backs):
        rows = plan.rows[i // inner]
        later.append(pltpu.make_async_copy(b, held.at[pl.ds(start, rows)], sems.at[i]))
        start += rows
    for c in copies + later:
        c.start()
    for c in copies:
        c.wait()
    experts = [info[plan.cands + d] for d in range(inner)]
    for r in range(outer):
        total = None
        for i in [0] if r == 0 else [outer - 1 + r, outer - r]:
            one, _ = picks(
                plan, metas[i].astype(F32), info[i], experts, key_ref[...], False
            )
            total = one if total is None else total + one
        pick_s[r * tok : (r + 1) * tok, :] = total.astype(BF)
    for c in later:
        c.wait()
    tile = 256

    def piece(at, size):
        sums = jnp.dot(pick_s[...], held[:, pl.ds(at, size)], preferred_element_type=F32)
        sums = sums.astype(BF)
        for r in range(outer):
            outs[r][:, pl.ds(at, size)] = sums[r * tok : (r + 1) * tok]

    @pl.loop(0, width // tile)
    def _(j):
        piece(pl.multiple_of(j * tile, tile), tile)

    piece(width, LANES)


def home_kernel(plan, *refs):
    parts, (routes_ref, comb_ref, tok_o, comb_o) = refs[: plan.outer], refs[plan.outer :]
    width, tok = plan.width, plan.tok
    total = parts[0][...].astype(F32)
    for p in parts[1:]:
        total += p[...].astype(F32)
    tok_o[...] = total[:, :width].astype(BF)
    found = total[:, width:]
    lane = lax.broadcasted_iota(jnp.int32, (tok, LANES), 1)
    slot = lax.broadcasted_iota(jnp.int32, (tok, plan.top), 1)
    out = jnp.zeros((tok, plan.top), F32)
    for k in range(plan.top):
        mine = jnp.where(lane == routes_ref[:, k : k + 1], found, 0.0)
        out = jnp.where(slot == k, jnp.sum(mine, axis=1, keepdims=True), out)
    comb_o[...] = (out / comb_ref[...].astype(F32)).astype(BF)


def on_device(plan, tokens, routes, combine, upstream, w_gate, w_up, w_down):
    tok, width, hidden = plan.tok, plan.width, plan.hidden
    inner, outer, part = plan.inner, plan.outer, plan.hidden // 2
    full = 2 * width + LANES
    shape = jax.ShapeDtypeStruct
    info = jnp.asarray(plan.table())[lax.axis_index("expert")]
    keys = [jnp.asarray(k) for k in plan.keys]
    swap = [(0, 1), (1, 0)]

    block = pl.pallas_call(
        functools.partial(pack_kernel, plan),
        out_shape=shape((tok, full), BF),
        in_specs=[VMEM] * 4,
        out_specs=VMEM,
        compiler_params=params(16),
        cost_estimate=cost(1e6, 4 * tok * full),
        name="pack",
    )(tokens, upstream, routes, combine)

    below, above = [block], [block]
    for _ in range(outer - 1):
        below.append(lax.ppermute(below[-1], "expert", plan.line(1)))
        above.append(lax.ppermute(above[-1], "expert", plan.line(-1)))
    blocks = [block] + below[1:] + above[1:]

    weights = []
    for w in (w_gate, w_up, w_down):
        weights += [w, lax.ppermute(w, "dp", swap)]

    got, mids, backs = [], [], []
    for c in range(2):
        rows, use = plan.rows[c], plan.use[c]
        count, n = inner * rows, len(use)
        sent = pl.pallas_call(
            functools.partial(compact_kernel, plan, c),
            out_shape=[shape((2 * rows, width), BF)] * inner,
            in_specs=[SMEM, VMEM] + [ANY] * n,
            out_specs=[VMEM] * inner,
            scratch_shapes=[
                pltpu.VMEM((n * tok, full), BF),
                pltpu.VMEM((n * tok, count), BF),
                pltpu.VMEM((n * tok, count), BF),
                pltpu.SemaphoreType.DMA((n,)),
            ],
            compiler_params=params(40),
            cost_estimate=cost(4 * n * tok * count * width, 2 * n * tok * full),
            name="compact",
        )(info, keys[c], *[blocks[i] for i in use])
        arrived = [sent[0]] + [
            lax.ppermute(sent[d], "expert", plan.across(d)) for d in range(1, inner)
        ]
        outs = pl.pallas_call(
            functools.partial(expert_kernel, plan, c),
            out_shape=[shape((count, hidden), BF)] * 3
            + [shape((rows, width + LANES), BF)] * inner,
            in_specs=[SMEM] + [ANY] * (inner + 6),
            out_specs=[VMEM] * (3 + inner),
            scratch_shapes=[
                pltpu.VMEM((count, width), BF),
                pltpu.VMEM((count, width), BF),
                pltpu.VMEM((width, hidden), BF),
                pltpu.VMEM((width, hidden), BF),
                pltpu.VMEM((hidden, width), BF),
                pltpu.VMEM((count, 1), F32),
                pltpu.SemaphoreType.DMA((2 * inner + 6,)),
            ],
            compiler_params=params(44),
            cost_estimate=cost(10 * count * hidden * width, 6 * hidden * width),
            name="expert",
        )(info, *arrived, *weights)
        got += arrived
        mids += outs[:3]
        backs += [outs[3]] + [
            lax.ppermute(outs[3 + d], "expert", plan.across(d)) for d in range(1, inner)
        ]

    count = inner * sum(plan.rows)

    def weight_grads(own, extra):
        return pl.pallas_call(
            functools.partial(weight_kernel, plan, own),
            out_shape=[
                shape((1, width, part), BF),
                shape((1, width, part), BF),
                shape((1, part, width), BF),
            ],
            in_specs=[ANY] * (2 * inner + 6) + [VMEM] * len(extra),
            out_specs=[VMEM] * 3,
            scratch_shapes=[
                pltpu.VMEM((count, width), BF),
                pltpu.VMEM((count, width), BF),
                pltpu.VMEM((count, part), BF),
                pltpu.VMEM((count, 2 * part), BF),
                pltpu.SemaphoreType.DMA((4 * inner + 6,)),
            ],
            compiler_params=params(44),
            cost_estimate=cost(6 * count * part * width, 4 * count * (width + hidden)),
            name="weight_grads",
        )(*got, *mids, *extra)

    theirs = [lax.ppermute(w, "dp", swap) for w in weight_grads(False, [])]
    grads = weight_grads(True, theirs)

    sums = pl.pallas_call(
        functools.partial(spread_kernel, plan),
        out_shape=[shape((tok, width + LANES), BF)] * outer,
        in_specs=[SMEM, VMEM] + [ANY] * (plan.cands + 2 * inner),
        out_specs=[VMEM] * outer,
        scratch_shapes=[
            pltpu.VMEM((count, width + LANES), BF),
            pltpu.VMEM((plan.cands, tok, LANES), BF),
            pltpu.VMEM((outer * tok, count), BF),
            pltpu.SemaphoreType.DMA((2 * inner,)),
            pltpu.SemaphoreType.DMA((plan.cands,)),
        ],
        compiler_params=params(32),
        cost_estimate=cost(2 * outer * tok * count * width, 2 * count * width),
        name="spread",
    )(info, jnp.concatenate(keys, axis=1), *blocks, *backs)
    home = [sums[0]] + [lax.ppermute(sums[r], "expert", plan.shift(r)) for r in range(1, outer)]
    grad_tokens, grad_combine = pl.pallas_call(
        functools.partial(home_kernel, plan),
        out_shape=[shape((tok, width), BF), shape((tok, plan.top), BF)],
        in_specs=[VMEM] * (outer + 2),
        out_specs=[VMEM] * 2,
        compiler_params=params(16),
        cost_estimate=cost(1e6, 2 * tok * width * (outer + 1)),
        name="home",
    )(*home, routes, combine)
    return (grad_tokens, grad_combine, *grads)


def solution(mesh):
    rows = P(("parts", "dp", "expert"), None)
    in_specs = (rows,) * 4 + (P("expert", None, "dp"),) * 2 + (P("expert", "dp", None),)
    out_specs = (rows,) * 2 + (P(("parts", "expert"), None, "dp"),) * 2
    out_specs += (P(("parts", "expert"), "dp", None),)
    shape = dict(mesh.shape)

    def whole(tokens, routes, combine, upstream, w_gate, w_up, w_down):
        devices = shape["parts"] * shape["dp"] * shape["expert"]
        plan = Plan(
            shape["expert"],
            tokens.shape[0] // devices,
            routes.shape[1],
            tokens.shape[1],
            w_gate.shape[2],
        )
        body = functools.partial(on_device, plan)
        return jax.shard_map(
            body, mesh=mesh, in_specs=in_specs, out_specs=out_specs, check_vma=False
        )(tokens, routes, combine, upstream, w_gate, w_up, w_down)

    return whole
```

time: 321 us -> 230 us (0.72)
  the two profiles are of different devices: /device:TPU:12 before, /device:TPU:0 now
where the time goes in v1:
time: 230 us; the launch traced here: 229 us
  waiting for transfers between devices  104 us (45%)
  Pallas kernels  59.8 us (26%)
  starting transfers between devices  37 us (16%)
  local copies, waits for them, and re-layouts  27 us (12%)
    ppermute x6, waiting for transfers between devices, on_device(): lax.ppermute(outs[3 + d], 'expert', plan.across(d))  28.8 us
    ppermute x6, waiting for transfers between devices, on_device(): lax.ppermute(sent[d], 'expert', plan.across(d))  28.6 us
    unnamed x93, local copies, waits for them, and re-layouts  26.3 us
    ppermute x3, waiting for transfers between devices, on_device(): lax.ppermute(sums[r], 'expert', plan.shift(r))  24.1 us
    pallas_call x2, Pallas kernels, weight_grads(): pl.pallas_call(functools.partial(weight_kernel, plan, own), out_shape=[sh...  22.7 us
    pallas_call x2, Pallas kernels, on_device(): pl.pallas_call(functools.partial(expert_kernel, plan, c), out_shape=[shap...  22.7 us
    ppermute x3, waiting for transfers between devices, on_device(): above.append(lax.ppermute(above[-1], 'expert', plan.line(-1)))  21.5 us
    ppermute x3, starting transfers between devices, on_device(): below.append(lax.ppermute(below[-1], 'expert', plan.line(1)))  15.2 us
  transfers between devices with their start and end apart: 27, of which 14 were waited for; matrix products, arithmetic and copies ran while one was open for 1% of the time, Pallas kernels for 19%

profile of v1, /device:TPU:0, one launch (start us, length us, event | category | flops | bytes accessed | tf_op | source)
XLA Modules:
  0.0 229.0 jit_solution(12432117383152514630)
XLA Ops:
  5.7 5.6 %collective-permute-start = (bf16[64,4224]{1,0:T(8,128)(2,1)S(1)}, bf16[64,4224]{1,0:T(8,128)(2,1)S(1)}, u32[]{:S(2)}, u32[]{:S(2)}) collective-permute-start(bf16[64,4224]{1,0:T(8,128)(2,1)S(1)} %pack.1.refs_2_), channel_id=1, source_target_pairs={{0,4},{1,5},{2,6},{3,7},{4,8},{5,9},{6,10},{7,11},{8,12},{9,13},{1... | collective-permute-start | bytes 1622024 | tf_op jit(solution)/shard_map/ppermute | solution.py:380
  12.0 9.6 %collective-permute-done.3.refs_4_.refs_6_ = bf16[64,4224]{1,0:T(8,128)(2,1)S(1)} collective-permute-done((bf16[64,4224]{1,0:T(8,128)(2,1)S(1)}, bf16[64,4224]{1,0:T(8,128)(2,1)S(1)}, u32[]{:S(2)}, u32[]{:S(2)}) %collective-permute-start.3) | collective-permute-done | bytes 540704 | tf_op jit(solution)/shard_map/ppermute | solution.py:381
  23.5 3.2 %compact.2 = (bf16[128,2048]{1,0:T(8,128)(2,1)S(1)}, bf16[128,2048]{1,0:T(8,128)(2,1)S(1)}, bf16[128,2048]{1,0:T(8,128)(2,1)S(1)}, bf16[128,2048]{1,0:T(8,128)(2,1)S(1)}) custom-call(s32[11]{0:T(128)S(1)} %dynamic-slice_bitcast_fusion.refs_0_, s32[1,256]{1,0:T(1,128)S(1)} %copy-done.31, bf16[64,4224]{1,0:T(8,128)(2,1)S(1)} %pack.1.refs_2_, ...), custom_call_target="tpu_custom_call" | custom-call | flops 402653184 | bytes 1622016 | tf_op jit(solution)/shard_map/compact/pallas_call | solution.py:392
  29.7 5.0 %collective-permute-start.1 = (bf16[64,4224]{1,0:T(8,128)(2,1)S(1)}, bf16[64,4224]{1,0:T(8,128)(2,1)S(1)}, u32[]{:S(2)}, u32[]{:S(2)}) collective-permute-start(bf16[64,4224]{1,0:T(8,128)(2,1)S(1)} %collective-permute-done.refs_3_), channel_id=1, source_target_pairs={{0,4},{1,5},{2,6},{3,7},{4,8},{5,9},{6,10},{7,11},{8,12},{9,13},{1... | collective-permute-start | bytes 1622024 | tf_op jit(solution)/shard_map/ppermute | solution.py:380
  35.4 4.2 %collective-permute-done.6.refs_2_.refs_1_ = bf16[128,2048]{1,0:T(8,128)(2,1)S(1)} collective-permute-done((bf16[128,2048]{1,0:T(8,128)(2,1)S(1)}, bf16[128,2048]{1,0:T(8,128)(2,1)S(1)}, u32[]{:S(2)}, u32[]{:S(2)}) %collective-permute-start.6) | collective-permute-done | bytes 524320 | tf_op jit(solution)/shard_map/ppermute | solution.py:408
  39.6 4.0 %collective-permute-done.4.refs_7_ = bf16[64,4224]{1,0:T(8,128)(2,1)S(1)} collective-permute-done((bf16[64,4224]{1,0:T(8,128)(2,1)S(1)}, bf16[64,4224]{1,0:T(8,128)(2,1)S(1)}, u32[]{:S(2)}, u32[]{:S(2)}) %collective-permute-start.4) | collective-permute-done | bytes 540704 | tf_op jit(solution)/shard_map/ppermute | solution.py:381
  44.9 4.6 %collective-permute-start.2 = (bf16[64,4224]{1,0:T(8,128)(2,1)S(1)}, bf16[64,4224]{1,0:T(8,128)(2,1)S(1)}, u32[]{:S(2)}, u32[]{:S(2)}) collective-permute-start(bf16[64,4224]{1,0:T(8,128)(2,1)S(1)} %collective-permute-done.1.refs_4_), channel_id=1, source_target_pairs={{0,4},{1,5},{2,6},{3,7},{4,8},{5,9},{6,10},{7,11},{8,12},{9,13},{1... | collective-permute-start | bytes 1622024 | tf_op jit(solution)/shard_map/ppermute | solution.py:380
  49.5 7.9 %collective-permute-done.5.refs_8_ = bf16[64,4224]{1,0:T(8,128)(2,1)S(1)} collective-permute-done((bf16[64,4224]{1,0:T(8,128)(2,1)S(1)}, bf16[64,4224]{1,0:T(8,128)(2,1)S(1)}, u32[]{:S(2)}, u32[]{:S(2)}) %collective-permute-start.5) | collective-permute-done | bytes 540704 | tf_op jit(solution)/shard_map/ppermute | solution.py:381
  60.4 5.0 %compact.3 = (bf16[160,2048]{1,0:T(8,128)(2,1)S(1)}, bf16[160,2048]{1,0:T(8,128)(2,1)S(1)}, bf16[160,2048]{1,0:T(8,128)(2,1)S(1)}, bf16[160,2048]{1,0:T(8,128)(2,1)S(1)}) custom-call(s32[11]{0:T(128)S(1)} %dynamic-slice_bitcast_fusion.refs_0_, s32[1,320]{1,0:T(1,128)S(1)} %copy-done.42, bf16[64,4224]{1,0:T(8,128)(2,1)S(1)} %pack.1.refs_2_, ...), custom_call_target="tpu_custom_call" | custom-call | flops 1174405120 | bytes 3784704 | tf_op jit(solution)/shard_map/compact/pallas_call | solution.py:392
  65.4 13.8 %collective-permute-done.7.refs_3_.refs_2_ = bf16[128,2048]{1,0:T(8,128)(2,1)S(1)} collective-permute-done((bf16[128,2048]{1,0:T(8,128)(2,1)S(1)}, bf16[128,2048]{1,0:T(8,128)(2,1)S(1)}, u32[]{:S(2)}, u32[]{:S(2)}) %collective-permute-start.7) | collective-permute-done | bytes 524320 | tf_op jit(solution)/shard_map/ppermute | solution.py:408
  89.0 10.9 %expert.2 = (bf16[256,768]{1,0:T(8,128)(2,1)S(1)}, bf16[256,768]{1,0:T(8,128)(2,1)S(1)}, bf16[256,768]{1,0:T(8,128)(2,1)S(1)}, bf16[64,2176]{1,0:T(8,128)(2,1)S(...) custom-call(s32[11]{0:T(128)S(1)} %dynamic-slice_bitcast_fusion.refs_0_, ...), custom_call_target="tpu_custom_call" | custom-call | flops 4026531840 | bytes 9437184 | tf_op jit(solution)/shard_map/expert/pallas_call | solution.py:410
  101.4 4.4 %collective-permute-done.16.refs_3_.refs_6_ = bf16[160,2048]{1,0:T(8,128)(2,1)S(1)} collective-permute-done((bf16[160,2048]{1,0:T(8,128)(2,1)S(1)}, bf16[160,2048]{1,0:T(8,128)(2,1)S(1)}, u32[]{:S(2)}, u32[]{:S(2)}) %collective-permute-start.16) | collective-permute-done | bytes 655392 | tf_op jit(solution)/shard_map/ppermute | solution.py:408
  105.8 6.1 %collective-permute-done.17.refs_4_.refs_7_ = bf16[160,2048]{1,0:T(8,128)(2,1)S(1)} collective-permute-done((bf16[160,2048]{1,0:T(8,128)(2,1)S(1)}, bf16[160,2048]{1,0:T(8,128)(2,1)S(1)}, u32[]{:S(2)}, u32[]{:S(2)}) %collective-permute-start.17) | collective-permute-done | bytes 655392 | tf_op jit(solution)/shard_map/ppermute | solution.py:408
  113.6 11.7 %expert.3 = (bf16[320,768]{1,0:T(8,128)(2,1)S(1)}, bf16[320,768]{1,0:T(8,128)(2,1)S(1)}, bf16[320,768]{1,0:T(8,128)(2,1)S(1)}, bf16[80,2176]{1,0:T(8,128)(2,1)S(...) custom-call(s32[11]{0:T(128)S(1)} %dynamic-slice_bitcast_fusion.refs_0_, ...), custom_call_target="tpu_custom_call" | custom-call | flops 5033164800 | bytes 9437184 | tf_op jit(solution)/shard_map/expert/pallas_call | solution.py:410
  125.5 10.4 %weight_grads.2 = (bf16[1,2048,384]{2,1,0:T(8,128)(2,1)}, bf16[1,2048,384]{2,1,0:T(8,128)(2,1)}, bf16[1,384,2048]{2,1,0:T(8,128)(2,1)}) custom-call(bf16[128,2048]{1,0:T(8,128)(2,1)S(1)} %get-tuple-element.39.refs_1_.refs_0_, bf16[128,2048]{1,0:T(8,128)(2,1)S(1)} %collective-permute-done.6.refs_2_.refs_1_, ...), custom_call_target="tpu_custom_call" | custom-call | flops 2717908992 | bytes 6488064 | tf_op jit(solution)/shard_map/weight_grads/pallas_call | solution.py:438
  138.4 7.2 %collective-permute-done.13.refs_11_ = bf16[64,2176]{1,0:T(8,128)(2,1)S(1)} collective-permute-done((bf16[64,2176]{1,0:T(8,128)(2,1)S(1)}, bf16[64,2176]{1,0:T(8,128)(2,1)S(1)}, u32[]{:S(2)}, u32[]{:S(2)}) %collective-permute-start.13) | collective-permute-done | bytes 278560 | tf_op jit(solution)/shard_map/ppermute | solution.py:432
  146.9 7.9 %collective-permute-done.14.refs_12_ = bf16[64,2176]{1,0:T(8,128)(2,1)S(1)} collective-permute-done((bf16[64,2176]{1,0:T(8,128)(2,1)S(1)}, bf16[64,2176]{1,0:T(8,128)(2,1)S(1)}, u32[]{:S(2)}, u32[]{:S(2)}) %collective-permute-start.14) | collective-permute-done | bytes 278560 | tf_op jit(solution)/shard_map/ppermute | solution.py:432
  155.1 2.3 %collective-permute-start.20 = (bf16[80,2176]{1,0:T(8,128)(2,1)S(1)}, bf16[80,2176]{1,0:T(8,128)(2,1)S(1)}, u32[]{:S(2)}, u32[]{:S(2)}) collective-permute-start(bf16[80,2176]{1,0:T(8,128)(2,1)S(1)} %get-tuple-element.54), channel_id=1, source_target_pairs={{0,3},{1,2},{2,1},{3,0},{4,7},{5,6},{6,5},{7,4},{8,11},{9,10},{10,... | collective-permute-start | bytes 1044488 | tf_op jit(solution)/shard_map/ppermute | solution.py:432
  157.4 13.7 %collective-permute-done.19.refs_15_ = bf16[80,2176]{1,0:T(8,128)(2,1)S(1)} collective-permute-done((bf16[80,2176]{1,0:T(8,128)(2,1)S(1)}, bf16[80,2176]{1,0:T(8,128)(2,1)S(1)}, u32[]{:S(2)}, u32[]{:S(2)}) %collective-permute-start.19) | collective-permute-done | bytes 348192 | tf_op jit(solution)/shard_map/ppermute | solution.py:432
  171.0 4.4 %spread.1 = (bf16[64,2176]{1,0:T(8,128)(2,1)S(1)}, bf16[64,2176]{1,0:T(8,128)(2,1)S(1)}, bf16[64,2176]{1,0:T(8,128)(2,1)S(1)}, bf16[64,2176]{1,0:T(8,128)(2,1)S(1)}) custom-call(s32[11]{0:T(128)S(1)} %dynamic-slice_bitcast_fusion.refs_0_, s32[1,576]{1,0:T(1,128)S(1)} %copy-done.30, bf16[64,4224]{1,0:T(8,128)(2,1)S(1)} %pack.1.refs_2_, ...), custom_call_target="tpu_custom_call" | custom-call | flops 603979776 | bytes 2359296 | tf_op jit(solution)/shard_map/spread/pallas_call | solution.py:462
  177.0 10.0 %collective-permute-done.21.refs_1_ = bf16[64,2176]{1,0:T(8,128)(2,1)S(1)} collective-permute-done((bf16[64,2176]{1,0:T(8,128)(2,1)S(1)}, bf16[64,2176]{1,0:T(8,128)(2,1)S(1)}, u32[]{:S(2)}, u32[]{:S(2)}) %collective-permute-start.21) | collective-permute-done | bytes 278560 | tf_op jit(solution)/shard_map/ppermute | solution.py:478
  187.0 10.0 %collective-permute-done.22.refs_2_ = bf16[64,2176]{1,0:T(8,128)(2,1)S(1)} collective-permute-done((bf16[64,2176]{1,0:T(8,128)(2,1)S(1)}, bf16[64,2176]{1,0:T(8,128)(2,1)S(1)}, u32[]{:S(2)}, u32[]{:S(2)}) %collective-permute-start.22) | collective-permute-done | bytes 278560 | tf_op jit(solution)/shard_map/ppermute | solution.py:478
  197.0 4.1 %collective-permute-done.23.refs_3_ = bf16[64,2176]{1,0:T(8,128)(2,1)S(1)} collective-permute-done((bf16[64,2176]{1,0:T(8,128)(2,1)S(1)}, bf16[64,2176]{1,0:T(8,128)(2,1)S(1)}, u32[]{:S(2)}, u32[]{:S(2)}) %collective-permute-start.23) | collective-permute-done | bytes 278560 | tf_op jit(solution)/shard_map/ppermute | solution.py:478
  216.7 12.3 %weight_grads.3 = (bf16[1,2048,384]{2,1,0:T(8,128)(2,1)}, bf16[1,2048,384]{2,1,0:T(8,128)(2,1)}, bf16[1,384,2048]{2,1,0:T(8,128)(2,1)}) custom-call(bf16[128,2048]{1,0:T(8,128)(2,1)S(1)} %copy-done.9, bf16[128,2048]{1,0:T(8,128)(2,1)S(1)} %copy-done.11, bf16[128,2048]{1,0:T(8,128)(2,1)S(1)} %copy-done.13, bf16[128,2048]{1,0:T(8,128)(2,1)S(1)} %copy-done.15, ...), custom_call_target="tpu_custom_call" | custom-call | flops 2717908992 | bytes 6488064 | tf_op jit(solution)/shard_map/weight_grads/pallas_call | solution.py:438
  (133 shorter events, 49.5 us)
Async XLA Ops:
  4.4 17.2 %collective-permute-start.3 = (bf16[64,4224]{1,0:T(8,128)(2,1)S(1)}, bf16[64,4224]{1,0:T(8,128)(2,1)S(1)}, u32[]{:S(2)}, u32[]{:S(2)}) collective-permute-start(bf16[64,4224]{1,0:T(8,128)(2,1)S(1)} %pack.1.refs_2_), channel_id=1, source_target_pairs={{4,0},{5,1},{6,2},{7,3},{8,4},{9,5},{10,6},{11,7},{12,8},{13,9},{1... | collective-permute-start | bytes 1622024 | tf_op jit(solution)/shard_map/ppermute | solution.py:381
  5.7 17.1 %collective-permute-start = (bf16[64,4224]{1,0:T(8,128)(2,1)S(1)}, bf16[64,4224]{1,0:T(8,128)(2,1)S(1)}, u32[]{:S(2)}, u32[]{:S(2)}) collective-permute-start(bf16[64,4224]{1,0:T(8,128)(2,1)S(1)} %pack.1.refs_2_), channel_id=1, source_target_pairs={{0,4},{1,5},{2,6},{3,7},{4,8},{5,9},{6,10},{7,11},{8,12},{9,13},{1... | collective-permute-start | bytes 1622024 | tf_op jit(solution)/shard_map/ppermute | solution.py:380
  26.7 12.9 %collective-permute-start.6 = (bf16[128,2048]{1,0:T(8,128)(2,1)S(1)}, bf16[128,2048]{1,0:T(8,128)(2,1)S(1)}, u32[]{:S(2)}, u32[]{:S(2)}) collective-permute-start(bf16[128,2048]{1,0:T(8,128)(2,1)S(1)} %get-tuple-element.40), channel_id=1, source_target_pairs={{0,1},{1,0},{2,3},{3,2},{4,5},{5,4},{6,7},{7,6},{8,9},{9,8},{10,11... | collective-permute-start | bytes 1572872 | tf_op jit(solution)/shard_map/ppermute | solution.py:408
  28.4 15.2 %collective-permute-start.4 = (bf16[64,4224]{1,0:T(8,128)(2,1)S(1)}, bf16[64,4224]{1,0:T(8,128)(2,1)S(1)}, u32[]{:S(2)}, u32[]{:S(2)}) collective-permute-start(bf16[64,4224]{1,0:T(8,128)(2,1)S(1)} %collective-permute-done.3.refs_4_.refs_6_), channel_id=1, source_target_pairs={{4,0},{5,1},{6,2},{7,3},{8,4},{9,5},{10,6},{11,7},{12,8},{13,9},{1... | collective-permute-start | bytes 1622024 | tf_op jit(solution)/shard_map/ppermute | solution.py:381
  29.7 15.2 %collective-permute-start.1 = (bf16[64,4224]{1,0:T(8,128)(2,1)S(1)}, bf16[64,4224]{1,0:T(8,128)(2,1)S(1)}, u32[]{:S(2)}, u32[]{:S(2)}) collective-permute-start(bf16[64,4224]{1,0:T(8,128)(2,1)S(1)} %collective-permute-done.refs_3_), channel_id=1, source_target_pairs={{0,4},{1,5},{2,6},{3,7},{4,8},{5,9},{6,10},{7,11},{8,12},{9,13},{1... | collective-permute-start | bytes 1622024 | tf_op jit(solution)/shard_map/ppermute | solution.py:380
  34.8 47.2 %collective-permute-start.9 = (bf16[1,2048,384]{2,1,0:T(8,128)(2,1)S(1)}, bf16[1,2048,384]{2,1,0:T(8,128)(2,1)S(1)}, u32[]{:S(2)}, u32[]{:S(2)}) collective-permute-start(bf16[1,2048,384]{2,1,0:T(8,128)(2,1)S(1)} %copy-done.32), channel_id=1, source_target_pairs={{0,16},{16,0},{1,17},{17,1},{2,18},{18,2},{3,19},{19,3},{4,20},{20... | collective-permute-start | bytes 4718600 | tf_op jit(solution)/shard_map/ppermute | solution.py:386
  34.9 49.0 %collective-permute-start.10 = (bf16[1,2048,384]{2,1,0:T(8,128)(2,1)}, bf16[1,2048,384]{2,1,0:T(8,128)(2,1)S(1)}, u32[]{:S(2)}, u32[]{:S(2)}) collective-permute-start(bf16[1,2048,384]{2,1,0:T(8,128)(2,1)} %refs_7_.3), channel_id=1, source_target_pairs={{0,16},{16,0},{1,17},{17,1},{2,18},{18,2},{3,19},{19,3},{4,20},{20... | collective-permute-start | bytes 4718600 | tf_op jit(solution)/shard_map/ppermute | solution.py:386
  39.6 44.3 %collective-permute-start.11 = (bf16[1,384,2048]{2,1,0:T(8,128)(2,1)}, bf16[1,384,2048]{2,1,0:T(8,128)(2,1)S(1)}, u32[]{:S(2)}, u32[]{:S(2)}) collective-permute-start(bf16[1,384,2048]{2,1,0:T(8,128)(2,1)} %refs_9_.3), channel_id=1, source_target_pairs={{0,16},{16,0},{1,17},{17,1},{2,18},{18,2},{3,19},{19,3},{4,20},{20... | collective-permute-start | bytes 4718600 | tf_op jit(solution)/shard_map/ppermute | solution.py:386
  43.6 13.8 %collective-permute-start.5 = (bf16[64,4224]{1,0:T(8,128)(2,1)S(1)}, bf16[64,4224]{1,0:T(8,128)(2,1)S(1)}, u32[]{:S(2)}, u32[]{:S(2)}) collective-permute-start(bf16[64,4224]{1,0:T(8,128)(2,1)S(1)} %collective-permute-done.4.refs_7_), channel_id=1, source_target_pairs={{4,0},{5,1},{6,2},{7,3},{8,4},{9,5},{10,6},{11,7},{12,8},{13,9},{1... | collective-permute-start | bytes 1622024 | tf_op jit(solution)/shard_map/ppermute | solution.py:381
  44.9 14.0 %collective-permute-start.2 = (bf16[64,4224]{1,0:T(8,128)(2,1)S(1)}, bf16[64,4224]{1,0:T(8,128)(2,1)S(1)}, u32[]{:S(2)}, u32[]{:S(2)}) collective-permute-start(bf16[64,4224]{1,0:T(8,128)(2,1)S(1)} %collective-permute-done.1.refs_4_), channel_id=1, source_target_pairs={{0,4},{1,5},{2,6},{3,7},{4,8},{5,9},{6,10},{7,11},{8,12},{9,13},{1... | collective-permute-start | bytes 1622024 | tf_op jit(solution)/shard_map/ppermute | solution.py:380
  57.4 21.9 %collective-permute-start.7 = (bf16[128,2048]{1,0:T(8,128)(2,1)S(1)}, bf16[128,2048]{1,0:T(8,128)(2,1)S(1)}, u32[]{:S(2)}, u32[]{:S(2)}) collective-permute-start(bf16[128,2048]{1,0:T(8,128)(2,1)S(1)} %get-tuple-element.41), channel_id=1, source_target_pairs={{0,2},{1,3},{2,0},{3,1},{4,6},{5,7},{6,4},{7,5},{8,10},{9,11},{10,... | collective-permute-start | bytes 1572872 | tf_op jit(solution)/shard_map/ppermute | solution.py:408
  58.9 21.7 %collective-permute-start.8 = (bf16[128,2048]{1,0:T(8,128)(2,1)S(1)}, bf16[128,2048]{1,0:T(8,128)(2,1)S(1)}, u32[]{:S(2)}, u32[]{:S(2)}) collective-permute-start(bf16[128,2048]{1,0:T(8,128)(2,1)S(1)} %get-tuple-element.42), channel_id=1, source_target_pairs={{0,3},{1,2},{2,1},{3,0},{4,7},{5,6},{6,5},{7,4},{8,11},{9,10},{10,... | collective-permute-start | bytes 1572872 | tf_op jit(solution)/shard_map/ppermute | solution.py:408
  79.3 22.1 %collective-permute-start.15 = (bf16[160,2048]{1,0:T(8,128)(2,1)S(1)}, bf16[160,2048]{1,0:T(8,128)(2,1)S(1)}, u32[]{:S(2)}, u32[]{:S(2)}) collective-permute-start(bf16[160,2048]{1,0:T(8,128)(2,1)S(1)} %get-tuple-element.48), channel_id=1, source_target_pairs={{0,1},{1,0},{2,3},{3,2},{4,5},{5,4},{6,7},{7,6},{8,9},{9,8},{10,11... | collective-permute-start | bytes 1966088 | tf_op jit(solution)/shard_map/ppermute | solution.py:408
  80.6 25.2 %collective-permute-start.16 = (bf16[160,2048]{1,0:T(8,128)(2,1)S(1)}, bf16[160,2048]{1,0:T(8,128)(2,1)S(1)}, u32[]{:S(2)}, u32[]{:S(2)}) collective-permute-start(bf16[160,2048]{1,0:T(8,128)(2,1)S(1)} %get-tuple-element.49), channel_id=1, source_target_pairs={{0,2},{1,3},{2,0},{3,1},{4,6},{5,7},{6,4},{7,5},{8,10},{9,11},{10,... | collective-permute-start | bytes 1966088 | tf_op jit(solution)/shard_map/ppermute | solution.py:408
  83.1 28.8 %collective-permute-start.17 = (bf16[160,2048]{1,0:T(8,128)(2,1)S(1)}, bf16[160,2048]{1,0:T(8,128)(2,1)S(1)}, u32[]{:S(2)}, u32[]{:S(2)}) collective-permute-start(bf16[160,2048]{1,0:T(8,128)(2,1)S(1)} %get-tuple-element.50), channel_id=1, source_target_pairs={{0,3},{1,2},{2,1},{3,0},{4,7},{5,6},{6,5},{7,4},{8,11},{9,10},{10,... | collective-permute-start | bytes 1966088 | tf_op jit(solution)/shard_map/ppermute | solution.py:408
  100.0 36.9 %collective-permute-start.12 = (bf16[64,2176]{1,0:T(8,128)(2,1)}, bf16[64,2176]{1,0:T(8,128)(2,1)}, u32[]{:S(2)}, u32[]{:S(2)}) collective-permute-start(bf16[64,2176]{1,0:T(8,128)(2,1)} %get-tuple-element.44), channel_id=1, source_target_pairs={{0,1},{1,0},{2,3},{3,2},{4,5},{5,4},{6,7},{7,6},{8,9},{9,8},{10,11... | collective-permute-start | bytes 835592 | tf_op jit(solution)/shard_map/ppermute | solution.py:432
  136.0 67.2 %collective-permute-start.24 = (bf16[1,2048,384]{2,1,0:T(8,128)(2,1)}, bf16[1,2048,384]{2,1,0:T(8,128)(2,1)S(1)}, u32[]{:S(2)}, u32[]{:S(2)}) collective-permute-start(bf16[1,2048,384]{2,1,0:T(8,128)(2,1)} %get-tuple-element.67), channel_id=1, source_target_pairs={{0,16},{16,0},{1,17},{17,1},{2,18},{18,2},{3,19},{19,3},{4,20},{20... | collective-permute-start | bytes 4718600 | tf_op jit(solution)/shard_map/ppermute | solution.py:459
  136.0 67.1 %collective-permute-start.25 = (bf16[1,2048,384]{2,1,0:T(8,128)(2,1)}, bf16[1,2048,384]{2,1,0:T(8,128)(2,1)}, u32[]{:S(2)}, u32[]{:S(2)}) collective-permute-start(bf16[1,2048,384]{2,1,0:T(8,128)(2,1)} %get-tuple-element.68), channel_id=1, source_target_pairs={{0,16},{16,0},{1,17},{17,1},{2,18},{18,2},{3,19},{19,3},{4,20},{20... | collective-permute-start | bytes 4718600 | tf_op jit(solution)/shard_map/ppermute | solution.py:459
  136.5 66.7 %collective-permute-start.26 = (bf16[1,384,2048]{2,1,0:T(8,128)(2,1)}, bf16[1,384,2048]{2,1,0:T(8,128)(2,1)}, u32[]{:S(2)}, u32[]{:S(2)}) collective-permute-start(bf16[1,384,2048]{2,1,0:T(8,128)(2,1)} %get-tuple-element.69), channel_id=1, source_target_pairs={{0,16},{16,0},{1,17},{17,1},{2,18},{18,2},{3,19},{19,3},{4,20},{20... | collective-permute-start | bytes 4718600 | tf_op jit(solution)/shard_map/ppermute | solution.py:459
  136.9 18.1 %collective-permute-start.18 = (bf16[80,2176]{1,0:T(8,128)(2,1)S(1)}, bf16[80,2176]{1,0:T(8,128)(2,1)S(1)}, u32[]{:S(2)}, u32[]{:S(2)}) collective-permute-start(bf16[80,2176]{1,0:T(8,128)(2,1)S(1)} %get-tuple-element.52), channel_id=1, source_target_pairs={{0,1},{1,0},{2,3},{3,2},{4,5},{5,4},{6,7},{7,6},{8,9},{9,8},{10,11... | collective-permute-start | bytes 1044488 | tf_op jit(solution)/shard_map/ppermute | solution.py:432
  154.8 16.3 %collective-permute-start.19 = (bf16[80,2176]{1,0:T(8,128)(2,1)S(1)}, bf16[80,2176]{1,0:T(8,128)(2,1)S(1)}, u32[]{:S(2)}, u32[]{:S(2)}) collective-permute-start(bf16[80,2176]{1,0:T(8,128)(2,1)S(1)} %get-tuple-element.53), channel_id=1, source_target_pairs={{0,2},{1,3},{2,0},{3,1},{4,6},{5,7},{6,4},{7,5},{8,10},{9,11},{10,... | collective-permute-start | bytes 1044488 | tf_op jit(solution)/shard_map/ppermute | solution.py:432
  155.1 16.0 %collective-permute-start.20 = (bf16[80,2176]{1,0:T(8,128)(2,1)S(1)}, bf16[80,2176]{1,0:T(8,128)(2,1)S(1)}, u32[]{:S(2)}, u32[]{:S(2)}) collective-permute-start(bf16[80,2176]{1,0:T(8,128)(2,1)S(1)} %get-tuple-element.54), channel_id=1, source_target_pairs={{0,3},{1,2},{2,1},{3,0},{4,7},{5,6},{6,5},{7,4},{8,11},{9,10},{10,... | collective-permute-start | bytes 1044488 | tf_op jit(solution)/shard_map/ppermute | solution.py:432
  176.0 20.9 %collective-permute-start.22 = (bf16[64,2176]{1,0:T(8,128)(2,1)S(1)}, bf16[64,2176]{1,0:T(8,128)(2,1)S(1)}, u32[]{:S(2)}, u32[]{:S(2)}) collective-permute-start(bf16[64,2176]{1,0:T(8,128)(2,1)S(1)} %get-tuple-element.57), channel_id=1, source_target_pairs={{0,8},{1,9},{2,10},{3,11},{4,12},{5,13},{6,14},{7,15},{8,0},{9,1},... | collective-permute-start | bytes 835592 | tf_op jit(solution)/shard_map/ppermute | solution.py:478
  187.0 14.1 %collective-permute-start.23 = (bf16[64,2176]{1,0:T(8,128)(2,1)S(1)}, bf16[64,2176]{1,0:T(8,128)(2,1)S(1)}, u32[]{:S(2)}, u32[]{:S(2)}) collective-permute-start(bf16[64,2176]{1,0:T(8,128)(2,1)S(1)} %get-tuple-element.58), channel_id=1, source_target_pairs={{0,12},{1,13},{2,14},{3,15},{4,0},{5,1},{6,2},{7,3},{8,4},{9,5},{1... | collective-permute-start | bytes 835592 | tf_op jit(solution)/shard_map/ppermute | solution.py:478
  (48 other events, 807.9 us)

commit v2 on v1

--- a/solution.py
+++ b/solution.py
@@ -14,14 +14,14 @@
 HALF = 64
 STRIDE = 1024
 NOWHERE = -(1 << 20)
-ANY = pl.BlockSpec(memory_space=pl.ANY)
+ANY = pl.BlockSpec(memory_space=pltpu.HBM)
 VMEM = pl.BlockSpec(memory_space=pltpu.VMEM)
 SMEM = pl.BlockSpec(memory_space=pltpu.SMEM)
 TN = (((0,), (0,)), ((), ()))
 NT = (((1,), (1,)), ((), ()))
 
 
-def params(megabytes):
+def params(megabytes=60):
     return pltpu.CompilerParams(vmem_limit_bytes=megabytes << 20)
 
 
@@ -53,7 +53,8 @@
         ]
 
     def order(self, z):
-        return sorted(range(self.outer), key=lambda s: abs(s - z))
+        rest = [s for s in range(self.outer) if s not in (z, z ^ 1)]
+        return [z ^ 1, z] + sorted(rest, key=lambda s: abs(s - z))
 
     def cand(self, z, source):
         if source == z:
@@ -73,7 +74,9 @@
             offs = [NOWHERE] * self.cands
             for slot, source in enumerate(self.order(z)):
                 offs[self.cand(z, source)] = slot * self.cap
-            rows.append(offs + [z * self.inner + self.partner(p, d) for d in range(self.inner)])
+            experts = [z * self.inner + self.partner(p, d) for d in range(self.inner)]
+            homes = [self.cand(z, z ^ r) for r in range(self.outer)]
+            rows.append(offs + experts + homes)
         return np.array(rows, np.int32)
 
     def line(self, step):
@@ -91,9 +94,9 @@
             for p in range(self.inner)
         ]
 
-    def shift(self, r):
+    def flip(self, r):
         return [
-            (z * self.inner + p, (z + r) % self.outer * self.inner + p)
+            (z * self.inner + p, (z ^ r) * self.inner + p)
             for z in range(self.outer)
             for p in range(self.inner)
         ]
@@ -103,19 +106,22 @@
     tok, width = plan.tok, plan.width
     out_ref[:, :width] = tok_ref[...]
     out_ref[:, width : 2 * width] = up_ref[...]
-    lane = lax.broadcasted_iota(jnp.int32, (tok, LANES), 1)
-    weight = jnp.zeros((tok, LANES), F32)
-    named = jnp.zeros((tok, LANES), F32)
+    kind = lax.broadcasted_iota(jnp.int32, (LANES, tok), 0)
+    weight = jnp.zeros((LANES, tok), F32)
+    named = jnp.zeros((LANES, tok), F32)
     comb = comb_ref[...].astype(F32)
     for k in range(plan.top):
-        e = routes_ref[:, k : k + 1]
-        weight = jnp.where(lane == e, comb[:, k : k + 1], weight)
-        named = jnp.where(lane == e + HALF, 1.0, named)
+        e = routes_ref[k : k + 1, :]
+        weight = jnp.where(kind == e, comb[k : k + 1, :], weight)
+        named = jnp.where(kind == e + HALF, 1.0, named)
     row = lax.broadcasted_iota(jnp.int32, (tok, tok), 0)
     col = lax.broadcasted_iota(jnp.int32, (tok, tok), 1)
-    upto = jnp.where(col <= row, 1.0, 0.0).astype(BF)
-    count = jnp.dot(upto, named.astype(BF), preferred_element_type=F32)
-    out_ref[:, 2 * width :] = (weight + count * named).astype(BF)
+    upto = jnp.where(row <= col, 1.0, 0.0).astype(BF)
+    count = jnp.dot(named.astype(BF), upto, preferred_element_type=F32)
+    table = (weight + count * named).astype(BF)
+    same = jnp.where(row == col, 1.0, 0.0).astype(BF)
+    turned = lax.dot_general(same, table, NT, preferred_element_type=F32)
+    out_ref[:, 2 * width :] = turned.astype(BF)
 
 
 def picks(plan, meta, off, experts, key, scaled):
@@ -154,22 +160,11 @@
         one, two = picks(plan, meta, info[use[i]], experts, key_ref[...], True)
         one_s[i * tok : (i + 1) * tok, :] = one.astype(BF)
         two_s[i * tok : (i + 1) * tok, :] = two.astype(BF)
-    tile = 512
     for part, source in ((0, one_s), (1, two_s)):
-
-        @pl.loop(0, width // tile)
-        def _(j):
-            at = pl.multiple_of(j * tile, tile)
-            got = lax.dot_general(
-                source[...],
-                held[:, pl.ds(pl.multiple_of(part * width + at, tile), tile)],
-                TN,
-                preferred_element_type=F32,
-            ).astype(BF)
-            for d in range(inner):
-                outs[d][part * rows : (part + 1) * rows, pl.ds(at, tile)] = got[
-                    d * rows : (d + 1) * rows
-                ]
+        have = held[:, part * width : (part + 1) * width]
+        found = lax.dot_general(source[...], have, TN, preferred_element_type=F32).astype(BF)
+        for d in range(inner):
+            outs[d][part * rows : (part + 1) * rows, :] = found[d * rows : (d + 1) * rows]
 
 
 def expert_kernel(plan, chunk, *refs):
@@ -190,29 +185,47 @@
         )
         for d, g in enumerate(got)
     ]
-    w_copies = []
-    for i in range(6):
-        half, where = pl.ds(i % 2 * part, part), (wg_s, wu_s, wd_s)[i // 2]
-        to = where.at[half] if i >= 4 else where.at[:, half]
-        w_copies.append(pltpu.make_async_copy(weights[i].at[0], to, sems.at[2 * inner + i]))
-    for c in x_copies + w_copies[:4] + d_copies + w_copies[4:]:
+    tile, tiles = 256, []
+    for n in range(hidden // tile):
+        for kind, where in ((0, wg_s), (1, wu_s), (2, wd_s)):
+            at, here = n * tile, []
+            while at < (n + 1) * tile:
+                half, start = divmod(at, part)
+                size = min((n + 1) * tile, (half + 1) * part) - at
+                source, to = pl.ds(start, size), pl.ds(at, size)
+                w = weights[2 * kind + half].at[0]
+                here.append((w.at[source], where.at[to]) if kind == 2 else (w.at[:, source], where.at[:, to]))
+                at += size
+            tiles.append(here)
+    w_copies, used = [], 2 * inner
+    for here in tiles:
+        w_copies.append([])
+        for source, to in here:
+            w_copies[-1].append(pltpu.make_async_copy(source, to, sems.at[used]))
+            used += 1
+    for c in x_copies + w_copies[0] + w_copies[1] + d_copies:
         c.start()
-    for c in x_copies + w_copies[:4] + d_copies + w_copies[4:]:
-        c.wait()
-    tile = 256
-    comb_s[...] = jnp.zeros_like(comb_s)
-
-    @pl.loop(0, hidden // tile)
-    def _(n):
-        at = pl.ds(pl.multiple_of(n * tile, tile), tile)
+    for here in w_copies[2:]:
+        for c in here:
+            c.start()
+    for n in range(hidden // tile):
+        at = slice(n * tile, (n + 1) * tile)
+        gate_w, up_w, down_w = w_copies[3 * n : 3 * n + 3]
+        for c in (x_copies if n == 0 else []) + gate_w:
+            c.wait()
         gate = jnp.dot(x_s[...], wg_s[:, at], preferred_element_type=F32)
+        for c in up_w:
+            c.wait()
         up = jnp.dot(x_s[...], wu_s[:, at], preferred_element_type=F32)
+        for c in (d_copies if n == 0 else []) + down_w:
+            c.wait()
         mixed = lax.dot_general(d_s[...], wd_s[at, :], NT, preferred_element_type=F32)
         logistic = jax.nn.sigmoid(gate)
         silu = gate * logistic
         hid = (silu * up).astype(BF)
         hid_o[:, at] = hid
-        comb_s[...] += jnp.sum(hid.astype(F32) * mixed, axis=1, keepdims=True)
+        comb = jnp.sum(hid.astype(F32) * mixed, axis=1, keepdims=True)
+        comb_s[...] = comb if n == 0 else comb_s[...] + comb
         gate_o[:, at] = (mixed * up * logistic * (1.0 + gate * (1.0 - logistic))).astype(BF)
         up_o[:, at] = (mixed * silu).astype(BF)
 
@@ -283,28 +296,25 @@
         g_o[0, to, :] = first.astype(BF)
         u_o[0, to, :] = second.astype(BF)
 
-    @pl.loop(0, width // tile)
-    def _(j):
-        to = pl.ds(pl.multiple_of(j * tile, tile), tile)
-        down = lax.dot_general(h_s[...], d_s[:, to], TN, preferred_element_type=F32)
-        if own:
-            down += theirs[2][0, :, to].astype(F32)
-        d_o[0, :, to] = down.astype(BF)
-
-
-def spread_kernel(plan, *refs):
-    inner, outer, tok, width = plan.inner, plan.outer, plan.tok, plan.width
+    down = lax.dot_general(h_s[...], d_s[...], TN, preferred_element_type=F32)
+    if own:
+        down += theirs[2][0].astype(F32)
+    d_o[0] = down.astype(BF)
+
+
+def spread_kernel(plan, homes, chunks, *refs):
+    inner, tok, width = plan.inner, plan.tok, plan.width
     info, key_ref = refs[:2]
     blocks = refs[2 : 2 + plan.cands]
-    backs = refs[2 + plan.cands : 2 + plan.cands + 2 * inner]
-    outs = refs[2 + plan.cands + 2 * inner :][:outer]
-    held, metas, pick_s, sems, meta_sems = refs[2 + plan.cands + 2 * inner + outer :]
-    copies, start = [], 0
+    at = 2 + plan.cands
+    backs = refs[at : at + chunks * inner]
+    outs = refs[-5 - len(homes) : -5]
+    held, metas, pick_s, sems, meta_sems = refs[-5:]
+    copies, later, start = [], [], 0
     for i, b in enumerate(blocks):
         copies.append(
             pltpu.make_async_copy(b.at[:, pl.ds(2 * width, LANES)], metas.at[i], meta_sems.at[i])
         )
-    later = []
     for i, b in enumerate(backs):
         rows = plan.rows[i // inner]
         later.append(pltpu.make_async_copy(b, held.at[pl.ds(start, rows)], sems.at[i]))
@@ -314,14 +324,11 @@
     for c in copies:
         c.wait()
     experts = [info[plan.cands + d] for d in range(inner)]
-    for r in range(outer):
-        total = None
-        for i in [0] if r == 0 else [outer - 1 + r, outer - r]:
-            one, _ = picks(
-                plan, metas[i].astype(F32), info[i], experts, key_ref[...], False
-            )
-            total = one if total is None else total + one
-        pick_s[r * tok : (r + 1) * tok, :] = total.astype(BF)
+    for i, r in enumerate(homes):
+        which = info[plan.cands + inner + r]
+        meta = metas[which].astype(F32)
+        one, _ = picks(plan, meta, info[which], experts, key_ref[...], False)
+        pick_s[i * tok : (i + 1) * tok, :] = one.astype(BF)
     for c in later:
         c.wait()
     tile = 256
@@ -329,8 +336,8 @@
     def piece(at, size):
         sums = jnp.dot(pick_s[...], held[:, pl.ds(at, size)], preferred_element_type=F32)
         sums = sums.astype(BF)
-        for r in range(outer):
-            outs[r][:, pl.ds(at, size)] = sums[r * tok : (r + 1) * tok]
+        for i in range(len(homes)):
+            outs[i][:, pl.ds(at, size)] = sums[i * tok : (i + 1) * tok]
 
     @pl.loop(0, width // tile)
     def _(j):
@@ -339,20 +346,29 @@
     piece(width, LANES)
 
 
-def home_kernel(plan, *refs):
-    parts, (routes_ref, comb_ref, tok_o, comb_o) = refs[: plan.outer], refs[plan.outer :]
+def add_kernel(a_ref, b_ref, o_ref):
+    o_ref[...] = (a_ref[...].astype(F32) + b_ref[...].astype(F32)).astype(BF)
+
+
+def home_kernel(plan, count, *refs):
+    parts = refs[:count]
+    routes_ref, comb_ref, _, tok_o, comb_o = refs[count:]
     width, tok = plan.width, plan.tok
     total = parts[0][...].astype(F32)
     for p in parts[1:]:
         total += p[...].astype(F32)
     tok_o[...] = total[:, :width].astype(BF)
-    found = total[:, width:]
-    lane = lax.broadcasted_iota(jnp.int32, (tok, LANES), 1)
-    slot = lax.broadcasted_iota(jnp.int32, (tok, plan.top), 1)
-    out = jnp.zeros((tok, plan.top), F32)
+    row = lax.broadcasted_iota(jnp.int32, (LANES, LANES), 0)
+    col = lax.broadcasted_iota(jnp.int32, (LANES, LANES), 1)
+    same = jnp.where(row == col, 1.0, 0.0).astype(BF)
+    found = total[:, width:].astype(BF)
+    found = lax.dot_general(same, found, NT, preferred_element_type=F32)
+    kind = lax.broadcasted_iota(jnp.int32, (LANES, tok), 0)
+    out = []
     for k in range(plan.top):
-        mine = jnp.where(lane == routes_ref[:, k : k + 1], found, 0.0)
-        out = jnp.where(slot == k, jnp.sum(mine, axis=1, keepdims=True), out)
+        mine = jnp.where(kind == routes_ref[k : k + 1, :], found, 0.0)
+        out.append(jnp.sum(mine, axis=0, keepdims=True))
+    out = jnp.concatenate(out, axis=0)
     comb_o[...] = (out / comb_ref[...].astype(F32)).astype(BF)
 
 
@@ -370,26 +386,26 @@
         out_shape=shape((tok, full), BF),
         in_specs=[VMEM] * 4,
         out_specs=VMEM,
-        compiler_params=params(16),
+        compiler_params=params(),
         cost_estimate=cost(1e6, 4 * tok * full),
         name="pack",
-    )(tokens, upstream, routes, combine)
-
-    below, above = [block], [block]
-    for _ in range(outer - 1):
-        below.append(lax.ppermute(below[-1], "expert", plan.line(1)))
-        above.append(lax.ppermute(above[-1], "expert", plan.line(-1)))
-    blocks = [block] + below[1:] + above[1:]
-
+    )(tokens, upstream, routes.T, combine.T)
+
+    others = [lax.ppermute(w, "dp", swap) for w in (w_gate, w_up, w_down)]
+    blocks = [block] * plan.cands
+    blocks[1] = lax.ppermute(block, "expert", plan.line(1))
+    blocks[outer] = lax.ppermute(block, "expert", plan.line(-1))
+    *others, blocks[1], blocks[outer] = lax.optimization_barrier(
+        (*others, blocks[1], blocks[outer])
+    )
     weights = []
-    for w in (w_gate, w_up, w_down):
-        weights += [w, lax.ppermute(w, "dp", swap)]
-
-    got, mids, backs = [], [], []
-    for c in range(2):
+    for w, other in zip((w_gate, w_up, w_down), others):
+        weights += [w, other]
+
+    def compact(c):
         rows, use = plan.rows[c], plan.use[c]
         count, n = inner * rows, len(use)
-        sent = pl.pallas_call(
+        return pl.pallas_call(
             functools.partial(compact_kernel, plan, c),
             out_shape=[shape((2 * rows, width), BF)] * inner,
             in_specs=[SMEM, VMEM] + [ANY] * n,
@@ -400,14 +416,15 @@
                 pltpu.VMEM((n * tok, count), BF),
                 pltpu.SemaphoreType.DMA((n,)),
             ],
-            compiler_params=params(40),
+            compiler_params=params(),
             cost_estimate=cost(4 * n * tok * count * width, 2 * n * tok * full),
             name="compact",
         )(info, keys[c], *[blocks[i] for i in use])
-        arrived = [sent[0]] + [
-            lax.ppermute(sent[d], "expert", plan.across(d)) for d in range(1, inner)
-        ]
-        outs = pl.pallas_call(
+
+    def expert(c, arrived):
+        rows = plan.rows[c]
+        count = inner * rows
+        return pl.pallas_call(
             functools.partial(expert_kernel, plan, c),
             out_shape=[shape((count, hidden), BF)] * 3
             + [shape((rows, width + LANES), BF)] * inner,
@@ -420,17 +437,40 @@
                 pltpu.VMEM((width, hidden), BF),
                 pltpu.VMEM((hidden, width), BF),
                 pltpu.VMEM((count, 1), F32),
-                pltpu.SemaphoreType.DMA((2 * inner + 6,)),
+                pltpu.SemaphoreType.DMA((2 * inner + 6 * (hidden // 128),)),
             ],
-            compiler_params=params(44),
+            compiler_params=params(),
             cost_estimate=cost(10 * count * hidden * width, 6 * hidden * width),
             name="expert",
         )(info, *arrived, *weights)
-        got += arrived
-        mids += outs[:3]
-        backs += [outs[3]] + [
-            lax.ppermute(outs[3 + d], "expert", plan.across(d)) for d in range(1, inner)
+
+    def cross(arrays):
+        return [arrays[0]] + [
+            lax.ppermute(arrays[d], "expert", plan.across(d)) for d in range(1, inner)
         ]
+
+    near = max((i if i < outer else i - outer + 1) for i in plan.use[0])
+    for r in range(2, near + 1):
+        blocks[r] = lax.ppermute(blocks[r - 1], "expert", plan.line(1))
+        blocks[outer - 1 + r] = lax.ppermute(blocks[outer - 2 + r], "expert", plan.line(-1))
+    sent = compact(0)
+    for r in range(near + 1, outer):
+        blocks[r] = lax.ppermute(blocks[r - 1], "expert", plan.line(1))
+        blocks[outer - 1 + r] = lax.ppermute(blocks[outer - 2 + r], "expert", plan.line(-1))
+        if r == near + 1:
+            blocks[r], blocks[outer - 1 + r], sent = lax.optimization_barrier(
+                (blocks[r], blocks[outer - 1 + r], sent)
+            )
+    got = cross(sent)
+    late = cross(compact(1))
+    outs = expert(0, got)
+    outs, late = lax.optimization_barrier((outs, late))
+    backs = cross(outs[3:])
+    more = expert(1, late)
+    backs, more = lax.optimization_barrier((backs, more))
+    got = got + late
+    mids = outs[:3] + more[:3]
+    backs = backs + cross(more[3:])
 
     count = inner * sum(plan.rows)
 
@@ -451,41 +491,73 @@
                 pltpu.VMEM((count, 2 * part), BF),
                 pltpu.SemaphoreType.DMA((4 * inner + 6,)),
             ],
-            compiler_params=params(44),
+            compiler_params=params(),
             cost_estimate=cost(6 * count * part * width, 4 * count * (width + hidden)),
             name="weight_grads",
         )(*got, *mids, *extra)
 
-    theirs = [lax.ppermute(w, "dp", swap) for w in weight_grads(False, [])]
+    def spread(homes, chunks, extra):
+        slots = inner * sum(plan.rows[:chunks])
+        return pl.pallas_call(
+            functools.partial(spread_kernel, plan, homes, chunks),
+            out_shape=[shape((tok, width + LANES), BF)] * len(homes),
+            in_specs=[SMEM, VMEM] + [ANY] * (plan.cands + chunks * inner + len(extra)),
+            out_specs=[VMEM] * len(homes),
+            scratch_shapes=[
+                pltpu.VMEM((slots, width + LANES), BF),
+                pltpu.VMEM((plan.cands, tok, LANES), BF),
+                pltpu.VMEM((len(homes) * tok, slots), BF),
+                pltpu.SemaphoreType.DMA((chunks * inner,)),
+                pltpu.SemaphoreType.DMA((plan.cands,)),
+            ],
+            compiler_params=params(),
+            cost_estimate=cost(2 * len(homes) * tok * slots * width, 2 * slots * width),
+            name="spread",
+        )(
+            info,
+            jnp.concatenate(keys[:chunks], axis=1),
+            *blocks,
+            *backs[: chunks * inner],
+            *extra,
+        )
+
+    (first,) = spread([1], 1, [mids[3]])
+    sums = {1: first}
+    came = [lax.ppermute(first, "expert", plan.flip(1))]
+    mine = weight_grads(False, [])
+    mine, backs = lax.optimization_barrier((mine, backs))
+    theirs = [lax.ppermute(w, "dp", swap) for w in mine]
+    rest = [r for r in range(outer) if r != 1]
+    sums.update(zip(rest, spread(rest, 2, [mine[0]])))
+    bit = 1
+    while bit < outer:
+        for r in range(bit, outer, 2 * bit):
+            if r == 1:
+                continue
+            sent = lax.ppermute(sums[r], "expert", plan.flip(bit))
+            if r == bit:
+                came.append(sent)
+            else:
+                sums[r - bit] = pl.pallas_call(
+                    add_kernel,
+                    out_shape=shape((tok, width + LANES), BF),
+                    in_specs=[VMEM] * 2,
+                    out_specs=VMEM,
+                    name="add",
+                )(sums[r - bit], sent)
+        bit *= 2
     grads = weight_grads(True, theirs)
-
-    sums = pl.pallas_call(
-        functools.partial(spread_kernel, plan),
-        out_shape=[shape((tok, width + LANES), BF)] * outer,
-        in_specs=[SMEM, VMEM] + [ANY] * (plan.cands + 2 * inner),
-        out_specs=[VMEM] * outer,
-        scratch_shapes=[
-            pltpu.VMEM((count, width + LANES), BF),
-            pltpu.VMEM((plan.cands, tok, LANES), BF),
-            pltpu.VMEM((outer * tok, count), BF),
-            pltpu.SemaphoreType.DMA((2 * inner,)),
-            pltpu.SemaphoreType.DMA((plan.cands,)),
-        ],
-        compiler_params=params(32),
-        cost_estimate=cost(2 * outer * tok * count * width, 2 * count * width),
-        name="spread",
-    )(info, jnp.concatenate(keys, axis=1), *blocks, *backs)
-    home = [sums[0]] + [lax.ppermute(sums[r], "expert", plan.shift(r)) for r in range(1, outer)]
+    home = [sums[0]] + came
     grad_tokens, grad_combine = pl.pallas_call(
-        functools.partial(home_kernel, plan),
-        out_shape=[shape((tok, width), BF), shape((tok, plan.top), BF)],
-        in_specs=[VMEM] * (outer + 2),
+        functools.partial(home_kernel, plan, len(home)),
+        out_shape=[shape((tok, width), BF), shape((plan.top, tok), BF)],
+        in_specs=[VMEM] * (len(home) + 2) + [ANY],
         out_specs=[VMEM] * 2,
-        compiler_params=params(16),
+        compiler_params=params(),
         cost_estimate=cost(1e6, 2 * tok * width * (outer + 1)),
         name="home",
-    )(*home, routes, combine)
-    return (grad_tokens, grad_combine, *grads)
+    )(*home, routes.T, combine.T, grads[0])
+    return (grad_tokens, grad_combine.T, *grads)
 
 
 def solution(mesh):

time: 230 us -> 176 us (0.77)
  waiting for transfers between devices: 104 us -> 53.8 us
  local copies, waits for them, and re-layouts: 27 us -> 7.07 us
  Pallas kernels: 59.8 us -> 76.4 us
    ppermute x27, waiting for transfers between devices: 104 us -> 53.8 us  [the longest x12 17.7 us: cross(): lax.ppermute(arrays[d], 'expert', plan.across(d))]
    unnamed x93 -> x44, local copies, waits for them, and re-layouts: 26.3 us -> 5.86 us
    pallas_call x6 -> x8, Pallas kernels: 36.7 us -> 52.4 us  [the longest x2 28.5 us: expert(): pl.pallas_call(functools.partial(expert_kernel, plan, c), out_shape=[shap...]
  transfers between devices with their start and end apart: 27 -> 27, of which waited for: 14 -> 12; matrix products, arithmetic and copies ran while one was open for 1% -> 1% of each run, Pallas kernels for 19% -> 42%
where the time goes in v2:
time: 176 us
  Pallas kernels  76.4 us (43%)
  waiting for transfers between devices  53.8 us (31%)
  starting transfers between devices  37.5 us (21%)
  local copies, waits for them, and re-layouts  7.07 us (4%)
    pallas_call x2, Pallas kernels, expert(): pl.pallas_call(functools.partial(expert_kernel, plan, c), out_shape=[shap...  28.5 us
    pallas_call x2, Pallas kernels, weight_grads(): pl.pallas_call(functools.partial(weight_kernel, plan, own), out_shape=[sh...  21.8 us
    ppermute x12, waiting for transfers between devices, cross(): lax.ppermute(arrays[d], 'expert', plan.across(d))  17.7 us
    ppermute x12, starting transfers between devices, cross(): lax.ppermute(arrays[d], 'expert', plan.across(d))  14.1 us
    ppermute x1, waiting for transfers between devices, on_device(): blocks[1] = lax.ppermute(block, 'expert', plan.line(1))  11.1 us
    pallas_call x2, Pallas kernels, compact(): pl.pallas_call(functools.partial(compact_kernel, plan, c), out_shape=[sha...  10.1 us
    pallas_call x2, Pallas kernels, spread(): pl.pallas_call(functools.partial(spread_kernel, plan, homes, chunks), out...  9.84 us
    ppermute x2, waiting for transfers between devices, on_device(): blocks[r] = lax.ppermute(blocks[r - 1], 'expert', plan.line(1))  9.18 us
  transfers between devices with their start and end apart: 27, of which 12 were waited for; matrix products, arithmetic and copies ran while one was open for 1% of the time, Pallas kernels for 42%

profile of v2, /device:TPU:0, one launch (start us, length us, event | category | flops | bytes accessed | tf_op | source)
XLA Modules:
  0.0 175.7 jit_solution(14606562969936788454)
XLA Ops:
  1.7 2.1 %pack.1.refs_2_ = bf16[64,4224]{1,0:T(8,128)(2,1)} custom-call(bf16[64,2048]{1,0:T(8,128)(2,1)} %tok_ref.1, bf16[64,2048]{1,0:T(8,128)(2,1)} %up_ref.1, s32[8,64]{1,0:T(8,128)} %bitcast.5, bf16[8,64]{1,0:T(8,128)(2,1)} %bitcast.7), custom_call_target="tpu_custom_call" | custom-call | flops 1000000 | bytes 1081344 | tf_op jit(solution)/shard_map/pack/pallas_call | solution.py:384
  3.8 4.6 %collective-permute-start.3 = (bf16[64,4224]{1,0:T(8,128)(2,1)}, bf16[64,4224]{1,0:T(8,128)(2,1)S(1)}, u32[]{:S(2)}, u32[]{:S(2)}) collective-permute-start(bf16[64,4224]{1,0:T(8,128)(2,1)} %pack.1.refs_2_), channel_id=1, source_target_pairs={{0,4},{1,5},{2,6},{3,7},{4,8},{5,9},{6,10},{7,11},{8,12},{9,13},{1... | collective-permute-start | bytes 1622024 | tf_op jit(solution)/shard_map/ppermute | solution.py:396
  9.7 11.1 %collective-permute-done.3.refs_3_ = bf16[64,4224]{1,0:T(8,128)(2,1)S(1)} collective-permute-done((bf16[64,4224]{1,0:T(8,128)(2,1)}, bf16[64,4224]{1,0:T(8,128)(2,1)S(1)}, u32[]{:S(2)}, u32[]{:S(2)}) %collective-permute-start.3) | collective-permute-done | bytes 540704 | tf_op jit(solution)/shard_map/ppermute | solution.py:396
  20.8 4.0 %collective-permute-done.4.refs_4_.refs_6_ = bf16[64,4224]{1,0:T(8,128)(2,1)S(1)} collective-permute-done((bf16[64,4224]{1,0:T(8,128)(2,1)}, bf16[64,4224]{1,0:T(8,128)(2,1)S(1)}, u32[]{:S(2)}, u32[]{:S(2)}) %collective-permute-start.4) | collective-permute-done | bytes 540704 | tf_op jit(solution)/shard_map/ppermute | solution.py:397
  26.0 3.5 %collective-permute-start.5 = (bf16[64,4224]{1,0:T(8,128)(2,1)S(1)}, bf16[64,4224]{1,0:T(8,128)(2,1)S(1)}, u32[]{:S(2)}, u32[]{:S(2)}) collective-permute-start(bf16[64,4224]{1,0:T(8,128)(2,1)S(1)} %collective-permute-done.3.refs_3_), channel_id=1, source_target_pairs={{0,4},{1,5},{2,6},{3,7},{4,8},{5,9},{6,10},{7,11},{8,12},{9,13},{1... | collective-permute-start | bytes 1622024 | tf_op jit(solution)/shard_map/ppermute | solution.py:458
  32.0 4.2 %compact.2 = (bf16[128,2048]{1,0:T(8,128)(2,1)}, bf16[128,2048]{1,0:T(8,128)(2,1)}, bf16[128,2048]{1,0:T(8,128)(2,1)}, bf16[128,2048]{1,0:T(8,128)(2,1)}) custom-call(s32[15]{0:T(128)} %dynamic-slice_bitcast_fusion.refs_0_, s32[1,256]{1,0:T(1,128)} %constant.15.clone.refs_1_, bf16[64,4224]{1,0:T(8,128)(2,1)} %pack.1.refs_2_, bf16[64,4224]{1,0:T(8,128)(2,1)} %copy-done, ...), custom_call_target="tpu_custom_call" | custom-call | flops 402653184 | bytes 1622016 | tf_op jit(solution)/shard_map/compact/pallas_call | solution.py:408
  36.2 4.3 %collective-permute-done.5.refs_4_ = bf16[64,4224]{1,0:T(8,128)(2,1)S(1)} collective-permute-done((bf16[64,4224]{1,0:T(8,128)(2,1)S(1)}, bf16[64,4224]{1,0:T(8,128)(2,1)S(1)}, u32[]{:S(2)}, u32[]{:S(2)}) %collective-permute-start.5) | collective-permute-done | bytes 540704 | tf_op jit(solution)/shard_map/ppermute | solution.py:458
  40.5 4.1 %collective-permute-done.6.refs_7_ = bf16[64,4224]{1,0:T(8,128)(2,1)S(1)} collective-permute-done((bf16[64,4224]{1,0:T(8,128)(2,1)S(1)}, bf16[64,4224]{1,0:T(8,128)(2,1)S(1)}, u32[]{:S(2)}, u32[]{:S(2)}) %collective-permute-start.6) | collective-permute-done | bytes 540704 | tf_op jit(solution)/shard_map/ppermute | solution.py:459
  44.6 3.5 %collective-permute-start.7 = (bf16[64,4224]{1,0:T(8,128)(2,1)S(1)}, bf16[64,4224]{1,0:T(8,128)(2,1)S(1)}, u32[]{:S(2)}, u32[]{:S(2)}) collective-permute-start(bf16[64,4224]{1,0:T(8,128)(2,1)S(1)} %collective-permute-done.5.refs_4_), channel_id=1, source_target_pairs={{0,4},{1,5},{2,6},{3,7},{4,8},{5,9},{6,10},{7,11},{8,12},{9,13},{1... | collective-permute-start | bytes 1622024 | tf_op jit(solution)/shard_map/ppermute | solution.py:458
  53.0 4.9 %collective-permute-done.7.refs_5_ = bf16[64,4224]{1,0:T(8,128)(2,1)S(1)} collective-permute-done((bf16[64,4224]{1,0:T(8,128)(2,1)S(1)}, bf16[64,4224]{1,0:T(8,128)(2,1)S(1)}, u32[]{:S(2)}, u32[]{:S(2)}) %collective-permute-start.7) | collective-permute-done | bytes 540704 | tf_op jit(solution)/shard_map/ppermute | solution.py:458
  57.9 4.1 %collective-permute-done.8.refs_8_ = bf16[64,4224]{1,0:T(8,128)(2,1)S(1)} collective-permute-done((bf16[64,4224]{1,0:T(8,128)(2,1)S(1)}, bf16[64,4224]{1,0:T(8,128)(2,1)S(1)}, u32[]{:S(2)}, u32[]{:S(2)}) %collective-permute-start.8) | collective-permute-done | bytes 540704 | tf_op jit(solution)/shard_map/ppermute | solution.py:459
  62.8 5.9 %compact.3 = (bf16[160,2048]{1,0:T(8,128)(2,1)}, bf16[160,2048]{1,0:T(8,128)(2,1)}, bf16[160,2048]{1,0:T(8,128)(2,1)}, bf16[160,2048]{1,0:T(8,128)(2,1)}) custom-call(s32[15]{0:T(128)} %dynamic-slice_bitcast_fusion.refs_0_, s32[1,320]{1,0:T(1,128)} %constant.16.clone.refs_1_, bf16[64,4224]{1,0:T(8,128)(2,1)} %pack.1.refs_2_, bf16[64,4224]{1,0:T(8,128)(2,1)} %copy-done, ...), custom_call_target="tpu_custom_call" | custom-call | flops 1174405120 | bytes 3784704 | tf_op jit(solution)/shard_map/compact/pallas_call | solution.py:408
  72.5 4.4 %collective-permute-done.11.refs_4_.refs_3_ = bf16[128,2048]{1,0:T(8,128)(2,1)} collective-permute-done((bf16[128,2048]{1,0:T(8,128)(2,1)}, bf16[128,2048]{1,0:T(8,128)(2,1)}, u32[]{:S(2)}, u32[]{:S(2)}) %collective-permute-start.11) | collective-permute-done | bytes 524320 | tf_op jit(solution)/shard_map/ppermute | solution.py:449
  76.9 13.4 %expert.2 = (bf16[256,768]{1,0:T(8,128)(2,1)}, bf16[256,768]{1,0:T(8,128)(2,1)}, bf16[256,768]{1,0:T(8,128)(2,1)}, bf16[64,2176]{1,0:T(8,128)(2,1)}, bf16[64,217...) custom-call(s32[15]{0:T(128)} %dynamic-slice_bitcast_fusion.refs_0_, ...), custom_call_target="tpu_custom_call" | custom-call | flops 4026531840 | bytes 9437184 | tf_op jit(solution)/shard_map/expert/pallas_call | solution.py:427
  90.4 11.5 %collective-permute-done.13.refs_3_.refs_6_ = bf16[160,2048]{1,0:T(8,128)(2,1)S(1)} collective-permute-done((bf16[160,2048]{1,0:T(8,128)(2,1)}, bf16[160,2048]{1,0:T(8,128)(2,1)S(1)}, u32[]{:S(2)}, u32[]{:S(2)}) %collective-permute-start.13) | collective-permute-done | bytes 655392 | tf_op jit(solution)/shard_map/ppermute | solution.py:449
  105.5 15.1 %expert.3 = (bf16[320,768]{1,0:T(8,128)(2,1)}, bf16[320,768]{1,0:T(8,128)(2,1)}, bf16[320,768]{1,0:T(8,128)(2,1)}, bf16[80,2176]{1,0:T(8,128)(2,1)}, bf16[80,217...) custom-call(s32[15]{0:T(128)} %dynamic-slice_bitcast_fusion.refs_0_, ...), custom_call_target="tpu_custom_call" | custom-call | flops 5033164800 | bytes 9437184 | tf_op jit(solution)/shard_map/expert/pallas_call | solution.py:427
  124.2 9.7 %weight_grads.2 = (bf16[1,2048,384]{2,1,0:T(8,128)(2,1)}, bf16[1,2048,384]{2,1,0:T(8,128)(2,1)}, bf16[1,384,2048]{2,1,0:T(8,128)(2,1)}) custom-call(bf16[128,2048]{1,0:T(8,128)(2,1)} %get-tuple-element.90.refs_1_.refs_0_, bf16[128,2048]{1,0:T(8,128)(2,1)} %copy-done.14, bf16[128,2048]{1,0:T(8,128)(2,1)} %copy-done.15, ...), custom_call_target="tpu_custom_call" | custom-call | flops 2717908992 | bytes 6488064 | tf_op jit(solution)/shard_map/weight_grads/pallas_call | solution.py:478
  136.8 5.7 %spread.2 = (bf16[64,2176]{1,0:T(8,128)(2,1)}, bf16[64,2176]{1,0:T(8,128)(2,1)}, bf16[64,2176]{1,0:T(8,128)(2,1)}) custom-call(s32[15]{0:T(128)} %dynamic-slice_bitcast_fusion.refs_0_, s32[1,576]{1,0:T(1,128)} %constant.20.refs_1_, bf16[64,4224]{1,0:T(8,128)(2,1)} %pack.1.refs_2_, bf16[64,4224]{1,0:T(8,128)(2,1)} %copy-done, bf16[64,4224]{1,0:T(8,128)(2,1)} %copy-done.2, ...), custom_call_target="tpu_custom_call" | custom-call | flops 452984832 | bytes 2359296 | tf_op jit(solution)/shard_map/spread/pallas_call | solution.py:501
  142.5 4.4 %collective-permute-start.22 = (bf16[64,2176]{1,0:T(8,128)(2,1)}, bf16[64,2176]{1,0:T(8,128)(2,1)S(1)}, u32[]{:S(2)}, u32[]{:S(2)}) collective-permute-start(bf16[64,2176]{1,0:T(8,128)(2,1)} %get-tuple-element.151), channel_id=1, source_target_pairs={{0,4},{1,5},{2,6},{3,7},{4,0},{5,1},{6,2},{7,3},{8,12},{9,13},{10,... | collective-permute-start | bytes 835592 | tf_op jit(solution)/shard_map/ppermute | solution.py:537
  146.9 4.2 %spread.3 = bf16[64,2176]{1,0:T(8,128)(2,1)} custom-call(s32[15]{0:T(128)} %dynamic-slice_bitcast_fusion.refs_0_, s32[1,256]{1,0:T(1,128)} %constant.15.clone.refs_1_, bf16[64,4224]{1,0:T(8,128)(2,1)} %pack.1.refs_2_, bf16[64,4224]{1,0:T(8,128)(2,1)} %copy-done, bf16[64,4224]{1,0:T(8,128)(2,1)} %copy-done.2, bf16[64,4224]{1,0:T(8,128)(2,1)} %copy-done.4, ...), custom_call_target="tpu_custom_call" | custom-call | flops 67108864 | bytes 1048576 | tf_op jit(solution)/shard_map/spread/pallas_call | solution.py:501
  151.1 3.5 %collective-permute-done.22.b_ref = bf16[64,2176]{1,0:T(8,128)(2,1)S(1)} collective-permute-done((bf16[64,2176]{1,0:T(8,128)(2,1)}, bf16[64,2176]{1,0:T(8,128)(2,1)S(1)}, u32[]{:S(2)}, u32[]{:S(2)}) %collective-permute-start.22) | collective-permute-done | bytes 278560 | tf_op jit(solution)/shard_map/ppermute | solution.py:537
  157.1 1.9 %collective-permute-start.23 = (bf16[64,2176]{1,0:T(8,128)(2,1)}, bf16[64,2176]{1,0:T(8,128)(2,1)S(1)}, u32[]{:S(2)}, u32[]{:S(2)}) collective-permute-start(bf16[64,2176]{1,0:T(8,128)(2,1)} %add.5), channel_id=1, source_target_pairs={{0,8},{1,9},{2,10},{3,11},{4,12},{5,13},{6,14},{7,15},{8,0},{9,1},... | collective-permute-start | bytes 835592 | tf_op jit(solution)/shard_map/ppermute | solution.py:537
  160.7 12.1 %weight_grads.3 = (bf16[1,2048,384]{2,1,0:T(8,128)(2,1)}, bf16[1,2048,384]{2,1,0:T(8,128)(2,1)}, bf16[1,384,2048]{2,1,0:T(8,128)(2,1)}) custom-call(bf16[128,2048]{1,0:T(8,128)(2,1)} %get-tuple-element.90.refs_1_.refs_0_, bf16[128,2048]{1,0:T(8,128)(2,1)} %copy-done.14, bf16[128,2048]{1,0:T(8,128)(2,1)} %copy-done.15, ...), custom_call_target="tpu_custom_call" | custom-call | flops 2717908992 | bytes 6488064 | tf_op jit(solution)/shard_map/weight_grads/pallas_call | solution.py:478
  173.5 2.2 %home.1 = (bf16[64,2048]{1,0:T(8,128)(2,1)}, bf16[8,64]{1,0:T(8,128)(2,1)}) custom-call(bf16[64,2176]{1,0:T(8,128)(2,1)} %get-tuple-element.149.refs_0_, bf16[64,2176]{1,0:T(8,128)(2,1)} %collective-permute-done.21.refs_1_, bf16[64,2176]{1,0:T(8,128)(2,1)} %copy-done.20, s32[8,64]{1,0:T(8,128)} %bitcast.6, bf16[8,64]{1,0:T(8,128)(2,1)} %bitcast.8, ...), custom_call_target="tpu_custom_call" | custom-call | flops 1000000 | bytes 1310720 | tf_op jit(solution)/shard_map/home/pallas_call | solution.py:551
  (86 shorter events, 30.4 us)
Async XLA Ops:
  0.6 24.2 %collective-permute-start = (bf16[1,2048,384]{2,1,0:T(8,128)(2,1)}, bf16[1,2048,384]{2,1,0:T(8,128)(2,1)S(1)}, u32[]{:S(2)}, u32[]{:S(2)}) collective-permute-start(bf16[1,2048,384]{2,1,0:T(8,128)(2,1)} %refs_5_.3), channel_id=1, source_target_pairs={{0,16},{16,0},{1,17},{17,1},{2,18},{18,2},{3,19},{19,3},{4,20},{20... | collective-permute-start | bytes 4718600 | tf_op jit(solution)/shard_map/ppermute | solution.py:394
  1.1 23.7 %collective-permute-start.1 = (bf16[1,2048,384]{2,1,0:T(8,128)(2,1)}, bf16[1,2048,384]{2,1,0:T(8,128)(2,1)}, u32[]{:S(2)}, u32[]{:S(2)}) collective-permute-start(bf16[1,2048,384]{2,1,0:T(8,128)(2,1)} %refs_7_.3), channel_id=1, source_target_pairs={{0,16},{16,0},{1,17},{17,1},{2,18},{18,2},{3,19},{19,3},{4,20},{20... | collective-permute-start | bytes 4718600 | tf_op jit(solution)/shard_map/ppermute | solution.py:394
  1.2 24.8 %collective-permute-start.2 = (bf16[1,384,2048]{2,1,0:T(8,128)(2,1)}, bf16[1,384,2048]{2,1,0:T(8,128)(2,1)}, u32[]{:S(2)}, u32[]{:S(2)}) collective-permute-start(bf16[1,384,2048]{2,1,0:T(8,128)(2,1)} %refs_9_.3), channel_id=1, source_target_pairs={{0,16},{16,0},{1,17},{17,1},{2,18},{18,2},{3,19},{19,3},{4,20},{20... | collective-permute-start | bytes 4718600 | tf_op jit(solution)/shard_map/ppermute | solution.py:394
  3.8 17.0 %collective-permute-start.3 = (bf16[64,4224]{1,0:T(8,128)(2,1)}, bf16[64,4224]{1,0:T(8,128)(2,1)S(1)}, u32[]{:S(2)}, u32[]{:S(2)}) collective-permute-start(bf16[64,4224]{1,0:T(8,128)(2,1)} %pack.1.refs_2_), channel_id=1, source_target_pairs={{0,4},{1,5},{2,6},{3,7},{4,8},{5,9},{6,10},{7,11},{8,12},{9,13},{1... | collective-permute-start | bytes 1622024 | tf_op jit(solution)/shard_map/ppermute | solution.py:396
  8.4 16.4 %collective-permute-start.4 = (bf16[64,4224]{1,0:T(8,128)(2,1)}, bf16[64,4224]{1,0:T(8,128)(2,1)S(1)}, u32[]{:S(2)}, u32[]{:S(2)}) collective-permute-start(bf16[64,4224]{1,0:T(8,128)(2,1)} %pack.1.refs_2_), channel_id=1, source_target_pairs={{4,0},{5,1},{6,2},{7,3},{8,4},{9,5},{10,6},{11,7},{12,8},{13,9},{1... | collective-permute-start | bytes 1622024 | tf_op jit(solution)/shard_map/ppermute | solution.py:397
  26.0 14.5 %collective-permute-start.5 = (bf16[64,4224]{1,0:T(8,128)(2,1)S(1)}, bf16[64,4224]{1,0:T(8,128)(2,1)S(1)}, u32[]{:S(2)}, u32[]{:S(2)}) collective-permute-start(bf16[64,4224]{1,0:T(8,128)(2,1)S(1)} %collective-permute-done.3.refs_3_), channel_id=1, source_target_pairs={{0,4},{1,5},{2,6},{3,7},{4,8},{5,9},{6,10},{7,11},{8,12},{9,13},{1... | collective-permute-start | bytes 1622024 | tf_op jit(solution)/shard_map/ppermute | solution.py:458
  29.5 15.1 %collective-permute-start.6 = (bf16[64,4224]{1,0:T(8,128)(2,1)S(1)}, bf16[64,4224]{1,0:T(8,128)(2,1)S(1)}, u32[]{:S(2)}, u32[]{:S(2)}) collective-permute-start(bf16[64,4224]{1,0:T(8,128)(2,1)S(1)} %collective-permute-done.4.refs_4_.refs_6_), channel_id=1, source_target_pairs={{4,0},{5,1},{6,2},{7,3},{8,4},{9,5},{10,6},{11,7},{12,8},{13,9},{1... | collective-permute-start | bytes 1622024 | tf_op jit(solution)/shard_map/ppermute | solution.py:459
  48.1 13.9 %collective-permute-start.8 = (bf16[64,4224]{1,0:T(8,128)(2,1)S(1)}, bf16[64,4224]{1,0:T(8,128)(2,1)S(1)}, u32[]{:S(2)}, u32[]{:S(2)}) collective-permute-start(bf16[64,4224]{1,0:T(8,128)(2,1)S(1)} %collective-permute-done.6.refs_7_), channel_id=1, source_target_pairs={{4,0},{5,1},{6,2},{7,3},{8,4},{9,5},{10,6},{11,7},{12,8},{13,9},{1... | collective-permute-start | bytes 1622024 | tf_op jit(solution)/shard_map/ppermute | solution.py:459
  49.4 22.4 %collective-permute-start.9 = (bf16[128,2048]{1,0:T(8,128)(2,1)}, bf16[128,2048]{1,0:T(8,128)(2,1)S(1)}, u32[]{:S(2)}, u32[]{:S(2)}) collective-permute-start(bf16[128,2048]{1,0:T(8,128)(2,1)} %get-tuple-element.91), channel_id=1, source_target_pairs={{0,1},{1,0},{2,3},{3,2},{4,5},{5,4},{6,7},{7,6},{8,9},{9,8},{10,11... | collective-permute-start | bytes 1572872 | tf_op jit(solution)/shard_map/ppermute | solution.py:449
  51.0 21.5 %collective-permute-start.10 = (bf16[128,2048]{1,0:T(8,128)(2,1)}, bf16[128,2048]{1,0:T(8,128)(2,1)S(1)}, u32[]{:S(2)}, u32[]{:S(2)}) collective-permute-start(bf16[128,2048]{1,0:T(8,128)(2,1)} %get-tuple-element.92), channel_id=1, source_target_pairs={{0,2},{1,3},{2,0},{3,1},{4,6},{5,7},{6,4},{7,5},{8,10},{9,11},{10,... | collective-permute-start | bytes 1572872 | tf_op jit(solution)/shard_map/ppermute | solution.py:449
  52.5 24.4 %collective-permute-start.11 = (bf16[128,2048]{1,0:T(8,128)(2,1)}, bf16[128,2048]{1,0:T(8,128)(2,1)}, u32[]{:S(2)}, u32[]{:S(2)}) collective-permute-start(bf16[128,2048]{1,0:T(8,128)(2,1)} %get-tuple-element.93), channel_id=1, source_target_pairs={{0,3},{1,2},{2,1},{3,0},{4,7},{5,6},{6,5},{7,4},{8,11},{9,10},{10,... | collective-permute-start | bytes 1572872 | tf_op jit(solution)/shard_map/ppermute | solution.py:449
  68.7 21.6 %collective-permute-start.12 = (bf16[160,2048]{1,0:T(8,128)(2,1)}, bf16[160,2048]{1,0:T(8,128)(2,1)S(1)}, u32[]{:S(2)}, u32[]{:S(2)}) collective-permute-start(bf16[160,2048]{1,0:T(8,128)(2,1)} %get-tuple-element.105), channel_id=1, source_target_pairs={{0,1},{1,0},{2,3},{3,2},{4,5},{5,4},{6,7},{7,6},{8,9},{9,8},{10,11... | collective-permute-start | bytes 1966088 | tf_op jit(solution)/shard_map/ppermute | solution.py:449
  70.3 31.5 %collective-permute-start.13 = (bf16[160,2048]{1,0:T(8,128)(2,1)}, bf16[160,2048]{1,0:T(8,128)(2,1)S(1)}, u32[]{:S(2)}, u32[]{:S(2)}) collective-permute-start(bf16[160,2048]{1,0:T(8,128)(2,1)} %get-tuple-element.106), channel_id=1, source_target_pairs={{0,2},{1,3},{2,0},{3,1},{4,6},{5,7},{6,4},{7,5},{8,10},{9,11},{10,... | collective-permute-start | bytes 1966088 | tf_op jit(solution)/shard_map/ppermute | solution.py:449
  71.8 30.2 %collective-permute-start.14 = (bf16[160,2048]{1,0:T(8,128)(2,1)}, bf16[160,2048]{1,0:T(8,128)(2,1)S(1)}, u32[]{:S(2)}, u32[]{:S(2)}) collective-permute-start(bf16[160,2048]{1,0:T(8,128)(2,1)} %get-tuple-element.107), channel_id=1, source_target_pairs={{0,3},{1,2},{2,1},{3,0},{4,7},{5,6},{6,5},{7,4},{8,11},{9,10},{10,... | collective-permute-start | bytes 1966088 | tf_op jit(solution)/shard_map/ppermute | solution.py:449
  102.0 18.6 %collective-permute-start.15 = (bf16[64,2176]{1,0:T(8,128)(2,1)}, bf16[64,2176]{1,0:T(8,128)(2,1)S(1)}, u32[]{:S(2)}, u32[]{:S(2)}) collective-permute-start(bf16[64,2176]{1,0:T(8,128)(2,1)} %get-tuple-element.116), channel_id=1, source_target_pairs={{0,1},{1,0},{2,3},{3,2},{4,5},{5,4},{6,7},{7,6},{8,9},{9,8},{10,11... | collective-permute-start | bytes 835592 | tf_op jit(solution)/shard_map/ppermute | solution.py:449
  103.3 17.3 %collective-permute-start.16 = (bf16[64,2176]{1,0:T(8,128)(2,1)}, bf16[64,2176]{1,0:T(8,128)(2,1)S(1)}, u32[]{:S(2)}, u32[]{:S(2)}) collective-permute-start(bf16[64,2176]{1,0:T(8,128)(2,1)} %get-tuple-element.117), channel_id=1, source_target_pairs={{0,2},{1,3},{2,0},{3,1},{4,6},{5,7},{6,4},{7,5},{8,10},{9,11},{10,... | collective-permute-start | bytes 835592 | tf_op jit(solution)/shard_map/ppermute | solution.py:449
  104.1 16.5 %collective-permute-start.17 = (bf16[64,2176]{1,0:T(8,128)(2,1)}, bf16[64,2176]{1,0:T(8,128)(2,1)S(1)}, u32[]{:S(2)}, u32[]{:S(2)}) collective-permute-start(bf16[64,2176]{1,0:T(8,128)(2,1)} %get-tuple-element.118), channel_id=1, source_target_pairs={{0,3},{1,2},{2,1},{3,0},{4,7},{5,6},{6,5},{7,4},{8,11},{9,10},{10,... | collective-permute-start | bytes 835592 | tf_op jit(solution)/shard_map/ppermute | solution.py:449
  120.6 13.3 %collective-permute-start.18 = (bf16[80,2176]{1,0:T(8,128)(2,1)}, bf16[80,2176]{1,0:T(8,128)(2,1)S(1)}, u32[]{:S(2)}, u32[]{:S(2)}) collective-permute-start(bf16[80,2176]{1,0:T(8,128)(2,1)} %get-tuple-element.137), channel_id=1, source_target_pairs={{0,1},{1,0},{2,3},{3,2},{4,5},{5,4},{6,7},{7,6},{8,9},{9,8},{10,11... | collective-permute-start | bytes 1044488 | tf_op jit(solution)/shard_map/ppermute | solution.py:449
  122.0 13.4 %collective-permute-start.19 = (bf16[80,2176]{1,0:T(8,128)(2,1)}, bf16[80,2176]{1,0:T(8,128)(2,1)S(1)}, u32[]{:S(2)}, u32[]{:S(2)}) collective-permute-start(bf16[80,2176]{1,0:T(8,128)(2,1)} %get-tuple-element.138), channel_id=1, source_target_pairs={{0,2},{1,3},{2,0},{3,1},{4,6},{5,7},{6,4},{7,5},{8,10},{9,11},{10,... | collective-permute-start | bytes 1044488 | tf_op jit(solution)/shard_map/ppermute | solution.py:449
  136.3 22.8 %collective-permute-start.24 = (bf16[1,2048,384]{2,1,0:T(8,128)(2,1)}, bf16[1,2048,384]{2,1,0:T(8,128)(2,1)S(1)}, u32[]{:S(2)}, u32[]{:S(2)}) collective-permute-start(bf16[1,2048,384]{2,1,0:T(8,128)(2,1)} %get-tuple-element.148.refs_17_), channel_id=1, source_target_pairs={{0,16},{16,0},{1,17},{17,1},{2,18},{18,2},{3,19},{19,3},{4,20},{20... | collective-permute-start | bytes 4718600 | tf_op jit(solution)/shard_map/ppermute | solution.py:529
  136.3 22.8 %collective-permute-start.25 = (bf16[1,2048,384]{2,1,0:T(8,128)(2,1)}, bf16[1,2048,384]{2,1,0:T(8,128)(2,1)S(1)}, u32[]{:S(2)}, u32[]{:S(2)}) collective-permute-start(bf16[1,2048,384]{2,1,0:T(8,128)(2,1)} %get-tuple-element.152), channel_id=1, source_target_pairs={{0,16},{16,0},{1,17},{17,1},{2,18},{18,2},{3,19},{19,3},{4,20},{20... | collective-permute-start | bytes 4718600 | tf_op jit(solution)/shard_map/ppermute | solution.py:529
  136.8 22.3 %collective-permute-start.26 = (bf16[1,384,2048]{2,1,0:T(8,128)(2,1)}, bf16[1,384,2048]{2,1,0:T(8,128)(2,1)}, u32[]{:S(2)}, u32[]{:S(2)}) collective-permute-start(bf16[1,384,2048]{2,1,0:T(8,128)(2,1)} %get-tuple-element.153), channel_id=1, source_target_pairs={{0,16},{16,0},{1,17},{17,1},{2,18},{18,2},{3,19},{19,3},{4,20},{20... | collective-permute-start | bytes 4718600 | tf_op jit(solution)/shard_map/ppermute | solution.py:529
  151.1 21.7 %collective-permute-start.21 = (bf16[64,2176]{1,0:T(8,128)(2,1)}, bf16[64,2176]{1,0:T(8,128)(2,1)}, u32[]{:S(2)}, u32[]{:S(2)}) collective-permute-start(bf16[64,2176]{1,0:T(8,128)(2,1)} %spread.3), channel_id=1, source_target_pairs={{0,4},{1,5},{2,6},{3,7},{4,0},{5,1},{6,2},{7,3},{8,12},{9,13},{10,... | collective-permute-start | bytes 835592 | tf_op jit(solution)/shard_map/ppermute | solution.py:526
  157.1 15.7 %collective-permute-start.23 = (bf16[64,2176]{1,0:T(8,128)(2,1)}, bf16[64,2176]{1,0:T(8,128)(2,1)S(1)}, u32[]{:S(2)}, u32[]{:S(2)}) collective-permute-start(bf16[64,2176]{1,0:T(8,128)(2,1)} %add.5), channel_id=1, source_target_pairs={{0,8},{1,9},{2,10},{3,11},{4,12},{5,13},{6,14},{7,15},{8,0},{9,1},... | collective-permute-start | bytes 835592 | tf_op jit(solution)/shard_map/ppermute | solution.py:537
  (25 other events, 180.5 us)

commit v3 on v2

--- a/solution.py
+++ b/solution.py
@@ -13,6 +13,7 @@
 LANES = 128
 HALF = 64
 STRIDE = 1024
+PARTS = 4
 NOWHERE = -(1 << 20)
 ANY = pl.BlockSpec(memory_space=pltpu.HBM)
 VMEM = pl.BlockSpec(memory_space=pltpu.VMEM)
@@ -40,29 +41,37 @@
         mean = tok * top // experts
         self.cap = min(tok, max(2, mean + tok * top // (8 * experts)))
         total = -(-self.outer * self.cap // 16) * 16
-        first = self.outer // 2 * self.cap // 16 * 16
-        self.chunks = ((0, first), (first, total))
-        self.rows = tuple(b - a for a, b in self.chunks)
+        step = self.outer // PARTS
+        marks = [k * step * self.cap // 16 * 16 for k in range(PARTS)] + [total]
+        self.chunks = [(marks[k], marks[k + 1]) for k in range(PARTS)]
+        self.rows = [b - a for a, b in self.chunks]
+        self.steps = [(k + 1) * step - 1 for k in range(PARTS)]
+        self.groups = [range(PARTS - 1), range(PARTS - 1, PARTS)]
+        self.spans = [(marks[g[0]], marks[g[-1] + 1]) for g in self.groups]
+        self.sizes = [b - a for a, b in self.spans]
         self.cands = 2 * self.outer - 1
-        self.use = (self.used(self.outer // 2), list(range(self.cands)))
-        self.keys = [
-            np.array(
-                [[d * STRIDE + q for d in range(self.inner) for q in range(a, b)]], np.int32
-            )
-            for a, b in self.chunks
-        ]
+        self.use = [self.used(*c) for c in self.chunks]
+
+    def keys(self, spans):
+        return np.array(
+            [[d * STRIDE + q for a, b in spans for d in range(self.inner) for q in range(a, b)]],
+            np.int32,
+        )
 
     def order(self, z):
         rest = [s for s in range(self.outer) if s not in (z, z ^ 1)]
-        return [z ^ 1, z] + sorted(rest, key=lambda s: abs(s - z))
+        return [z, z ^ 1] + sorted(rest, key=lambda s: abs(s - z))
 
     def cand(self, z, source):
         if source == z:
             return 0
         return z - source if source < z else self.outer - 1 + source - z
 
-    def used(self, slots):
-        return sorted({self.cand(z, s) for z in range(self.outer) for s in self.order(z)[:slots]})
+    def used(self, a, b):
+        slots = [k for k in range(self.outer) if k * self.cap < b and (k + 1) * self.cap > a]
+        return sorted(
+            {self.cand(z, self.order(z)[k]) for z in range(self.outer) for k in slots}
+        )
 
     def partner(self, p, d):
         return p ^ d if self.inner & (self.inner - 1) == 0 else (d - p) % self.inner
@@ -167,37 +176,42 @@
             outs[d][part * rows : (part + 1) * rows, :] = found[d * rows : (d + 1) * rows]
 
 
-def expert_kernel(plan, chunk, *refs):
-    inner, rows, width, hidden = plan.inner, plan.rows[chunk], plan.width, plan.hidden
-    part, count = hidden // 2, plan.inner * plan.rows[chunk]
+def pieces(plan, group, got, x_s, d_s, sems, base=0):
+    inner, size, first = plan.inner, plan.sizes[group], plan.spans[group][0]
+    x_copies, d_copies = [], []
+    for i, g in enumerate(got):
+        c, d = plan.groups[group][i // inner], i % inner
+        rows = plan.rows[c]
+        to = pl.ds(base + d * size + plan.chunks[c][0] - first, rows)
+        x_copies.append(pltpu.make_async_copy(g.at[pl.ds(0, rows)], x_s.at[to], sems.at[2 * i]))
+        d_copies.append(
+            pltpu.make_async_copy(g.at[pl.ds(rows, rows)], d_s.at[to], sems.at[2 * i + 1])
+        )
+    return x_copies, d_copies
+
+
+def expert_kernel(plan, group, *refs):
+    inner, rows, width, hidden = plan.inner, plan.sizes[group], plan.width, plan.hidden
+    part, count, n = hidden // 2, inner * rows, inner * len(plan.groups[group])
     info = refs[0]
-    got, weights = refs[1 : 1 + inner], refs[1 + inner : 7 + inner]
-    hid_o, gate_o, up_o = refs[7 + inner : 10 + inner]
-    backs = refs[10 + inner : 10 + 2 * inner]
-    x_s, d_s, wg_s, wu_s, wd_s, comb_s, sems = refs[10 + 2 * inner :]
-    x_copies = [
-        pltpu.make_async_copy(g.at[pl.ds(0, rows)], x_s.at[pl.ds(d * rows, rows)], sems.at[d])
-        for d, g in enumerate(got)
-    ]
-    d_copies = [
-        pltpu.make_async_copy(
-            g.at[pl.ds(rows, rows)], d_s.at[pl.ds(d * rows, rows)], sems.at[inner + d]
-        )
-        for d, g in enumerate(got)
-    ]
+    got, weights = refs[1 : 1 + n], refs[1 + n : 7 + n]
+    hid_o, gate_o, up_o = refs[7 + n : 10 + n]
+    backs = refs[10 + n : 10 + n + inner]
+    x_s, d_s, wg_s, wu_s, wd_s, comb_s, sems = refs[10 + n + inner :]
+    x_copies, d_copies = pieces(plan, group, got, x_s, d_s, sems)
     tile, tiles = 256, []
-    for n in range(hidden // tile):
+    for t in range(hidden // tile):
         for kind, where in ((0, wg_s), (1, wu_s), (2, wd_s)):
-            at, here = n * tile, []
-            while at < (n + 1) * tile:
+            at, here = t * tile, []
+            while at < (t + 1) * tile:
                 half, start = divmod(at, part)
-                size = min((n + 1) * tile, (half + 1) * part) - at
+                size = min((t + 1) * tile, (half + 1) * part) - at
                 source, to = pl.ds(start, size), pl.ds(at, size)
                 w = weights[2 * kind + half].at[0]
                 here.append((w.at[source], where.at[to]) if kind == 2 else (w.at[:, source], where.at[:, to]))
                 at += size
             tiles.append(here)
-    w_copies, used = [], 2 * inner
+    w_copies, used = [], 2 * n
     for here in tiles:
         w_copies.append([])
         for source, to in here:
@@ -208,16 +222,16 @@
     for here in w_copies[2:]:
         for c in here:
             c.start()
-    for n in range(hidden // tile):
-        at = slice(n * tile, (n + 1) * tile)
-        gate_w, up_w, down_w = w_copies[3 * n : 3 * n + 3]
-        for c in (x_copies if n == 0 else []) + gate_w:
+    for t in range(hidden // tile):
+        at = slice(t * tile, (t + 1) * tile)
+        gate_w, up_w, down_w = w_copies[3 * t : 3 * t + 3]
+        for c in (x_copies if t == 0 else []) + gate_w:
             c.wait()
         gate = jnp.dot(x_s[...], wg_s[:, at], preferred_element_type=F32)
         for c in up_w:
             c.wait()
         up = jnp.dot(x_s[...], wu_s[:, at], preferred_element_type=F32)
-        for c in (d_copies if n == 0 else []) + down_w:
+        for c in (d_copies if t == 0 else []) + down_w:
             c.wait()
         mixed = lax.dot_general(d_s[...], wd_s[at, :], NT, preferred_element_type=F32)
         logistic = jax.nn.sigmoid(gate)
@@ -225,7 +239,7 @@
         hid = (silu * up).astype(BF)
         hid_o[:, at] = hid
         comb = jnp.sum(hid.astype(F32) * mixed, axis=1, keepdims=True)
-        comb_s[...] = comb if n == 0 else comb_s[...] + comb
+        comb_s[...] = comb if t == 0 else comb_s[...] + comb
         gate_o[:, at] = (mixed * up * logistic * (1.0 + gate * (1.0 - logistic))).astype(BF)
         up_o[:, at] = (mixed * silu).astype(BF)
 
@@ -248,37 +262,29 @@
 
 def weight_kernel(plan, own, *refs):
     inner, width, hidden = plan.inner, plan.width, plan.hidden
-    part, counts = hidden // 2, [inner * r for r in plan.rows]
-    got = refs[: 2 * inner]
-    mids = refs[2 * inner : 2 * inner + 6]
-    at = 2 * inner + 6
+    part, n = hidden // 2, plan.inner * PARTS
+    got, mids = refs[:n], refs[n : n + 6]
+    at = n + 6
     theirs = refs[at : at + 3] if own else None
     at += 3 if own else 0
     g_o, u_o, d_o = refs[at : at + 3]
-    x_s, d_s, h_s, gu_s, sems = refs[at + 3 :]
-    x_copies, d_copies = [], []
-    start = 0
-    for c in range(2):
-        rows = plan.rows[c]
-        for d in range(inner):
-            g, to = got[c * inner + d], pl.ds(start, rows)
-            i = c * inner + d
-            x_copies.append(pltpu.make_async_copy(g.at[pl.ds(0, rows)], x_s.at[to], sems.at[i]))
-            d_copies.append(
-                pltpu.make_async_copy(g.at[pl.ds(rows, rows)], d_s.at[to], sems.at[2 * inner + i])
+    x_s, d_s, h_s, gu_s, sems, mid_sems = refs[at + 3 :]
+    everything, base, taken = [], 0, 0
+    half = pl.ds(0 if own else part, part)
+    for g in range(2):
+        many = inner * len(plan.groups[g])
+        mine = got[taken : taken + many]
+        at_sems = sems.at[pl.ds(2 * taken, 2 * many)]
+        x_copies, d_copies = pieces(plan, g, mine, x_s, d_s, at_sems, base)
+        everything += x_copies + d_copies
+        to = pl.ds(base, inner * plan.sizes[g])
+        spots = (h_s.at[to], gu_s.at[to, pl.ds(0, part)], gu_s.at[to, pl.ds(part, part)])
+        for i, (m, s) in enumerate(zip(mids[3 * g : 3 * g + 3], spots)):
+            everything.append(
+                pltpu.make_async_copy(m.at[:, half], s, mid_sems.at[3 * g + i])
             )
-            start += rows
-    m_copies = []
-    half = pl.ds(0 if own else part, part)
-    for c in range(2):
-        to = pl.ds(0 if c == 0 else counts[0], counts[c])
-        hid, gate, up = mids[3 * c : 3 * c + 3]
-        spots = (h_s.at[to], gu_s.at[to, pl.ds(0, part)], gu_s.at[to, pl.ds(part, part)])
-        for i, (m, s) in enumerate(zip((hid, gate, up), spots)):
-            m_copies.append(
-                pltpu.make_async_copy(m.at[:, half], s, sems.at[4 * inner + 3 * c + i])
-            )
-    everything = x_copies + m_copies + d_copies
+        taken += many
+        base += inner * plan.sizes[g]
     for c in everything:
         c.start()
     for c in everything:
@@ -302,12 +308,12 @@
     d_o[0] = down.astype(BF)
 
 
-def spread_kernel(plan, homes, chunks, *refs):
+def spread_kernel(plan, homes, groups, *refs):
     inner, tok, width = plan.inner, plan.tok, plan.width
     info, key_ref = refs[:2]
     blocks = refs[2 : 2 + plan.cands]
     at = 2 + plan.cands
-    backs = refs[at : at + chunks * inner]
+    backs = refs[at : at + groups * inner]
     outs = refs[-5 - len(homes) : -5]
     held, metas, pick_s, sems, meta_sems = refs[-5:]
     copies, later, start = [], [], 0
@@ -316,7 +322,7 @@
             pltpu.make_async_copy(b.at[:, pl.ds(2 * width, LANES)], metas.at[i], meta_sems.at[i])
         )
     for i, b in enumerate(backs):
-        rows = plan.rows[i // inner]
+        rows = plan.sizes[i // inner]
         later.append(pltpu.make_async_copy(b, held.at[pl.ds(start, rows)], sems.at[i]))
         start += rows
     for c in copies + later:
@@ -378,7 +384,6 @@
     full = 2 * width + LANES
     shape = jax.ShapeDtypeStruct
     info = jnp.asarray(plan.table())[lax.axis_index("expert")]
-    keys = [jnp.asarray(k) for k in plan.keys]
     swap = [(0, 1), (1, 0)]
 
     block = pl.pallas_call(
@@ -419,16 +424,16 @@
             compiler_params=params(),
             cost_estimate=cost(4 * n * tok * count * width, 2 * n * tok * full),
             name="compact",
-        )(info, keys[c], *[blocks[i] for i in use])
-
-    def expert(c, arrived):
-        rows = plan.rows[c]
+        )(info, jnp.asarray(plan.keys([plan.chunks[c]])), *[blocks[i] for i in use])
+
+    def expert(g, arrived):
+        rows, n = plan.sizes[g], inner * len(plan.groups[g])
         count = inner * rows
         return pl.pallas_call(
-            functools.partial(expert_kernel, plan, c),
+            functools.partial(expert_kernel, plan, g),
             out_shape=[shape((count, hidden), BF)] * 3
             + [shape((rows, width + LANES), BF)] * inner,
-            in_specs=[SMEM] + [ANY] * (inner + 6),
+            in_specs=[SMEM] + [ANY] * (n + 6),
             out_specs=[VMEM] * (3 + inner),
             scratch_shapes=[
                 pltpu.VMEM((count, width), BF),
@@ -437,7 +442,7 @@
                 pltpu.VMEM((width, hidden), BF),
                 pltpu.VMEM((hidden, width), BF),
                 pltpu.VMEM((count, 1), F32),
-                pltpu.SemaphoreType.DMA((2 * inner + 6 * (hidden // 128),)),
+                pltpu.SemaphoreType.DMA((2 * n + 6 * (hidden // 128),)),
             ],
             compiler_params=params(),
             cost_estimate=cost(10 * count * hidden * width, 6 * hidden * width),
@@ -449,26 +454,27 @@
             lax.ppermute(arrays[d], "expert", plan.across(d)) for d in range(1, inner)
         ]
 
-    near = max((i if i < outer else i - outer + 1) for i in plan.use[0])
-    for r in range(2, near + 1):
-        blocks[r] = lax.ppermute(blocks[r - 1], "expert", plan.line(1))
-        blocks[outer - 1 + r] = lax.ppermute(blocks[outer - 2 + r], "expert", plan.line(-1))
-    sent = compact(0)
-    for r in range(near + 1, outer):
-        blocks[r] = lax.ppermute(blocks[r - 1], "expert", plan.line(1))
-        blocks[outer - 1 + r] = lax.ppermute(blocks[outer - 2 + r], "expert", plan.line(-1))
-        if r == near + 1:
-            blocks[r], blocks[outer - 1 + r], sent = lax.optimization_barrier(
-                (blocks[r], blocks[outer - 1 + r], sent)
+    got, done = [], 1
+    for c in range(PARTS):
+        for r in range(done + 1, plan.steps[c] + 1):
+            blocks[r] = lax.ppermute(blocks[r - 1], "expert", plan.line(1))
+            blocks[outer - 1 + r] = lax.ppermute(blocks[outer - 2 + r], "expert", plan.line(-1))
+        done = max(done, plan.steps[c])
+        if c >= 2:
+            got[c - 2], low, high = lax.optimization_barrier(
+                (got[c - 2], blocks[done], blocks[outer - 1 + done])
             )
-    got = cross(sent)
-    late = cross(compact(1))
-    outs = expert(0, got)
+            blocks[done], blocks[outer - 1 + done] = low, high
+        sent = compact(c)
+        got.append(cross(sent))
+    outs = expert(0, sum(got[:-1], []))
+    late = got[-1]
     outs, late = lax.optimization_barrier((outs, late))
+    got[-1] = late
     backs = cross(outs[3:])
     more = expert(1, late)
     backs, more = lax.optimization_barrier((backs, more))
-    got = got + late
+    got = sum(got, [])
     mids = outs[:3] + more[:3]
     backs = backs + cross(more[3:])
 
@@ -482,32 +488,33 @@
                 shape((1, width, part), BF),
                 shape((1, part, width), BF),
             ],
-            in_specs=[ANY] * (2 * inner + 6) + [VMEM] * len(extra),
+            in_specs=[ANY] * (inner * PARTS + 6) + [VMEM] * len(extra),
             out_specs=[VMEM] * 3,
             scratch_shapes=[
                 pltpu.VMEM((count, width), BF),
                 pltpu.VMEM((count, width), BF),
                 pltpu.VMEM((count, part), BF),
                 pltpu.VMEM((count, 2 * part), BF),
-                pltpu.SemaphoreType.DMA((4 * inner + 6,)),
+                pltpu.SemaphoreType.DMA((2 * inner * PARTS,)),
+                pltpu.SemaphoreType.DMA((6,)),
             ],
             compiler_params=params(),
             cost_estimate=cost(6 * count * part * width, 4 * count * (width + hidden)),
             name="weight_grads",
         )(*got, *mids, *extra)
 
-    def spread(homes, chunks, extra):
-        slots = inner * sum(plan.rows[:chunks])
+    def spread(homes, groups, extra):
+        slots = inner * sum(plan.sizes[:groups])
         return pl.pallas_call(
-            functools.partial(spread_kernel, plan, homes, chunks),
+            functools.partial(spread_kernel, plan, homes, groups),
             out_shape=[shape((tok, width + LANES), BF)] * len(homes),
-            in_specs=[SMEM, VMEM] + [ANY] * (plan.cands + chunks * inner + len(extra)),
+            in_specs=[SMEM, VMEM] + [ANY] * (plan.cands + groups * inner + len(extra)),
             out_specs=[VMEM] * len(homes),
             scratch_shapes=[
                 pltpu.VMEM((slots, width + LANES), BF),
                 pltpu.VMEM((plan.cands, tok, LANES), BF),
                 pltpu.VMEM((len(homes) * tok, slots), BF),
-                pltpu.SemaphoreType.DMA((chunks * inner,)),
+                pltpu.SemaphoreType.DMA((groups * inner,)),
                 pltpu.SemaphoreType.DMA((plan.cands,)),
             ],
             compiler_params=params(),
@@ -515,20 +522,20 @@
             name="spread",
         )(
             info,
-            jnp.concatenate(keys[:chunks], axis=1),
+            jnp.asarray(plan.keys(plan.spans[:groups])),
             *blocks,
-            *backs[: chunks * inner],
+            *backs[: groups * inner],
             *extra,
         )
 
     (first,) = spread([1], 1, [mids[3]])
-    sums = {1: first}
+    sums = {}
+    mine = weight_grads(False, [])
+    mine, backs, first = lax.optimization_barrier((mine, backs, first))
     came = [lax.ppermute(first, "expert", plan.flip(1))]
-    mine = weight_grads(False, [])
-    mine, backs = lax.optimization_barrier((mine, backs))
     theirs = [lax.ppermute(w, "dp", swap) for w in mine]
     rest = [r for r in range(outer) if r != 1]
-    sums.update(zip(rest, spread(rest, 2, [mine[0]])))
+    sums.update(zip(rest, spread(rest, 2, [mine[0], first])))
     bit = 1
     while bit < outer:
         for r in range(bit, outer, 2 * bit):

time: 176 us -> 179 us (1.017)
  waiting for transfers between devices: 53.8 us -> 38.6 us
  starting transfers between devices: 37.5 us -> 48 us
  Pallas kernels: 76.4 us -> 84.1 us
    ppermute x1, waiting for transfers between devices: 11.1 us -> 1.3 us  [on_device(): blocks[1] = lax.ppermute(block, 'expert', plan.line(1))]
    ppermute x2, waiting for transfers between devices: 9.18 us -> 0.01 us  [on_device(): blocks[r] = lax.ppermute(blocks[r - 1], 'expert', plan.line(1))]
    ppermute x2, waiting for transfers between devices: 8.29 us -> 0.01 us  [on_device(): lax.ppermute(blocks[outer - 2 + r], 'expert', plan.line(-1))]
    ppermute x1, waiting for transfers between devices: 4.04 us -> 11.1 us  [on_device(): blocks[outer] = lax.ppermute(block, 'expert', plan.line(-1))]
    ppermute x12 -> x18, starting transfers between devices: 14.1 us -> 21 us  [cross(): lax.ppermute(arrays[d], 'expert', plan.across(d))]
    pallas_call x2 -> x4, Pallas kernels: 10.1 us -> 15.6 us  [compact(): pl.pallas_call(functools.partial(compact_kernel, plan, c), out_shape=[sha...]
    ppermute x2, waiting for transfers between devices: 3.46 us -> 7.74 us  [on_device(): sent = lax.ppermute(sums[r], 'expert', plan.flip(bit))]
    ppermute x12 -> x18, waiting for transfers between devices: 17.7 us -> 18.4 us  [cross(): lax.ppermute(arrays[d], 'expert', plan.across(d))]
  transfers between devices with their start and end apart: 27 -> 33, of which waited for: 12 -> 8; matrix products, arithmetic and copies ran while one was open for 1% -> 1% of each run, Pallas kernels for 42% -> 46%
where the time goes in v3:
time: 179 us; the launch traced here: 178 us
  Pallas kernels  84.1 us (47%)
  starting transfers between devices  48 us (27%)
  waiting for transfers between devices  38.6 us (22%)
  local copies, waits for them, and re-layouts  6.55 us (4%)
    pallas_call x2, Pallas kernels, expert(): pl.pallas_call(functools.partial(expert_kernel, plan, g), out_shape=[shap...  29.8 us
    pallas_call x2, Pallas kernels, weight_grads(): pl.pallas_call(functools.partial(weight_kernel, plan, own), out_shape=[sh...  22.3 us
    ppermute x18, starting transfers between devices, cross(): lax.ppermute(arrays[d], 'expert', plan.across(d))  21 us
    ppermute x18, waiting for transfers between devices, cross(): lax.ppermute(arrays[d], 'expert', plan.across(d))  18.4 us
    pallas_call x4, Pallas kernels, compact(): pl.pallas_call(functools.partial(compact_kernel, plan, c), out_shape=[sha...  15.6 us
    ppermute x1, waiting for transfers between devices, on_device(): blocks[outer] = lax.ppermute(block, 'expert', plan.line(-1))  11.1 us
    pallas_call x2, Pallas kernels, spread(): pl.pallas_call(functools.partial(spread_kernel, plan, homes, groups), out...  10.2 us
    ppermute x2, starting transfers between devices, on_device(): blocks[r] = lax.ppermute(blocks[r - 1], 'expert', plan.line(1))  8.6 us
  transfers between devices with their start and end apart: 33, of which 8 were waited for; matrix products, arithmetic and copies ran while one was open for 1% of the time, Pallas kernels for 46%

profile of v3, /device:TPU:0, one launch (start us, length us, event | category | flops | bytes accessed | tf_op | source)
XLA Modules:
  0.0 178.3 jit_solution(17735788472621294863)
XLA Ops:
  1.7 2.1 %pack.1.refs_2_ = bf16[64,4224]{1,0:T(8,128)(2,1)} custom-call(bf16[64,2048]{1,0:T(8,128)(2,1)} %tok_ref.1, bf16[64,2048]{1,0:T(8,128)(2,1)} %up_ref.1, s32[8,64]{1,0:T(8,128)} %bitcast.5, bf16[8,64]{1,0:T(8,128)(2,1)} %bitcast.7), custom_call_target="tpu_custom_call" | custom-call | flops 1000000 | bytes 1081344 | tf_op jit(solution)/shard_map/pack/pallas_call | solution.py:389
  5.1 5.2 %collective-permute-start.3 = (bf16[64,4224]{1,0:T(8,128)(2,1)}, bf16[64,4224]{1,0:T(8,128)(2,1)S(1)}, u32[]{:S(2)}, u32[]{:S(2)}) collective-permute-start(bf16[64,4224]{1,0:T(8,128)(2,1)} %pack.1.refs_2_), channel_id=1, source_target_pairs={{0,4},{1,5},{2,6},{3,7},{4,8},{5,9},{6,10},{7,11},{8,12},{9,13},{1... | collective-permute-start | bytes 1622024 | tf_op jit(solution)/shard_map/ppermute | solution.py:401
  10.3 11.1 %collective-permute-done.4.refs_4_.refs_5_.refs_6_ = bf16[64,4224]{1,0:T(8,128)(2,1)S(1)} collective-permute-done((bf16[64,4224]{1,0:T(8,128)(2,1)}, bf16[64,4224]{1,0:T(8,128)(2,1)S(1)}, u32[]{:S(2)}, u32[]{:S(2)}) %collective-permute-start.4) | collective-permute-done | bytes 540704 | tf_op jit(solution)/shard_map/ppermute | solution.py:402
  23.9 4.3 %collective-permute-start.8 = (bf16[64,4224]{1,0:T(8,128)(2,1)S(1)}, bf16[64,4224]{1,0:T(8,128)(2,1)S(1)}, u32[]{:S(2)}, u32[]{:S(2)}) collective-permute-start(bf16[64,4224]{1,0:T(8,128)(2,1)S(1)} %collective-permute-done.3.refs_3_.refs_2_), channel_id=1, source_target_pairs={{0,4},{1,5},{2,6},{3,7},{4,8},{5,9},{6,10},{7,11},{8,12},{9,13},{1... | collective-permute-start | bytes 1622024 | tf_op jit(solution)/shard_map/ppermute | solution.py:460
  30.7 3.3 %compact.4 = (bf16[64,2048]{1,0:T(8,128)(2,1)}, bf16[64,2048]{1,0:T(8,128)(2,1)}, bf16[64,2048]{1,0:T(8,128)(2,1)}, bf16[64,2048]{1,0:T(8,128)(2,1)}) custom-call(s32[15]{0:T(128)} %dynamic-slice_bitcast_fusion.refs_0_, s32[1,128]{1,0:T(1,128)} %constant.23.clone.refs_1_, bf16[64,4224]{1,0:T(8,128)(2,1)} %pack.1.refs_2_), custom_call_target="tpu_custom_call" | custom-call | flops 67108864 | bytes 540672 | tf_op jit(solution)/shard_map/compact/pallas_call | solution.py:413
  37.6 6.0 %collective-permute-done.5.refs_2_.refs_1_ = bf16[64,2048]{1,0:T(8,128)(2,1)S(1)} collective-permute-done((bf16[64,2048]{1,0:T(8,128)(2,1)}, bf16[64,2048]{1,0:T(8,128)(2,1)S(1)}, u32[]{:S(2)}, u32[]{:S(2)}) %collective-permute-start.5) | collective-permute-done | bytes 262176 | tf_op jit(solution)/shard_map/ppermute | solution.py:454
  43.5 5.0 %collective-permute-done.6.refs_3_.refs_2_ = bf16[64,2048]{1,0:T(8,128)(2,1)S(1)} collective-permute-done((bf16[64,2048]{1,0:T(8,128)(2,1)}, bf16[64,2048]{1,0:T(8,128)(2,1)S(1)}, u32[]{:S(2)}, u32[]{:S(2)}) %collective-permute-start.6) | collective-permute-done | bytes 262176 | tf_op jit(solution)/shard_map/ppermute | solution.py:454
  48.6 4.3 %collective-permute-start.13 = (bf16[64,4224]{1,0:T(8,128)(2,1)S(1)}, bf16[64,4224]{1,0:T(8,128)(2,1)S(1)}, u32[]{:S(2)}, u32[]{:S(2)}) collective-permute-start(bf16[64,4224]{1,0:T(8,128)(2,1)S(1)} %collective-permute-done.8.refs_3_.refs_4_), channel_id=1, source_target_pairs={{0,4},{1,5},{2,6},{3,7},{4,8},{5,9},{6,10},{7,11},{8,12},{9,13},{1... | collective-permute-start | bytes 1622024 | tf_op jit(solution)/shard_map/ppermute | solution.py:460
  54.2 3.6 %compact.5 = (bf16[64,2048]{1,0:T(8,128)(2,1)}, bf16[64,2048]{1,0:T(8,128)(2,1)}, bf16[64,2048]{1,0:T(8,128)(2,1)}, bf16[64,2048]{1,0:T(8,128)(2,1)}) custom-call(s32[15]{0:T(128)} %dynamic-slice_bitcast_fusion.refs_0_, s32[1,128]{1,0:T(1,128)} %constant.24.clone.refs_1_, bf16[64,4224]{1,0:T(8,128)(2,1)} %pack.1.refs_2_, bf16[64,4224]{1,0:T(8,128)(2,1)} %copy-done.1, ...), custom_call_target="tpu_custom_call" | custom-call | flops 201326592 | bytes 1622016 | tf_op jit(solution)/shard_map/compact/pallas_call | solution.py:413
  61.4 3.8 %compact.6 = (bf16[64,2048]{1,0:T(8,128)(2,1)}, bf16[64,2048]{1,0:T(8,128)(2,1)}, bf16[64,2048]{1,0:T(8,128)(2,1)}, bf16[64,2048]{1,0:T(8,128)(2,1)}) custom-call(s32[15]{0:T(128)} %dynamic-slice_bitcast_fusion.refs_0_, s32[1,128]{1,0:T(1,128)} %constant.25.clone.refs_1_, bf16[64,4224]{1,0:T(8,128)(2,1)} %copy-done.1, bf16[64,4224]{1,0:T(8,128)(2,1)} %copy-done.2, ...), custom_call_target="tpu_custom_call" | custom-call | flops 268435456 | bytes 2162688 | tf_op jit(solution)/shard_map/compact/pallas_call | solution.py:413
  65.2 2.1 %collective-permute-done.10.refs_6_.refs_5_ = bf16[64,2048]{1,0:T(8,128)(2,1)S(1)} collective-permute-done((bf16[64,2048]{1,0:T(8,128)(2,1)}, bf16[64,2048]{1,0:T(8,128)(2,1)S(1)}, u32[]{:S(2)}, u32[]{:S(2)}) %collective-permute-start.10) | collective-permute-done | bytes 262176 | tf_op jit(solution)/shard_map/ppermute | solution.py:454
  69.4 4.6 %collective-permute-done.12.refs_8_.refs_7_ = bf16[64,2048]{1,0:T(8,128)(2,1)S(1)} collective-permute-done((bf16[64,2048]{1,0:T(8,128)(2,1)}, bf16[64,2048]{1,0:T(8,128)(2,1)S(1)}, u32[]{:S(2)}, u32[]{:S(2)}) %collective-permute-start.12) | collective-permute-done | bytes 262176 | tf_op jit(solution)/shard_map/ppermute | solution.py:454
  76.2 4.9 %compact.7 = (bf16[96,2048]{1,0:T(8,128)(2,1)}, bf16[96,2048]{1,0:T(8,128)(2,1)}, bf16[96,2048]{1,0:T(8,128)(2,1)}, bf16[96,2048]{1,0:T(8,128)(2,1)}) custom-call(s32[15]{0:T(128)} %dynamic-slice_bitcast_fusion.refs_0_, s32[1,192]{1,0:T(1,128)} %constant.26.clone.refs_1_, bf16[64,4224]{1,0:T(8,128)(2,1)} %copy-done.1, bf16[64,4224]{1,0:T(8,128)(2,1)} %copy-done.2, ...), custom_call_target="tpu_custom_call" | custom-call | flops 603979776 | bytes 3244032 | tf_op jit(solution)/shard_map/compact/pallas_call | solution.py:413
  85.4 17.3 %expert.2 = (bf16[384,768]{1,0:T(8,128)(2,1)}, bf16[384,768]{1,0:T(8,128)(2,1)}, bf16[384,768]{1,0:T(8,128)(2,1)}, bf16[96,2176]{1,0:T(8,128)(2,1)}, bf16[96,217...) custom-call(s32[15]{0:T(128)} %dynamic-slice_bitcast_fusion.refs_0_, ...), custom_call_target="tpu_custom_call" | custom-call | flops 6039797760 | bytes 9437184 | tf_op jit(solution)/shard_map/expert/pallas_call | solution.py:432
  106.3 12.6 %expert.3 = (bf16[192,768]{1,0:T(8,128)(2,1)}, bf16[192,768]{1,0:T(8,128)(2,1)}, bf16[192,768]{1,0:T(8,128)(2,1)}, bf16[48,2176]{1,0:T(8,128)(2,1)}, bf16[48,217...) custom-call(s32[15]{0:T(128)} %dynamic-slice_bitcast_fusion.refs_0_, ...), custom_call_target="tpu_custom_call" | custom-call | flops 3019898880 | bytes 9437184 | tf_op jit(solution)/shard_map/expert/pallas_call | solution.py:432
  122.5 4.5 %spread.2.refs_18_ = bf16[64,2176]{1,0:T(8,128)(2,1)} custom-call(s32[15]{0:T(128)} %dynamic-slice_bitcast_fusion.refs_0_, s32[1,384]{1,0:T(1,128)} %constant.27.clone.refs_1_, bf16[64,4224]{1,0:T(8,128)(2,1)} %pack.1.refs_2_, bf16[64,4224]{1,0:T(8,128)(2,1)} %copy-done.1, bf16[64,4224]{1,0:T(8,128)(2,1)} %copy-done.2, bf16[64,4224]{1,0:T(8,128)(2,1)} %copy-done.4, ...), custom_call_target="tpu_custom_call" | custom-call | flops 100663296 | bytes 1572864 | tf_op jit(solution)/shard_map/spread/pallas_call | solution.py:508
  127.0 10.0 %weight_grads.2 = (bf16[1,2048,384]{2,1,0:T(8,128)(2,1)}, bf16[1,2048,384]{2,1,0:T(8,128)(2,1)}, bf16[1,384,2048]{2,1,0:T(8,128)(2,1)}) custom-call(bf16[64,2048]{1,0:T(8,128)(2,1)} %get-tuple-element.111.refs_1_.refs_0_, bf16[64,2048]{1,0:T(8,128)(2,1)} %copy-done.16, bf16[64,2048]{1,0:T(8,128)(2,1)} %copy-done.17, bf16[64,2048]{1,0:T(8,128)(2,1)} %copy-done.18, ...), custom_call_target="tpu_custom_call" | custom-call | flops 2717908992 | bytes 6488064 | tf_op jit(solution)/shard_map/weight_grads/pallas_call | solution.py:484
  138.3 5.8 %spread.3 = (bf16[64,2176]{1,0:T(8,128)(2,1)}, bf16[64,2176]{1,0:T(8,128)(2,1)}, bf16[64,2176]{1,0:T(8,128)(2,1)}) custom-call(s32[15]{0:T(128)} %dynamic-slice_bitcast_fusion.refs_0_, s32[1,576]{1,0:T(1,128)} %constant.28.clone.refs_1_, bf16[64,4224]{1,0:T(8,128)(2,1)} %pack.1.refs_2_, bf16[64,4224]{1,0:T(8,128)(2,1)} %copy-done.1, ...), custom_call_target="tpu_custom_call" | custom-call | flops 452984832 | bytes 2359296 | tf_op jit(solution)/shard_map/spread/pallas_call | solution.py:508
  144.0 2.8 %collective-permute-start.28 = (bf16[64,2176]{1,0:T(8,128)(2,1)}, bf16[64,2176]{1,0:T(8,128)(2,1)}, u32[]{:S(2)}, u32[]{:S(2)}) collective-permute-start(bf16[64,2176]{1,0:T(8,128)(2,1)} %get-tuple-element.181), channel_id=1, source_target_pairs={{0,4},{1,5},{2,6},{3,7},{4,0},{5,1},{6,2},{7,3},{8,12},{9,13},{10,... | collective-permute-start | bytes 835592 | tf_op jit(solution)/shard_map/ppermute | solution.py:544
  146.9 7.7 %collective-permute-done.28.b_ref = bf16[64,2176]{1,0:T(8,128)(2,1)} collective-permute-done((bf16[64,2176]{1,0:T(8,128)(2,1)}, bf16[64,2176]{1,0:T(8,128)(2,1)}, u32[]{:S(2)}, u32[]{:S(2)}) %collective-permute-start.28) | collective-permute-done | bytes 278560 | tf_op jit(solution)/shard_map/ppermute | solution.py:544
  154.7 1.8 %add.5 = bf16[64,2176]{1,0:T(8,128)(2,1)} custom-call(bf16[64,2176]{1,0:T(8,128)(2,1)} %get-tuple-element.180.a_ref, bf16[64,2176]{1,0:T(8,128)(2,1)} %collective-permute-done.28.b_ref), custom_call_target="tpu_custom_call" | custom-call | tf_op jit(solution)/shard_map/add/pallas_call | solution.py:548
  156.5 4.9 %collective-permute-start.29 = (bf16[64,2176]{1,0:T(8,128)(2,1)}, bf16[64,2176]{1,0:T(8,128)(2,1)S(1)}, u32[]{:S(2)}, u32[]{:S(2)}) collective-permute-start(bf16[64,2176]{1,0:T(8,128)(2,1)} %add.5), channel_id=1, source_target_pairs={{0,8},{1,9},{2,10},{3,11},{4,12},{5,13},{6,14},{7,15},{8,0},{9,1},... | collective-permute-start | bytes 835592 | tf_op jit(solution)/shard_map/ppermute | solution.py:544
  163.0 12.3 %weight_grads.3 = (bf16[1,2048,384]{2,1,0:T(8,128)(2,1)}, bf16[1,2048,384]{2,1,0:T(8,128)(2,1)}, bf16[1,384,2048]{2,1,0:T(8,128)(2,1)}) custom-call(bf16[64,2048]{1,0:T(8,128)(2,1)} %get-tuple-element.111.refs_1_.refs_0_, bf16[64,2048]{1,0:T(8,128)(2,1)} %copy-done.16, bf16[64,2048]{1,0:T(8,128)(2,1)} %copy-done.17, bf16[64,2048]{1,0:T(8,128)(2,1)} %copy-done.18, ...), custom_call_target="tpu_custom_call" | custom-call | flops 2717908992 | bytes 6488064 | tf_op jit(solution)/shard_map/weight_grads/pallas_call | solution.py:484
  176.1 2.2 %home.1 = (bf16[64,2048]{1,0:T(8,128)(2,1)}, bf16[8,64]{1,0:T(8,128)(2,1)}) custom-call(bf16[64,2176]{1,0:T(8,128)(2,1)} %get-tuple-element.179.refs_0_, bf16[64,2176]{1,0:T(8,128)(2,1)} %collective-permute-done.27.refs_1_, bf16[64,2176]{1,0:T(8,128)(2,1)} %copy-done.15, s32[8,64]{1,0:T(8,128)} %bitcast.6, bf16[8,64]{1,0:T(8,128)(2,1)} %bitcast.8, ...), custom_call_target="tpu_custom_call" | custom-call | flops 1000000 | bytes 1310720 | tf_op jit(solution)/shard_map/home/pallas_call | solution.py:558
  (112 shorter events, 35.1 us)
Async XLA Ops:
  0.6 22.1 %collective-permute-start = (bf16[1,2048,384]{2,1,0:T(8,128)(2,1)}, bf16[1,2048,384]{2,1,0:T(8,128)(2,1)S(1)}, u32[]{:S(2)}, u32[]{:S(2)}) collective-permute-start(bf16[1,2048,384]{2,1,0:T(8,128)(2,1)} %refs_5_.1), channel_id=1, source_target_pairs={{0,16},{16,0},{1,17},{17,1},{2,18},{18,2},{3,19},{19,3},{4,20},{20... | collective-permute-start | bytes 4718600 | tf_op jit(solution)/shard_map/ppermute | solution.py:399
  1.1 21.6 %collective-permute-start.1 = (bf16[1,2048,384]{2,1,0:T(8,128)(2,1)}, bf16[1,2048,384]{2,1,0:T(8,128)(2,1)}, u32[]{:S(2)}, u32[]{:S(2)}) collective-permute-start(bf16[1,2048,384]{2,1,0:T(8,128)(2,1)} %refs_7_.1), channel_id=1, source_target_pairs={{0,16},{16,0},{1,17},{17,1},{2,18},{18,2},{3,19},{19,3},{4,20},{20... | collective-permute-start | bytes 4718600 | tf_op jit(solution)/shard_map/ppermute | solution.py:399
  1.2 22.6 %collective-permute-start.2 = (bf16[1,384,2048]{2,1,0:T(8,128)(2,1)}, bf16[1,384,2048]{2,1,0:T(8,128)(2,1)}, u32[]{:S(2)}, u32[]{:S(2)}) collective-permute-start(bf16[1,384,2048]{2,1,0:T(8,128)(2,1)} %refs_9_.1), channel_id=1, source_target_pairs={{0,16},{16,0},{1,17},{17,1},{2,18},{18,2},{3,19},{19,3},{4,20},{20... | collective-permute-start | bytes 4718600 | tf_op jit(solution)/shard_map/ppermute | solution.py:399
  3.8 17.6 %collective-permute-start.4 = (bf16[64,4224]{1,0:T(8,128)(2,1)}, bf16[64,4224]{1,0:T(8,128)(2,1)S(1)}, u32[]{:S(2)}, u32[]{:S(2)}) collective-permute-start(bf16[64,4224]{1,0:T(8,128)(2,1)} %pack.1.refs_2_), channel_id=1, source_target_pairs={{4,0},{5,1},{6,2},{7,3},{8,4},{9,5},{10,6},{11,7},{12,8},{13,9},{1... | collective-permute-start | bytes 1622024 | tf_op jit(solution)/shard_map/ppermute | solution.py:402
  5.1 17.6 %collective-permute-start.3 = (bf16[64,4224]{1,0:T(8,128)(2,1)}, bf16[64,4224]{1,0:T(8,128)(2,1)S(1)}, u32[]{:S(2)}, u32[]{:S(2)}) collective-permute-start(bf16[64,4224]{1,0:T(8,128)(2,1)} %pack.1.refs_2_), channel_id=1, source_target_pairs={{0,4},{1,5},{2,6},{3,7},{4,8},{5,9},{6,10},{7,11},{8,12},{9,13},{1... | collective-permute-start | bytes 1622024 | tf_op jit(solution)/shard_map/ppermute | solution.py:401
  23.9 24.7 %collective-permute-start.8 = (bf16[64,4224]{1,0:T(8,128)(2,1)S(1)}, bf16[64,4224]{1,0:T(8,128)(2,1)S(1)}, u32[]{:S(2)}, u32[]{:S(2)}) collective-permute-start(bf16[64,4224]{1,0:T(8,128)(2,1)S(1)} %collective-permute-done.3.refs_3_.refs_2_), channel_id=1, source_target_pairs={{0,4},{1,5},{2,6},{3,7},{4,8},{5,9},{6,10},{7,11},{8,12},{9,13},{1... | collective-permute-start | bytes 1622024 | tf_op jit(solution)/shard_map/ppermute | solution.py:460
  28.2 20.4 %collective-permute-start.9 = (bf16[64,4224]{1,0:T(8,128)(2,1)S(1)}, bf16[64,4224]{1,0:T(8,128)(2,1)S(1)}, u32[]{:S(2)}, u32[]{:S(2)}) collective-permute-start(bf16[64,4224]{1,0:T(8,128)(2,1)S(1)} %collective-permute-done.4.refs_4_.refs_5_.refs_6_), channel_id=1, source_target_pairs={{4,0},{5,1},{6,2},{7,3},{8,4},{9,5},{10,6},{11,7},{12,8},{13,9},{1... | collective-permute-start | bytes 1622024 | tf_op jit(solution)/shard_map/ppermute | solution.py:461
  48.6 26.6 %collective-permute-start.13 = (bf16[64,4224]{1,0:T(8,128)(2,1)S(1)}, bf16[64,4224]{1,0:T(8,128)(2,1)S(1)}, u32[]{:S(2)}, u32[]{:S(2)}) collective-permute-start(bf16[64,4224]{1,0:T(8,128)(2,1)S(1)} %collective-permute-done.8.refs_3_.refs_4_), channel_id=1, source_target_pairs={{0,4},{1,5},{2,6},{3,7},{4,8},{5,9},{6,10},{7,11},{8,12},{9,13},{1... | collective-permute-start | bytes 1622024 | tf_op jit(solution)/shard_map/ppermute | solution.py:460
  52.9 22.3 %collective-permute-start.14 = (bf16[64,4224]{1,0:T(8,128)(2,1)S(1)}, bf16[64,4224]{1,0:T(8,128)(2,1)S(1)}, u32[]{:S(2)}, u32[]{:S(2)}) collective-permute-start(bf16[64,4224]{1,0:T(8,128)(2,1)S(1)} %collective-permute-done.9.refs_5_.refs_6_.refs_7_), channel_id=1, source_target_pairs={{4,0},{5,1},{6,2},{7,3},{8,4},{9,5},{10,6},{11,7},{12,8},{13,9},{1... | collective-permute-start | bytes 1622024 | tf_op jit(solution)/shard_map/ppermute | solution.py:461
  67.4 16.1 %collective-permute-start.15 = (bf16[64,2048]{1,0:T(8,128)(2,1)}, bf16[64,2048]{1,0:T(8,128)(2,1)S(1)}, u32[]{:S(2)}, u32[]{:S(2)}) collective-permute-start(bf16[64,2048]{1,0:T(8,128)(2,1)} %get-tuple-element.120), channel_id=1, source_target_pairs={{0,1},{1,0},{2,3},{3,2},{4,5},{5,4},{6,7},{7,6},{8,9},{9,8},{10,11... | collective-permute-start | bytes 786440 | tf_op jit(solution)/shard_map/ppermute | solution.py:454
  68.6 16.0 %collective-permute-start.16 = (bf16[64,2048]{1,0:T(8,128)(2,1)}, bf16[64,2048]{1,0:T(8,128)(2,1)S(1)}, u32[]{:S(2)}, u32[]{:S(2)}) collective-permute-start(bf16[64,2048]{1,0:T(8,128)(2,1)} %get-tuple-element.121), channel_id=1, source_target_pairs={{0,2},{1,3},{2,0},{3,1},{4,6},{5,7},{6,4},{7,5},{8,10},{9,11},{10,... | collective-permute-start | bytes 786440 | tf_op jit(solution)/shard_map/ppermute | solution.py:454
  81.1 21.6 %collective-permute-start.18 = (bf16[96,2048]{1,0:T(8,128)(2,1)}, bf16[96,2048]{1,0:T(8,128)(2,1)S(1)}, u32[]{:S(2)}, u32[]{:S(2)}) collective-permute-start(bf16[96,2048]{1,0:T(8,128)(2,1)} %get-tuple-element.134), channel_id=1, source_target_pairs={{0,1},{1,0},{2,3},{3,2},{4,5},{5,4},{6,7},{7,6},{8,9},{9,8},{10,11... | collective-permute-start | bytes 1179656 | tf_op jit(solution)/shard_map/ppermute | solution.py:454
  81.9 20.7 %collective-permute-start.19 = (bf16[96,2048]{1,0:T(8,128)(2,1)}, bf16[96,2048]{1,0:T(8,128)(2,1)S(1)}, u32[]{:S(2)}, u32[]{:S(2)}) collective-permute-start(bf16[96,2048]{1,0:T(8,128)(2,1)} %get-tuple-element.135), channel_id=1, source_target_pairs={{0,2},{1,3},{2,0},{3,1},{4,6},{5,7},{6,4},{7,5},{8,10},{9,11},{10,... | collective-permute-start | bytes 1179656 | tf_op jit(solution)/shard_map/ppermute | solution.py:454
  83.5 19.2 %collective-permute-start.20 = (bf16[96,2048]{1,0:T(8,128)(2,1)}, bf16[96,2048]{1,0:T(8,128)(2,1)S(1)}, u32[]{:S(2)}, u32[]{:S(2)}) collective-permute-start(bf16[96,2048]{1,0:T(8,128)(2,1)} %get-tuple-element.136), channel_id=1, source_target_pairs={{0,3},{1,2},{2,1},{3,0},{4,7},{5,6},{6,5},{7,4},{8,11},{9,10},{10,... | collective-permute-start | bytes 1179656 | tf_op jit(solution)/shard_map/ppermute | solution.py:454
  102.7 16.1 %collective-permute-start.21 = (bf16[96,2176]{1,0:T(8,128)(2,1)}, bf16[96,2176]{1,0:T(8,128)(2,1)S(1)}, u32[]{:S(2)}, u32[]{:S(2)}) collective-permute-start(bf16[96,2176]{1,0:T(8,128)(2,1)} %get-tuple-element.145), channel_id=1, source_target_pairs={{0,1},{1,0},{2,3},{3,2},{4,5},{5,4},{6,7},{7,6},{8,9},{9,8},{10,11... | collective-permute-start | bytes 1253384 | tf_op jit(solution)/shard_map/ppermute | solution.py:454
  103.5 15.3 %collective-permute-start.22 = (bf16[96,2176]{1,0:T(8,128)(2,1)}, bf16[96,2176]{1,0:T(8,128)(2,1)S(1)}, u32[]{:S(2)}, u32[]{:S(2)}) collective-permute-start(bf16[96,2176]{1,0:T(8,128)(2,1)} %get-tuple-element.146), channel_id=1, source_target_pairs={{0,2},{1,3},{2,0},{3,1},{4,6},{5,7},{6,4},{7,5},{8,10},{9,11},{10,... | collective-permute-start | bytes 1253384 | tf_op jit(solution)/shard_map/ppermute | solution.py:454
  118.9 18.0 %collective-permute-start.24 = (bf16[48,2176]{1,0:T(8,128)(2,1)}, bf16[48,2176]{1,0:T(8,128)(2,1)S(1)}, u32[]{:S(2)}, u32[]{:S(2)}) collective-permute-start(bf16[48,2176]{1,0:T(8,128)(2,1)} %get-tuple-element.166), channel_id=1, source_target_pairs={{0,1},{1,0},{2,3},{3,2},{4,5},{5,4},{6,7},{7,6},{8,9},{9,8},{10,11... | collective-permute-start | bytes 626696 | tf_op jit(solution)/shard_map/ppermute | solution.py:454
  120.2 16.7 %collective-permute-start.25 = (bf16[48,2176]{1,0:T(8,128)(2,1)}, bf16[48,2176]{1,0:T(8,128)(2,1)S(1)}, u32[]{:S(2)}, u32[]{:S(2)}) collective-permute-start(bf16[48,2176]{1,0:T(8,128)(2,1)} %get-tuple-element.167), channel_id=1, source_target_pairs={{0,2},{1,3},{2,0},{3,1},{4,6},{5,7},{6,4},{7,5},{8,10},{9,11},{10,... | collective-permute-start | bytes 626696 | tf_op jit(solution)/shard_map/ppermute | solution.py:454
  121.2 15.7 %collective-permute-start.26 = (bf16[48,2176]{1,0:T(8,128)(2,1)}, bf16[48,2176]{1,0:T(8,128)(2,1)S(1)}, u32[]{:S(2)}, u32[]{:S(2)}) collective-permute-start(bf16[48,2176]{1,0:T(8,128)(2,1)} %get-tuple-element.168), channel_id=1, source_target_pairs={{0,3},{1,2},{2,1},{3,0},{4,7},{5,6},{6,5},{7,4},{8,11},{9,10},{10,... | collective-permute-start | bytes 626696 | tf_op jit(solution)/shard_map/ppermute | solution.py:454
  137.7 23.6 %collective-permute-start.31 = (bf16[1,2048,384]{2,1,0:T(8,128)(2,1)}, bf16[1,2048,384]{2,1,0:T(8,128)(2,1)S(1)}, u32[]{:S(2)}, u32[]{:S(2)}) collective-permute-start(bf16[1,2048,384]{2,1,0:T(8,128)(2,1)} %get-tuple-element.182), channel_id=1, source_target_pairs={{0,16},{16,0},{1,17},{17,1},{2,18},{18,2},{3,19},{19,3},{4,20},{20... | collective-permute-start | bytes 4718600 | tf_op jit(solution)/shard_map/ppermute | solution.py:536
  137.7 23.6 %collective-permute-start.32 = (bf16[1,384,2048]{2,1,0:T(8,128)(2,1)}, bf16[1,384,2048]{2,1,0:T(8,128)(2,1)S(1)}, u32[]{:S(2)}, u32[]{:S(2)}) collective-permute-start(bf16[1,384,2048]{2,1,0:T(8,128)(2,1)} %get-tuple-element.183), channel_id=1, source_target_pairs={{0,16},{16,0},{1,17},{17,1},{2,18},{18,2},{3,19},{19,3},{4,20},{20... | collective-permute-start | bytes 4718600 | tf_op jit(solution)/shard_map/ppermute | solution.py:536
  138.3 23.1 %collective-permute-start.30 = (bf16[1,2048,384]{2,1,0:T(8,128)(2,1)}, bf16[1,2048,384]{2,1,0:T(8,128)(2,1)}, u32[]{:S(2)}, u32[]{:S(2)}) collective-permute-start(bf16[1,2048,384]{2,1,0:T(8,128)(2,1)} %get-tuple-element.177.refs_17_), channel_id=1, source_target_pairs={{0,16},{16,0},{1,17},{17,1},{2,18},{18,2},{3,19},{19,3},{4,20},{20... | collective-permute-start | bytes 4718600 | tf_op jit(solution)/shard_map/ppermute | solution.py:536
  146.8 28.5 %collective-permute-start.27 = (bf16[64,2176]{1,0:T(8,128)(2,1)S(1)}, bf16[64,2176]{1,0:T(8,128)(2,1)}, u32[]{:S(2)}, u32[]{:S(2)}) collective-permute-start(bf16[64,2176]{1,0:T(8,128)(2,1)S(1)} %copy-done.11), channel_id=1, source_target_pairs={{0,4},{1,5},{2,6},{3,7},{4,0},{5,1},{6,2},{7,3},{8,12},{9,13},{10,... | collective-permute-start | bytes 835592 | tf_op jit(solution)/shard_map/ppermute | solution.py:535
  156.5 18.9 %collective-permute-start.29 = (bf16[64,2176]{1,0:T(8,128)(2,1)}, bf16[64,2176]{1,0:T(8,128)(2,1)S(1)}, u32[]{:S(2)}, u32[]{:S(2)}) collective-permute-start(bf16[64,2176]{1,0:T(8,128)(2,1)} %add.5), channel_id=1, source_target_pairs={{0,8},{1,9},{2,10},{3,11},{4,12},{5,13},{6,14},{7,15},{8,0},{9,1},... | collective-permute-start | bytes 835592 | tf_op jit(solution)/shard_map/ppermute | solution.py:544
  (37 other events, 356.7 us)

commit v4 on v3

--- a/solution.py
+++ b/solution.py
@@ -199,7 +199,7 @@
     backs = refs[10 + n : 10 + n + inner]
     x_s, d_s, wg_s, wu_s, wd_s, comb_s, sems = refs[10 + n + inner :]
     x_copies, d_copies = pieces(plan, group, got, x_s, d_s, sems)
-    tile, tiles = 256, []
+    tile, tiles = hidden, []
     for t in range(hidden // tile):
         for kind, where in ((0, wg_s), (1, wu_s), (2, wd_s)):
             at, here = t * tile, []
@@ -243,7 +243,7 @@
         gate_o[:, at] = (mixed * up * logistic * (1.0 + gate * (1.0 - logistic))).astype(BF)
         up_o[:, at] = (mixed * silu).astype(BF)
 
-    wide = 256
+    wide = width // 2
 
     @pl.loop(0, width // wide)
     def _(j):
@@ -289,7 +289,7 @@
         c.start()
     for c in everything:
         c.wait()
-    tile = 256
+    tile = width // 2
 
     @pl.loop(0, width // tile)
     def _(j):
@@ -337,19 +337,9 @@
         pick_s[i * tok : (i + 1) * tok, :] = one.astype(BF)
     for c in later:
         c.wait()
-    tile = 256
-
-    def piece(at, size):
-        sums = jnp.dot(pick_s[...], held[:, pl.ds(at, size)], preferred_element_type=F32)
-        sums = sums.astype(BF)
-        for i in range(len(homes)):
-            outs[i][:, pl.ds(at, size)] = sums[i * tok : (i + 1) * tok]
-
-    @pl.loop(0, width // tile)
-    def _(j):
-        piece(pl.multiple_of(j * tile, tile), tile)
-
-    piece(width, LANES)
+    sums = jnp.dot(pick_s[...], held[...], preferred_element_type=F32).astype(BF)
+    for i in range(len(homes)):
+        outs[i][...] = sums[i * tok : (i + 1) * tok]
 
 
 def add_kernel(a_ref, b_ref, o_ref):
@@ -400,13 +390,6 @@
     blocks = [block] * plan.cands
     blocks[1] = lax.ppermute(block, "expert", plan.line(1))
     blocks[outer] = lax.ppermute(block, "expert", plan.line(-1))
-    *others, blocks[1], blocks[outer] = lax.optimization_barrier(
-        (*others, blocks[1], blocks[outer])
-    )
-    weights = []
-    for w, other in zip((w_gate, w_up, w_down), others):
-        weights += [w, other]
-
     def compact(c):
         rows, use = plan.rows[c], plan.use[c]
         count, n = inner * rows, len(use)
@@ -460,23 +443,23 @@
             blocks[r] = lax.ppermute(blocks[r - 1], "expert", plan.line(1))
             blocks[outer - 1 + r] = lax.ppermute(blocks[outer - 2 + r], "expert", plan.line(-1))
         done = max(done, plan.steps[c])
-        if c >= 2:
-            got[c - 2], low, high = lax.optimization_barrier(
-                (got[c - 2], blocks[done], blocks[outer - 1 + done])
-            )
-            blocks[done], blocks[outer - 1 + done] = low, high
         sent = compact(c)
+        if c == 0:
+            others, sent = lax.optimization_barrier((others, sent))
+        else:
+            got[-1], sent = lax.optimization_barrier((got[-1], sent))
         got.append(cross(sent))
+    weights = []
+    for w, other in zip((w_gate, w_up, w_down), others):
+        weights += [w, other]
     outs = expert(0, sum(got[:-1], []))
     late = got[-1]
     outs, late = lax.optimization_barrier((outs, late))
     got[-1] = late
     backs = cross(outs[3:])
     more = expert(1, late)
-    backs, more = lax.optimization_barrier((backs, more))
     got = sum(got, [])
     mids = outs[:3] + more[:3]
-    backs = backs + cross(more[3:])
 
     count = inner * sum(plan.rows)
 
@@ -528,9 +511,11 @@
             *extra,
         )
 
-    (first,) = spread([1], 1, [mids[3]])
+    mine = weight_grads(False, [])
+    backs, more, mine = lax.optimization_barrier((backs, more, mine))
+    backs = backs + cross(more[3:])
+    (first,) = spread([1], 1, [])
     sums = {}
-    mine = weight_grads(False, [])
     mine, backs, first = lax.optimization_barrier((mine, backs, first))
     came = [lax.ppermute(first, "expert", plan.flip(1))]
     theirs = [lax.ppermute(w, "dp", swap) for w in mine]

time: 179 us -> 158 us (0.88)
  Pallas kernels: 84.1 us -> 72.4 us
  waiting for transfers between devices: 38.6 us -> 33.4 us
  starting transfers between devices: 48 us -> 45.8 us
  local copies, waits for them, and re-layouts: 6.55 us -> 4.51 us
    ppermute x18, waiting for transfers between devices: 18.4 us -> 11.6 us  [cross(): lax.ppermute(arrays[d], 'expert', plan.across(d))]
    pallas_call x2, Pallas kernels: 29.8 us -> 23.4 us  [expert(): pl.pallas_call(functools.partial(expert_kernel, plan, g), out_shape=[shap...]
    ppermute x2, starting transfers between devices: 7.66 us -> 4.48 us  [on_device(): sent = lax.ppermute(sums[r], 'expert', plan.flip(bit))]
    pallas_call x2, Pallas kernels: 22.3 us -> 19.6 us  [weight_grads(): pl.pallas_call(functools.partial(weight_kernel, plan, own), out_shape=[sh...]
    pallas_call x2, Pallas kernels: 10.2 us -> 7.84 us  [spread(): pl.pallas_call(functools.partial(spread_kernel, plan, homes, groups), out...]
    unnamed x56 -> x58, local copies, waits for them, and re-layouts: 5.35 us -> 3.3 us
    ppermute x2, waiting for transfers between devices: 0.01 us -> 1.97 us  [on_device(): lax.ppermute(blocks[outer - 2 + r], 'expert', plan.line(-1))]
  transfers between devices with their start and end apart: 33 -> 33, of which waited for: 8 -> 10; matrix products, arithmetic and copies ran while one was open for 1% -> 1% of each run, Pallas kernels for 46% -> 45%
where the time goes in v4:
time: 158 us; the launch traced here: 157 us
  Pallas kernels  72.4 us (46%)
  starting transfers between devices  45.8 us (29%)
  waiting for transfers between devices  33.4 us (21%)
  local copies, waits for them, and re-layouts  4.51 us (3%)
    pallas_call x2, Pallas kernels, expert(): pl.pallas_call(functools.partial(expert_kernel, plan, g), out_shape=[shap...  23.4 us
    ppermute x18, starting transfers between devices, cross(): lax.ppermute(arrays[d], 'expert', plan.across(d))  21.2 us
    pallas_call x2, Pallas kernels, weight_grads(): pl.pallas_call(functools.partial(weight_kernel, plan, own), out_shape=[sh...  19.6 us
    pallas_call x4, Pallas kernels, compact(): pl.pallas_call(functools.partial(compact_kernel, plan, c), out_shape=[sha...  15.4 us
    ppermute x18, waiting for transfers between devices, cross(): lax.ppermute(arrays[d], 'expert', plan.across(d))  11.6 us
    ppermute x1, waiting for transfers between devices, on_device(): blocks[outer] = lax.ppermute(block, 'expert', plan.line(-1))  11.1 us
    ppermute x2, starting transfers between devices, on_device(): blocks[r] = lax.ppermute(blocks[r - 1], 'expert', plan.line(1))  9.16 us
    ppermute x2, waiting for transfers between devices, on_device(): sent = lax.ppermute(sums[r], 'expert', plan.flip(bit))  8.68 us
  transfers between devices with their start and end apart: 33, of which 10 were waited for; matrix products, arithmetic and copies ran while one was open for 1% of the time, Pallas kernels for 45%

profile of v4, /device:TPU:0, one launch (start us, length us, event | category | flops | bytes accessed | tf_op | source)
XLA Modules:
  0.0 157.2 jit_solution(13376274472563458631)
XLA Ops:
  1.7 2.1 %pack.1.refs_2_ = bf16[64,4224]{1,0:T(8,128)(2,1)} custom-call(bf16[64,2048]{1,0:T(8,128)(2,1)} %tok_ref.1, bf16[64,2048]{1,0:T(8,128)(2,1)} %up_ref.1, s32[8,64]{1,0:T(8,128)} %bitcast.5, bf16[8,64]{1,0:T(8,128)(2,1)} %bitcast.7), custom_call_target="tpu_custom_call" | custom-call | flops 1000000 | bytes 1081344 | tf_op jit(solution)/shard_map/pack/pallas_call | solution.py:379
  5.1 5.2 %collective-permute-start = (bf16[64,4224]{1,0:T(8,128)(2,1)}, bf16[64,4224]{1,0:T(8,128)(2,1)S(1)}, u32[]{:S(2)}, u32[]{:S(2)}) collective-permute-start(bf16[64,4224]{1,0:T(8,128)(2,1)} %pack.1.refs_2_), channel_id=1, source_target_pairs={{0,4},{1,5},{2,6},{3,7},{4,8},{5,9},{6,10},{7,11},{8,12},{9,13},{1... | collective-permute-start | bytes 1622024 | tf_op jit(solution)/shard_map/ppermute | solution.py:391
  10.3 11.1 %collective-permute-done.3.refs_4_.refs_5_.refs_6_ = bf16[64,4224]{1,0:T(8,128)(2,1)S(1)} collective-permute-done((bf16[64,4224]{1,0:T(8,128)(2,1)}, bf16[64,4224]{1,0:T(8,128)(2,1)S(1)}, u32[]{:S(2)}, u32[]{:S(2)}) %collective-permute-start.3) | collective-permute-done | bytes 540704 | tf_op jit(solution)/shard_map/ppermute | solution.py:392
  22.7 4.6 %collective-permute-start.1 = (bf16[64,4224]{1,0:T(8,128)(2,1)S(1)}, bf16[64,4224]{1,0:T(8,128)(2,1)S(1)}, u32[]{:S(2)}, u32[]{:S(2)}) collective-permute-start(bf16[64,4224]{1,0:T(8,128)(2,1)S(1)} %collective-permute-done.refs_3_.refs_2_), channel_id=1, source_target_pairs={{0,4},{1,5},{2,6},{3,7},{4,8},{5,9},{6,10},{7,11},{8,12},{9,13},{1... | collective-permute-start | bytes 1622024 | tf_op jit(solution)/shard_map/ppermute | solution.py:443
  28.5 3.2 %compact.4 = (bf16[64,2048]{1,0:T(8,128)(2,1)}, bf16[64,2048]{1,0:T(8,128)(2,1)}, bf16[64,2048]{1,0:T(8,128)(2,1)}, bf16[64,2048]{1,0:T(8,128)(2,1)}) custom-call(s32[15]{0:T(128)} %dynamic-slice_bitcast_fusion.refs_0_, s32[1,128]{1,0:T(1,128)} %constant.23.clone.refs_1_, bf16[64,4224]{1,0:T(8,128)(2,1)} %pack.1.refs_2_), custom_call_target="tpu_custom_call" | custom-call | flops 67108864 | bytes 540672 | tf_op jit(solution)/shard_map/compact/pallas_call | solution.py:396
  35.4 2.0 %collective-permute-done.4.refs_5_.refs_6_.refs_7_ = bf16[64,4224]{1,0:T(8,128)(2,1)S(1)} collective-permute-done((bf16[64,4224]{1,0:T(8,128)(2,1)S(1)}, bf16[64,4224]{1,0:T(8,128)(2,1)S(1)}, u32[]{:S(2)}, u32[]{:S(2)}) %collective-permute-start.4) | collective-permute-done | bytes 540704 | tf_op jit(solution)/shard_map/ppermute | solution.py:444
  38.6 4.6 %collective-permute-start.2 = (bf16[64,4224]{1,0:T(8,128)(2,1)S(1)}, bf16[64,4224]{1,0:T(8,128)(2,1)S(1)}, u32[]{:S(2)}, u32[]{:S(2)}) collective-permute-start(bf16[64,4224]{1,0:T(8,128)(2,1)S(1)} %collective-permute-done.1.refs_3_.refs_4_), channel_id=1, source_target_pairs={{0,4},{1,5},{2,6},{3,7},{4,8},{5,9},{6,10},{7,11},{8,12},{9,13},{1... | collective-permute-start | bytes 1622024 | tf_op jit(solution)/shard_map/ppermute | solution.py:443
  43.3 3.6 %compact.5 = (bf16[64,2048]{1,0:T(8,128)(2,1)}, bf16[64,2048]{1,0:T(8,128)(2,1)}, bf16[64,2048]{1,0:T(8,128)(2,1)}, bf16[64,2048]{1,0:T(8,128)(2,1)}) custom-call(s32[15]{0:T(128)} %dynamic-slice_bitcast_fusion.refs_0_, s32[1,128]{1,0:T(1,128)} %constant.24.clone.refs_1_, bf16[64,4224]{1,0:T(8,128)(2,1)} %pack.1.refs_2_, bf16[64,4224]{1,0:T(8,128)(2,1)} %copy-done.1, ...), custom_call_target="tpu_custom_call" | custom-call | flops 201326592 | bytes 1622016 | tf_op jit(solution)/shard_map/compact/pallas_call | solution.py:396
  50.5 3.8 %compact.6 = (bf16[64,2048]{1,0:T(8,128)(2,1)}, bf16[64,2048]{1,0:T(8,128)(2,1)}, bf16[64,2048]{1,0:T(8,128)(2,1)}, bf16[64,2048]{1,0:T(8,128)(2,1)}) custom-call(s32[15]{0:T(128)} %dynamic-slice_bitcast_fusion.refs_0_, s32[1,128]{1,0:T(1,128)} %constant.25.clone.refs_1_, bf16[64,4224]{1,0:T(8,128)(2,1)} %copy-done.1, bf16[64,4224]{1,0:T(8,128)(2,1)} %copy-done.3, ...), custom_call_target="tpu_custom_call" | custom-call | flops 268435456 | bytes 2162688 | tf_op jit(solution)/shard_map/compact/pallas_call | solution.py:396
  54.3 2.2 %collective-permute-done.12.refs_6_.refs_5_ = bf16[64,2048]{1,0:T(8,128)(2,1)S(1)} collective-permute-done((bf16[64,2048]{1,0:T(8,128)(2,1)}, bf16[64,2048]{1,0:T(8,128)(2,1)S(1)}, u32[]{:S(2)}, u32[]{:S(2)}) %collective-permute-start.12) | collective-permute-done | bytes 262176 | tf_op jit(solution)/shard_map/ppermute | solution.py:437
  56.5 4.0 %collective-permute-done.13.refs_7_.refs_6_ = bf16[64,2048]{1,0:T(8,128)(2,1)S(1)} collective-permute-done((bf16[64,2048]{1,0:T(8,128)(2,1)}, bf16[64,2048]{1,0:T(8,128)(2,1)S(1)}, u32[]{:S(2)}, u32[]{:S(2)}) %collective-permute-start.13) | collective-permute-done | bytes 262176 | tf_op jit(solution)/shard_map/ppermute | solution.py:437
  65.6 4.8 %compact.7 = (bf16[96,2048]{1,0:T(8,128)(2,1)}, bf16[96,2048]{1,0:T(8,128)(2,1)}, bf16[96,2048]{1,0:T(8,128)(2,1)}, bf16[96,2048]{1,0:T(8,128)(2,1)}) custom-call(s32[15]{0:T(128)} %dynamic-slice_bitcast_fusion.refs_0_, s32[1,192]{1,0:T(1,128)} %constant.26.clone.refs_1_, bf16[64,4224]{1,0:T(8,128)(2,1)} %copy-done.1, bf16[64,4224]{1,0:T(8,128)(2,1)} %copy-done.3, ...), custom_call_target="tpu_custom_call" | custom-call | flops 603979776 | bytes 3244032 | tf_op jit(solution)/shard_map/compact/pallas_call | solution.py:396
  71.5 2.1 %collective-permute-done.17.refs_12_.refs_11_ = bf16[64,2048]{1,0:T(8,128)(2,1)} collective-permute-done((bf16[64,2048]{1,0:T(8,128)(2,1)}, bf16[64,2048]{1,0:T(8,128)(2,1)}, u32[]{:S(2)}, u32[]{:S(2)}) %collective-permute-start.17) | collective-permute-done | bytes 262176 | tf_op jit(solution)/shard_map/ppermute | solution.py:437
  77.0 13.3 %expert.2 = (bf16[384,768]{1,0:T(8,128)(2,1)}, bf16[384,768]{1,0:T(8,128)(2,1)}, bf16[384,768]{1,0:T(8,128)(2,1)}, bf16[96,2176]{1,0:T(8,128)(2,1)}, bf16[96,217...) custom-call(s32[15]{0:T(128)} %dynamic-slice_bitcast_fusion.refs_0_, ...), custom_call_target="tpu_custom_call" | custom-call | flops 6039797760 | bytes 9437184 | tf_op jit(solution)/shard_map/expert/pallas_call | solution.py:415
  94.7 10.1 %expert.3 = (bf16[192,768]{1,0:T(8,128)(2,1)}, bf16[192,768]{1,0:T(8,128)(2,1)}, bf16[192,768]{1,0:T(8,128)(2,1)}, bf16[48,2176]{1,0:T(8,128)(2,1)}, bf16[48,217...) custom-call(s32[15]{0:T(128)} %dynamic-slice_bitcast_fusion.refs_0_, ...), custom_call_target="tpu_custom_call" | custom-call | flops 3019898880 | bytes 9437184 | tf_op jit(solution)/shard_map/expert/pallas_call | solution.py:415
  104.9 8.6 %weight_grads.2 = (bf16[1,2048,384]{2,1,0:T(8,128)(2,1)}, bf16[1,2048,384]{2,1,0:T(8,128)(2,1)}, bf16[1,384,2048]{2,1,0:T(8,128)(2,1)}) custom-call(bf16[64,2048]{1,0:T(8,128)(2,1)} %get-tuple-element.123.refs_1_.refs_0_, bf16[64,2048]{1,0:T(8,128)(2,1)} %copy-done.17, bf16[64,2048]{1,0:T(8,128)(2,1)} %copy-done.18, bf16[64,2048]{1,0:T(8,128)(2,1)} %copy-done.19, ...), custom_call_target="tpu_custom_call" | custom-call | flops 2717908992 | bytes 6488064 | tf_op jit(solution)/shard_map/weight_grads/pallas_call | solution.py:467
  117.2 3.4 %spread.2.refs_18_ = bf16[64,2176]{1,0:T(8,128)(2,1)} custom-call(s32[15]{0:T(128)} %dynamic-slice_bitcast_fusion.refs_0_, s32[1,384]{1,0:T(1,128)} %constant.27.clone.refs_1_, bf16[64,4224]{1,0:T(8,128)(2,1)} %pack.1.refs_2_, bf16[64,4224]{1,0:T(8,128)(2,1)} %copy-done.1, bf16[64,4224]{1,0:T(8,128)(2,1)} %copy-done.3, bf16[64,4224]{1,0:T(8,128)(2,1)} %copy-done.5, ...), custom_call_target="tpu_custom_call" | custom-call | flops 100663296 | bytes 1572864 | tf_op jit(solution)/shard_map/spread/pallas_call | solution.py:491
  122.9 4.4 %spread.3 = (bf16[64,2176]{1,0:T(8,128)(2,1)}, bf16[64,2176]{1,0:T(8,128)(2,1)}, bf16[64,2176]{1,0:T(8,128)(2,1)}) custom-call(s32[15]{0:T(128)} %dynamic-slice_bitcast_fusion.refs_0_, s32[1,576]{1,0:T(1,128)} %constant.28.clone.refs_1_, bf16[64,4224]{1,0:T(8,128)(2,1)} %pack.1.refs_2_, bf16[64,4224]{1,0:T(8,128)(2,1)} %copy-done.1, ...), custom_call_target="tpu_custom_call" | custom-call | flops 452984832 | bytes 2359296 | tf_op jit(solution)/shard_map/spread/pallas_call | solution.py:491
  127.3 1.8 %collective-permute-start.28 = (bf16[64,2176]{1,0:T(8,128)(2,1)}, bf16[64,2176]{1,0:T(8,128)(2,1)S(1)}, u32[]{:S(2)}, u32[]{:S(2)}) collective-permute-start(bf16[64,2176]{1,0:T(8,128)(2,1)} %get-tuple-element.209), channel_id=1, source_target_pairs={{0,4},{1,5},{2,6},{3,7},{4,0},{5,1},{6,2},{7,3},{8,12},{9,13},{10,... | collective-permute-start | bytes 835592 | tf_op jit(solution)/shard_map/ppermute | solution.py:529
  129.4 7.7 %collective-permute-done.28.b_ref = bf16[64,2176]{1,0:T(8,128)(2,1)S(1)} collective-permute-done((bf16[64,2176]{1,0:T(8,128)(2,1)}, bf16[64,2176]{1,0:T(8,128)(2,1)S(1)}, u32[]{:S(2)}, u32[]{:S(2)}) %collective-permute-start.28) | collective-permute-done | bytes 278560 | tf_op jit(solution)/shard_map/ppermute | solution.py:529
  137.8 1.8 %add.5 = bf16[64,2176]{1,0:T(8,128)(2,1)} custom-call(bf16[64,2176]{1,0:T(8,128)(2,1)} %get-tuple-element.208.a_ref, bf16[64,2176]{1,0:T(8,128)(2,1)} %copy-done.14), custom_call_target="tpu_custom_call" | custom-call | tf_op jit(solution)/shard_map/add/pallas_call | solution.py:533
  139.6 2.7 %collective-permute-start.29 = (bf16[64,2176]{1,0:T(8,128)(2,1)}, bf16[64,2176]{1,0:T(8,128)(2,1)S(1)}, u32[]{:S(2)}, u32[]{:S(2)}) collective-permute-start(bf16[64,2176]{1,0:T(8,128)(2,1)} %add.5), channel_id=1, source_target_pairs={{0,8},{1,9},{2,10},{3,11},{4,12},{5,13},{6,14},{7,15},{8,0},{9,1},... | collective-permute-start | bytes 835592 | tf_op jit(solution)/shard_map/ppermute | solution.py:529
  142.3 11.0 %weight_grads.3 = (bf16[1,2048,384]{2,1,0:T(8,128)(2,1)}, bf16[1,2048,384]{2,1,0:T(8,128)(2,1)}, bf16[1,384,2048]{2,1,0:T(8,128)(2,1)}) custom-call(bf16[64,2048]{1,0:T(8,128)(2,1)} %get-tuple-element.123.refs_1_.refs_0_, bf16[64,2048]{1,0:T(8,128)(2,1)} %copy-done.17, bf16[64,2048]{1,0:T(8,128)(2,1)} %copy-done.18, bf16[64,2048]{1,0:T(8,128)(2,1)} %copy-done.19, ...), custom_call_target="tpu_custom_call" | custom-call | flops 2717908992 | bytes 6488064 | tf_op jit(solution)/shard_map/weight_grads/pallas_call | solution.py:467
  155.0 2.2 %home.1 = (bf16[64,2048]{1,0:T(8,128)(2,1)}, bf16[8,64]{1,0:T(8,128)(2,1)}) custom-call(bf16[64,2176]{1,0:T(8,128)(2,1)} %get-tuple-element.207.refs_0_, bf16[64,2176]{1,0:T(8,128)(2,1)} %copy-done.15, bf16[64,2176]{1,0:T(8,128)(2,1)} %copy-done.16, s32[8,64]{1,0:T(8,128)} %bitcast.6, bf16[8,64]{1,0:T(8,128)(2,1)} %bitcast.8, ...), custom_call_target="tpu_custom_call" | custom-call | flops 1000000 | bytes 1310720 | tf_op jit(solution)/shard_map/home/pallas_call | solution.py:543
  (114 shorter events, 35.9 us)
Async XLA Ops:
  0.6 31.1 %collective-permute-start.6 = (bf16[1,2048,384]{2,1,0:T(8,128)(2,1)}, bf16[1,2048,384]{2,1,0:T(8,128)(2,1)}, u32[]{:S(2)}, u32[]{:S(2)}) collective-permute-start(bf16[1,2048,384]{2,1,0:T(8,128)(2,1)} %refs_5_.1), channel_id=1, source_target_pairs={{0,16},{16,0},{1,17},{17,1},{2,18},{18,2},{3,19},{19,3},{4,20},{20... | collective-permute-start | bytes 4718600 | tf_op jit(solution)/shard_map/ppermute | solution.py:389
  1.1 30.6 %collective-permute-start.7 = (bf16[1,2048,384]{2,1,0:T(8,128)(2,1)}, bf16[1,2048,384]{2,1,0:T(8,128)(2,1)}, u32[]{:S(2)}, u32[]{:S(2)}) collective-permute-start(bf16[1,2048,384]{2,1,0:T(8,128)(2,1)} %refs_7_.1), channel_id=1, source_target_pairs={{0,16},{16,0},{1,17},{17,1},{2,18},{18,2},{3,19},{19,3},{4,20},{20... | collective-permute-start | bytes 4718600 | tf_op jit(solution)/shard_map/ppermute | solution.py:389
  1.2 30.6 %collective-permute-start.8 = (bf16[1,384,2048]{2,1,0:T(8,128)(2,1)}, bf16[1,384,2048]{2,1,0:T(8,128)(2,1)}, u32[]{:S(2)}, u32[]{:S(2)}) collective-permute-start(bf16[1,384,2048]{2,1,0:T(8,128)(2,1)} %refs_9_.1), channel_id=1, source_target_pairs={{0,16},{16,0},{1,17},{17,1},{2,18},{18,2},{3,19},{19,3},{4,20},{20... | collective-permute-start | bytes 4718600 | tf_op jit(solution)/shard_map/ppermute | solution.py:389
  3.8 17.6 %collective-permute-start.3 = (bf16[64,4224]{1,0:T(8,128)(2,1)}, bf16[64,4224]{1,0:T(8,128)(2,1)S(1)}, u32[]{:S(2)}, u32[]{:S(2)}) collective-permute-start(bf16[64,4224]{1,0:T(8,128)(2,1)} %pack.1.refs_2_), channel_id=1, source_target_pairs={{4,0},{5,1},{6,2},{7,3},{8,4},{9,5},{10,6},{11,7},{12,8},{13,9},{1... | collective-permute-start | bytes 1622024 | tf_op jit(solution)/shard_map/ppermute | solution.py:392
  5.1 17.6 %collective-permute-start = (bf16[64,4224]{1,0:T(8,128)(2,1)}, bf16[64,4224]{1,0:T(8,128)(2,1)S(1)}, u32[]{:S(2)}, u32[]{:S(2)}) collective-permute-start(bf16[64,4224]{1,0:T(8,128)(2,1)} %pack.1.refs_2_), channel_id=1, source_target_pairs={{0,4},{1,5},{2,6},{3,7},{4,8},{5,9},{6,10},{7,11},{8,12},{9,13},{1... | collective-permute-start | bytes 1622024 | tf_op jit(solution)/shard_map/ppermute | solution.py:391
  21.4 15.9 %collective-permute-start.4 = (bf16[64,4224]{1,0:T(8,128)(2,1)S(1)}, bf16[64,4224]{1,0:T(8,128)(2,1)S(1)}, u32[]{:S(2)}, u32[]{:S(2)}) collective-permute-start(bf16[64,4224]{1,0:T(8,128)(2,1)S(1)} %collective-permute-done.3.refs_4_.refs_5_.refs_6_), channel_id=1, source_target_pairs={{4,0},{5,1},{6,2},{7,3},{8,4},{9,5},{10,6},{11,7},{12,8},{13,9},{1... | collective-permute-start | bytes 1622024 | tf_op jit(solution)/shard_map/ppermute | solution.py:444
  22.7 15.9 %collective-permute-start.1 = (bf16[64,4224]{1,0:T(8,128)(2,1)S(1)}, bf16[64,4224]{1,0:T(8,128)(2,1)S(1)}, u32[]{:S(2)}, u32[]{:S(2)}) collective-permute-start(bf16[64,4224]{1,0:T(8,128)(2,1)S(1)} %collective-permute-done.refs_3_.refs_2_), channel_id=1, source_target_pairs={{0,4},{1,5},{2,6},{3,7},{4,8},{5,9},{6,10},{7,11},{8,12},{9,13},{1... | collective-permute-start | bytes 1622024 | tf_op jit(solution)/shard_map/ppermute | solution.py:443
  31.8 15.1 %collective-permute-start.9 = (bf16[64,2048]{1,0:T(8,128)(2,1)}, bf16[64,2048]{1,0:T(8,128)(2,1)S(1)}, u32[]{:S(2)}, u32[]{:S(2)}) collective-permute-start(bf16[64,2048]{1,0:T(8,128)(2,1)} %get-tuple-element.116), channel_id=1, source_target_pairs={{0,1},{1,0},{2,3},{3,2},{4,5},{5,4},{6,7},{7,6},{8,9},{9,8},{10,11... | collective-permute-start | bytes 786440 | tf_op jit(solution)/shard_map/ppermute | solution.py:437
  33.5 13.4 %collective-permute-start.10 = (bf16[64,2048]{1,0:T(8,128)(2,1)}, bf16[64,2048]{1,0:T(8,128)(2,1)S(1)}, u32[]{:S(2)}, u32[]{:S(2)}) collective-permute-start(bf16[64,2048]{1,0:T(8,128)(2,1)} %get-tuple-element.117), channel_id=1, source_target_pairs={{0,2},{1,3},{2,0},{3,1},{4,6},{5,7},{6,4},{7,5},{8,10},{9,11},{10,... | collective-permute-start | bytes 786440 | tf_op jit(solution)/shard_map/ppermute | solution.py:437
  35.1 11.9 %collective-permute-start.11 = (bf16[64,2048]{1,0:T(8,128)(2,1)}, bf16[64,2048]{1,0:T(8,128)(2,1)S(1)}, u32[]{:S(2)}, u32[]{:S(2)}) collective-permute-start(bf16[64,2048]{1,0:T(8,128)(2,1)} %get-tuple-element.118), channel_id=1, source_target_pairs={{0,3},{1,2},{2,1},{3,0},{4,7},{5,6},{6,5},{7,4},{8,11},{9,10},{10,... | collective-permute-start | bytes 786440 | tf_op jit(solution)/shard_map/ppermute | solution.py:437
  37.3 26.7 %collective-permute-start.5 = (bf16[64,4224]{1,0:T(8,128)(2,1)S(1)}, bf16[64,4224]{1,0:T(8,128)(2,1)S(1)}, u32[]{:S(2)}, u32[]{:S(2)}) collective-permute-start(bf16[64,4224]{1,0:T(8,128)(2,1)S(1)} %collective-permute-done.4.refs_5_.refs_6_.refs_7_), channel_id=1, source_target_pairs={{4,0},{5,1},{6,2},{7,3},{8,4},{9,5},{10,6},{11,7},{12,8},{13,9},{1... | collective-permute-start | bytes 1622024 | tf_op jit(solution)/shard_map/ppermute | solution.py:444
  38.6 25.4 %collective-permute-start.2 = (bf16[64,4224]{1,0:T(8,128)(2,1)S(1)}, bf16[64,4224]{1,0:T(8,128)(2,1)S(1)}, u32[]{:S(2)}, u32[]{:S(2)}) collective-permute-start(bf16[64,4224]{1,0:T(8,128)(2,1)S(1)} %collective-permute-done.1.refs_3_.refs_4_), channel_id=1, source_target_pairs={{0,4},{1,5},{2,6},{3,7},{4,8},{5,9},{6,10},{7,11},{8,12},{9,13},{1... | collective-permute-start | bytes 1622024 | tf_op jit(solution)/shard_map/ppermute | solution.py:443
  48.5 11.9 %collective-permute-start.13 = (bf16[64,2048]{1,0:T(8,128)(2,1)}, bf16[64,2048]{1,0:T(8,128)(2,1)S(1)}, u32[]{:S(2)}, u32[]{:S(2)}) collective-permute-start(bf16[64,2048]{1,0:T(8,128)(2,1)} %get-tuple-element.129), channel_id=1, source_target_pairs={{0,2},{1,3},{2,0},{3,1},{4,6},{5,7},{6,4},{7,5},{8,10},{9,11},{10,... | collective-permute-start | bytes 786440 | tf_op jit(solution)/shard_map/ppermute | solution.py:437
  73.5 16.8 %collective-permute-start.18 = (bf16[96,2048]{1,0:T(8,128)(2,1)}, bf16[96,2048]{1,0:T(8,128)(2,1)S(1)}, u32[]{:S(2)}, u32[]{:S(2)}) collective-permute-start(bf16[96,2048]{1,0:T(8,128)(2,1)} %get-tuple-element.162), channel_id=1, source_target_pairs={{0,1},{1,0},{2,3},{3,2},{4,5},{5,4},{6,7},{7,6},{8,9},{9,8},{10,11... | collective-permute-start | bytes 1179656 | tf_op jit(solution)/shard_map/ppermute | solution.py:437
  73.9 16.4 %collective-permute-start.19 = (bf16[96,2048]{1,0:T(8,128)(2,1)}, bf16[96,2048]{1,0:T(8,128)(2,1)S(1)}, u32[]{:S(2)}, u32[]{:S(2)}) collective-permute-start(bf16[96,2048]{1,0:T(8,128)(2,1)} %get-tuple-element.163), channel_id=1, source_target_pairs={{0,2},{1,3},{2,0},{3,1},{4,6},{5,7},{6,4},{7,5},{8,10},{9,11},{10,... | collective-permute-start | bytes 1179656 | tf_op jit(solution)/shard_map/ppermute | solution.py:437
  75.5 15.8 %collective-permute-start.20 = (bf16[96,2048]{1,0:T(8,128)(2,1)}, bf16[96,2048]{1,0:T(8,128)(2,1)S(1)}, u32[]{:S(2)}, u32[]{:S(2)}) collective-permute-start(bf16[96,2048]{1,0:T(8,128)(2,1)} %get-tuple-element.164), channel_id=1, source_target_pairs={{0,3},{1,2},{2,1},{3,0},{4,7},{5,6},{6,5},{7,4},{8,11},{9,10},{10,... | collective-permute-start | bytes 1179656 | tf_op jit(solution)/shard_map/ppermute | solution.py:437
  91.2 22.3 %collective-permute-start.21 = (bf16[96,2176]{1,0:T(8,128)(2,1)}, bf16[96,2176]{1,0:T(8,128)(2,1)S(1)}, u32[]{:S(2)}, u32[]{:S(2)}) collective-permute-start(bf16[96,2176]{1,0:T(8,128)(2,1)} %get-tuple-element.166), channel_id=1, source_target_pairs={{0,1},{1,0},{2,3},{3,2},{4,5},{5,4},{6,7},{7,6},{8,9},{9,8},{10,11... | collective-permute-start | bytes 1253384 | tf_op jit(solution)/shard_map/ppermute | solution.py:437
  91.6 21.9 %collective-permute-start.22 = (bf16[96,2176]{1,0:T(8,128)(2,1)}, bf16[96,2176]{1,0:T(8,128)(2,1)S(1)}, u32[]{:S(2)}, u32[]{:S(2)}) collective-permute-start(bf16[96,2176]{1,0:T(8,128)(2,1)} %get-tuple-element.167), channel_id=1, source_target_pairs={{0,2},{1,3},{2,0},{3,1},{4,6},{5,7},{6,4},{7,5},{8,10},{9,11},{10,... | collective-permute-start | bytes 1253384 | tf_op jit(solution)/shard_map/ppermute | solution.py:437
  93.1 20.5 %collective-permute-start.23 = (bf16[96,2176]{1,0:T(8,128)(2,1)}, bf16[96,2176]{1,0:T(8,128)(2,1)S(1)}, u32[]{:S(2)}, u32[]{:S(2)}) collective-permute-start(bf16[96,2176]{1,0:T(8,128)(2,1)} %get-tuple-element.168), channel_id=1, source_target_pairs={{0,3},{1,2},{2,1},{3,0},{4,7},{5,6},{6,5},{7,4},{8,11},{9,10},{10,... | collective-permute-start | bytes 1253384 | tf_op jit(solution)/shard_map/ppermute | solution.py:437
  122.2 20.1 %collective-permute-start.31 = (bf16[1,2048,384]{2,1,0:T(8,128)(2,1)}, bf16[1,2048,384]{2,1,0:T(8,128)(2,1)}, u32[]{:S(2)}, u32[]{:S(2)}) collective-permute-start(bf16[1,2048,384]{2,1,0:T(8,128)(2,1)} %get-tuple-element.210), channel_id=1, source_target_pairs={{0,16},{16,0},{1,17},{17,1},{2,18},{18,2},{3,19},{19,3},{4,20},{20... | collective-permute-start | bytes 4718600 | tf_op jit(solution)/shard_map/ppermute | solution.py:521
  122.2 20.1 %collective-permute-start.32 = (bf16[1,384,2048]{2,1,0:T(8,128)(2,1)}, bf16[1,384,2048]{2,1,0:T(8,128)(2,1)}, u32[]{:S(2)}, u32[]{:S(2)}) collective-permute-start(bf16[1,384,2048]{2,1,0:T(8,128)(2,1)} %get-tuple-element.211), channel_id=1, source_target_pairs={{0,16},{16,0},{1,17},{17,1},{2,18},{18,2},{3,19},{19,3},{4,20},{20... | collective-permute-start | bytes 4718600 | tf_op jit(solution)/shard_map/ppermute | solution.py:521
  122.7 19.6 %collective-permute-start.30 = (bf16[1,2048,384]{2,1,0:T(8,128)(2,1)S(1)}, bf16[1,2048,384]{2,1,0:T(8,128)(2,1)}, u32[]{:S(2)}, u32[]{:S(2)}) collective-permute-start(bf16[1,2048,384]{2,1,0:T(8,128)(2,1)S(1)} %copy-done.9), channel_id=1, source_target_pairs={{0,16},{16,0},{1,17},{17,1},{2,18},{18,2},{3,19},{19,3},{4,20},{20... | collective-permute-start | bytes 4718600 | tf_op jit(solution)/shard_map/ppermute | solution.py:521
  129.1 24.2 %collective-permute-start.27 = (bf16[64,2176]{1,0:T(8,128)(2,1)S(1)}, bf16[64,2176]{1,0:T(8,128)(2,1)S(1)}, u32[]{:S(2)}, u32[]{:S(2)}) collective-permute-start(bf16[64,2176]{1,0:T(8,128)(2,1)S(1)} %copy-done.10), channel_id=1, source_target_pairs={{0,4},{1,5},{2,6},{3,7},{4,0},{5,1},{6,2},{7,3},{8,12},{9,13},{10,... | collective-permute-start | bytes 835592 | tf_op jit(solution)/shard_map/ppermute | solution.py:520
  139.6 14.8 %collective-permute-start.29 = (bf16[64,2176]{1,0:T(8,128)(2,1)}, bf16[64,2176]{1,0:T(8,128)(2,1)S(1)}, u32[]{:S(2)}, u32[]{:S(2)}) collective-permute-start(bf16[64,2176]{1,0:T(8,128)(2,1)} %add.5), channel_id=1, source_target_pairs={{0,8},{1,9},{2,10},{3,11},{4,12},{5,13},{6,14},{7,15},{8,0},{9,1},... | collective-permute-start | bytes 835592 | tf_op jit(solution)/shard_map/ppermute | solution.py:529
  (38 other events, 348.3 us)

commit v5 on v4

--- a/solution.py
+++ b/solution.py
@@ -51,6 +51,11 @@
         self.sizes = [b - a for a, b in self.spans]
         self.cands = 2 * self.outer - 1
         self.use = [self.used(*c) for c in self.chunks]
+        needed = set().union(*self.use)
+        self.last = [
+            max(i for i in needed if 0 < i < outer),
+            max(i for i in needed if i >= outer) - outer + 1,
+        ]
 
     def keys(self, spans):
         return np.array(
@@ -62,10 +67,32 @@
         rest = [s for s in range(self.outer) if s not in (z, z ^ 1)]
         return [z, z ^ 1] + sorted(rest, key=lambda s: abs(s - z))
 
+    def swap(self, z, odd):
+        to = z - 1 if (z % 2 == 0) == odd else z + 1
+        return to if 0 <= to < self.outer else z
+
+    def trace(self):
+        held = {0: list(range(self.outer))}
+        for chain in (0, 1):
+            last = held[0]
+            for r in range(1, self.outer):
+                odd = (r % 2 == 0) == (chain == 0)
+                last = [last[self.swap(z, odd)] for z in range(self.outer)]
+                held[chain * (self.outer - 1) + r] = last
+        return held
+
     def cand(self, z, source):
-        if source == z:
-            return 0
-        return z - source if source < z else self.outer - 1 + source - z
+        step = lambda i: i if i < self.outer else i - self.outer + 1
+        found = [i for i, held in self.trace().items() if held[z] == source]
+        return min(found, key=lambda i: (step(i), i))
+
+    def exchange(self, r, chain):
+        odd = (r % 2 == 0) == (chain == 0)
+        return [
+            (z * self.inner + p, self.swap(z, odd) * self.inner + p)
+            for z in range(self.outer)
+            for p in range(self.inner)
+        ]
 
     def used(self, a, b):
         slots = [k for k in range(self.outer) if k * self.cap < b and (k + 1) * self.cap > a]
@@ -87,14 +114,6 @@
             homes = [self.cand(z, z ^ r) for r in range(self.outer)]
             rows.append(offs + experts + homes)
         return np.array(rows, np.int32)
-
-    def line(self, step):
-        return [
-            (z * self.inner + p, (z + step) * self.inner + p)
-            for z in range(self.outer)
-            for p in range(self.inner)
-            if 0 <= z + step < self.outer
-        ]
 
     def across(self, d):
         return [
@@ -388,8 +407,15 @@
 
     others = [lax.ppermute(w, "dp", swap) for w in (w_gate, w_up, w_down)]
     blocks = [block] * plan.cands
-    blocks[1] = lax.ppermute(block, "expert", plan.line(1))
-    blocks[outer] = lax.ppermute(block, "expert", plan.line(-1))
+
+    def hop(r):
+        for chain in (0, 1):
+            if r <= plan.last[chain]:
+                i = chain * (outer - 1) + r
+                before = block if r == 1 else blocks[i - 1]
+                blocks[i] = lax.ppermute(before, "expert", plan.exchange(r, chain))
+
+    hop(1)
     def compact(c):
         rows, use = plan.rows[c], plan.use[c]
         count, n = inner * rows, len(use)
@@ -440,12 +466,14 @@
     got, done = [], 1
     for c in range(PARTS):
         for r in range(done + 1, plan.steps[c] + 1):
-            blocks[r] = lax.ppermute(blocks[r - 1], "expert", plan.line(1))
-            blocks[outer - 1 + r] = lax.ppermute(blocks[outer - 2 + r], "expert", plan.line(-1))
+            hop(r)
         done = max(done, plan.steps[c])
         sent = compact(c)
         if c == 0:
             others, sent = lax.optimization_barrier((others, sent))
+            blocks[done], blocks[outer - 1 + done], sent = lax.optimization_barrier(
+                (blocks[done], blocks[outer - 1 + done], sent)
+            )
         else:
             got[-1], sent = lax.optimization_barrier((got[-1], sent))
         got.append(cross(sent))
@@ -512,7 +540,6 @@
         )
 
     mine = weight_grads(False, [])
-    backs, more, mine = lax.optimization_barrier((backs, more, mine))
     backs = backs + cross(more[3:])
     (first,) = spread([1], 1, [])
     sums = {}

time: 158 us -> 153 us (0.968)
  waiting for transfers between devices: 33.4 us -> 28.4 us
  local copies, waits for them, and re-layouts: 4.51 us -> 6.69 us
    ppermute x6 -> x5, waiting for transfers between devices: 13.1 us -> 8.3 us  [hop(): blocks[i] = lax.ppermute(before, 'expert', plan.exchange(r, chain))]
    ppermute x2, starting transfers between devices: 4.48 us -> 1.59 us  [on_device(): sent = lax.ppermute(sums[r], 'expert', plan.flip(bit))]
    unnamed x58 -> x56, local copies, waits for them, and re-layouts: 3.3 us -> 5.49 us
    ppermute x18, waiting for transfers between devices: 11.6 us -> 9.65 us  [cross(): lax.ppermute(arrays[d], 'expert', plan.across(d))]
    ppermute x2, waiting for transfers between devices: 8.68 us -> 10.4 us  [on_device(): sent = lax.ppermute(sums[r], 'expert', plan.flip(bit))]
    ppermute x6 -> x5, starting transfers between devices: 18.2 us -> 19.8 us  [hop(): blocks[i] = lax.ppermute(before, 'expert', plan.exchange(r, chain))]
  transfers between devices with their start and end apart: 33 -> 32, of which waited for: 10 -> 6; matrix products, arithmetic and copies ran while one was open for 1% -> 1% of each run, Pallas kernels for 45% -> 45%
where the time goes in v5:
time: 153 us
  Pallas kernels  71.2 us (47%)
  starting transfers between devices  45.5 us (30%)
  waiting for transfers between devices  28.4 us (19%)
  local copies, waits for them, and re-layouts  6.69 us (4%)
    pallas_call x2, Pallas kernels, expert(): pl.pallas_call(functools.partial(expert_kernel, plan, g), out_shape=[shap...  23.3 us
    ppermute x18, starting transfers between devices, cross(): lax.ppermute(arrays[d], 'expert', plan.across(d))  21.1 us
    ppermute x5, starting transfers between devices, hop(): blocks[i] = lax.ppermute(before, 'expert', plan.exchange(r, chain))  19.8 us
    pallas_call x2, Pallas kernels, weight_grads(): pl.pallas_call(functools.partial(weight_kernel, plan, own), out_shape=[sh...  19.5 us
    pallas_call x4, Pallas kernels, compact(): pl.pallas_call(functools.partial(compact_kernel, plan, c), out_shape=[sha...  14.4 us
    ppermute x2, waiting for transfers between devices, on_device(): sent = lax.ppermute(sums[r], 'expert', plan.flip(bit))  10.4 us
    ppermute x18, waiting for transfers between devices, cross(): lax.ppermute(arrays[d], 'expert', plan.across(d))  9.65 us
    ppermute x5, waiting for transfers between devices, hop(): blocks[i] = lax.ppermute(before, 'expert', plan.exchange(r, chain))  8.3 us
  transfers between devices with their start and end apart: 32, of which 6 were waited for; matrix products, arithmetic and copies ran while one was open for 1% of the time, Pallas kernels for 45%

profile of v5, /device:TPU:0, one launch (start us, length us, event | category | flops | bytes accessed | tf_op | source)
XLA Modules:
  0.0 152.9 jit_solution(3122675875462863244)
XLA Ops:
  1.7 2.1 %pack.1.refs_2_.refs_8_ = bf16[64,4224]{1,0:T(8,128)(2,1)} custom-call(bf16[64,2048]{1,0:T(8,128)(2,1)} %tok_ref.1, bf16[64,2048]{1,0:T(8,128)(2,1)} %up_ref.1, s32[8,64]{1,0:T(8,128)} %bitcast.5, bf16[8,64]{1,0:T(8,128)(2,1)} %bitcast.7), custom_call_target="tpu_custom_call" | custom-call | flops 1000000 | bytes 1081344 | tf_op jit(solution)/shard_map/pack/pallas_call | solution.py:398
  3.8 1.7 %collective-permute-start.1 = (bf16[64,4224]{1,0:T(8,128)(2,1)}, bf16[64,4224]{1,0:T(8,128)(2,1)S(1)}, u32[]{:S(2)}, u32[]{:S(2)}) collective-permute-start(bf16[64,4224]{1,0:T(8,128)(2,1)} %pack.1.refs_2_.refs_8_), channel_id=1, source_target_pairs={{0,0},{1,1},{2,2},{3,3},{4,8},{5,9},{6,10},{7,11},{8,4},{9,5},{10,... | collective-permute-start | bytes 1622024 | tf_op jit(solution)/shard_map/ppermute | solution.py:416
  5.5 4.5 %collective-permute-start = (bf16[64,4224]{1,0:T(8,128)(2,1)}, bf16[64,4224]{1,0:T(8,128)(2,1)S(1)}, u32[]{:S(2)}, u32[]{:S(2)}) collective-permute-start(bf16[64,4224]{1,0:T(8,128)(2,1)} %pack.1.refs_2_.refs_8_), channel_id=1, source_target_pairs={{0,4},{1,5},{2,6},{3,7},{4,0},{5,1},{6,2},{7,3},{8,12},{9,13},{10,... | collective-permute-start | bytes 1622024 | tf_op jit(solution)/shard_map/ppermute | solution.py:416
  11.2 3.3 %compact.4 = (bf16[64,2048]{1,0:T(8,128)(2,1)}, bf16[64,2048]{1,0:T(8,128)(2,1)}, bf16[64,2048]{1,0:T(8,128)(2,1)}, bf16[64,2048]{1,0:T(8,128)(2,1)}) custom-call(s32[15]{0:T(128)} %dynamic-slice_bitcast_fusion.refs_0_, s32[1,128]{1,0:T(1,128)} %constant.23.clone.refs_1_, bf16[64,4224]{1,0:T(8,128)(2,1)} %pack.1.refs_2_.refs_8_), custom_call_target="tpu_custom_call" | custom-call | flops 67108864 | bytes 540672 | tf_op jit(solution)/shard_map/compact/pallas_call | solution.py:422
  14.5 8.3 %collective-permute-done.refs_3_.refs_2_ = bf16[64,4224]{1,0:T(8,128)(2,1)S(1)} collective-permute-done((bf16[64,4224]{1,0:T(8,128)(2,1)}, bf16[64,4224]{1,0:T(8,128)(2,1)S(1)}, u32[]{:S(2)}, u32[]{:S(2)}) %collective-permute-start) | collective-permute-done | bytes 540704 | tf_op jit(solution)/shard_map/ppermute | solution.py:416
  23.5 3.5 %collective-permute-start.7 = (bf16[64,4224]{1,0:T(8,128)(2,1)S(1)}, bf16[64,4224]{1,0:T(8,128)(2,1)S(1)}, u32[]{:S(2)}, u32[]{:S(2)}) collective-permute-start(bf16[64,4224]{1,0:T(8,128)(2,1)S(1)} %collective-permute-done.1.refs_3_.refs_4_.refs_6_), channel_id=1, source_target_pairs={{0,4},{1,5},{2,6},{3,7},{4,0},{5,1},{6,2},{7,3},{8,12},{9,13},{10,... | collective-permute-start | bytes 1622024 | tf_op jit(solution)/shard_map/ppermute | solution.py:416
  30.5 9.5 %collective-permute-start.6 = (bf16[64,4224]{1,0:T(8,128)(2,1)S(1)}, bf16[64,4224]{1,0:T(8,128)(2,1)S(1)}, u32[]{:S(2)}, u32[]{:S(2)}) collective-permute-start(bf16[64,4224]{1,0:T(8,128)(2,1)S(1)} %collective-permute-done.5.refs_2_.refs_4_), channel_id=1, source_target_pairs={{0,4},{1,5},{2,6},{3,7},{4,0},{5,1},{6,2},{7,3},{8,12},{9,13},{10,... | collective-permute-start | bytes 1622024 | tf_op jit(solution)/shard_map/ppermute | solution.py:416
  40.0 3.4 %compact.5 = (bf16[64,2048]{1,0:T(8,128)(2,1)}, bf16[64,2048]{1,0:T(8,128)(2,1)}, bf16[64,2048]{1,0:T(8,128)(2,1)}, bf16[64,2048]{1,0:T(8,128)(2,1)}) custom-call(s32[15]{0:T(128)} %dynamic-slice_bitcast_fusion.refs_0_, s32[1,128]{1,0:T(1,128)} %constant.24.clone.refs_1_, bf16[64,4224]{1,0:T(8,128)(2,1)} %pack.1.refs_2_.refs_8_, bf16[64,4224]{1,0:T(8,128)(2,1)} %copy-done.1), custom_call_target="tpu_custom_call" | custom-call | flops 134217728 | bytes 1081344 | tf_op jit(solution)/shard_map/compact/pallas_call | solution.py:422
  47.8 3.6 %compact.6 = (bf16[64,2048]{1,0:T(8,128)(2,1)}, bf16[64,2048]{1,0:T(8,128)(2,1)}, bf16[64,2048]{1,0:T(8,128)(2,1)}, bf16[64,2048]{1,0:T(8,128)(2,1)}) custom-call(s32[15]{0:T(128)} %dynamic-slice_bitcast_fusion.refs_0_, s32[1,128]{1,0:T(1,128)} %constant.25.clone.refs_1_, bf16[64,4224]{1,0:T(8,128)(2,1)} %copy-done.1, bf16[64,4224]{1,0:T(8,128)(2,1)} %copy-done, ...), custom_call_target="tpu_custom_call" | custom-call | flops 201326592 | bytes 1622016 | tf_op jit(solution)/shard_map/compact/pallas_call | solution.py:422
  52.9 4.0 %collective-permute-done.12.refs_7_.refs_6_ = bf16[64,2048]{1,0:T(8,128)(2,1)S(1)} collective-permute-done((bf16[64,2048]{1,0:T(8,128)(2,1)}, bf16[64,2048]{1,0:T(8,128)(2,1)S(1)}, u32[]{:S(2)}, u32[]{:S(2)}) %collective-permute-start.12) | collective-permute-done | bytes 262176 | tf_op jit(solution)/shard_map/ppermute | solution.py:463
  61.3 4.1 %compact.7 = (bf16[96,2048]{1,0:T(8,128)(2,1)}, bf16[96,2048]{1,0:T(8,128)(2,1)}, bf16[96,2048]{1,0:T(8,128)(2,1)}, bf16[96,2048]{1,0:T(8,128)(2,1)}) custom-call(s32[15]{0:T(128)} %dynamic-slice_bitcast_fusion.refs_0_, s32[1,192]{1,0:T(1,128)} %constant.26.clone.refs_1_, bf16[64,4224]{1,0:T(8,128)(2,1)} %copy-done.3, bf16[64,4224]{1,0:T(8,128)(2,1)} %copy-done.4, ...), custom_call_target="tpu_custom_call" | custom-call | flops 402653184 | bytes 2162688 | tf_op jit(solution)/shard_map/compact/pallas_call | solution.py:422
  65.4 4.1 %collective-permute-done.15.refs_11_.refs_10_ = bf16[64,2048]{1,0:T(8,128)(2,1)S(1)} collective-permute-done((bf16[64,2048]{1,0:T(8,128)(2,1)}, bf16[64,2048]{1,0:T(8,128)(2,1)S(1)}, u32[]{:S(2)}, u32[]{:S(2)}) %collective-permute-start.15) | collective-permute-done | bytes 262176 | tf_op jit(solution)/shard_map/ppermute | solution.py:463
  70.5 1.6 %collective-permute-start.18 = (bf16[96,2048]{1,0:T(8,128)(2,1)}, bf16[96,2048]{1,0:T(8,128)(2,1)S(1)}, u32[]{:S(2)}, u32[]{:S(2)}) collective-permute-start(bf16[96,2048]{1,0:T(8,128)(2,1)} %get-tuple-element.164), channel_id=1, source_target_pairs={{0,2},{1,3},{2,0},{3,1},{4,6},{5,7},{6,4},{7,5},{8,10},{9,11},{10,... | collective-permute-start | bytes 1179656 | tf_op jit(solution)/shard_map/ppermute | solution.py:463
  72.1 1.7 %collective-permute-start.19 = (bf16[96,2048]{1,0:T(8,128)(2,1)}, bf16[96,2048]{1,0:T(8,128)(2,1)S(1)}, u32[]{:S(2)}, u32[]{:S(2)}) collective-permute-start(bf16[96,2048]{1,0:T(8,128)(2,1)} %get-tuple-element.165), channel_id=1, source_target_pairs={{0,3},{1,2},{2,1},{3,0},{4,7},{5,6},{6,5},{7,4},{8,11},{9,10},{10,... | collective-permute-start | bytes 1179656 | tf_op jit(solution)/shard_map/ppermute | solution.py:463
  73.8 13.2 %expert.2 = (bf16[384,768]{1,0:T(8,128)(2,1)}, bf16[384,768]{1,0:T(8,128)(2,1)}, bf16[384,768]{1,0:T(8,128)(2,1)}, bf16[96,2176]{1,0:T(8,128)(2,1)}, bf16[96,217...) custom-call(s32[15]{0:T(128)} %dynamic-slice_bitcast_fusion.refs_0_, ...), custom_call_target="tpu_custom_call" | custom-call | flops 6039797760 | bytes 9437184 | tf_op jit(solution)/shard_map/expert/pallas_call | solution.py:441
  90.7 10.1 %expert.3 = (bf16[192,768]{1,0:T(8,128)(2,1)}, bf16[192,768]{1,0:T(8,128)(2,1)}, bf16[192,768]{1,0:T(8,128)(2,1)}, bf16[48,2176]{1,0:T(8,128)(2,1)}, bf16[48,217...) custom-call(s32[15]{0:T(128)} %dynamic-slice_bitcast_fusion.refs_0_, ...), custom_call_target="tpu_custom_call" | custom-call | flops 3019898880 | bytes 9437184 | tf_op jit(solution)/shard_map/expert/pallas_call | solution.py:441
  104.3 8.6 %weight_grads.2 = (bf16[1,2048,384]{2,1,0:T(8,128)(2,1)}, bf16[1,2048,384]{2,1,0:T(8,128)(2,1)}, bf16[1,384,2048]{2,1,0:T(8,128)(2,1)}) custom-call(bf16[64,2048]{1,0:T(8,128)(2,1)} %get-tuple-element.124.refs_1_.refs_0_, bf16[64,2048]{1,0:T(8,128)(2,1)} %copy-done.16, bf16[64,2048]{1,0:T(8,128)(2,1)} %copy-done.17, bf16[64,2048]{1,0:T(8,128)(2,1)} %copy-done.18, ...), custom_call_target="tpu_custom_call" | custom-call | flops 2717908992 | bytes 6488064 | tf_op jit(solution)/shard_map/weight_grads/pallas_call | solution.py:495
  114.5 3.4 %spread.2.refs_18_ = bf16[64,2176]{1,0:T(8,128)(2,1)} custom-call(s32[15]{0:T(128)} %dynamic-slice_bitcast_fusion.refs_0_, s32[1,384]{1,0:T(1,128)} %constant.27.clone.refs_1_, bf16[64,4224]{1,0:T(8,128)(2,1)} %pack.1.refs_2_.refs_8_, bf16[64,4224]{1,0:T(8,128)(2,1)} %copy-done.1, bf16[64,4224]{1,0:T(8,128)(2,1)} %copy-done.3, bf16[64,4224]{1,0:T(8,128)(2,1)} %copy-done.4, ...), custom_call_target="tpu_custom_call" | custom-call | flops 100663296 | bytes 1572864 | tf_op jit(solution)/shard_map/spread/pallas_call | solution.py:519
  118.7 4.4 %spread.3 = (bf16[64,2176]{1,0:T(8,128)(2,1)}, bf16[64,2176]{1,0:T(8,128)(2,1)}, bf16[64,2176]{1,0:T(8,128)(2,1)}) custom-call(s32[15]{0:T(128)} %dynamic-slice_bitcast_fusion.refs_0_, s32[1,576]{1,0:T(1,128)} %constant.28.clone.refs_1_, bf16[64,4224]{1,0:T(8,128)(2,1)} %pack.1.refs_2_.refs_8_, bf16[64,4224]{1,0:T(8,128)(2,1)} %copy-done.1, ...), custom_call_target="tpu_custom_call" | custom-call | flops 452984832 | bytes 2359296 | tf_op jit(solution)/shard_map/spread/pallas_call | solution.py:519
  125.2 7.7 %collective-permute-done.27.b_ref = bf16[64,2176]{1,0:T(8,128)(2,1)S(1)} collective-permute-done((bf16[64,2176]{1,0:T(8,128)(2,1)}, bf16[64,2176]{1,0:T(8,128)(2,1)S(1)}, u32[]{:S(2)}, u32[]{:S(2)}) %collective-permute-start.27) | collective-permute-done | bytes 278560 | tf_op jit(solution)/shard_map/ppermute | solution.py:556
  133.6 1.8 %add.5 = bf16[64,2176]{1,0:T(8,128)(2,1)} custom-call(bf16[64,2176]{1,0:T(8,128)(2,1)} %get-tuple-element.198.a_ref, bf16[64,2176]{1,0:T(8,128)(2,1)} %copy-done.13), custom_call_target="tpu_custom_call" | custom-call | tf_op jit(solution)/shard_map/add/pallas_call | solution.py:560
  136.2 11.0 %weight_grads.3 = (bf16[1,2048,384]{2,1,0:T(8,128)(2,1)}, bf16[1,2048,384]{2,1,0:T(8,128)(2,1)}, bf16[1,384,2048]{2,1,0:T(8,128)(2,1)}) custom-call(bf16[64,2048]{1,0:T(8,128)(2,1)} %get-tuple-element.124.refs_1_.refs_0_, bf16[64,2048]{1,0:T(8,128)(2,1)} %copy-done.16, bf16[64,2048]{1,0:T(8,128)(2,1)} %copy-done.17, bf16[64,2048]{1,0:T(8,128)(2,1)} %copy-done.18, ...), custom_call_target="tpu_custom_call" | custom-call | flops 2717908992 | bytes 6488064 | tf_op jit(solution)/shard_map/weight_grads/pallas_call | solution.py:495
  147.2 2.7 %collective-permute-done.28.refs_2_ = bf16[64,2176]{1,0:T(8,128)(2,1)S(1)} collective-permute-done((bf16[64,2176]{1,0:T(8,128)(2,1)}, bf16[64,2176]{1,0:T(8,128)(2,1)S(1)}, u32[]{:S(2)}, u32[]{:S(2)}) %collective-permute-start.28) | collective-permute-done | bytes 278560 | tf_op jit(solution)/shard_map/ppermute | solution.py:556
  150.6 2.2 %home.1 = (bf16[64,2048]{1,0:T(8,128)(2,1)}, bf16[8,64]{1,0:T(8,128)(2,1)}) custom-call(bf16[64,2176]{1,0:T(8,128)(2,1)} %get-tuple-element.197.refs_0_, bf16[64,2176]{1,0:T(8,128)(2,1)} %copy-done.14, bf16[64,2176]{1,0:T(8,128)(2,1)} %copy-done.15, s32[8,64]{1,0:T(8,128)} %bitcast.6, bf16[8,64]{1,0:T(8,128)(2,1)} %bitcast.8, ...), custom_call_target="tpu_custom_call" | custom-call | flops 1000000 | bytes 1310720 | tf_op jit(solution)/shard_map/home/pallas_call | solution.py:570
  (110 shorter events, 31.3 us)
Async XLA Ops:
  0.6 13.8 %collective-permute-start.2 = (bf16[1,2048,384]{2,1,0:T(8,128)(2,1)}, bf16[1,2048,384]{2,1,0:T(8,128)(2,1)S(1)}, u32[]{:S(2)}, u32[]{:S(2)}) collective-permute-start(bf16[1,2048,384]{2,1,0:T(8,128)(2,1)} %refs_5_.1), channel_id=1, source_target_pairs={{0,16},{16,0},{1,17},{17,1},{2,18},{18,2},{3,19},{19,3},{4,20},{20... | collective-permute-start | bytes 4718600 | tf_op jit(solution)/shard_map/ppermute | solution.py:408
  1.1 13.3 %collective-permute-start.3 = (bf16[1,2048,384]{2,1,0:T(8,128)(2,1)}, bf16[1,2048,384]{2,1,0:T(8,128)(2,1)}, u32[]{:S(2)}, u32[]{:S(2)}) collective-permute-start(bf16[1,2048,384]{2,1,0:T(8,128)(2,1)} %refs_7_.1), channel_id=1, source_target_pairs={{0,16},{16,0},{1,17},{17,1},{2,18},{18,2},{3,19},{19,3},{4,20},{20... | collective-permute-start | bytes 4718600 | tf_op jit(solution)/shard_map/ppermute | solution.py:408
  1.2 13.3 %collective-permute-start.4 = (bf16[1,384,2048]{2,1,0:T(8,128)(2,1)}, bf16[1,384,2048]{2,1,0:T(8,128)(2,1)}, u32[]{:S(2)}, u32[]{:S(2)}) collective-permute-start(bf16[1,384,2048]{2,1,0:T(8,128)(2,1)} %refs_9_.1), channel_id=1, source_target_pairs={{0,16},{16,0},{1,17},{17,1},{2,18},{18,2},{3,19},{19,3},{4,20},{20... | collective-permute-start | bytes 4718600 | tf_op jit(solution)/shard_map/ppermute | solution.py:408
  5.5 17.3 %collective-permute-start = (bf16[64,4224]{1,0:T(8,128)(2,1)}, bf16[64,4224]{1,0:T(8,128)(2,1)S(1)}, u32[]{:S(2)}, u32[]{:S(2)}) collective-permute-start(bf16[64,4224]{1,0:T(8,128)(2,1)} %pack.1.refs_2_.refs_8_), channel_id=1, source_target_pairs={{0,4},{1,5},{2,6},{3,7},{4,0},{5,1},{6,2},{7,3},{8,12},{9,13},{10,... | collective-permute-start | bytes 1622024 | tf_op jit(solution)/shard_map/ppermute | solution.py:416
  23.5 23.5 %collective-permute-start.7 = (bf16[64,4224]{1,0:T(8,128)(2,1)S(1)}, bf16[64,4224]{1,0:T(8,128)(2,1)S(1)}, u32[]{:S(2)}, u32[]{:S(2)}) collective-permute-start(bf16[64,4224]{1,0:T(8,128)(2,1)S(1)} %collective-permute-done.1.refs_3_.refs_4_.refs_6_), channel_id=1, source_target_pairs={{0,4},{1,5},{2,6},{3,7},{4,0},{5,1},{6,2},{7,3},{8,12},{9,13},{10,... | collective-permute-start | bytes 1622024 | tf_op jit(solution)/shard_map/ppermute | solution.py:416
  27.0 16.4 %collective-permute-start.8 = (bf16[64,2048]{1,0:T(8,128)(2,1)}, bf16[64,2048]{1,0:T(8,128)(2,1)S(1)}, u32[]{:S(2)}, u32[]{:S(2)}) collective-permute-start(bf16[64,2048]{1,0:T(8,128)(2,1)} %get-tuple-element.117), channel_id=1, source_target_pairs={{0,1},{1,0},{2,3},{3,2},{4,5},{5,4},{6,7},{7,6},{8,9},{9,8},{10,11... | collective-permute-start | bytes 786440 | tf_op jit(solution)/shard_map/ppermute | solution.py:463
  28.5 15.0 %collective-permute-start.9 = (bf16[64,2048]{1,0:T(8,128)(2,1)}, bf16[64,2048]{1,0:T(8,128)(2,1)S(1)}, u32[]{:S(2)}, u32[]{:S(2)}) collective-permute-start(bf16[64,2048]{1,0:T(8,128)(2,1)} %get-tuple-element.118), channel_id=1, source_target_pairs={{0,2},{1,3},{2,0},{3,1},{4,6},{5,7},{6,4},{7,5},{8,10},{9,11},{10,... | collective-permute-start | bytes 786440 | tf_op jit(solution)/shard_map/ppermute | solution.py:463
  30.0 13.5 %collective-permute-start.10 = (bf16[64,2048]{1,0:T(8,128)(2,1)}, bf16[64,2048]{1,0:T(8,128)(2,1)S(1)}, u32[]{:S(2)}, u32[]{:S(2)}) collective-permute-start(bf16[64,2048]{1,0:T(8,128)(2,1)} %get-tuple-element.119), channel_id=1, source_target_pairs={{0,3},{1,2},{2,1},{3,0},{4,7},{5,6},{6,5},{7,4},{8,11},{9,10},{10,... | collective-permute-start | bytes 786440 | tf_op jit(solution)/shard_map/ppermute | solution.py:463
  30.5 30.0 %collective-permute-start.6 = (bf16[64,4224]{1,0:T(8,128)(2,1)S(1)}, bf16[64,4224]{1,0:T(8,128)(2,1)S(1)}, u32[]{:S(2)}, u32[]{:S(2)}) collective-permute-start(bf16[64,4224]{1,0:T(8,128)(2,1)S(1)} %collective-permute-done.5.refs_2_.refs_4_), channel_id=1, source_target_pairs={{0,4},{1,5},{2,6},{3,7},{4,0},{5,1},{6,2},{7,3},{8,12},{9,13},{10,... | collective-permute-start | bytes 1622024 | tf_op jit(solution)/shard_map/ppermute | solution.py:416
  45.0 11.9 %collective-permute-start.12 = (bf16[64,2048]{1,0:T(8,128)(2,1)}, bf16[64,2048]{1,0:T(8,128)(2,1)S(1)}, u32[]{:S(2)}, u32[]{:S(2)}) collective-permute-start(bf16[64,2048]{1,0:T(8,128)(2,1)} %get-tuple-element.130), channel_id=1, source_target_pairs={{0,2},{1,3},{2,0},{3,1},{4,6},{5,7},{6,4},{7,5},{8,10},{9,11},{10,... | collective-permute-start | bytes 786440 | tf_op jit(solution)/shard_map/ppermute | solution.py:463
  70.3 16.8 %collective-permute-start.17 = (bf16[96,2048]{1,0:T(8,128)(2,1)}, bf16[96,2048]{1,0:T(8,128)(2,1)S(1)}, u32[]{:S(2)}, u32[]{:S(2)}) collective-permute-start(bf16[96,2048]{1,0:T(8,128)(2,1)} %get-tuple-element.163), channel_id=1, source_target_pairs={{0,1},{1,0},{2,3},{3,2},{4,5},{5,4},{6,7},{7,6},{8,9},{9,8},{10,11... | collective-permute-start | bytes 1179656 | tf_op jit(solution)/shard_map/ppermute | solution.py:463
  70.5 16.6 %collective-permute-start.18 = (bf16[96,2048]{1,0:T(8,128)(2,1)}, bf16[96,2048]{1,0:T(8,128)(2,1)S(1)}, u32[]{:S(2)}, u32[]{:S(2)}) collective-permute-start(bf16[96,2048]{1,0:T(8,128)(2,1)} %get-tuple-element.164), channel_id=1, source_target_pairs={{0,2},{1,3},{2,0},{3,1},{4,6},{5,7},{6,4},{7,5},{8,10},{9,11},{10,... | collective-permute-start | bytes 1179656 | tf_op jit(solution)/shard_map/ppermute | solution.py:463
  72.1 15.0 %collective-permute-start.19 = (bf16[96,2048]{1,0:T(8,128)(2,1)}, bf16[96,2048]{1,0:T(8,128)(2,1)S(1)}, u32[]{:S(2)}, u32[]{:S(2)}) collective-permute-start(bf16[96,2048]{1,0:T(8,128)(2,1)} %get-tuple-element.165), channel_id=1, source_target_pairs={{0,3},{1,2},{2,1},{3,0},{4,7},{5,6},{6,5},{7,4},{8,11},{9,10},{10,... | collective-permute-start | bytes 1179656 | tf_op jit(solution)/shard_map/ppermute | solution.py:463
  87.1 15.6 %collective-permute-start.20 = (bf16[96,2176]{1,0:T(8,128)(2,1)}, bf16[96,2176]{1,0:T(8,128)(2,1)S(1)}, u32[]{:S(2)}, u32[]{:S(2)}) collective-permute-start(bf16[96,2176]{1,0:T(8,128)(2,1)} %get-tuple-element.180), channel_id=1, source_target_pairs={{0,1},{1,0},{2,3},{3,2},{4,5},{5,4},{6,7},{7,6},{8,9},{9,8},{10,11... | collective-permute-start | bytes 1253384 | tf_op jit(solution)/shard_map/ppermute | solution.py:463
  87.6 25.4 %collective-permute-start.21 = (bf16[96,2176]{1,0:T(8,128)(2,1)}, bf16[96,2176]{1,0:T(8,128)(2,1)S(1)}, u32[]{:S(2)}, u32[]{:S(2)}) collective-permute-start(bf16[96,2176]{1,0:T(8,128)(2,1)} %get-tuple-element.181), channel_id=1, source_target_pairs={{0,2},{1,3},{2,0},{3,1},{4,6},{5,7},{6,4},{7,5},{8,10},{9,11},{10,... | collective-permute-start | bytes 1253384 | tf_op jit(solution)/shard_map/ppermute | solution.py:463
  89.1 23.8 %collective-permute-start.22 = (bf16[96,2176]{1,0:T(8,128)(2,1)}, bf16[96,2176]{1,0:T(8,128)(2,1)S(1)}, u32[]{:S(2)}, u32[]{:S(2)}) collective-permute-start(bf16[96,2176]{1,0:T(8,128)(2,1)} %get-tuple-element.182), channel_id=1, source_target_pairs={{0,3},{1,2},{2,1},{3,0},{4,7},{5,6},{6,5},{7,4},{8,11},{9,10},{10,... | collective-permute-start | bytes 1253384 | tf_op jit(solution)/shard_map/ppermute | solution.py:463
  100.8 17.1 %collective-permute-start.23 = (bf16[48,2176]{1,0:T(8,128)(2,1)}, bf16[48,2176]{1,0:T(8,128)(2,1)S(1)}, u32[]{:S(2)}, u32[]{:S(2)}) collective-permute-start(bf16[48,2176]{1,0:T(8,128)(2,1)} %get-tuple-element.184), channel_id=1, source_target_pairs={{0,1},{1,0},{2,3},{3,2},{4,5},{5,4},{6,7},{7,6},{8,9},{9,8},{10,11... | collective-permute-start | bytes 626696 | tf_op jit(solution)/shard_map/ppermute | solution.py:463
  101.2 16.7 %collective-permute-start.24 = (bf16[48,2176]{1,0:T(8,128)(2,1)}, bf16[48,2176]{1,0:T(8,128)(2,1)S(1)}, u32[]{:S(2)}, u32[]{:S(2)}) collective-permute-start(bf16[48,2176]{1,0:T(8,128)(2,1)} %get-tuple-element.185), channel_id=1, source_target_pairs={{0,2},{1,3},{2,0},{3,1},{4,6},{5,7},{6,4},{7,5},{8,10},{9,11},{10,... | collective-permute-start | bytes 626696 | tf_op jit(solution)/shard_map/ppermute | solution.py:463
  102.8 15.1 %collective-permute-start.25 = (bf16[48,2176]{1,0:T(8,128)(2,1)}, bf16[48,2176]{1,0:T(8,128)(2,1)S(1)}, u32[]{:S(2)}, u32[]{:S(2)}) collective-permute-start(bf16[48,2176]{1,0:T(8,128)(2,1)} %get-tuple-element.186), channel_id=1, source_target_pairs={{0,3},{1,2},{2,1},{3,0},{4,7},{5,6},{6,5},{7,4},{8,11},{9,10},{10,... | collective-permute-start | bytes 626696 | tf_op jit(solution)/shard_map/ppermute | solution.py:463
  117.9 18.3 %collective-permute-start.30 = (bf16[1,2048,384]{2,1,0:T(8,128)(2,1)}, bf16[1,2048,384]{2,1,0:T(8,128)(2,1)}, u32[]{:S(2)}, u32[]{:S(2)}) collective-permute-start(bf16[1,2048,384]{2,1,0:T(8,128)(2,1)} %get-tuple-element.200), channel_id=1, source_target_pairs={{0,16},{16,0},{1,17},{17,1},{2,18},{18,2},{3,19},{19,3},{4,20},{20... | collective-permute-start | bytes 4718600 | tf_op jit(solution)/shard_map/ppermute | solution.py:548
  118.0 18.2 %collective-permute-start.31 = (bf16[1,384,2048]{2,1,0:T(8,128)(2,1)}, bf16[1,384,2048]{2,1,0:T(8,128)(2,1)}, u32[]{:S(2)}, u32[]{:S(2)}) collective-permute-start(bf16[1,384,2048]{2,1,0:T(8,128)(2,1)} %get-tuple-element.201), channel_id=1, source_target_pairs={{0,16},{16,0},{1,17},{17,1},{2,18},{18,2},{3,19},{19,3},{4,20},{20... | collective-permute-start | bytes 4718600 | tf_op jit(solution)/shard_map/ppermute | solution.py:548
  118.5 17.7 %collective-permute-start.29 = (bf16[1,2048,384]{2,1,0:T(8,128)(2,1)S(1)}, bf16[1,2048,384]{2,1,0:T(8,128)(2,1)}, u32[]{:S(2)}, u32[]{:S(2)}) collective-permute-start(bf16[1,2048,384]{2,1,0:T(8,128)(2,1)S(1)} %copy-done.8), channel_id=1, source_target_pairs={{0,16},{16,0},{1,17},{17,1},{2,18},{18,2},{3,19},{19,3},{4,20},{20... | collective-permute-start | bytes 4718600 | tf_op jit(solution)/shard_map/ppermute | solution.py:548
  123.9 23.3 %collective-permute-start.26 = (bf16[64,2176]{1,0:T(8,128)(2,1)S(1)}, bf16[64,2176]{1,0:T(8,128)(2,1)S(1)}, u32[]{:S(2)}, u32[]{:S(2)}) collective-permute-start(bf16[64,2176]{1,0:T(8,128)(2,1)S(1)} %copy-done.9), channel_id=1, source_target_pairs={{0,4},{1,5},{2,6},{3,7},{4,0},{5,1},{6,2},{7,3},{8,12},{9,13},{10,... | collective-permute-start | bytes 835592 | tf_op jit(solution)/shard_map/ppermute | solution.py:547
  135.4 14.6 %collective-permute-start.28 = (bf16[64,2176]{1,0:T(8,128)(2,1)}, bf16[64,2176]{1,0:T(8,128)(2,1)S(1)}, u32[]{:S(2)}, u32[]{:S(2)}) collective-permute-start(bf16[64,2176]{1,0:T(8,128)(2,1)} %add.5), channel_id=1, source_target_pairs={{0,8},{1,9},{2,10},{3,11},{4,12},{5,13},{6,14},{7,15},{8,0},{9,1},... | collective-permute-start | bytes 835592 | tf_op jit(solution)/shard_map/ppermute | solution.py:556
  (36 other events, 350.1 us)

commit v6 on v5

--- a/solution.py
+++ b/solution.py
@@ -43,6 +43,8 @@
         total = -(-self.outer * self.cap // 16) * 16
         step = self.outer // PARTS
         marks = [k * step * self.cap // 16 * 16 for k in range(PARTS)] + [total]
+        if marks[1] >= 32:
+            marks[1] = marks[1] // 32 * 16
         self.chunks = [(marks[k], marks[k + 1]) for k in range(PARTS)]
         self.rows = [b - a for a, b in self.chunks]
         self.steps = [(k + 1) * step - 1 for k in range(PARTS)]
@@ -213,10 +215,16 @@
     inner, rows, width, hidden = plan.inner, plan.sizes[group], plan.width, plan.hidden
     part, count, n = hidden // 2, inner * rows, inner * len(plan.groups[group])
     info = refs[0]
-    got, weights = refs[1 : 1 + n], refs[1 + n : 7 + n]
-    hid_o, gate_o, up_o = refs[7 + n : 10 + n]
-    backs = refs[10 + n : 10 + n + inner]
-    x_s, d_s, wg_s, wu_s, wd_s, comb_s, sems = refs[10 + n + inner :]
+    got, weights = refs[1 : 1 + n], refs[1 + n : 6 + n]
+    hid_o, gate_o, up_o = refs[6 + n : 9 + n]
+    backs = refs[9 + n : 9 + n + inner]
+    x_s, d_s, wg_s, wu_s, wd_s, comb_s, sems = refs[9 + n + inner :]
+    own_g, own_u, own_d, both, other_d = [w.at[0] for w in weights]
+    views = [
+        (own_g, both.at[:, pl.ds(0, part)]),
+        (own_u, both.at[:, pl.ds(part, part)]),
+        (own_d, other_d),
+    ]
     x_copies, d_copies = pieces(plan, group, got, x_s, d_s, sems)
     tile, tiles = hidden, []
     for t in range(hidden // tile):
@@ -226,7 +234,7 @@
                 half, start = divmod(at, part)
                 size = min((t + 1) * tile, (half + 1) * part) - at
                 source, to = pl.ds(start, size), pl.ds(at, size)
-                w = weights[2 * kind + half].at[0]
+                w = views[kind][half]
                 here.append((w.at[source], where.at[to]) if kind == 2 else (w.at[:, source], where.at[:, to]))
                 at += size
             tiles.append(here)
@@ -405,7 +413,7 @@
         name="pack",
     )(tokens, upstream, routes.T, combine.T)
 
-    others = [lax.ppermute(w, "dp", swap) for w in (w_gate, w_up, w_down)]
+    gate_up = jnp.concatenate([w_gate, w_up], axis=2)
     blocks = [block] * plan.cands
 
     def hop(r):
@@ -414,6 +422,9 @@
                 i = chain * (outer - 1) + r
                 before = block if r == 1 else blocks[i - 1]
                 blocks[i] = lax.ppermute(before, "expert", plan.exchange(r, chain))
+        if 1 < r <= min(plan.last):
+            i = outer - 1 + r
+            blocks[r], blocks[i] = lax.optimization_barrier((blocks[r], blocks[i]))
 
     hop(1)
     def compact(c):
@@ -442,7 +453,7 @@
             functools.partial(expert_kernel, plan, g),
             out_shape=[shape((count, hidden), BF)] * 3
             + [shape((rows, width + LANES), BF)] * inner,
-            in_specs=[SMEM] + [ANY] * (n + 6),
+            in_specs=[SMEM] + [ANY] * (n + 5),
             out_specs=[VMEM] * (3 + inner),
             scratch_shapes=[
                 pltpu.VMEM((count, width), BF),
@@ -469,17 +480,21 @@
             hop(r)
         done = max(done, plan.steps[c])
         sent = compact(c)
+        if c > 0:
+            got[-1], sent = lax.optimization_barrier((got[-1], sent))
+        if c == PARTS - 2:
+            gate_up, sent = lax.optimization_barrier((gate_up, sent))
+            gate_up = lax.ppermute(gate_up, "dp", swap)
+        if c == PARTS - 1:
+            gate_up, sent = lax.optimization_barrier((gate_up, sent))
+            down = lax.ppermute(lax.optimization_barrier((w_down, sent))[0], "dp", swap)
+        got.append(cross(sent))
         if c == 0:
-            others, sent = lax.optimization_barrier((others, sent))
-            blocks[done], blocks[outer - 1 + done], sent = lax.optimization_barrier(
-                (blocks[done], blocks[outer - 1 + done], sent)
+            i = outer - 1 + done
+            got[0], blocks[done], blocks[i] = lax.optimization_barrier(
+                (got[0], blocks[done], blocks[i])
             )
-        else:
-            got[-1], sent = lax.optimization_barrier((got[-1], sent))
-        got.append(cross(sent))
-    weights = []
-    for w, other in zip((w_gate, w_up, w_down), others):
-        weights += [w, other]
+    weights = [w_gate, w_up, w_down, gate_up, down]
     outs = expert(0, sum(got[:-1], []))
     late = got[-1]
     outs, late = lax.optimization_barrier((outs, late))

time: 153 us -> 156 us (1.020)
  starting transfers between devices: 45.5 us -> 35.2 us
  waiting for transfers between devices: 28.4 us -> 35.9 us
  other arithmetic: 0 us -> 3.27 us
  local copies, waits for them, and re-layouts: 6.69 us -> 8.82 us
    ppermute x5, starting transfers between devices: 19.8 us -> 10.1 us  [hop(): blocks[i] = lax.ppermute(before, 'expert', plan.exchange(r, chain))]
    ppermute x18, waiting for transfers between devices: 9.65 us -> 15.6 us  [cross(): lax.ppermute(arrays[d], 'expert', plan.across(d))]
    concatenate x0 -> x1, other arithmetic: none -> 3.27 us  [on_device(): gate_up = jnp.concatenate([w_gate, w_up], axis=2)]
    ppermute x5, waiting for transfers between devices: 8.3 us -> 10.9 us  [hop(): blocks[i] = lax.ppermute(before, 'expert', plan.exchange(r, chain))]
    unnamed x56 -> x52, local copies, waits for them, and re-layouts: 5.49 us -> 7.62 us
  transfers between devices with their start and end apart: 32 -> 31, of which waited for: 6 -> 9; matrix products, arithmetic and copies ran while one was open for 1% -> 3% of each run, Pallas kernels for 45% -> 43%
where the time goes in v6:
time: 156 us
  Pallas kernels  71.4 us (46%)
  waiting for transfers between devices  35.9 us (23%)
  starting transfers between devices  35.2 us (23%)
  local copies, waits for them, and re-layouts  8.82 us (6%)
  other arithmetic  3.27 us (2%)
    pallas_call x2, Pallas kernels, expert(): pl.pallas_call(functools.partial(expert_kernel, plan, g), out_shape=[shap...  23.4 us
    ppermute x18, starting transfers between devices, cross(): lax.ppermute(arrays[d], 'expert', plan.across(d))  21.2 us
    pallas_call x2, Pallas kernels, weight_grads(): pl.pallas_call(functools.partial(weight_kernel, plan, own), out_shape=[sh...  19.6 us
    ppermute x18, waiting for transfers between devices, cross(): lax.ppermute(arrays[d], 'expert', plan.across(d))  15.6 us
    pallas_call x4, Pallas kernels, compact(): pl.pallas_call(functools.partial(compact_kernel, plan, c), out_shape=[sha...  14.4 us
    ppermute x5, waiting for transfers between devices, hop(): blocks[i] = lax.ppermute(before, 'expert', plan.exchange(r, chain))  10.9 us
    ppermute x5, starting transfers between devices, hop(): blocks[i] = lax.ppermute(before, 'expert', plan.exchange(r, chain))  10.1 us
    ppermute x2, waiting for transfers between devices, on_device(): sent = lax.ppermute(sums[r], 'expert', plan.flip(bit))  9.31 us
  transfers between devices with their start and end apart: 31, of which 9 were waited for; matrix products, arithmetic and copies ran while one was open for 3% of the time, Pallas kernels for 43%

profile of v6, /device:TPU:0, one launch (start us, length us, event | category | flops | bytes accessed | tf_op | source)
XLA Modules:
  0.0 155.7 jit_solution(4964594525702269382)
XLA Ops:
  0.6 2.3 %pack.1.refs_2_.refs_8_ = bf16[64,4224]{1,0:T(8,128)(2,1)} custom-call(bf16[64,2048]{1,0:T(8,128)(2,1)} %tok_ref.1, bf16[64,2048]{1,0:T(8,128)(2,1)} %up_ref.1, s32[8,64]{1,0:T(8,128)} %bitcast.5, bf16[8,64]{1,0:T(8,128)(2,1)} %bitcast.7), custom_call_target="tpu_custom_call" | custom-call | flops 1000000 | bytes 1081344 | tf_op jit(solution)/shard_map/pack/pallas_call | solution.py:406
  4.6 4.9 %collective-permute-start.3 = (bf16[64,4224]{1,0:T(8,128)(2,1)}, bf16[64,4224]{1,0:T(8,128)(2,1)S(1)}, u32[]{:S(2)}, u32[]{:S(2)}) collective-permute-start(bf16[64,4224]{1,0:T(8,128)(2,1)} %pack.1.refs_2_.refs_8_), channel_id=1, source_target_pairs={{0,4},{1,5},{2,6},{3,7},{4,0},{5,1},{6,2},{7,3},{8,12},{9,13},{10,... | collective-permute-start | bytes 1622024 | tf_op jit(solution)/shard_map/ppermute | solution.py:424
  10.7 3.0 %compact.4 = (bf16[32,2048]{1,0:T(8,128)(2,1)}, bf16[32,2048]{1,0:T(8,128)(2,1)}, bf16[32,2048]{1,0:T(8,128)(2,1)}, bf16[32,2048]{1,0:T(8,128)(2,1)}) custom-call(s32[15]{0:T(128)} %dynamic-slice_bitcast_fusion.refs_0_, s32[1,64]{1,0:T(1,128)} %constant.23.clone.refs_1_, bf16[64,4224]{1,0:T(8,128)(2,1)} %pack.1.refs_2_.refs_8_), custom_call_target="tpu_custom_call" | custom-call | flops 33554432 | bytes 540672 | tf_op jit(solution)/shard_map/compact/pallas_call | solution.py:433
  17.2 2.4 %collective-permute-done.refs_2_.refs_1_ = bf16[32,2048]{1,0:T(8,128)(2,1)S(1)} collective-permute-done((bf16[32,2048]{1,0:T(8,128)(2,1)}, bf16[32,2048]{1,0:T(8,128)(2,1)S(1)}, u32[]{:S(2)}, u32[]{:S(2)}) %collective-permute-start) | collective-permute-done | bytes 131104 | tf_op jit(solution)/shard_map/ppermute | solution.py:474
  19.7 3.5 %collective-permute-done.1.refs_3_.refs_2_ = bf16[32,2048]{1,0:T(8,128)(2,1)S(1)} collective-permute-done((bf16[32,2048]{1,0:T(8,128)(2,1)}, bf16[32,2048]{1,0:T(8,128)(2,1)S(1)}, u32[]{:S(2)}, u32[]{:S(2)}) %collective-permute-start.1) | collective-permute-done | bytes 131104 | tf_op jit(solution)/shard_map/ppermute | solution.py:474
  24.6 2.6 %collective-permute-start.6 = (bf16[64,4224]{1,0:T(8,128)(2,1)S(1)}, bf16[64,4224]{1,0:T(8,128)(2,1)S(1)}, u32[]{:S(2)}, u32[]{:S(2)}) collective-permute-start(bf16[64,4224]{1,0:T(8,128)(2,1)S(1)} %collective-permute-done.4.refs_3_.refs_4_.refs_6_), channel_id=1, source_target_pairs={{0,4},{1,5},{2,6},{3,7},{4,0},{5,1},{6,2},{7,3},{8,12},{9,13},{10,... | collective-permute-start | bytes 1622024 | tf_op jit(solution)/shard_map/ppermute | solution.py:424
  27.2 3.7 %compact.5 = (bf16[96,2048]{1,0:T(8,128)(2,1)}, bf16[96,2048]{1,0:T(8,128)(2,1)}, bf16[96,2048]{1,0:T(8,128)(2,1)}, bf16[96,2048]{1,0:T(8,128)(2,1)}) custom-call(s32[15]{0:T(128)} %dynamic-slice_bitcast_fusion.refs_0_, s32[1,192]{1,0:T(1,128)} %constant.24.clone.refs_1_, bf16[64,4224]{1,0:T(8,128)(2,1)} %pack.1.refs_2_.refs_8_, bf16[64,4224]{1,0:T(8,128)(2,1)} %copy-done.2), custom_call_target="tpu_custom_call" | custom-call | flops 201326592 | bytes 1081344 | tf_op jit(solution)/shard_map/compact/pallas_call | solution.py:433
  34.5 3.3 %pad_maximum_fusion = bf16[1,2048,768]{2,1,0:T(8,128)(2,1)} fusion(bf16[1,2048,384]{2,1,0:T(8,128)(2,1)} %refs_6_.1, bf16[1,2048,384]{2,1,0:T(8,128)(2,1)S(1)} %copy-done.9), kind=kLoop, calls=%fused_computation | loop fusion | flops 6291456 | bytes 6291456 | tf_op jit(solution)/shard_map/concatenate | solution.py:416
  38.6 3.6 %compact.6 = (bf16[64,2048]{1,0:T(8,128)(2,1)}, bf16[64,2048]{1,0:T(8,128)(2,1)}, bf16[64,2048]{1,0:T(8,128)(2,1)}, bf16[64,2048]{1,0:T(8,128)(2,1)}) custom-call(s32[15]{0:T(128)} %dynamic-slice_bitcast_fusion.refs_0_, s32[1,128]{1,0:T(1,128)} %constant.25.clone.refs_1_, bf16[64,4224]{1,0:T(8,128)(2,1)} %copy-done.2, bf16[64,4224]{1,0:T(8,128)(2,1)} %copy-done, ...), custom_call_target="tpu_custom_call" | custom-call | flops 201326592 | bytes 1622016 | tf_op jit(solution)/shard_map/compact/pallas_call | solution.py:433
  43.4 6.2 %collective-permute-done.9.refs_7_.refs_6_ = bf16[96,2048]{1,0:T(8,128)(2,1)} collective-permute-done((bf16[96,2048]{1,0:T(8,128)(2,1)}, bf16[96,2048]{1,0:T(8,128)(2,1)}, u32[]{:S(2)}, u32[]{:S(2)}) %collective-permute-start.9) | collective-permute-done | bytes 393248 | tf_op jit(solution)/shard_map/ppermute | solution.py:474
  51.6 1.8 %collective-permute-start.13 = (bf16[64,2048]{1,0:T(8,128)(2,1)}, bf16[64,2048]{1,0:T(8,128)(2,1)S(1)}, u32[]{:S(2)}, u32[]{:S(2)}) collective-permute-start(bf16[64,2048]{1,0:T(8,128)(2,1)} %get-tuple-element.151), channel_id=1, source_target_pairs={{0,3},{1,2},{2,1},{3,0},{4,7},{5,6},{6,5},{7,4},{8,11},{9,10},{10,... | collective-permute-start | bytes 786440 | tf_op jit(solution)/shard_map/ppermute | solution.py:474
  53.3 10.9 %collective-permute-done.7.refs_3_.refs_5_ = bf16[64,4224]{1,0:T(8,128)(2,1)S(1)} collective-permute-done((bf16[64,4224]{1,0:T(8,128)(2,1)S(1)}, bf16[64,4224]{1,0:T(8,128)(2,1)S(1)}, u32[]{:S(2)}, u32[]{:S(2)}) %collective-permute-start.7) | collective-permute-done | bytes 540704 | tf_op jit(solution)/shard_map/ppermute | solution.py:424
  65.1 4.1 %compact.7 = (bf16[96,2048]{1,0:T(8,128)(2,1)}, bf16[96,2048]{1,0:T(8,128)(2,1)}, bf16[96,2048]{1,0:T(8,128)(2,1)}, bf16[96,2048]{1,0:T(8,128)(2,1)}) custom-call(s32[15]{0:T(128)} %dynamic-slice_bitcast_fusion.refs_0_, s32[1,192]{1,0:T(1,128)} %constant.26.clone.refs_1_, bf16[64,4224]{1,0:T(8,128)(2,1)} %copy-done.3, bf16[64,4224]{1,0:T(8,128)(2,1)} %copy-done.4, ...), custom_call_target="tpu_custom_call" | custom-call | flops 402653184 | bytes 2162688 | tf_op jit(solution)/shard_map/compact/pallas_call | solution.py:433
  71.1 1.8 %collective-permute-start.18 = (bf16[96,2048]{1,0:T(8,128)(2,1)}, bf16[96,2048]{1,0:T(8,128)(2,1)S(1)}, u32[]{:S(2)}, u32[]{:S(2)}) collective-permute-start(bf16[96,2048]{1,0:T(8,128)(2,1)} %get-tuple-element.169), channel_id=1, source_target_pairs={{0,3},{1,2},{2,1},{3,0},{4,7},{5,6},{6,5},{7,4},{8,11},{9,10},{10,... | collective-permute-start | bytes 1179656 | tf_op jit(solution)/shard_map/ppermute | solution.py:474
  74.1 13.3 %expert.2 = (bf16[384,768]{1,0:T(8,128)(2,1)}, bf16[384,768]{1,0:T(8,128)(2,1)}, bf16[384,768]{1,0:T(8,128)(2,1)}, bf16[96,2176]{1,0:T(8,128)(2,1)}, bf16[96,217...) custom-call(s32[15]{0:T(128)} %dynamic-slice_bitcast_fusion.refs_0_, ...), custom_call_target="tpu_custom_call" | custom-call | flops 6039797760 | bytes 9437184 | tf_op jit(solution)/shard_map/expert/pallas_call | solution.py:452
  87.4 2.3 %collective-permute-done.18.refs_4_.refs_15_ = bf16[96,2048]{1,0:T(8,128)(2,1)S(1)} collective-permute-done((bf16[96,2048]{1,0:T(8,128)(2,1)}, bf16[96,2048]{1,0:T(8,128)(2,1)S(1)}, u32[]{:S(2)}, u32[]{:S(2)}) %collective-permute-start.18) | collective-permute-done | bytes 393248 | tf_op jit(solution)/shard_map/ppermute | solution.py:474
  93.2 10.1 %expert.3 = (bf16[192,768]{1,0:T(8,128)(2,1)}, bf16[192,768]{1,0:T(8,128)(2,1)}, bf16[192,768]{1,0:T(8,128)(2,1)}, bf16[48,2176]{1,0:T(8,128)(2,1)}, bf16[48,217...) custom-call(s32[15]{0:T(128)} %dynamic-slice_bitcast_fusion.refs_0_, ...), custom_call_target="tpu_custom_call" | custom-call | flops 3019898880 | bytes 9437184 | tf_op jit(solution)/shard_map/expert/pallas_call | solution.py:452
  106.9 8.6 %weight_grads.2 = (bf16[1,2048,384]{2,1,0:T(8,128)(2,1)}, bf16[1,2048,384]{2,1,0:T(8,128)(2,1)}, bf16[1,384,2048]{2,1,0:T(8,128)(2,1)}) custom-call(bf16[32,2048]{1,0:T(8,128)(2,1)} %get-tuple-element.128.refs_1_.refs_0_, bf16[32,2048]{1,0:T(8,128)(2,1)} %copy-done.22, bf16[32,2048]{1,0:T(8,128)(2,1)} %copy-done.23, bf16[32,2048]{1,0:T(8,128)(2,1)} %copy-done.24, ...), custom_call_target="tpu_custom_call" | custom-call | flops 2717908992 | bytes 6488064 | tf_op jit(solution)/shard_map/weight_grads/pallas_call | solution.py:510
  117.0 3.4 %spread.2.refs_18_ = bf16[64,2176]{1,0:T(8,128)(2,1)} custom-call(s32[15]{0:T(128)} %dynamic-slice_bitcast_fusion.refs_0_, s32[1,384]{1,0:T(1,128)} %constant.27.clone.refs_1_, bf16[64,4224]{1,0:T(8,128)(2,1)} %pack.1.refs_2_.refs_8_, bf16[64,4224]{1,0:T(8,128)(2,1)} %copy-done.2, bf16[64,4224]{1,0:T(8,128)(2,1)} %copy-done.3, bf16[64,4224]{1,0:T(8,128)(2,1)} %copy-done.4, ...), custom_call_target="tpu_custom_call" | custom-call | flops 100663296 | bytes 1572864 | tf_op jit(solution)/shard_map/spread/pallas_call | solution.py:534
  121.8 4.4 %spread.3 = (bf16[64,2176]{1,0:T(8,128)(2,1)}, bf16[64,2176]{1,0:T(8,128)(2,1)}, bf16[64,2176]{1,0:T(8,128)(2,1)}) custom-call(s32[15]{0:T(128)} %dynamic-slice_bitcast_fusion.refs_0_, s32[1,576]{1,0:T(1,128)} %constant.28.clone.refs_1_, bf16[64,4224]{1,0:T(8,128)(2,1)} %pack.1.refs_2_.refs_8_, bf16[64,4224]{1,0:T(8,128)(2,1)} %copy-done.2, ...), custom_call_target="tpu_custom_call" | custom-call | flops 452984832 | bytes 2359296 | tf_op jit(solution)/shard_map/spread/pallas_call | solution.py:534
  128.3 7.7 %collective-permute-done.26.b_ref = bf16[64,2176]{1,0:T(8,128)(2,1)} collective-permute-done((bf16[64,2176]{1,0:T(8,128)(2,1)}, bf16[64,2176]{1,0:T(8,128)(2,1)}, u32[]{:S(2)}, u32[]{:S(2)}) %collective-permute-start.26) | collective-permute-done | bytes 278560 | tf_op jit(solution)/shard_map/ppermute | solution.py:571
  136.0 1.8 %add.5 = bf16[64,2176]{1,0:T(8,128)(2,1)} custom-call(bf16[64,2176]{1,0:T(8,128)(2,1)} %get-tuple-element.210.a_ref, bf16[64,2176]{1,0:T(8,128)(2,1)} %collective-permute-done.26.b_ref), custom_call_target="tpu_custom_call" | custom-call | tf_op jit(solution)/shard_map/add/pallas_call | solution.py:575
  140.2 11.0 %weight_grads.3 = (bf16[1,2048,384]{2,1,0:T(8,128)(2,1)}, bf16[1,2048,384]{2,1,0:T(8,128)(2,1)}, bf16[1,384,2048]{2,1,0:T(8,128)(2,1)}) custom-call(bf16[32,2048]{1,0:T(8,128)(2,1)} %get-tuple-element.128.refs_1_.refs_0_, bf16[32,2048]{1,0:T(8,128)(2,1)} %copy-done.22, bf16[32,2048]{1,0:T(8,128)(2,1)} %copy-done.23, bf16[32,2048]{1,0:T(8,128)(2,1)} %copy-done.24, ...), custom_call_target="tpu_custom_call" | custom-call | flops 2717908992 | bytes 6488064 | tf_op jit(solution)/shard_map/weight_grads/pallas_call | solution.py:510
  153.5 2.2 %home.1 = (bf16[64,2048]{1,0:T(8,128)(2,1)}, bf16[8,64]{1,0:T(8,128)(2,1)}) custom-call(bf16[64,2176]{1,0:T(8,128)(2,1)} %get-tuple-element.209.refs_0_, bf16[64,2176]{1,0:T(8,128)(2,1)} %collective-permute-done.25.refs_1_, bf16[64,2176]{1,0:T(8,128)(2,1)} %copy-done.15, s32[8,64]{1,0:T(8,128)} %bitcast.6, bf16[8,64]{1,0:T(8,128)(2,1)} %bitcast.8, ...), custom_call_target="tpu_custom_call" | custom-call | flops 1000000 | bytes 1310720 | tf_op jit(solution)/shard_map/home/pallas_call | solution.py:585
  (105 shorter events, 35.9 us)
Async XLA Ops:
  2.9 20.3 %collective-permute-start.4 = (bf16[64,4224]{1,0:T(8,128)(2,1)}, bf16[64,4224]{1,0:T(8,128)(2,1)S(1)}, u32[]{:S(2)}, u32[]{:S(2)}) collective-permute-start(bf16[64,4224]{1,0:T(8,128)(2,1)} %pack.1.refs_2_.refs_8_), channel_id=1, source_target_pairs={{0,0},{1,1},{2,2},{3,3},{4,8},{5,9},{6,10},{7,11},{8,4},{9,5},{10,... | collective-permute-start | bytes 1622024 | tf_op jit(solution)/shard_map/ppermute | solution.py:424
  4.6 18.6 %collective-permute-start.3 = (bf16[64,4224]{1,0:T(8,128)(2,1)}, bf16[64,4224]{1,0:T(8,128)(2,1)S(1)}, u32[]{:S(2)}, u32[]{:S(2)}) collective-permute-start(bf16[64,4224]{1,0:T(8,128)(2,1)} %pack.1.refs_2_.refs_8_), channel_id=1, source_target_pairs={{0,4},{1,5},{2,6},{3,7},{4,0},{5,1},{6,2},{7,3},{8,12},{9,13},{10,... | collective-permute-start | bytes 1622024 | tf_op jit(solution)/shard_map/ppermute | solution.py:424
  23.9 13.8 %collective-permute-start.5 = (bf16[64,4224]{1,0:T(8,128)(2,1)S(1)}, bf16[64,4224]{1,0:T(8,128)(2,1)S(1)}, u32[]{:S(2)}, u32[]{:S(2)}) collective-permute-start(bf16[64,4224]{1,0:T(8,128)(2,1)S(1)} %collective-permute-done.3.refs_3_.refs_2_), channel_id=1, source_target_pairs={{0,0},{1,1},{2,2},{3,3},{4,8},{5,9},{6,10},{7,11},{8,4},{9,5},{10,... | collective-permute-start | bytes 1622024 | tf_op jit(solution)/shard_map/ppermute | solution.py:424
  31.9 17.7 %collective-permute-start.9 = (bf16[96,2048]{1,0:T(8,128)(2,1)}, bf16[96,2048]{1,0:T(8,128)(2,1)}, u32[]{:S(2)}, u32[]{:S(2)}) collective-permute-start(bf16[96,2048]{1,0:T(8,128)(2,1)} %get-tuple-element.134), channel_id=1, source_target_pairs={{0,2},{1,3},{2,0},{3,1},{4,6},{5,7},{6,4},{7,5},{8,10},{9,11},{10,... | collective-permute-start | bytes 1179656 | tf_op jit(solution)/shard_map/ppermute | solution.py:474
  32.8 16.8 %collective-permute-start.10 = (bf16[96,2048]{1,0:T(8,128)(2,1)}, bf16[96,2048]{1,0:T(8,128)(2,1)}, u32[]{:S(2)}, u32[]{:S(2)}) collective-permute-start(bf16[96,2048]{1,0:T(8,128)(2,1)} %get-tuple-element.135), channel_id=1, source_target_pairs={{0,3},{1,2},{2,1},{3,0},{4,7},{5,6},{6,5},{7,4},{8,11},{9,10},{10,... | collective-permute-start | bytes 1179656 | tf_op jit(solution)/shard_map/ppermute | solution.py:474
  49.5 19.7 %collective-permute-start.14 = (bf16[1,2048,768]{2,1,0:T(8,128)(2,1)}, bf16[1,2048,768]{2,1,0:T(8,128)(2,1)}, u32[]{:S(2)}, u32[]{:S(2)}) collective-permute-start(bf16[1,2048,768]{2,1,0:T(8,128)(2,1)} %pad_maximum_fusion), channel_id=1, source_target_pairs={{0,16},{16,0},{1,17},{17,1},{2,18},{18,2},{3,19},{19,3},{4,20},{20... | collective-permute-start | bytes 9437192 | tf_op jit(solution)/shard_map/ppermute | solution.py:487
  49.5 14.7 %collective-permute-start.7 = (bf16[64,4224]{1,0:T(8,128)(2,1)S(1)}, bf16[64,4224]{1,0:T(8,128)(2,1)S(1)}, u32[]{:S(2)}, u32[]{:S(2)}) collective-permute-start(bf16[64,4224]{1,0:T(8,128)(2,1)S(1)} %collective-permute-done.5.refs_2_.refs_4_), channel_id=1, source_target_pairs={{0,4},{1,5},{2,6},{3,7},{4,0},{5,1},{6,2},{7,3},{8,12},{9,13},{10,... | collective-permute-start | bytes 1622024 | tf_op jit(solution)/shard_map/ppermute | solution.py:424
  49.8 19.3 %collective-permute-start.11 = (bf16[64,2048]{1,0:T(8,128)(2,1)}, bf16[64,2048]{1,0:T(8,128)(2,1)S(1)}, u32[]{:S(2)}, u32[]{:S(2)}) collective-permute-start(bf16[64,2048]{1,0:T(8,128)(2,1)} %get-tuple-element.149), channel_id=1, source_target_pairs={{0,1},{1,0},{2,3},{3,2},{4,5},{5,4},{6,7},{7,6},{8,9},{9,8},{10,11... | collective-permute-start | bytes 786440 | tf_op jit(solution)/shard_map/ppermute | solution.py:474
  50.3 18.9 %collective-permute-start.12 = (bf16[64,2048]{1,0:T(8,128)(2,1)}, bf16[64,2048]{1,0:T(8,128)(2,1)S(1)}, u32[]{:S(2)}, u32[]{:S(2)}) collective-permute-start(bf16[64,2048]{1,0:T(8,128)(2,1)} %get-tuple-element.150), channel_id=1, source_target_pairs={{0,2},{1,3},{2,0},{3,1},{4,6},{5,7},{6,4},{7,5},{8,10},{9,11},{10,... | collective-permute-start | bytes 786440 | tf_op jit(solution)/shard_map/ppermute | solution.py:474
  51.6 17.6 %collective-permute-start.13 = (bf16[64,2048]{1,0:T(8,128)(2,1)}, bf16[64,2048]{1,0:T(8,128)(2,1)S(1)}, u32[]{:S(2)}, u32[]{:S(2)}) collective-permute-start(bf16[64,2048]{1,0:T(8,128)(2,1)} %get-tuple-element.151), channel_id=1, source_target_pairs={{0,3},{1,2},{2,1},{3,0},{4,7},{5,6},{6,5},{7,4},{8,11},{9,10},{10,... | collective-permute-start | bytes 786440 | tf_op jit(solution)/shard_map/ppermute | solution.py:474
  69.3 18.0 %collective-permute-start.16 = (bf16[96,2048]{1,0:T(8,128)(2,1)}, bf16[96,2048]{1,0:T(8,128)(2,1)S(1)}, u32[]{:S(2)}, u32[]{:S(2)}) collective-permute-start(bf16[96,2048]{1,0:T(8,128)(2,1)} %get-tuple-element.167), channel_id=1, source_target_pairs={{0,1},{1,0},{2,3},{3,2},{4,5},{5,4},{6,7},{7,6},{8,9},{9,8},{10,11... | collective-permute-start | bytes 1179656 | tf_op jit(solution)/shard_map/ppermute | solution.py:474
  69.9 17.5 %collective-permute-start.17 = (bf16[96,2048]{1,0:T(8,128)(2,1)}, bf16[96,2048]{1,0:T(8,128)(2,1)S(1)}, u32[]{:S(2)}, u32[]{:S(2)}) collective-permute-start(bf16[96,2048]{1,0:T(8,128)(2,1)} %get-tuple-element.168), channel_id=1, source_target_pairs={{0,2},{1,3},{2,0},{3,1},{4,6},{5,7},{6,4},{7,5},{8,10},{9,11},{10,... | collective-permute-start | bytes 1179656 | tf_op jit(solution)/shard_map/ppermute | solution.py:474
  71.1 18.6 %collective-permute-start.18 = (bf16[96,2048]{1,0:T(8,128)(2,1)}, bf16[96,2048]{1,0:T(8,128)(2,1)S(1)}, u32[]{:S(2)}, u32[]{:S(2)}) collective-permute-start(bf16[96,2048]{1,0:T(8,128)(2,1)} %get-tuple-element.169), channel_id=1, source_target_pairs={{0,3},{1,2},{2,1},{3,0},{4,7},{5,6},{6,5},{7,4},{8,11},{9,10},{10,... | collective-permute-start | bytes 1179656 | tf_op jit(solution)/shard_map/ppermute | solution.py:474
  89.7 16.0 %collective-permute-start.19 = (bf16[96,2176]{1,0:T(8,128)(2,1)}, bf16[96,2176]{1,0:T(8,128)(2,1)S(1)}, u32[]{:S(2)}, u32[]{:S(2)}) collective-permute-start(bf16[96,2176]{1,0:T(8,128)(2,1)} %get-tuple-element.192), channel_id=1, source_target_pairs={{0,1},{1,0},{2,3},{3,2},{4,5},{5,4},{6,7},{7,6},{8,9},{9,8},{10,11... | collective-permute-start | bytes 1253384 | tf_op jit(solution)/shard_map/ppermute | solution.py:474
  91.3 24.2 %collective-permute-start.20 = (bf16[96,2176]{1,0:T(8,128)(2,1)}, bf16[96,2176]{1,0:T(8,128)(2,1)S(1)}, u32[]{:S(2)}, u32[]{:S(2)}) collective-permute-start(bf16[96,2176]{1,0:T(8,128)(2,1)} %get-tuple-element.193), channel_id=1, source_target_pairs={{0,2},{1,3},{2,0},{3,1},{4,6},{5,7},{6,4},{7,5},{8,10},{9,11},{10,... | collective-permute-start | bytes 1253384 | tf_op jit(solution)/shard_map/ppermute | solution.py:474
  92.1 23.4 %collective-permute-start.21 = (bf16[96,2176]{1,0:T(8,128)(2,1)}, bf16[96,2176]{1,0:T(8,128)(2,1)S(1)}, u32[]{:S(2)}, u32[]{:S(2)}) collective-permute-start(bf16[96,2176]{1,0:T(8,128)(2,1)} %get-tuple-element.194), channel_id=1, source_target_pairs={{0,3},{1,2},{2,1},{3,0},{4,7},{5,6},{6,5},{7,4},{8,11},{9,10},{10,... | collective-permute-start | bytes 1253384 | tf_op jit(solution)/shard_map/ppermute | solution.py:474
  103.3 17.1 %collective-permute-start.22 = (bf16[48,2176]{1,0:T(8,128)(2,1)}, bf16[48,2176]{1,0:T(8,128)(2,1)S(1)}, u32[]{:S(2)}, u32[]{:S(2)}) collective-permute-start(bf16[48,2176]{1,0:T(8,128)(2,1)} %get-tuple-element.196), channel_id=1, source_target_pairs={{0,1},{1,0},{2,3},{3,2},{4,5},{5,4},{6,7},{7,6},{8,9},{9,8},{10,11... | collective-permute-start | bytes 626696 | tf_op jit(solution)/shard_map/ppermute | solution.py:474
  105.0 15.5 %collective-permute-start.23 = (bf16[48,2176]{1,0:T(8,128)(2,1)}, bf16[48,2176]{1,0:T(8,128)(2,1)S(1)}, u32[]{:S(2)}, u32[]{:S(2)}) collective-permute-start(bf16[48,2176]{1,0:T(8,128)(2,1)} %get-tuple-element.197), channel_id=1, source_target_pairs={{0,2},{1,3},{2,0},{3,1},{4,6},{5,7},{6,4},{7,5},{8,10},{9,11},{10,... | collective-permute-start | bytes 626696 | tf_op jit(solution)/shard_map/ppermute | solution.py:474
  105.7 14.7 %collective-permute-start.24 = (bf16[48,2176]{1,0:T(8,128)(2,1)}, bf16[48,2176]{1,0:T(8,128)(2,1)S(1)}, u32[]{:S(2)}, u32[]{:S(2)}) collective-permute-start(bf16[48,2176]{1,0:T(8,128)(2,1)} %get-tuple-element.198), channel_id=1, source_target_pairs={{0,3},{1,2},{2,1},{3,0},{4,7},{5,6},{6,5},{7,4},{8,11},{9,10},{10,... | collective-permute-start | bytes 626696 | tf_op jit(solution)/shard_map/ppermute | solution.py:474
  121.2 17.8 %collective-permute-start.29 = (bf16[1,2048,384]{2,1,0:T(8,128)(2,1)}, bf16[1,2048,384]{2,1,0:T(8,128)(2,1)S(1)}, u32[]{:S(2)}, u32[]{:S(2)}) collective-permute-start(bf16[1,2048,384]{2,1,0:T(8,128)(2,1)} %get-tuple-element.212), channel_id=1, source_target_pairs={{0,16},{16,0},{1,17},{17,1},{2,18},{18,2},{3,19},{19,3},{4,20},{20... | collective-permute-start | bytes 4718600 | tf_op jit(solution)/shard_map/ppermute | solution.py:563
  121.2 17.8 %collective-permute-start.30 = (bf16[1,384,2048]{2,1,0:T(8,128)(2,1)}, bf16[1,384,2048]{2,1,0:T(8,128)(2,1)}, u32[]{:S(2)}, u32[]{:S(2)}) collective-permute-start(bf16[1,384,2048]{2,1,0:T(8,128)(2,1)} %get-tuple-element.213), channel_id=1, source_target_pairs={{0,16},{16,0},{1,17},{17,1},{2,18},{18,2},{3,19},{19,3},{4,20},{20... | collective-permute-start | bytes 4718600 | tf_op jit(solution)/shard_map/ppermute | solution.py:563
  121.8 17.3 %collective-permute-start.28 = (bf16[1,2048,384]{2,1,0:T(8,128)(2,1)S(1)}, bf16[1,2048,384]{2,1,0:T(8,128)(2,1)}, u32[]{:S(2)}, u32[]{:S(2)}) collective-permute-start(bf16[1,2048,384]{2,1,0:T(8,128)(2,1)S(1)} %copy-done.8), channel_id=1, source_target_pairs={{0,16},{16,0},{1,17},{17,1},{2,18},{18,2},{3,19},{19,3},{4,20},{20... | collective-permute-start | bytes 4718600 | tf_op jit(solution)/shard_map/ppermute | solution.py:563
  126.5 24.6 %collective-permute-start.25 = (bf16[64,2176]{1,0:T(8,128)(2,1)S(1)}, bf16[64,2176]{1,0:T(8,128)(2,1)}, u32[]{:S(2)}, u32[]{:S(2)}) collective-permute-start(bf16[64,2176]{1,0:T(8,128)(2,1)S(1)} %copy-done.11), channel_id=1, source_target_pairs={{0,4},{1,5},{2,6},{3,7},{4,0},{5,1},{6,2},{7,3},{8,12},{9,13},{10,... | collective-permute-start | bytes 835592 | tf_op jit(solution)/shard_map/ppermute | solution.py:562
  137.8 14.9 %collective-permute-start.27 = (bf16[64,2176]{1,0:T(8,128)(2,1)}, bf16[64,2176]{1,0:T(8,128)(2,1)S(1)}, u32[]{:S(2)}, u32[]{:S(2)}) collective-permute-start(bf16[64,2176]{1,0:T(8,128)(2,1)} %add.5), channel_id=1, source_target_pairs={{0,8},{1,9},{2,10},{3,11},{4,12},{5,13},{6,14},{7,15},{8,0},{9,1},... | collective-permute-start | bytes 835592 | tf_op jit(solution)/shard_map/ppermute | solution.py:571
  (33 other events, 291.7 us)

commit v7 on v6

--- a/solution.py
+++ b/solution.py
@@ -45,6 +45,7 @@
         marks = [k * step * self.cap // 16 * 16 for k in range(PARTS)] + [total]
         if marks[1] >= 32:
             marks[1] = marks[1] // 32 * 16
+            marks[2] = marks[1] + 32
         self.chunks = [(marks[k], marks[k + 1]) for k in range(PARTS)]
         self.rows = [b - a for a, b in self.chunks]
         self.steps = [(k + 1) * step - 1 for k in range(PARTS)]
@@ -294,45 +295,59 @@
     at = n + 6
     theirs = refs[at : at + 3] if own else None
     at += 3 if own else 0
-    g_o, u_o, d_o = refs[at : at + 3]
-    x_s, d_s, h_s, gu_s, sems, mid_sems = refs[at + 3 :]
-    everything, base, taken = [], 0, 0
+    outs = refs[at : at + 3]
+    x_s, d_s, h_s, gu_s, g_s, u_s, w_s, sems, mid_sems, out_sems = refs[at + 3 : at + 13]
+    kept = refs[at + 13 :]
+    first, second, base, taken = [], [], 0, 0
     half = pl.ds(0 if own else part, part)
     for g in range(2):
         many = inner * len(plan.groups[g])
         mine = got[taken : taken + many]
         at_sems = sems.at[pl.ds(2 * taken, 2 * many)]
         x_copies, d_copies = pieces(plan, g, mine, x_s, d_s, at_sems, base)
-        everything += x_copies + d_copies
+        first += x_copies
+        second += d_copies
         to = pl.ds(base, inner * plan.sizes[g])
         spots = (h_s.at[to], gu_s.at[to, pl.ds(0, part)], gu_s.at[to, pl.ds(part, part)])
         for i, (m, s) in enumerate(zip(mids[3 * g : 3 * g + 3], spots)):
-            everything.append(
-                pltpu.make_async_copy(m.at[:, half], s, mid_sems.at[3 * g + i])
-            )
+            copy = pltpu.make_async_copy(m.at[:, half], s, mid_sems.at[3 * g + i])
+            (second if i == 0 else first).append(copy)
         taken += many
         base += inner * plan.sizes[g]
-    for c in everything:
+    came = []
+    if own:
+        came = [
+            pltpu.make_async_copy(t.at[0], k, out_sems.at[5 + i])
+            for i, (t, k) in enumerate(zip(theirs, kept))
+        ]
+    for c in first + came[:2] + second + came[2:]:
         c.start()
-    for c in everything:
+    for c in first + came[:2]:
         c.wait()
-    tile = width // 2
-
-    @pl.loop(0, width // tile)
-    def _(j):
-        to = pl.ds(pl.multiple_of(j * tile, tile), tile)
+    tile, left = width // 2, []
+    for j in range(2):
+        to = slice(j * tile, (j + 1) * tile)
         both = lax.dot_general(x_s[:, to], gu_s[...], TN, preferred_element_type=F32)
-        first, second = both[:, :part], both[:, part:]
-        if own:
-            first += theirs[0][0, to, :].astype(F32)
-            second += theirs[1][0, to, :].astype(F32)
-        g_o[0, to, :] = first.astype(BF)
-        u_o[0, to, :] = second.astype(BF)
-
+        for i, (o, s) in enumerate(zip(outs, (g_s, u_s))):
+            value = both[:, i * part : (i + 1) * part]
+            if own:
+                value += kept[i][to, :].astype(F32)
+            s[to, :] = value.astype(BF)
+            rows = pl.ds(j * tile, tile)
+            left.append(
+                pltpu.make_async_copy(s.at[rows], o.at[0, rows], out_sems.at[2 * j + i])
+            )
+            left[-1].start()
+    for c in second + came[2:]:
+        c.wait()
     down = lax.dot_general(h_s[...], d_s[...], TN, preferred_element_type=F32)
     if own:
-        down += theirs[2][0].astype(F32)
-    d_o[0] = down.astype(BF)
+        down += kept[2][...].astype(F32)
+    w_s[...] = down.astype(BF)
+    left.append(pltpu.make_async_copy(w_s, outs[2].at[0], out_sems.at[4]))
+    left[-1].start()
+    for c in left:
+        c.wait()
 
 
 def spread_kernel(plan, homes, groups, *refs):
@@ -506,6 +521,12 @@
 
     count = inner * sum(plan.rows)
 
+    grad_scratch = [
+        pltpu.VMEM((width, part), BF),
+        pltpu.VMEM((width, part), BF),
+        pltpu.VMEM((part, width), BF),
+    ]
+
     def weight_grads(own, extra):
         return pl.pallas_call(
             functools.partial(weight_kernel, plan, own),
@@ -514,15 +535,18 @@
                 shape((1, width, part), BF),
                 shape((1, part, width), BF),
             ],
-            in_specs=[ANY] * (inner * PARTS + 6) + [VMEM] * len(extra),
-            out_specs=[VMEM] * 3,
+            in_specs=[ANY] * (inner * PARTS + 6 + len(extra)),
+            out_specs=[ANY] * 3,
             scratch_shapes=[
                 pltpu.VMEM((count, width), BF),
                 pltpu.VMEM((count, width), BF),
                 pltpu.VMEM((count, part), BF),
                 pltpu.VMEM((count, 2 * part), BF),
+                *grad_scratch,
                 pltpu.SemaphoreType.DMA((2 * inner * PARTS,)),
                 pltpu.SemaphoreType.DMA((6,)),
+                pltpu.SemaphoreType.DMA((8,)),
+                *(grad_scratch if own else []),
             ],
             compiler_params=params(),
             cost_estimate=cost(6 * count * part * width, 4 * count * (width + hidden)),

time: 156 us -> 153 us (0.981)
  Pallas kernels: 71.4 us -> 69.1 us
    ppermute x18, waiting for transfers between devices: 15.6 us -> 13.3 us  [cross(): lax.ppermute(arrays[d], 'expert', plan.across(d))]
    pallas_call x2, Pallas kernels: 19.6 us -> 17.3 us  [weight_grads(): pl.pallas_call(functools.partial(weight_kernel, plan, own), out_shape=[sh...]
where the time goes in v7:
time: 153 us; the launch traced here: 152 us
  Pallas kernels  69.1 us (45%)
  starting transfers between devices  35.7 us (23%)
  waiting for transfers between devices  34.8 us (23%)
  local copies, waits for them, and re-layouts  8.04 us (5%)
  other arithmetic  3.34 us (2%)
    pallas_call x2, Pallas kernels, expert(): pl.pallas_call(functools.partial(expert_kernel, plan, g), out_shape=[shap...  23.3 us
    ppermute x18, starting transfers between devices, cross(): lax.ppermute(arrays[d], 'expert', plan.across(d))  21.2 us
    pallas_call x2, Pallas kernels, weight_grads(): pl.pallas_call(functools.partial(weight_kernel, plan, own), out_shape=[sh...  17.3 us
    pallas_call x4, Pallas kernels, compact(): pl.pallas_call(functools.partial(compact_kernel, plan, c), out_shape=[sha...  14.4 us
    ppermute x18, waiting for transfers between devices, cross(): lax.ppermute(arrays[d], 'expert', plan.across(d))  13.3 us
    ppermute x5, waiting for transfers between devices, hop(): blocks[i] = lax.ppermute(before, 'expert', plan.exchange(r, chain))  10.8 us
    ppermute x2, waiting for transfers between devices, on_device(): sent = lax.ppermute(sums[r], 'expert', plan.flip(bit))  10.5 us
    ppermute x5, starting transfers between devices, hop(): blocks[i] = lax.ppermute(before, 'expert', plan.exchange(r, chain))  10 us
  transfers between devices with their start and end apart: 31, of which 9 were waited for; matrix products, arithmetic and copies ran while one was open for 3% of the time, Pallas kernels for 43%

profile of v7, /device:TPU:0, one launch (start us, length us, event | category | flops | bytes accessed | tf_op | source)
XLA Modules:
  0.0 152.0 jit_solution(10882574324925866851)
XLA Ops:
  0.6 2.2 %pack.1.refs_2_.refs_8_ = bf16[64,4224]{1,0:T(8,128)(2,1)} custom-call(bf16[64,2048]{1,0:T(8,128)(2,1)} %tok_ref.1, bf16[64,2048]{1,0:T(8,128)(2,1)} %up_ref.1, s32[8,64]{1,0:T(8,128)} %bitcast.5, bf16[8,64]{1,0:T(8,128)(2,1)} %bitcast.7), custom_call_target="tpu_custom_call" | custom-call | flops 1000000 | bytes 1081344 | tf_op jit(solution)/shard_map/pack/pallas_call | solution.py:421
  4.6 4.9 %collective-permute-start.3 = (bf16[64,4224]{1,0:T(8,128)(2,1)}, bf16[64,4224]{1,0:T(8,128)(2,1)S(1)}, u32[]{:S(2)}, u32[]{:S(2)}) collective-permute-start(bf16[64,4224]{1,0:T(8,128)(2,1)} %pack.1.refs_2_.refs_8_), channel_id=1, source_target_pairs={{0,4},{1,5},{2,6},{3,7},{4,0},{5,1},{6,2},{7,3},{8,12},{9,13},{10,... | collective-permute-start | bytes 1622024 | tf_op jit(solution)/shard_map/ppermute | solution.py:439
  10.7 3.0 %compact.4 = (bf16[32,2048]{1,0:T(8,128)(2,1)}, bf16[32,2048]{1,0:T(8,128)(2,1)}, bf16[32,2048]{1,0:T(8,128)(2,1)}, bf16[32,2048]{1,0:T(8,128)(2,1)}) custom-call(s32[15]{0:T(128)} %dynamic-slice_bitcast_fusion.refs_0_, s32[1,64]{1,0:T(1,128)} %constant.23.clone.refs_1_, bf16[64,4224]{1,0:T(8,128)(2,1)} %pack.1.refs_2_.refs_8_), custom_call_target="tpu_custom_call" | custom-call | flops 33554432 | bytes 540672 | tf_op jit(solution)/shard_map/compact/pallas_call | solution.py:448
  17.2 2.4 %collective-permute-done.refs_2_.refs_1_ = bf16[32,2048]{1,0:T(8,128)(2,1)S(1)} collective-permute-done((bf16[32,2048]{1,0:T(8,128)(2,1)}, bf16[32,2048]{1,0:T(8,128)(2,1)S(1)}, u32[]{:S(2)}, u32[]{:S(2)}) %collective-permute-start) | collective-permute-done | bytes 131104 | tf_op jit(solution)/shard_map/ppermute | solution.py:489
  19.7 3.5 %collective-permute-done.1.refs_3_.refs_2_ = bf16[32,2048]{1,0:T(8,128)(2,1)S(1)} collective-permute-done((bf16[32,2048]{1,0:T(8,128)(2,1)}, bf16[32,2048]{1,0:T(8,128)(2,1)S(1)}, u32[]{:S(2)}, u32[]{:S(2)}) %collective-permute-start.1) | collective-permute-done | bytes 131104 | tf_op jit(solution)/shard_map/ppermute | solution.py:489
  24.2 2.4 %collective-permute-start.6 = (bf16[64,4224]{1,0:T(8,128)(2,1)S(1)}, bf16[64,4224]{1,0:T(8,128)(2,1)S(1)}, u32[]{:S(2)}, u32[]{:S(2)}) collective-permute-start(bf16[64,4224]{1,0:T(8,128)(2,1)S(1)} %collective-permute-done.4.refs_3_.refs_4_.refs_6_), channel_id=1, source_target_pairs={{0,4},{1,5},{2,6},{3,7},{4,0},{5,1},{6,2},{7,3},{8,12},{9,13},{10,... | collective-permute-start | bytes 1622024 | tf_op jit(solution)/shard_map/ppermute | solution.py:439
  26.6 3.4 %compact.5 = (bf16[64,2048]{1,0:T(8,128)(2,1)}, bf16[64,2048]{1,0:T(8,128)(2,1)}, bf16[64,2048]{1,0:T(8,128)(2,1)}, bf16[64,2048]{1,0:T(8,128)(2,1)}) custom-call(s32[15]{0:T(128)} %dynamic-slice_bitcast_fusion.refs_0_, s32[1,128]{1,0:T(1,128)} %constant.24.clone.refs_1_, bf16[64,4224]{1,0:T(8,128)(2,1)} %pack.1.refs_2_.refs_8_, bf16[64,4224]{1,0:T(8,128)(2,1)} %copy-done.1), custom_call_target="tpu_custom_call" | custom-call | flops 134217728 | bytes 1081344 | tf_op jit(solution)/shard_map/compact/pallas_call | solution.py:448
  33.5 3.3 %pad_maximum_fusion = bf16[1,2048,768]{2,1,0:T(8,128)(2,1)} fusion(bf16[1,2048,384]{2,1,0:T(8,128)(2,1)} %refs_6_.1, bf16[1,2048,384]{2,1,0:T(8,128)(2,1)S(1)} %copy-done.9), kind=kLoop, calls=%fused_computation | loop fusion | flops 6291456 | bytes 6291456 | tf_op jit(solution)/shard_map/concatenate | solution.py:431
  37.7 3.9 %compact.6 = (bf16[96,2048]{1,0:T(8,128)(2,1)}, bf16[96,2048]{1,0:T(8,128)(2,1)}, bf16[96,2048]{1,0:T(8,128)(2,1)}, bf16[96,2048]{1,0:T(8,128)(2,1)}) custom-call(s32[15]{0:T(128)} %dynamic-slice_bitcast_fusion.refs_0_, s32[1,192]{1,0:T(1,128)} %constant.25.clone.refs_1_, bf16[64,4224]{1,0:T(8,128)(2,1)} %copy-done.1, bf16[64,4224]{1,0:T(8,128)(2,1)} %copy-done, ...), custom_call_target="tpu_custom_call" | custom-call | flops 301989888 | bytes 1622016 | tf_op jit(solution)/shard_map/compact/pallas_call | solution.py:448
  46.9 10.8 %collective-permute-done.7.refs_3_.refs_5_ = bf16[64,4224]{1,0:T(8,128)(2,1)S(1)} collective-permute-done((bf16[64,4224]{1,0:T(8,128)(2,1)S(1)}, bf16[64,4224]{1,0:T(8,128)(2,1)S(1)}, u32[]{:S(2)}, u32[]{:S(2)}) %collective-permute-start.7) | collective-permute-done | bytes 540704 | tf_op jit(solution)/shard_map/ppermute | solution.py:439
  58.5 4.1 %compact.7 = (bf16[96,2048]{1,0:T(8,128)(2,1)}, bf16[96,2048]{1,0:T(8,128)(2,1)}, bf16[96,2048]{1,0:T(8,128)(2,1)}, bf16[96,2048]{1,0:T(8,128)(2,1)}) custom-call(s32[15]{0:T(128)} %dynamic-slice_bitcast_fusion.refs_0_, s32[1,192]{1,0:T(1,128)} %constant.26.clone.refs_1_, bf16[64,4224]{1,0:T(8,128)(2,1)} %copy-done.3, bf16[64,4224]{1,0:T(8,128)(2,1)} %copy-done.4, ...), custom_call_target="tpu_custom_call" | custom-call | flops 402653184 | bytes 2162688 | tf_op jit(solution)/shard_map/compact/pallas_call | solution.py:448
  62.7 1.9 %collective-permute-done.12.refs_11_.refs_10_ = bf16[96,2048]{1,0:T(8,128)(2,1)S(1)} collective-permute-done((bf16[96,2048]{1,0:T(8,128)(2,1)}, bf16[96,2048]{1,0:T(8,128)(2,1)S(1)}, u32[]{:S(2)}, u32[]{:S(2)}) %collective-permute-start.12) | collective-permute-done | bytes 393248 | tf_op jit(solution)/shard_map/ppermute | solution.py:489
  68.4 13.1 %expert.2 = (bf16[384,768]{1,0:T(8,128)(2,1)}, bf16[384,768]{1,0:T(8,128)(2,1)}, bf16[384,768]{1,0:T(8,128)(2,1)}, bf16[96,2176]{1,0:T(8,128)(2,1)}, bf16[96,217...) custom-call(s32[15]{0:T(128)} %dynamic-slice_bitcast_fusion.refs_0_, ...), custom_call_target="tpu_custom_call" | custom-call | flops 6039797760 | bytes 9437184 | tf_op jit(solution)/shard_map/expert/pallas_call | solution.py:467
  81.6 4.0 %collective-permute-done.18.refs_4_.refs_15_ = bf16[96,2048]{1,0:T(8,128)(2,1)S(1)} collective-permute-done((bf16[96,2048]{1,0:T(8,128)(2,1)}, bf16[96,2048]{1,0:T(8,128)(2,1)S(1)}, u32[]{:S(2)}, u32[]{:S(2)}) %collective-permute-start.18) | collective-permute-done | bytes 393248 | tf_op jit(solution)/shard_map/ppermute | solution.py:489
  89.9 10.2 %expert.3 = (bf16[192,768]{1,0:T(8,128)(2,1)}, bf16[192,768]{1,0:T(8,128)(2,1)}, bf16[192,768]{1,0:T(8,128)(2,1)}, bf16[48,2176]{1,0:T(8,128)(2,1)}, bf16[48,217...) custom-call(s32[15]{0:T(128)} %dynamic-slice_bitcast_fusion.refs_0_, ...), custom_call_target="tpu_custom_call" | custom-call | flops 3019898880 | bytes 9437184 | tf_op jit(solution)/shard_map/expert/pallas_call | solution.py:467
  103.6 8.1 %weight_grads.2 = (bf16[1,2048,384]{2,1,0:T(8,128)(2,1)}, bf16[1,2048,384]{2,1,0:T(8,128)(2,1)}, bf16[1,384,2048]{2,1,0:T(8,128)(2,1)}) custom-call(bf16[32,2048]{1,0:T(8,128)(2,1)} %get-tuple-element.128.refs_1_.refs_0_, bf16[32,2048]{1,0:T(8,128)(2,1)} %copy-done.23, bf16[32,2048]{1,0:T(8,128)(2,1)} %copy-done.24, bf16[32,2048]{1,0:T(8,128)(2,1)} %copy-done.25, ...), custom_call_target="tpu_custom_call" | custom-call | flops 2717908992 | bytes 6488064 | tf_op jit(solution)/shard_map/weight_grads/pallas_call | solution.py:531
  113.4 3.4 %spread.2.refs_18_ = bf16[64,2176]{1,0:T(8,128)(2,1)} custom-call(s32[15]{0:T(128)} %dynamic-slice_bitcast_fusion.refs_0_, s32[1,384]{1,0:T(1,128)} %constant.27.clone.refs_1_, bf16[64,4224]{1,0:T(8,128)(2,1)} %pack.1.refs_2_.refs_8_, bf16[64,4224]{1,0:T(8,128)(2,1)} %copy-done.1, bf16[64,4224]{1,0:T(8,128)(2,1)} %copy-done.3, bf16[64,4224]{1,0:T(8,128)(2,1)} %copy-done.4, ...), custom_call_target="tpu_custom_call" | custom-call | flops 100663296 | bytes 1572864 | tf_op jit(solution)/shard_map/spread/pallas_call | solution.py:558
  118.1 4.4 %spread.3 = (bf16[64,2176]{1,0:T(8,128)(2,1)}, bf16[64,2176]{1,0:T(8,128)(2,1)}, bf16[64,2176]{1,0:T(8,128)(2,1)}) custom-call(s32[15]{0:T(128)} %dynamic-slice_bitcast_fusion.refs_0_, s32[1,576]{1,0:T(1,128)} %constant.28.clone.refs_1_, bf16[64,4224]{1,0:T(8,128)(2,1)} %pack.1.refs_2_.refs_8_, bf16[64,4224]{1,0:T(8,128)(2,1)} %copy-done.1, ...), custom_call_target="tpu_custom_call" | custom-call | flops 452984832 | bytes 2359296 | tf_op jit(solution)/shard_map/spread/pallas_call | solution.py:558
  124.6 7.7 %collective-permute-done.26.b_ref = bf16[64,2176]{1,0:T(8,128)(2,1)} collective-permute-done((bf16[64,2176]{1,0:T(8,128)(2,1)}, bf16[64,2176]{1,0:T(8,128)(2,1)}, u32[]{:S(2)}, u32[]{:S(2)}) %collective-permute-start.26) | collective-permute-done | bytes 278560 | tf_op jit(solution)/shard_map/ppermute | solution.py:595
  132.3 1.8 %add.5 = bf16[64,2176]{1,0:T(8,128)(2,1)} custom-call(bf16[64,2176]{1,0:T(8,128)(2,1)} %get-tuple-element.210.a_ref, bf16[64,2176]{1,0:T(8,128)(2,1)} %collective-permute-done.26.b_ref), custom_call_target="tpu_custom_call" | custom-call | tf_op jit(solution)/shard_map/add/pallas_call | solution.py:599
  134.1 1.8 %collective-permute-start.27 = (bf16[64,2176]{1,0:T(8,128)(2,1)}, bf16[64,2176]{1,0:T(8,128)(2,1)S(1)}, u32[]{:S(2)}, u32[]{:S(2)}) collective-permute-start(bf16[64,2176]{1,0:T(8,128)(2,1)} %add.5), channel_id=1, source_target_pairs={{0,8},{1,9},{2,10},{3,11},{4,12},{5,13},{6,14},{7,15},{8,0},{9,1},... | collective-permute-start | bytes 835592 | tf_op jit(solution)/shard_map/ppermute | solution.py:595
  137.2 9.2 %weight_grads.3 = (bf16[1,2048,384]{2,1,0:T(8,128)(2,1)}, bf16[1,2048,384]{2,1,0:T(8,128)(2,1)}, bf16[1,384,2048]{2,1,0:T(8,128)(2,1)}) custom-call(bf16[32,2048]{1,0:T(8,128)(2,1)} %get-tuple-element.128.refs_1_.refs_0_, bf16[32,2048]{1,0:T(8,128)(2,1)} %copy-done.23, bf16[32,2048]{1,0:T(8,128)(2,1)} %copy-done.24, bf16[32,2048]{1,0:T(8,128)(2,1)} %copy-done.25, ...), custom_call_target="tpu_custom_call" | custom-call | flops 2717908992 | bytes 6488064 | tf_op jit(solution)/shard_map/weight_grads/pallas_call | solution.py:531
  146.4 2.7 %collective-permute-done.27.refs_2_ = bf16[64,2176]{1,0:T(8,128)(2,1)S(1)} collective-permute-done((bf16[64,2176]{1,0:T(8,128)(2,1)}, bf16[64,2176]{1,0:T(8,128)(2,1)S(1)}, u32[]{:S(2)}, u32[]{:S(2)}) %collective-permute-start.27) | collective-permute-done | bytes 278560 | tf_op jit(solution)/shard_map/ppermute | solution.py:595
  149.8 2.2 %home.1 = (bf16[64,2048]{1,0:T(8,128)(2,1)}, bf16[8,64]{1,0:T(8,128)(2,1)}) custom-call(bf16[64,2176]{1,0:T(8,128)(2,1)} %get-tuple-element.209.refs_0_, bf16[64,2176]{1,0:T(8,128)(2,1)} %collective-permute-done.25.refs_1_, bf16[64,2176]{1,0:T(8,128)(2,1)} %copy-done.18, s32[8,64]{1,0:T(8,128)} %bitcast.6, bf16[8,64]{1,0:T(8,128)(2,1)} %bitcast.8, ...), custom_call_target="tpu_custom_call" | custom-call | flops 1000000 | bytes 1310720 | tf_op jit(solution)/shard_map/home/pallas_call | solution.py:609
  (105 shorter events, 36.2 us)
Async XLA Ops:
  2.9 20.3 %collective-permute-start.4 = (bf16[64,4224]{1,0:T(8,128)(2,1)}, bf16[64,4224]{1,0:T(8,128)(2,1)S(1)}, u32[]{:S(2)}, u32[]{:S(2)}) collective-permute-start(bf16[64,4224]{1,0:T(8,128)(2,1)} %pack.1.refs_2_.refs_8_), channel_id=1, source_target_pairs={{0,0},{1,1},{2,2},{3,3},{4,8},{5,9},{6,10},{7,11},{8,4},{9,5},{10,... | collective-permute-start | bytes 1622024 | tf_op jit(solution)/shard_map/ppermute | solution.py:439
  4.6 18.6 %collective-permute-start.3 = (bf16[64,4224]{1,0:T(8,128)(2,1)}, bf16[64,4224]{1,0:T(8,128)(2,1)S(1)}, u32[]{:S(2)}, u32[]{:S(2)}) collective-permute-start(bf16[64,4224]{1,0:T(8,128)(2,1)} %pack.1.refs_2_.refs_8_), channel_id=1, source_target_pairs={{0,4},{1,5},{2,6},{3,7},{4,0},{5,1},{6,2},{7,3},{8,12},{9,13},{10,... | collective-permute-start | bytes 1622024 | tf_op jit(solution)/shard_map/ppermute | solution.py:439
  23.3 13.6 %collective-permute-start.5 = (bf16[64,4224]{1,0:T(8,128)(2,1)S(1)}, bf16[64,4224]{1,0:T(8,128)(2,1)S(1)}, u32[]{:S(2)}, u32[]{:S(2)}) collective-permute-start(bf16[64,4224]{1,0:T(8,128)(2,1)S(1)} %collective-permute-done.3.refs_3_.refs_2_), channel_id=1, source_target_pairs={{0,0},{1,1},{2,2},{3,3},{4,8},{5,9},{6,10},{7,11},{8,4},{9,5},{10,... | collective-permute-start | bytes 1622024 | tf_op jit(solution)/shard_map/ppermute | solution.py:439
  24.2 12.7 %collective-permute-start.6 = (bf16[64,4224]{1,0:T(8,128)(2,1)S(1)}, bf16[64,4224]{1,0:T(8,128)(2,1)S(1)}, u32[]{:S(2)}, u32[]{:S(2)}) collective-permute-start(bf16[64,4224]{1,0:T(8,128)(2,1)S(1)} %collective-permute-done.4.refs_3_.refs_4_.refs_6_), channel_id=1, source_target_pairs={{0,4},{1,5},{2,6},{3,7},{4,0},{5,1},{6,2},{7,3},{8,12},{9,13},{10,... | collective-permute-start | bytes 1622024 | tf_op jit(solution)/shard_map/ppermute | solution.py:439
  31.0 12.0 %collective-permute-start.9 = (bf16[64,2048]{1,0:T(8,128)(2,1)}, bf16[64,2048]{1,0:T(8,128)(2,1)}, u32[]{:S(2)}, u32[]{:S(2)}) collective-permute-start(bf16[64,2048]{1,0:T(8,128)(2,1)} %get-tuple-element.134), channel_id=1, source_target_pairs={{0,2},{1,3},{2,0},{3,1},{4,6},{5,7},{6,4},{7,5},{8,10},{9,11},{10,... | collective-permute-start | bytes 786440 | tf_op jit(solution)/shard_map/ppermute | solution.py:489
  43.0 21.6 %collective-permute-start.14 = (bf16[1,2048,768]{2,1,0:T(8,128)(2,1)}, bf16[1,2048,768]{2,1,0:T(8,128)(2,1)}, u32[]{:S(2)}, u32[]{:S(2)}) collective-permute-start(bf16[1,2048,768]{2,1,0:T(8,128)(2,1)} %pad_maximum_fusion), channel_id=1, source_target_pairs={{0,16},{16,0},{1,17},{17,1},{2,18},{18,2},{3,19},{19,3},{4,20},{20... | collective-permute-start | bytes 9437192 | tf_op jit(solution)/shard_map/ppermute | solution.py:502
  43.0 14.7 %collective-permute-start.7 = (bf16[64,4224]{1,0:T(8,128)(2,1)S(1)}, bf16[64,4224]{1,0:T(8,128)(2,1)S(1)}, u32[]{:S(2)}, u32[]{:S(2)}) collective-permute-start(bf16[64,4224]{1,0:T(8,128)(2,1)S(1)} %collective-permute-done.5.refs_2_.refs_4_), channel_id=1, source_target_pairs={{0,4},{1,5},{2,6},{3,7},{4,0},{5,1},{6,2},{7,3},{8,12},{9,13},{10,... | collective-permute-start | bytes 1622024 | tf_op jit(solution)/shard_map/ppermute | solution.py:439
  43.4 19.3 %collective-permute-start.11 = (bf16[96,2048]{1,0:T(8,128)(2,1)}, bf16[96,2048]{1,0:T(8,128)(2,1)S(1)}, u32[]{:S(2)}, u32[]{:S(2)}) collective-permute-start(bf16[96,2048]{1,0:T(8,128)(2,1)} %get-tuple-element.149), channel_id=1, source_target_pairs={{0,1},{1,0},{2,3},{3,2},{4,5},{5,4},{6,7},{7,6},{8,9},{9,8},{10,11... | collective-permute-start | bytes 1179656 | tf_op jit(solution)/shard_map/ppermute | solution.py:489
  45.0 19.5 %collective-permute-start.12 = (bf16[96,2048]{1,0:T(8,128)(2,1)}, bf16[96,2048]{1,0:T(8,128)(2,1)S(1)}, u32[]{:S(2)}, u32[]{:S(2)}) collective-permute-start(bf16[96,2048]{1,0:T(8,128)(2,1)} %get-tuple-element.150), channel_id=1, source_target_pairs={{0,2},{1,3},{2,0},{3,1},{4,6},{5,7},{6,4},{7,5},{8,10},{9,11},{10,... | collective-permute-start | bytes 1179656 | tf_op jit(solution)/shard_map/ppermute | solution.py:489
  46.4 18.2 %collective-permute-start.13 = (bf16[96,2048]{1,0:T(8,128)(2,1)}, bf16[96,2048]{1,0:T(8,128)(2,1)S(1)}, u32[]{:S(2)}, u32[]{:S(2)}) collective-permute-start(bf16[96,2048]{1,0:T(8,128)(2,1)} %get-tuple-element.151), channel_id=1, source_target_pairs={{0,3},{1,2},{2,1},{3,0},{4,7},{5,6},{6,5},{7,4},{8,11},{9,10},{10,... | collective-permute-start | bytes 1179656 | tf_op jit(solution)/shard_map/ppermute | solution.py:489
  64.7 16.9 %collective-permute-start.16 = (bf16[96,2048]{1,0:T(8,128)(2,1)}, bf16[96,2048]{1,0:T(8,128)(2,1)S(1)}, u32[]{:S(2)}, u32[]{:S(2)}) collective-permute-start(bf16[96,2048]{1,0:T(8,128)(2,1)} %get-tuple-element.167), channel_id=1, source_target_pairs={{0,1},{1,0},{2,3},{3,2},{4,5},{5,4},{6,7},{7,6},{8,9},{9,8},{10,11... | collective-permute-start | bytes 1179656 | tf_op jit(solution)/shard_map/ppermute | solution.py:489
  65.7 15.8 %collective-permute-start.17 = (bf16[96,2048]{1,0:T(8,128)(2,1)}, bf16[96,2048]{1,0:T(8,128)(2,1)S(1)}, u32[]{:S(2)}, u32[]{:S(2)}) collective-permute-start(bf16[96,2048]{1,0:T(8,128)(2,1)} %get-tuple-element.168), channel_id=1, source_target_pairs={{0,2},{1,3},{2,0},{3,1},{4,6},{5,7},{6,4},{7,5},{8,10},{9,11},{10,... | collective-permute-start | bytes 1179656 | tf_op jit(solution)/shard_map/ppermute | solution.py:489
  66.6 19.0 %collective-permute-start.18 = (bf16[96,2048]{1,0:T(8,128)(2,1)}, bf16[96,2048]{1,0:T(8,128)(2,1)S(1)}, u32[]{:S(2)}, u32[]{:S(2)}) collective-permute-start(bf16[96,2048]{1,0:T(8,128)(2,1)} %get-tuple-element.169), channel_id=1, source_target_pairs={{0,3},{1,2},{2,1},{3,0},{4,7},{5,6},{6,5},{7,4},{8,11},{9,10},{10,... | collective-permute-start | bytes 1179656 | tf_op jit(solution)/shard_map/ppermute | solution.py:489
  86.4 16.1 %collective-permute-start.19 = (bf16[96,2176]{1,0:T(8,128)(2,1)}, bf16[96,2176]{1,0:T(8,128)(2,1)S(1)}, u32[]{:S(2)}, u32[]{:S(2)}) collective-permute-start(bf16[96,2176]{1,0:T(8,128)(2,1)} %get-tuple-element.192), channel_id=1, source_target_pairs={{0,1},{1,0},{2,3},{3,2},{4,5},{5,4},{6,7},{7,6},{8,9},{9,8},{10,11... | collective-permute-start | bytes 1253384 | tf_op jit(solution)/shard_map/ppermute | solution.py:489
  87.4 24.4 %collective-permute-start.20 = (bf16[96,2176]{1,0:T(8,128)(2,1)}, bf16[96,2176]{1,0:T(8,128)(2,1)S(1)}, u32[]{:S(2)}, u32[]{:S(2)}) collective-permute-start(bf16[96,2176]{1,0:T(8,128)(2,1)} %get-tuple-element.193), channel_id=1, source_target_pairs={{0,2},{1,3},{2,0},{3,1},{4,6},{5,7},{6,4},{7,5},{8,10},{9,11},{10,... | collective-permute-start | bytes 1253384 | tf_op jit(solution)/shard_map/ppermute | solution.py:489
  88.7 23.1 %collective-permute-start.21 = (bf16[96,2176]{1,0:T(8,128)(2,1)}, bf16[96,2176]{1,0:T(8,128)(2,1)S(1)}, u32[]{:S(2)}, u32[]{:S(2)}) collective-permute-start(bf16[96,2176]{1,0:T(8,128)(2,1)} %get-tuple-element.194), channel_id=1, source_target_pairs={{0,3},{1,2},{2,1},{3,0},{4,7},{5,6},{6,5},{7,4},{8,11},{9,10},{10,... | collective-permute-start | bytes 1253384 | tf_op jit(solution)/shard_map/ppermute | solution.py:489
  100.1 16.7 %collective-permute-start.22 = (bf16[48,2176]{1,0:T(8,128)(2,1)}, bf16[48,2176]{1,0:T(8,128)(2,1)S(1)}, u32[]{:S(2)}, u32[]{:S(2)}) collective-permute-start(bf16[48,2176]{1,0:T(8,128)(2,1)} %get-tuple-element.196), channel_id=1, source_target_pairs={{0,1},{1,0},{2,3},{3,2},{4,5},{5,4},{6,7},{7,6},{8,9},{9,8},{10,11... | collective-permute-start | bytes 626696 | tf_op jit(solution)/shard_map/ppermute | solution.py:489
  101.1 15.7 %collective-permute-start.23 = (bf16[48,2176]{1,0:T(8,128)(2,1)}, bf16[48,2176]{1,0:T(8,128)(2,1)S(1)}, u32[]{:S(2)}, u32[]{:S(2)}) collective-permute-start(bf16[48,2176]{1,0:T(8,128)(2,1)} %get-tuple-element.197), channel_id=1, source_target_pairs={{0,2},{1,3},{2,0},{3,1},{4,6},{5,7},{6,4},{7,5},{8,10},{9,11},{10,... | collective-permute-start | bytes 626696 | tf_op jit(solution)/shard_map/ppermute | solution.py:489
  102.5 14.3 %collective-permute-start.24 = (bf16[48,2176]{1,0:T(8,128)(2,1)}, bf16[48,2176]{1,0:T(8,128)(2,1)S(1)}, u32[]{:S(2)}, u32[]{:S(2)}) collective-permute-start(bf16[48,2176]{1,0:T(8,128)(2,1)} %get-tuple-element.198), channel_id=1, source_target_pairs={{0,3},{1,2},{2,1},{3,0},{4,7},{5,6},{6,5},{7,4},{8,11},{9,10},{10,... | collective-permute-start | bytes 626696 | tf_op jit(solution)/shard_map/ppermute | solution.py:489
  117.6 18.4 %collective-permute-start.29 = (bf16[1,2048,384]{2,1,0:T(8,128)(2,1)}, bf16[1,2048,384]{2,1,0:T(8,128)(2,1)S(1)}, u32[]{:S(2)}, u32[]{:S(2)}) collective-permute-start(bf16[1,2048,384]{2,1,0:T(8,128)(2,1)} %get-tuple-element.212), channel_id=1, source_target_pairs={{0,16},{16,0},{1,17},{17,1},{2,18},{18,2},{3,19},{19,3},{4,20},{20... | collective-permute-start | bytes 4718600 | tf_op jit(solution)/shard_map/ppermute | solution.py:587
  117.6 18.4 %collective-permute-start.30 = (bf16[1,384,2048]{2,1,0:T(8,128)(2,1)}, bf16[1,384,2048]{2,1,0:T(8,128)(2,1)}, u32[]{:S(2)}, u32[]{:S(2)}) collective-permute-start(bf16[1,384,2048]{2,1,0:T(8,128)(2,1)} %get-tuple-element.213), channel_id=1, source_target_pairs={{0,16},{16,0},{1,17},{17,1},{2,18},{18,2},{3,19},{19,3},{4,20},{20... | collective-permute-start | bytes 4718600 | tf_op jit(solution)/shard_map/ppermute | solution.py:587
  118.1 17.9 %collective-permute-start.28 = (bf16[1,2048,384]{2,1,0:T(8,128)(2,1)S(1)}, bf16[1,2048,384]{2,1,0:T(8,128)(2,1)}, u32[]{:S(2)}, u32[]{:S(2)}) collective-permute-start(bf16[1,2048,384]{2,1,0:T(8,128)(2,1)S(1)} %copy-done.8), channel_id=1, source_target_pairs={{0,16},{16,0},{1,17},{17,1},{2,18},{18,2},{3,19},{19,3},{4,20},{20... | collective-permute-start | bytes 4718600 | tf_op jit(solution)/shard_map/ppermute | solution.py:587
  123.6 22.7 %collective-permute-start.25 = (bf16[64,2176]{1,0:T(8,128)(2,1)S(1)}, bf16[64,2176]{1,0:T(8,128)(2,1)}, u32[]{:S(2)}, u32[]{:S(2)}) collective-permute-start(bf16[64,2176]{1,0:T(8,128)(2,1)S(1)} %copy-done.11), channel_id=1, source_target_pairs={{0,4},{1,5},{2,6},{3,7},{4,0},{5,1},{6,2},{7,3},{8,12},{9,13},{10,... | collective-permute-start | bytes 835592 | tf_op jit(solution)/shard_map/ppermute | solution.py:586
  134.1 15.0 %collective-permute-start.27 = (bf16[64,2176]{1,0:T(8,128)(2,1)}, bf16[64,2176]{1,0:T(8,128)(2,1)S(1)}, u32[]{:S(2)}, u32[]{:S(2)}) collective-permute-start(bf16[64,2176]{1,0:T(8,128)(2,1)} %add.5), channel_id=1, source_target_pairs={{0,8},{1,9},{2,10},{3,11},{4,12},{5,13},{6,14},{7,15},{8,0},{9,1},... | collective-permute-start | bytes 835592 | tf_op jit(solution)/shard_map/ppermute | solution.py:595
  (33 other events, 220.2 us)

commit v8 on v7

--- a/solution.py
+++ b/solution.py
@@ -43,9 +43,6 @@
         total = -(-self.outer * self.cap // 16) * 16
         step = self.outer // PARTS
         marks = [k * step * self.cap // 16 * 16 for k in range(PARTS)] + [total]
-        if marks[1] >= 32:
-            marks[1] = marks[1] // 32 * 16
-            marks[2] = marks[1] + 32
         self.chunks = [(marks[k], marks[k + 1]) for k in range(PARTS)]
         self.rows = [b - a for a, b in self.chunks]
         self.steps = [(k + 1) * step - 1 for k in range(PARTS)]
@@ -495,7 +492,12 @@
             hop(r)
         done = max(done, plan.steps[c])
         sent = compact(c)
-        if c > 0:
+        i = outer - 1 + done
+        if c == 1:
+            got[0], sent, blocks[done], blocks[i] = lax.optimization_barrier(
+                (got[0], sent, blocks[done], blocks[i])
+            )
+        elif c > 1:
             got[-1], sent = lax.optimization_barrier((got[-1], sent))
         if c == PARTS - 2:
             gate_up, sent = lax.optimization_barrier((gate_up, sent))
@@ -504,15 +506,9 @@
             gate_up, sent = lax.optimization_barrier((gate_up, sent))
             down = lax.ppermute(lax.optimization_barrier((w_down, sent))[0], "dp", swap)
         got.append(cross(sent))
-        if c == 0:
-            i = outer - 1 + done
-            got[0], blocks[done], blocks[i] = lax.optimization_barrier(
-                (got[0], blocks[done], blocks[i])
-            )
     weights = [w_gate, w_up, w_down, gate_up, down]
     outs = expert(0, sum(got[:-1], []))
     late = got[-1]
-    outs, late = lax.optimization_barrier((outs, late))
     got[-1] = late
     backs = cross(outs[3:])
     more = expert(1, late)

time: 153 us -> 153 us (level)
  waiting for transfers between devices: 34.8 us -> 31.2 us
  starting transfers between devices: 35.7 us -> 38.5 us
    ppermute x18, waiting for transfers between devices: 13.3 us -> 5.39 us  [cross(): lax.ppermute(arrays[d], 'expert', plan.across(d))]
    ppermute x5, waiting for transfers between devices: 10.8 us -> 15.9 us  [hop(): blocks[i] = lax.ppermute(before, 'expert', plan.exchange(r, chain))]
    ppermute x5, starting transfers between devices: 10 us -> 11.9 us  [hop(): blocks[i] = lax.ppermute(before, 'expert', plan.exchange(r, chain))]
    unnamed x52 -> x50, local copies, waits for them, and re-layouts: 6.84 us -> 7.63 us
  transfers between devices with their start and end apart: 31 -> 31, of which waited for: 9 -> 8; matrix products, arithmetic and copies ran while one was open for 3% -> 3% of each run, Pallas kernels for 43% -> 43%
where the time goes in v8:
time: 153 us; the launch traced here: 152 us
  Pallas kernels  69.2 us (45%)
  starting transfers between devices  38.5 us (25%)
  waiting for transfers between devices  31.2 us (20%)
  local copies, waits for them, and re-layouts  8.83 us (6%)
  other arithmetic  3.34 us (2%)
    pallas_call x2, Pallas kernels, expert(): pl.pallas_call(functools.partial(expert_kernel, plan, g), out_shape=[shap...  23.4 us
    ppermute x18, starting transfers between devices, cross(): lax.ppermute(arrays[d], 'expert', plan.across(d))  21.2 us
    pallas_call x2, Pallas kernels, weight_grads(): pl.pallas_call(functools.partial(weight_kernel, plan, own), out_shape=[sh...  17.3 us
    ppermute x5, waiting for transfers between devices, hop(): blocks[i] = lax.ppermute(before, 'expert', plan.exchange(r, chain))  15.9 us
    pallas_call x4, Pallas kernels, compact(): pl.pallas_call(functools.partial(compact_kernel, plan, c), out_shape=[sha...  14.4 us
    ppermute x5, starting transfers between devices, hop(): blocks[i] = lax.ppermute(before, 'expert', plan.exchange(r, chain))  11.9 us
    ppermute x2, waiting for transfers between devices, on_device(): sent = lax.ppermute(sums[r], 'expert', plan.flip(bit))  9.77 us
    pallas_call x2, Pallas kernels, spread(): pl.pallas_call(functools.partial(spread_kernel, plan, homes, groups), out...  7.93 us
  transfers between devices with their start and end apart: 31, of which 8 were waited for; matrix products, arithmetic and copies ran while one was open for 3% of the time, Pallas kernels for 43%

profile of v8, /device:TPU:0, one launch (start us, length us, event | category | flops | bytes accessed | tf_op | source)
XLA Modules:
  0.0 152.1 jit_solution(2950801156784112282)
XLA Ops:
  0.6 2.2 %pack.1.refs_2_.refs_8_ = bf16[64,4224]{1,0:T(8,128)(2,1)} custom-call(bf16[64,2048]{1,0:T(8,128)(2,1)} %tok_ref.1, bf16[64,2048]{1,0:T(8,128)(2,1)} %up_ref.1, s32[8,64]{1,0:T(8,128)} %bitcast.5, bf16[8,64]{1,0:T(8,128)(2,1)} %bitcast.7), custom_call_target="tpu_custom_call" | custom-call | flops 1000000 | bytes 1081344 | tf_op jit(solution)/shard_map/pack/pallas_call | solution.py:418
  2.9 3.0 %collective-permute-start.3 = (bf16[64,4224]{1,0:T(8,128)(2,1)}, bf16[64,4224]{1,0:T(8,128)(2,1)S(1)}, u32[]{:S(2)}, u32[]{:S(2)}) collective-permute-start(bf16[64,4224]{1,0:T(8,128)(2,1)} %pack.1.refs_2_.refs_8_), channel_id=1, source_target_pairs={{0,4},{1,5},{2,6},{3,7},{4,0},{5,1},{6,2},{7,3},{8,12},{9,13},{10,... | collective-permute-start | bytes 1622024 | tf_op jit(solution)/shard_map/ppermute | solution.py:436
  8.8 3.2 %compact.4 = (bf16[64,2048]{1,0:T(8,128)(2,1)}, bf16[64,2048]{1,0:T(8,128)(2,1)}, bf16[64,2048]{1,0:T(8,128)(2,1)}, bf16[64,2048]{1,0:T(8,128)(2,1)}) custom-call(s32[15]{0:T(128)} %dynamic-slice_bitcast_fusion.refs_0_, s32[1,128]{1,0:T(1,128)} %constant.23.clone.refs_1_, bf16[64,4224]{1,0:T(8,128)(2,1)} %pack.1.refs_2_.refs_8_), custom_call_target="tpu_custom_call" | custom-call | flops 67108864 | bytes 540672 | tf_op jit(solution)/shard_map/compact/pallas_call | solution.py:445
  15.6 2.8 %collective-permute-done.3.refs_3_.refs_2_ = bf16[64,4224]{1,0:T(8,128)(2,1)S(1)} collective-permute-done((bf16[64,4224]{1,0:T(8,128)(2,1)}, bf16[64,4224]{1,0:T(8,128)(2,1)S(1)}, u32[]{:S(2)}, u32[]{:S(2)}) %collective-permute-start.3) | collective-permute-done | bytes 540704 | tf_op jit(solution)/shard_map/ppermute | solution.py:436
  19.2 3.4 %compact.5 = (bf16[64,2048]{1,0:T(8,128)(2,1)}, bf16[64,2048]{1,0:T(8,128)(2,1)}, bf16[64,2048]{1,0:T(8,128)(2,1)}, bf16[64,2048]{1,0:T(8,128)(2,1)}) custom-call(s32[15]{0:T(128)} %dynamic-slice_bitcast_fusion.refs_0_, s32[1,128]{1,0:T(1,128)} %constant.24.clone.refs_1_, bf16[64,4224]{1,0:T(8,128)(2,1)} %pack.1.refs_2_.refs_8_, bf16[64,4224]{1,0:T(8,128)(2,1)} %copy-done), custom_call_target="tpu_custom_call" | custom-call | flops 134217728 | bytes 1081344 | tf_op jit(solution)/shard_map/compact/pallas_call | solution.py:445
  22.7 4.2 %collective-permute-done.1.refs_3_.refs_2_ = bf16[64,2048]{1,0:T(8,128)(2,1)S(1)} collective-permute-done((bf16[64,2048]{1,0:T(8,128)(2,1)}, bf16[64,2048]{1,0:T(8,128)(2,1)S(1)}, u32[]{:S(2)}, u32[]{:S(2)}) %collective-permute-start.1) | collective-permute-done | bytes 262176 | tf_op jit(solution)/shard_map/ppermute | solution.py:486
  28.7 3.7 %collective-permute-start.6 = (bf16[64,4224]{1,0:T(8,128)(2,1)S(1)}, bf16[64,4224]{1,0:T(8,128)(2,1)S(1)}, u32[]{:S(2)}, u32[]{:S(2)}) collective-permute-start(bf16[64,4224]{1,0:T(8,128)(2,1)S(1)} %collective-permute-done.4.refs_3_.refs_4_.refs_6_), channel_id=1, source_target_pairs={{0,4},{1,5},{2,6},{3,7},{4,0},{5,1},{6,2},{7,3},{8,12},{9,13},{10,... | collective-permute-start | bytes 1622024 | tf_op jit(solution)/shard_map/ppermute | solution.py:436
  35.8 3.3 %pad_maximum_fusion = bf16[1,2048,768]{2,1,0:T(8,128)(2,1)} fusion(bf16[1,2048,384]{2,1,0:T(8,128)(2,1)} %refs_6_.1, bf16[1,2048,384]{2,1,0:T(8,128)(2,1)S(1)} %copy-done.9), kind=kLoop, calls=%fused_computation | loop fusion | flops 6291456 | bytes 6291456 | tf_op jit(solution)/shard_map/concatenate | solution.py:428
  39.2 3.7 %collective-permute-done.6.refs_4_.refs_5_.refs_7_ = bf16[64,4224]{1,0:T(8,128)(2,1)S(1)} collective-permute-done((bf16[64,4224]{1,0:T(8,128)(2,1)S(1)}, bf16[64,4224]{1,0:T(8,128)(2,1)S(1)}, u32[]{:S(2)}, u32[]{:S(2)}) %collective-permute-start.6) | collective-permute-done | bytes 540704 | tf_op jit(solution)/shard_map/ppermute | solution.py:436
  43.7 3.6 %compact.6 = (bf16[64,2048]{1,0:T(8,128)(2,1)}, bf16[64,2048]{1,0:T(8,128)(2,1)}, bf16[64,2048]{1,0:T(8,128)(2,1)}, bf16[64,2048]{1,0:T(8,128)(2,1)}) custom-call(s32[15]{0:T(128)} %dynamic-slice_bitcast_fusion.refs_0_, s32[1,128]{1,0:T(1,128)} %constant.25.clone.refs_1_, bf16[64,4224]{1,0:T(8,128)(2,1)} %copy-done, bf16[64,4224]{1,0:T(8,128)(2,1)} %copy-done.1, ...), custom_call_target="tpu_custom_call" | custom-call | flops 201326592 | bytes 1622016 | tf_op jit(solution)/shard_map/compact/pallas_call | solution.py:445
  52.7 9.4 %collective-permute-done.7.refs_3_.refs_5_ = bf16[64,4224]{1,0:T(8,128)(2,1)S(1)} collective-permute-done((bf16[64,4224]{1,0:T(8,128)(2,1)S(1)}, bf16[64,4224]{1,0:T(8,128)(2,1)S(1)}, u32[]{:S(2)}, u32[]{:S(2)}) %collective-permute-start.7) | collective-permute-done | bytes 540704 | tf_op jit(solution)/shard_map/ppermute | solution.py:436
  62.9 4.1 %compact.7 = (bf16[96,2048]{1,0:T(8,128)(2,1)}, bf16[96,2048]{1,0:T(8,128)(2,1)}, bf16[96,2048]{1,0:T(8,128)(2,1)}, bf16[96,2048]{1,0:T(8,128)(2,1)}) custom-call(s32[15]{0:T(128)} %dynamic-slice_bitcast_fusion.refs_0_, s32[1,192]{1,0:T(1,128)} %constant.26.clone.refs_1_, bf16[64,4224]{1,0:T(8,128)(2,1)} %copy-done.3, bf16[64,4224]{1,0:T(8,128)(2,1)} %copy-done.4, ...), custom_call_target="tpu_custom_call" | custom-call | flops 402653184 | bytes 2162688 | tf_op jit(solution)/shard_map/compact/pallas_call | solution.py:445
  70.9 13.1 %expert.2 = (bf16[384,768]{1,0:T(8,128)(2,1)}, bf16[384,768]{1,0:T(8,128)(2,1)}, bf16[384,768]{1,0:T(8,128)(2,1)}, bf16[96,2176]{1,0:T(8,128)(2,1)}, bf16[96,217...) custom-call(s32[15]{0:T(128)} %dynamic-slice_bitcast_fusion.refs_0_, ...), custom_call_target="tpu_custom_call" | custom-call | flops 6039797760 | bytes 9437184 | tf_op jit(solution)/shard_map/expert/pallas_call | solution.py:464
  90.3 10.2 %expert.3 = (bf16[192,768]{1,0:T(8,128)(2,1)}, bf16[192,768]{1,0:T(8,128)(2,1)}, bf16[192,768]{1,0:T(8,128)(2,1)}, bf16[48,2176]{1,0:T(8,128)(2,1)}, bf16[48,217...) custom-call(s32[15]{0:T(128)} %dynamic-slice_bitcast_fusion.refs_0_, ...), custom_call_target="tpu_custom_call" | custom-call | flops 3019898880 | bytes 9437184 | tf_op jit(solution)/shard_map/expert/pallas_call | solution.py:464
  101.6 2.5 %collective-permute-start.24 = (bf16[48,2176]{1,0:T(8,128)(2,1)}, bf16[48,2176]{1,0:T(8,128)(2,1)S(1)}, u32[]{:S(2)}, u32[]{:S(2)}) collective-permute-start(bf16[48,2176]{1,0:T(8,128)(2,1)} %get-tuple-element.168), channel_id=1, source_target_pairs={{0,3},{1,2},{2,1},{3,0},{4,7},{5,6},{6,5},{7,4},{8,11},{9,10},{10,... | collective-permute-start | bytes 626696 | tf_op jit(solution)/shard_map/ppermute | solution.py:486
  104.1 8.1 %weight_grads.2 = (bf16[1,2048,384]{2,1,0:T(8,128)(2,1)}, bf16[1,2048,384]{2,1,0:T(8,128)(2,1)}, bf16[1,384,2048]{2,1,0:T(8,128)(2,1)}) custom-call(bf16[64,2048]{1,0:T(8,128)(2,1)} %get-tuple-element.109.refs_1_.refs_0_, bf16[64,2048]{1,0:T(8,128)(2,1)} %copy-done.16, bf16[64,2048]{1,0:T(8,128)(2,1)} %copy-done.17, bf16[64,2048]{1,0:T(8,128)(2,1)} %copy-done.18, ...), custom_call_target="tpu_custom_call" | custom-call | flops 2717908992 | bytes 6488064 | tf_op jit(solution)/shard_map/weight_grads/pallas_call | solution.py:527
  113.1 3.5 %spread.2.refs_18_ = bf16[64,2176]{1,0:T(8,128)(2,1)} custom-call(s32[15]{0:T(128)} %dynamic-slice_bitcast_fusion.refs_0_, s32[1,384]{1,0:T(1,128)} %constant.27.clone.refs_1_, bf16[64,4224]{1,0:T(8,128)(2,1)} %pack.1.refs_2_.refs_8_, bf16[64,4224]{1,0:T(8,128)(2,1)} %copy-done, bf16[64,4224]{1,0:T(8,128)(2,1)} %copy-done.3, bf16[64,4224]{1,0:T(8,128)(2,1)} %copy-done.4, ...), custom_call_target="tpu_custom_call" | custom-call | flops 100663296 | bytes 1572864 | tf_op jit(solution)/shard_map/spread/pallas_call | solution.py:554
  118.1 4.4 %spread.3 = (bf16[64,2176]{1,0:T(8,128)(2,1)}, bf16[64,2176]{1,0:T(8,128)(2,1)}, bf16[64,2176]{1,0:T(8,128)(2,1)}) custom-call(s32[15]{0:T(128)} %dynamic-slice_bitcast_fusion.refs_0_, s32[1,576]{1,0:T(1,128)} %constant.28.clone.refs_1_, bf16[64,4224]{1,0:T(8,128)(2,1)} %pack.1.refs_2_.refs_8_, bf16[64,4224]{1,0:T(8,128)(2,1)} %copy-done, ...), custom_call_target="tpu_custom_call" | custom-call | flops 452984832 | bytes 2359296 | tf_op jit(solution)/shard_map/spread/pallas_call | solution.py:554
  124.6 7.7 %collective-permute-done.26.b_ref = bf16[64,2176]{1,0:T(8,128)(2,1)} collective-permute-done((bf16[64,2176]{1,0:T(8,128)(2,1)}, bf16[64,2176]{1,0:T(8,128)(2,1)}, u32[]{:S(2)}, u32[]{:S(2)}) %collective-permute-start.26) | collective-permute-done | bytes 278560 | tf_op jit(solution)/shard_map/ppermute | solution.py:591
  132.3 1.8 %add.5 = bf16[64,2176]{1,0:T(8,128)(2,1)} custom-call(bf16[64,2176]{1,0:T(8,128)(2,1)} %get-tuple-element.180.a_ref, bf16[64,2176]{1,0:T(8,128)(2,1)} %collective-permute-done.26.b_ref), custom_call_target="tpu_custom_call" | custom-call | tf_op jit(solution)/shard_map/add/pallas_call | solution.py:595
  134.1 2.6 %collective-permute-start.27 = (bf16[64,2176]{1,0:T(8,128)(2,1)}, bf16[64,2176]{1,0:T(8,128)(2,1)S(1)}, u32[]{:S(2)}, u32[]{:S(2)}) collective-permute-start(bf16[64,2176]{1,0:T(8,128)(2,1)} %add.5), channel_id=1, source_target_pairs={{0,8},{1,9},{2,10},{3,11},{4,12},{5,13},{6,14},{7,15},{8,0},{9,1},... | collective-permute-start | bytes 835592 | tf_op jit(solution)/shard_map/ppermute | solution.py:591
  137.9 9.2 %weight_grads.3 = (bf16[1,2048,384]{2,1,0:T(8,128)(2,1)}, bf16[1,2048,384]{2,1,0:T(8,128)(2,1)}, bf16[1,384,2048]{2,1,0:T(8,128)(2,1)}) custom-call(bf16[64,2048]{1,0:T(8,128)(2,1)} %get-tuple-element.109.refs_1_.refs_0_, bf16[64,2048]{1,0:T(8,128)(2,1)} %copy-done.16, bf16[64,2048]{1,0:T(8,128)(2,1)} %copy-done.17, bf16[64,2048]{1,0:T(8,128)(2,1)} %copy-done.18, ...), custom_call_target="tpu_custom_call" | custom-call | flops 2717908992 | bytes 6488064 | tf_op jit(solution)/shard_map/weight_grads/pallas_call | solution.py:527
  147.1 2.0 %collective-permute-done.27.refs_2_ = bf16[64,2176]{1,0:T(8,128)(2,1)S(1)} collective-permute-done((bf16[64,2176]{1,0:T(8,128)(2,1)}, bf16[64,2176]{1,0:T(8,128)(2,1)S(1)}, u32[]{:S(2)}, u32[]{:S(2)}) %collective-permute-start.27) | collective-permute-done | bytes 278560 | tf_op jit(solution)/shard_map/ppermute | solution.py:591
  149.9 2.2 %home.1 = (bf16[64,2048]{1,0:T(8,128)(2,1)}, bf16[8,64]{1,0:T(8,128)(2,1)}) custom-call(bf16[64,2176]{1,0:T(8,128)(2,1)} %get-tuple-element.179.refs_0_, bf16[64,2176]{1,0:T(8,128)(2,1)} %collective-permute-done.25.refs_1_, bf16[64,2176]{1,0:T(8,128)(2,1)} %copy-done.15, s32[8,64]{1,0:T(8,128)} %bitcast.6, bf16[8,64]{1,0:T(8,128)(2,1)} %bitcast.8, ...), custom_call_target="tpu_custom_call" | custom-call | flops 1000000 | bytes 1310720 | tf_op jit(solution)/shard_map/home/pallas_call | solution.py:605
  (103 shorter events, 36.8 us)
Async XLA Ops:
  2.9 15.5 %collective-permute-start.3 = (bf16[64,4224]{1,0:T(8,128)(2,1)}, bf16[64,4224]{1,0:T(8,128)(2,1)S(1)}, u32[]{:S(2)}, u32[]{:S(2)}) collective-permute-start(bf16[64,4224]{1,0:T(8,128)(2,1)} %pack.1.refs_2_.refs_8_), channel_id=1, source_target_pairs={{0,4},{1,5},{2,6},{3,7},{4,0},{5,1},{6,2},{7,3},{8,12},{9,13},{10,... | collective-permute-start | bytes 1622024 | tf_op jit(solution)/shard_map/ppermute | solution.py:436
  5.9 21.0 %collective-permute-start.4 = (bf16[64,4224]{1,0:T(8,128)(2,1)}, bf16[64,4224]{1,0:T(8,128)(2,1)S(1)}, u32[]{:S(2)}, u32[]{:S(2)}) collective-permute-start(bf16[64,4224]{1,0:T(8,128)(2,1)} %pack.1.refs_2_.refs_8_), channel_id=1, source_target_pairs={{0,0},{1,1},{2,2},{3,3},{4,8},{5,9},{6,10},{7,11},{8,4},{9,5},{10,... | collective-permute-start | bytes 1622024 | tf_op jit(solution)/shard_map/ppermute | solution.py:436
  28.7 14.2 %collective-permute-start.6 = (bf16[64,4224]{1,0:T(8,128)(2,1)S(1)}, bf16[64,4224]{1,0:T(8,128)(2,1)S(1)}, u32[]{:S(2)}, u32[]{:S(2)}) collective-permute-start(bf16[64,4224]{1,0:T(8,128)(2,1)S(1)} %collective-permute-done.4.refs_3_.refs_4_.refs_6_), channel_id=1, source_target_pairs={{0,4},{1,5},{2,6},{3,7},{4,0},{5,1},{6,2},{7,3},{8,12},{9,13},{10,... | collective-permute-start | bytes 1622024 | tf_op jit(solution)/shard_map/ppermute | solution.py:436
  32.3 15.0 %collective-permute-start.8 = (bf16[64,2048]{1,0:T(8,128)(2,1)}, bf16[64,2048]{1,0:T(8,128)(2,1)}, u32[]{:S(2)}, u32[]{:S(2)}) collective-permute-start(bf16[64,2048]{1,0:T(8,128)(2,1)} %get-tuple-element.114), channel_id=1, source_target_pairs={{0,1},{1,0},{2,3},{3,2},{4,5},{5,4},{6,7},{7,6},{8,9},{9,8},{10,11... | collective-permute-start | bytes 786440 | tf_op jit(solution)/shard_map/ppermute | solution.py:486
  33.5 13.8 %collective-permute-start.9 = (bf16[64,2048]{1,0:T(8,128)(2,1)}, bf16[64,2048]{1,0:T(8,128)(2,1)}, u32[]{:S(2)}, u32[]{:S(2)}) collective-permute-start(bf16[64,2048]{1,0:T(8,128)(2,1)} %get-tuple-element.115), channel_id=1, source_target_pairs={{0,2},{1,3},{2,0},{3,1},{4,6},{5,7},{6,4},{7,5},{8,10},{9,11},{10,... | collective-permute-start | bytes 786440 | tf_op jit(solution)/shard_map/ppermute | solution.py:486
  47.3 19.8 %collective-permute-start.14 = (bf16[1,2048,768]{2,1,0:T(8,128)(2,1)}, bf16[1,2048,768]{2,1,0:T(8,128)(2,1)}, u32[]{:S(2)}, u32[]{:S(2)}) collective-permute-start(bf16[1,2048,768]{2,1,0:T(8,128)(2,1)} %pad_maximum_fusion), channel_id=1, source_target_pairs={{0,16},{16,0},{1,17},{17,1},{2,18},{18,2},{3,19},{19,3},{4,20},{20... | collective-permute-start | bytes 9437192 | tf_op jit(solution)/shard_map/ppermute | solution.py:504
  47.4 14.7 %collective-permute-start.7 = (bf16[64,4224]{1,0:T(8,128)(2,1)S(1)}, bf16[64,4224]{1,0:T(8,128)(2,1)S(1)}, u32[]{:S(2)}, u32[]{:S(2)}) collective-permute-start(bf16[64,4224]{1,0:T(8,128)(2,1)S(1)} %collective-permute-done.5.refs_2_.refs_4_), channel_id=1, source_target_pairs={{0,4},{1,5},{2,6},{3,7},{4,0},{5,1},{6,2},{7,3},{8,12},{9,13},{10,... | collective-permute-start | bytes 1622024 | tf_op jit(solution)/shard_map/ppermute | solution.py:436
  49.2 17.8 %collective-permute-start.11 = (bf16[64,2048]{1,0:T(8,128)(2,1)}, bf16[64,2048]{1,0:T(8,128)(2,1)S(1)}, u32[]{:S(2)}, u32[]{:S(2)}) collective-permute-start(bf16[64,2048]{1,0:T(8,128)(2,1)} %get-tuple-element.130), channel_id=1, source_target_pairs={{0,1},{1,0},{2,3},{3,2},{4,5},{5,4},{6,7},{7,6},{8,9},{9,8},{10,11... | collective-permute-start | bytes 786440 | tf_op jit(solution)/shard_map/ppermute | solution.py:486
  50.7 16.4 %collective-permute-start.12 = (bf16[64,2048]{1,0:T(8,128)(2,1)}, bf16[64,2048]{1,0:T(8,128)(2,1)S(1)}, u32[]{:S(2)}, u32[]{:S(2)}) collective-permute-start(bf16[64,2048]{1,0:T(8,128)(2,1)} %get-tuple-element.131), channel_id=1, source_target_pairs={{0,2},{1,3},{2,0},{3,1},{4,6},{5,7},{6,4},{7,5},{8,10},{9,11},{10,... | collective-permute-start | bytes 786440 | tf_op jit(solution)/shard_map/ppermute | solution.py:486
  51.2 15.9 %collective-permute-start.13 = (bf16[64,2048]{1,0:T(8,128)(2,1)}, bf16[64,2048]{1,0:T(8,128)(2,1)S(1)}, u32[]{:S(2)}, u32[]{:S(2)}) collective-permute-start(bf16[64,2048]{1,0:T(8,128)(2,1)} %get-tuple-element.132), channel_id=1, source_target_pairs={{0,3},{1,2},{2,1},{3,0},{4,7},{5,6},{6,5},{7,4},{8,11},{9,10},{10,... | collective-permute-start | bytes 786440 | tf_op jit(solution)/shard_map/ppermute | solution.py:486
  67.2 18.9 %collective-permute-start.15 = (bf16[96,2048]{1,0:T(8,128)(2,1)}, bf16[96,2048]{1,0:T(8,128)(2,1)S(1)}, u32[]{:S(2)}, u32[]{:S(2)}) collective-permute-start(bf16[96,2048]{1,0:T(8,128)(2,1)} %get-tuple-element.147), channel_id=1, source_target_pairs={{0,1},{1,0},{2,3},{3,2},{4,5},{5,4},{6,7},{7,6},{8,9},{9,8},{10,11... | collective-permute-start | bytes 1179656 | tf_op jit(solution)/shard_map/ppermute | solution.py:486
  68.7 20.1 %collective-permute-start.16 = (bf16[96,2048]{1,0:T(8,128)(2,1)}, bf16[96,2048]{1,0:T(8,128)(2,1)S(1)}, u32[]{:S(2)}, u32[]{:S(2)}) collective-permute-start(bf16[96,2048]{1,0:T(8,128)(2,1)} %get-tuple-element.148), channel_id=1, source_target_pairs={{0,2},{1,3},{2,0},{3,1},{4,6},{5,7},{6,4},{7,5},{8,10},{9,11},{10,... | collective-permute-start | bytes 1179656 | tf_op jit(solution)/shard_map/ppermute | solution.py:486
  69.3 19.5 %collective-permute-start.17 = (bf16[96,2048]{1,0:T(8,128)(2,1)}, bf16[96,2048]{1,0:T(8,128)(2,1)S(1)}, u32[]{:S(2)}, u32[]{:S(2)}) collective-permute-start(bf16[96,2048]{1,0:T(8,128)(2,1)} %get-tuple-element.149), channel_id=1, source_target_pairs={{0,3},{1,2},{2,1},{3,0},{4,7},{5,6},{6,5},{7,4},{8,11},{9,10},{10,... | collective-permute-start | bytes 1179656 | tf_op jit(solution)/shard_map/ppermute | solution.py:486
  84.1 17.5 %collective-permute-start.19 = (bf16[96,2176]{1,0:T(8,128)(2,1)}, bf16[96,2176]{1,0:T(8,128)(2,1)S(1)}, u32[]{:S(2)}, u32[]{:S(2)}) collective-permute-start(bf16[96,2176]{1,0:T(8,128)(2,1)} %get-tuple-element.162), channel_id=1, source_target_pairs={{0,1},{1,0},{2,3},{3,2},{4,5},{5,4},{6,7},{7,6},{8,9},{9,8},{10,11... | collective-permute-start | bytes 1253384 | tf_op jit(solution)/shard_map/ppermute | solution.py:486
  85.6 26.6 %collective-permute-start.20 = (bf16[96,2176]{1,0:T(8,128)(2,1)}, bf16[96,2176]{1,0:T(8,128)(2,1)S(1)}, u32[]{:S(2)}, u32[]{:S(2)}) collective-permute-start(bf16[96,2176]{1,0:T(8,128)(2,1)} %get-tuple-element.163), channel_id=1, source_target_pairs={{0,2},{1,3},{2,0},{3,1},{4,6},{5,7},{6,4},{7,5},{8,10},{9,11},{10,... | collective-permute-start | bytes 1253384 | tf_op jit(solution)/shard_map/ppermute | solution.py:486
  86.1 26.1 %collective-permute-start.21 = (bf16[96,2176]{1,0:T(8,128)(2,1)}, bf16[96,2176]{1,0:T(8,128)(2,1)S(1)}, u32[]{:S(2)}, u32[]{:S(2)}) collective-permute-start(bf16[96,2176]{1,0:T(8,128)(2,1)} %get-tuple-element.164), channel_id=1, source_target_pairs={{0,3},{1,2},{2,1},{3,0},{4,7},{5,6},{6,5},{7,4},{8,11},{9,10},{10,... | collective-permute-start | bytes 1253384 | tf_op jit(solution)/shard_map/ppermute | solution.py:486
  100.5 16.2 %collective-permute-start.22 = (bf16[48,2176]{1,0:T(8,128)(2,1)}, bf16[48,2176]{1,0:T(8,128)(2,1)S(1)}, u32[]{:S(2)}, u32[]{:S(2)}) collective-permute-start(bf16[48,2176]{1,0:T(8,128)(2,1)} %get-tuple-element.166), channel_id=1, source_target_pairs={{0,1},{1,0},{2,3},{3,2},{4,5},{5,4},{6,7},{7,6},{8,9},{9,8},{10,11... | collective-permute-start | bytes 626696 | tf_op jit(solution)/shard_map/ppermute | solution.py:486
  101.0 15.7 %collective-permute-start.23 = (bf16[48,2176]{1,0:T(8,128)(2,1)}, bf16[48,2176]{1,0:T(8,128)(2,1)S(1)}, u32[]{:S(2)}, u32[]{:S(2)}) collective-permute-start(bf16[48,2176]{1,0:T(8,128)(2,1)} %get-tuple-element.167), channel_id=1, source_target_pairs={{0,2},{1,3},{2,0},{3,1},{4,6},{5,7},{6,4},{7,5},{8,10},{9,11},{10,... | collective-permute-start | bytes 626696 | tf_op jit(solution)/shard_map/ppermute | solution.py:486
  101.6 15.1 %collective-permute-start.24 = (bf16[48,2176]{1,0:T(8,128)(2,1)}, bf16[48,2176]{1,0:T(8,128)(2,1)S(1)}, u32[]{:S(2)}, u32[]{:S(2)}) collective-permute-start(bf16[48,2176]{1,0:T(8,128)(2,1)} %get-tuple-element.168), channel_id=1, source_target_pairs={{0,3},{1,2},{2,1},{3,0},{4,7},{5,6},{6,5},{7,4},{8,11},{9,10},{10,... | collective-permute-start | bytes 626696 | tf_op jit(solution)/shard_map/ppermute | solution.py:486
  117.6 19.2 %collective-permute-start.29 = (bf16[1,2048,384]{2,1,0:T(8,128)(2,1)}, bf16[1,2048,384]{2,1,0:T(8,128)(2,1)S(1)}, u32[]{:S(2)}, u32[]{:S(2)}) collective-permute-start(bf16[1,2048,384]{2,1,0:T(8,128)(2,1)} %get-tuple-element.182), channel_id=1, source_target_pairs={{0,16},{16,0},{1,17},{17,1},{2,18},{18,2},{3,19},{19,3},{4,20},{20... | collective-permute-start | bytes 4718600 | tf_op jit(solution)/shard_map/ppermute | solution.py:583
  117.6 19.2 %collective-permute-start.30 = (bf16[1,384,2048]{2,1,0:T(8,128)(2,1)}, bf16[1,384,2048]{2,1,0:T(8,128)(2,1)}, u32[]{:S(2)}, u32[]{:S(2)}) collective-permute-start(bf16[1,384,2048]{2,1,0:T(8,128)(2,1)} %get-tuple-element.183), channel_id=1, source_target_pairs={{0,16},{16,0},{1,17},{17,1},{2,18},{18,2},{3,19},{19,3},{4,20},{20... | collective-permute-start | bytes 4718600 | tf_op jit(solution)/shard_map/ppermute | solution.py:583
  118.1 18.7 %collective-permute-start.28 = (bf16[1,2048,384]{2,1,0:T(8,128)(2,1)S(1)}, bf16[1,2048,384]{2,1,0:T(8,128)(2,1)}, u32[]{:S(2)}, u32[]{:S(2)}) collective-permute-start(bf16[1,2048,384]{2,1,0:T(8,128)(2,1)S(1)} %copy-done.8), channel_id=1, source_target_pairs={{0,16},{16,0},{1,17},{17,1},{2,18},{18,2},{3,19},{19,3},{4,20},{20... | collective-permute-start | bytes 4718600 | tf_op jit(solution)/shard_map/ppermute | solution.py:583
  124.3 22.8 %collective-permute-start.25 = (bf16[64,2176]{1,0:T(8,128)(2,1)S(1)}, bf16[64,2176]{1,0:T(8,128)(2,1)}, u32[]{:S(2)}, u32[]{:S(2)}) collective-permute-start(bf16[64,2176]{1,0:T(8,128)(2,1)S(1)} %copy-done.11), channel_id=1, source_target_pairs={{0,4},{1,5},{2,6},{3,7},{4,0},{5,1},{6,2},{7,3},{8,12},{9,13},{10,... | collective-permute-start | bytes 835592 | tf_op jit(solution)/shard_map/ppermute | solution.py:582
  134.1 15.0 %collective-permute-start.27 = (bf16[64,2176]{1,0:T(8,128)(2,1)}, bf16[64,2176]{1,0:T(8,128)(2,1)S(1)}, u32[]{:S(2)}, u32[]{:S(2)}) collective-permute-start(bf16[64,2176]{1,0:T(8,128)(2,1)} %add.5), channel_id=1, source_target_pairs={{0,8},{1,9},{2,10},{3,11},{4,12},{5,13},{6,14},{7,15},{8,0},{9,1},... | collective-permute-start | bytes 835592 | tf_op jit(solution)/shard_map/ppermute | solution.py:591
  (32 other events, 232.1 us)

commit v9 on v7

--- a/solution.py
+++ b/solution.py
@@ -288,13 +288,13 @@
         backs[d][:, width:] = comb[d * rows : (d + 1) * rows]
 
 
-def weight_kernel(plan, own, *refs):
+def weight_kernel(plan, own, extra, *refs):
     inner, width, hidden = plan.inner, plan.width, plan.hidden
     part, n = hidden // 2, plan.inner * PARTS
     got, mids = refs[:n], refs[n : n + 6]
     at = n + 6
     theirs = refs[at : at + 3] if own else None
-    at += 3 if own else 0
+    at += extra
     outs = refs[at : at + 3]
     x_s, d_s, h_s, gu_s, g_s, u_s, w_s, sems, mid_sems, out_sems = refs[at + 3 : at + 13]
     kept = refs[at + 13 :]
@@ -511,13 +511,13 @@
             )
     weights = [w_gate, w_up, w_down, gate_up, down]
     outs = expert(0, sum(got[:-1], []))
-    late = got[-1]
-    outs, late = lax.optimization_barrier((outs, late))
+    outs = list(outs)
+    outs[0], late = lax.optimization_barrier((outs[0], got[-1]))
     got[-1] = late
     backs = cross(outs[3:])
     more = expert(1, late)
     got = sum(got, [])
-    mids = outs[:3] + more[:3]
+    mids = outs[:3] + list(more[:3])
 
     count = inner * sum(plan.rows)
 
@@ -529,7 +529,7 @@
 
     def weight_grads(own, extra):
         return pl.pallas_call(
-            functools.partial(weight_kernel, plan, own),
+            functools.partial(weight_kernel, plan, own, len(extra)),
             out_shape=[
                 shape((1, width, part), BF),
                 shape((1, width, part), BF),
@@ -578,31 +578,27 @@
             *extra,
         )
 
-    mine = weight_grads(False, [])
+    mine = weight_grads(False, backs[1:inner])
     backs = backs + cross(more[3:])
-    (first,) = spread([1], 1, [])
-    sums = {}
-    mine, backs, first = lax.optimization_barrier((mine, backs, first))
-    came = [lax.ppermute(first, "expert", plan.flip(1))]
+    mine, backs = lax.optimization_barrier((mine, backs))
     theirs = [lax.ppermute(w, "dp", swap) for w in mine]
-    rest = [r for r in range(outer) if r != 1]
-    sums.update(zip(rest, spread(rest, 2, [mine[0], first])))
-    bit = 1
+    sums = dict(enumerate(spread(list(range(outer)), 2, [mine[0]])))
+    came, bit = [], 1
     while bit < outer:
-        for r in range(bit, outer, 2 * bit):
-            if r == 1:
-                continue
+        for r in range(outer - bit, 0, -2 * bit):
             sent = lax.ppermute(sums[r], "expert", plan.flip(bit))
             if r == bit:
                 came.append(sent)
-            else:
-                sums[r - bit] = pl.pallas_call(
-                    add_kernel,
-                    out_shape=shape((tok, width + LANES), BF),
-                    in_specs=[VMEM] * 2,
-                    out_specs=VMEM,
-                    name="add",
-                )(sums[r - bit], sent)
+                continue
+            if bit == 1:
+                sums[1], sent = lax.optimization_barrier((sums[1], sent))
+            sums[r - bit] = pl.pallas_call(
+                add_kernel,
+                out_shape=shape((tok, width + LANES), BF),
+                in_specs=[VMEM] * 2,
+                out_specs=VMEM,
+                name="add",
+            )(sums[r - bit], sent)
         bit *= 2
     grads = weight_grads(True, theirs)
     home = [sums[0]] + came

time: 153 us -> 150 us (0.980)
  Pallas kernels: 69.1 us -> 66 us
    pallas_call x2 -> x1, Pallas kernels: 7.78 us -> 4.73 us  [spread(): pl.pallas_call(functools.partial(spread_kernel, plan, homes, groups), out...]
    ppermute x2 -> x3, starting transfers between devices: 2.96 us -> 3.88 us  [on_device(): sent = lax.ppermute(sums[r], 'expert', plan.flip(bit))]
    ppermute x2 -> x3, waiting for transfers between devices: 10.5 us -> 9.95 us  [on_device(): sent = lax.ppermute(sums[r], 'expert', plan.flip(bit))]
    unnamed x52 -> x54, local copies, waits for them, and re-layouts: 6.84 us -> 7.25 us
  transfers between devices with their start and end apart: 31 -> 31, of which waited for: 9 -> 10; matrix products, arithmetic and copies ran while one was open for 3% -> 3% of each run, Pallas kernels for 43% -> 41%
where the time goes in v9:
time: 150 us; the launch traced here: 149 us
  Pallas kernels  66 us (44%)
  starting transfers between devices  35.9 us (24%)
  waiting for transfers between devices  34.7 us (23%)
  local copies, waits for them, and re-layouts  8.45 us (6%)
  other arithmetic  3.33 us (2%)
    pallas_call x2, Pallas kernels, expert(): pl.pallas_call(functools.partial(expert_kernel, plan, g), out_shape=[shap...  23.3 us
    ppermute x18, starting transfers between devices, cross(): lax.ppermute(arrays[d], 'expert', plan.across(d))  21.3 us
    pallas_call x2, Pallas kernels, weight_grads(): pl.pallas_call(functools.partial(weight_kernel, plan, own, len(extra)), o...  17.3 us
    pallas_call x4, Pallas kernels, compact(): pl.pallas_call(functools.partial(compact_kernel, plan, c), out_shape=[sha...  14.4 us
    ppermute x18, waiting for transfers between devices, cross(): lax.ppermute(arrays[d], 'expert', plan.across(d))  13.7 us
    ppermute x5, waiting for transfers between devices, hop(): blocks[i] = lax.ppermute(before, 'expert', plan.exchange(r, chain))  10.8 us
    ppermute x5, starting transfers between devices, hop(): blocks[i] = lax.ppermute(before, 'expert', plan.exchange(r, chain))  10.1 us
    ppermute x3, waiting for transfers between devices, on_device(): sent = lax.ppermute(sums[r], 'expert', plan.flip(bit))  9.95 us
  transfers between devices with their start and end apart: 31, of which 10 were waited for; matrix products, arithmetic and copies ran while one was open for 3% of the time, Pallas kernels for 41%

profile of v9, /device:TPU:0, one launch (start us, length us, event | category | flops | bytes accessed | tf_op | source)
XLA Modules:
  0.0 149.3 jit_solution(7598333033193863314)
XLA Ops:
  0.6 2.2 %pack.1.refs_2_.refs_8_ = bf16[64,4224]{1,0:T(8,128)(2,1)} custom-call(bf16[64,2048]{1,0:T(8,128)(2,1)} %tok_ref.1, bf16[64,2048]{1,0:T(8,128)(2,1)} %up_ref.1, s32[8,64]{1,0:T(8,128)} %bitcast.5, bf16[8,64]{1,0:T(8,128)(2,1)} %bitcast.7), custom_call_target="tpu_custom_call" | custom-call | flops 1000000 | bytes 1081344 | tf_op jit(solution)/shard_map/pack/pallas_call | solution.py:421
  2.9 1.7 %collective-permute-start.4 = (bf16[64,4224]{1,0:T(8,128)(2,1)}, bf16[64,4224]{1,0:T(8,128)(2,1)S(1)}, u32[]{:S(2)}, u32[]{:S(2)}) collective-permute-start(bf16[64,4224]{1,0:T(8,128)(2,1)} %pack.1.refs_2_.refs_8_), channel_id=1, source_target_pairs={{0,0},{1,1},{2,2},{3,3},{4,8},{5,9},{6,10},{7,11},{8,4},{9,5},{10,... | collective-permute-start | bytes 1622024 | tf_op jit(solution)/shard_map/ppermute | solution.py:439
  4.6 4.9 %collective-permute-start.3 = (bf16[64,4224]{1,0:T(8,128)(2,1)}, bf16[64,4224]{1,0:T(8,128)(2,1)S(1)}, u32[]{:S(2)}, u32[]{:S(2)}) collective-permute-start(bf16[64,4224]{1,0:T(8,128)(2,1)} %pack.1.refs_2_.refs_8_), channel_id=1, source_target_pairs={{0,4},{1,5},{2,6},{3,7},{4,0},{5,1},{6,2},{7,3},{8,12},{9,13},{10,... | collective-permute-start | bytes 1622024 | tf_op jit(solution)/shard_map/ppermute | solution.py:439
  10.7 3.0 %compact.4 = (bf16[32,2048]{1,0:T(8,128)(2,1)}, bf16[32,2048]{1,0:T(8,128)(2,1)}, bf16[32,2048]{1,0:T(8,128)(2,1)}, bf16[32,2048]{1,0:T(8,128)(2,1)}) custom-call(s32[15]{0:T(128)} %dynamic-slice_bitcast_fusion.refs_0_, s32[1,64]{1,0:T(1,128)} %constant.21.clone.refs_1_, bf16[64,4224]{1,0:T(8,128)(2,1)} %pack.1.refs_2_.refs_8_), custom_call_target="tpu_custom_call" | custom-call | flops 33554432 | bytes 540672 | tf_op jit(solution)/shard_map/compact/pallas_call | solution.py:448
  17.2 2.4 %collective-permute-done.refs_2_.refs_1_ = bf16[32,2048]{1,0:T(8,128)(2,1)S(1)} collective-permute-done((bf16[32,2048]{1,0:T(8,128)(2,1)}, bf16[32,2048]{1,0:T(8,128)(2,1)S(1)}, u32[]{:S(2)}, u32[]{:S(2)}) %collective-permute-start) | collective-permute-done | bytes 131104 | tf_op jit(solution)/shard_map/ppermute | solution.py:489
  19.6 3.6 %collective-permute-done.1.refs_3_.refs_2_ = bf16[32,2048]{1,0:T(8,128)(2,1)S(1)} collective-permute-done((bf16[32,2048]{1,0:T(8,128)(2,1)}, bf16[32,2048]{1,0:T(8,128)(2,1)S(1)}, u32[]{:S(2)}, u32[]{:S(2)}) %collective-permute-start.1) | collective-permute-done | bytes 131104 | tf_op jit(solution)/shard_map/ppermute | solution.py:489
  24.1 2.5 %collective-permute-start.6 = (bf16[64,4224]{1,0:T(8,128)(2,1)S(1)}, bf16[64,4224]{1,0:T(8,128)(2,1)S(1)}, u32[]{:S(2)}, u32[]{:S(2)}) collective-permute-start(bf16[64,4224]{1,0:T(8,128)(2,1)S(1)} %collective-permute-done.4.refs_3_.refs_4_.refs_6_), channel_id=1, source_target_pairs={{0,4},{1,5},{2,6},{3,7},{4,0},{5,1},{6,2},{7,3},{8,12},{9,13},{10,... | collective-permute-start | bytes 1622024 | tf_op jit(solution)/shard_map/ppermute | solution.py:439
  26.6 3.4 %compact.5 = (bf16[64,2048]{1,0:T(8,128)(2,1)}, bf16[64,2048]{1,0:T(8,128)(2,1)}, bf16[64,2048]{1,0:T(8,128)(2,1)}, bf16[64,2048]{1,0:T(8,128)(2,1)}) custom-call(s32[15]{0:T(128)} %dynamic-slice_bitcast_fusion.refs_0_, s32[1,128]{1,0:T(1,128)} %constant.22.clone.refs_1_, bf16[64,4224]{1,0:T(8,128)(2,1)} %pack.1.refs_2_.refs_8_, bf16[64,4224]{1,0:T(8,128)(2,1)} %copy-done.2), custom_call_target="tpu_custom_call" | custom-call | flops 134217728 | bytes 1081344 | tf_op jit(solution)/shard_map/compact/pallas_call | solution.py:448
  33.5 3.3 %pad_maximum_fusion = bf16[1,2048,768]{2,1,0:T(8,128)(2,1)} fusion(bf16[1,2048,384]{2,1,0:T(8,128)(2,1)} %refs_6_.1, bf16[1,2048,384]{2,1,0:T(8,128)(2,1)S(1)} %copy-done.5), kind=kLoop, calls=%fused_computation | loop fusion | flops 6291456 | bytes 6291456 | tf_op jit(solution)/shard_map/concatenate | solution.py:431
  37.7 3.9 %compact.6 = (bf16[96,2048]{1,0:T(8,128)(2,1)}, bf16[96,2048]{1,0:T(8,128)(2,1)}, bf16[96,2048]{1,0:T(8,128)(2,1)}, bf16[96,2048]{1,0:T(8,128)(2,1)}) custom-call(s32[15]{0:T(128)} %dynamic-slice_bitcast_fusion.refs_0_, s32[1,192]{1,0:T(1,128)} %constant.23.clone.refs_1_, bf16[64,4224]{1,0:T(8,128)(2,1)} %copy-done.2, bf16[64,4224]{1,0:T(8,128)(2,1)} %copy-done, ...), custom_call_target="tpu_custom_call" | custom-call | flops 301989888 | bytes 1622016 | tf_op jit(solution)/shard_map/compact/pallas_call | solution.py:448
  43.4 1.6 %collective-permute-start.11 = (bf16[96,2048]{1,0:T(8,128)(2,1)}, bf16[96,2048]{1,0:T(8,128)(2,1)S(1)}, u32[]{:S(2)}, u32[]{:S(2)}) collective-permute-start(bf16[96,2048]{1,0:T(8,128)(2,1)} %get-tuple-element.145), channel_id=1, source_target_pairs={{0,1},{1,0},{2,3},{3,2},{4,5},{5,4},{6,7},{7,6},{8,9},{9,8},{10,11... | collective-permute-start | bytes 1179656 | tf_op jit(solution)/shard_map/ppermute | solution.py:489
  46.9 10.8 %collective-permute-done.7.refs_3_.refs_5_ = bf16[64,4224]{1,0:T(8,128)(2,1)S(1)} collective-permute-done((bf16[64,4224]{1,0:T(8,128)(2,1)S(1)}, bf16[64,4224]{1,0:T(8,128)(2,1)S(1)}, u32[]{:S(2)}, u32[]{:S(2)}) %collective-permute-start.7) | collective-permute-done | bytes 540704 | tf_op jit(solution)/shard_map/ppermute | solution.py:439
  58.5 4.1 %compact.7 = (bf16[96,2048]{1,0:T(8,128)(2,1)}, bf16[96,2048]{1,0:T(8,128)(2,1)}, bf16[96,2048]{1,0:T(8,128)(2,1)}, bf16[96,2048]{1,0:T(8,128)(2,1)}) custom-call(s32[15]{0:T(128)} %dynamic-slice_bitcast_fusion.refs_0_, s32[1,192]{1,0:T(1,128)} %constant.24.clone.refs_1_, bf16[64,4224]{1,0:T(8,128)(2,1)} %copy-done.3, bf16[64,4224]{1,0:T(8,128)(2,1)} %copy-done.4, ...), custom_call_target="tpu_custom_call" | custom-call | flops 402653184 | bytes 2162688 | tf_op jit(solution)/shard_map/compact/pallas_call | solution.py:448
  62.7 1.9 %collective-permute-done.12.refs_11_.refs_10_ = bf16[96,2048]{1,0:T(8,128)(2,1)S(1)} collective-permute-done((bf16[96,2048]{1,0:T(8,128)(2,1)}, bf16[96,2048]{1,0:T(8,128)(2,1)S(1)}, u32[]{:S(2)}, u32[]{:S(2)}) %collective-permute-start.12) | collective-permute-done | bytes 393248 | tf_op jit(solution)/shard_map/ppermute | solution.py:489
  66.6 1.6 %collective-permute-start.18 = (bf16[96,2048]{1,0:T(8,128)(2,1)}, bf16[96,2048]{1,0:T(8,128)(2,1)S(1)}, u32[]{:S(2)}, u32[]{:S(2)}) collective-permute-start(bf16[96,2048]{1,0:T(8,128)(2,1)} %get-tuple-element.165), channel_id=1, source_target_pairs={{0,3},{1,2},{2,1},{3,0},{4,7},{5,6},{6,5},{7,4},{8,11},{9,10},{10,... | collective-permute-start | bytes 1179656 | tf_op jit(solution)/shard_map/ppermute | solution.py:489
  68.4 13.1 %expert.2 = (bf16[384,768]{1,0:T(8,128)(2,1)}, bf16[384,768]{1,0:T(8,128)(2,1)}, bf16[384,768]{1,0:T(8,128)(2,1)}, bf16[96,2176]{1,0:T(8,128)(2,1)}, bf16[96,217...) custom-call(s32[15]{0:T(128)} %dynamic-slice_bitcast_fusion.refs_0_, ...), custom_call_target="tpu_custom_call" | custom-call | flops 6039797760 | bytes 9437184 | tf_op jit(solution)/shard_map/expert/pallas_call | solution.py:467
  86.6 10.2 %expert.3 = (bf16[192,768]{1,0:T(8,128)(2,1)}, bf16[192,768]{1,0:T(8,128)(2,1)}, bf16[192,768]{1,0:T(8,128)(2,1)}, bf16[48,2176]{1,0:T(8,128)(2,1)}, bf16[48,217...) custom-call(s32[15]{0:T(128)} %dynamic-slice_bitcast_fusion.refs_0_, ...), custom_call_target="tpu_custom_call" | custom-call | flops 3019898880 | bytes 9437184 | tf_op jit(solution)/shard_map/expert/pallas_call | solution.py:467
  100.4 3.7 %collective-permute-done.21.refs_24_.refs_12_ = bf16[96,2176]{1,0:T(8,128)(2,1)S(1)} collective-permute-done((bf16[96,2176]{1,0:T(8,128)(2,1)}, bf16[96,2176]{1,0:T(8,128)(2,1)S(1)}, u32[]{:S(2)}, u32[]{:S(2)}) %collective-permute-start.21) | collective-permute-done | bytes 417824 | tf_op jit(solution)/shard_map/ppermute | solution.py:489
  104.9 8.1 %weight_grads.2 = (bf16[1,2048,384]{2,1,0:T(8,128)(2,1)}, bf16[1,2048,384]{2,1,0:T(8,128)(2,1)}, bf16[1,384,2048]{2,1,0:T(8,128)(2,1)}) custom-call(bf16[32,2048]{1,0:T(8,128)(2,1)} %get-tuple-element.124.refs_1_.refs_0_, bf16[32,2048]{1,0:T(8,128)(2,1)} %copy-done.24, bf16[32,2048]{1,0:T(8,128)(2,1)} %copy-done.25, bf16[32,2048]{1,0:T(8,128)(2,1)} %copy-done.26, ...), custom_call_target="tpu_custom_call" | custom-call | flops 2717908992 | bytes 6488064 | tf_op jit(solution)/shard_map/weight_grads/pallas_call | solution.py:531
  114.3 4.7 %spread.1 = (bf16[64,2176]{1,0:T(8,128)(2,1)}, bf16[64,2176]{1,0:T(8,128)(2,1)}, bf16[64,2176]{1,0:T(8,128)(2,1)}, bf16[64,2176]{1,0:T(8,128)(2,1)}) custom-call(s32[15]{0:T(128)} %dynamic-slice_bitcast_fusion.refs_0_, s32[1,576]{1,0:T(1,128)} %constant.25.clone.refs_1_, bf16[64,4224]{1,0:T(8,128)(2,1)} %pack.1.refs_2_.refs_8_, bf16[64,4224]{1,0:T(8,128)(2,1)} %copy-done.2, ...), custom_call_target="tpu_custom_call" | custom-call | flops 603979776 | bytes 2359296 | tf_op jit(solution)/shard_map/spread/pallas_call | solution.py:558
  120.0 8.4 %collective-permute-done.25.b_ref = bf16[64,2176]{1,0:T(8,128)(2,1)S(1)} collective-permute-done((bf16[64,2176]{1,0:T(8,128)(2,1)}, bf16[64,2176]{1,0:T(8,128)(2,1)S(1)}, u32[]{:S(2)}, u32[]{:S(2)}) %collective-permute-start.25) | collective-permute-done | bytes 278560 | tf_op jit(solution)/shard_map/ppermute | solution.py:589
  129.1 1.8 %add.5 = bf16[64,2176]{1,0:T(8,128)(2,1)} custom-call(bf16[64,2176]{1,0:T(8,128)(2,1)} %get-tuple-element.202.a_ref, bf16[64,2176]{1,0:T(8,128)(2,1)} %copy-done.17), custom_call_target="tpu_custom_call" | custom-call | tf_op jit(solution)/shard_map/add/pallas_call | solution.py:595
  135.6 9.2 %weight_grads.3 = (bf16[1,2048,384]{2,1,0:T(8,128)(2,1)}, bf16[1,2048,384]{2,1,0:T(8,128)(2,1)}, bf16[1,384,2048]{2,1,0:T(8,128)(2,1)}) custom-call(bf16[32,2048]{1,0:T(8,128)(2,1)} %get-tuple-element.124.refs_1_.refs_0_, bf16[32,2048]{1,0:T(8,128)(2,1)} %copy-done.24, bf16[32,2048]{1,0:T(8,128)(2,1)} %copy-done.25, bf16[32,2048]{1,0:T(8,128)(2,1)} %copy-done.26, ...), custom_call_target="tpu_custom_call" | custom-call | flops 2717908992 | bytes 6488064 | tf_op jit(solution)/shard_map/weight_grads/pallas_call | solution.py:531
  147.1 2.2 %home.1 = (bf16[64,2048]{1,0:T(8,128)(2,1)}, bf16[8,64]{1,0:T(8,128)(2,1)}) custom-call(bf16[64,2176]{1,0:T(8,128)(2,1)} %get-tuple-element.198.refs_0_, bf16[64,2176]{1,0:T(8,128)(2,1)} %copy-done.19, bf16[64,2176]{1,0:T(8,128)(2,1)} %copy-done.18, s32[8,64]{1,0:T(8,128)} %bitcast.6, bf16[8,64]{1,0:T(8,128)(2,1)} %bitcast.8, ...), custom_call_target="tpu_custom_call" | custom-call | flops 1000000 | bytes 1310720 | tf_op jit(solution)/shard_map/home/pallas_call | solution.py:605
  (106 shorter events, 35.9 us)
Async XLA Ops:
  2.9 20.3 %collective-permute-start.4 = (bf16[64,4224]{1,0:T(8,128)(2,1)}, bf16[64,4224]{1,0:T(8,128)(2,1)S(1)}, u32[]{:S(2)}, u32[]{:S(2)}) collective-permute-start(bf16[64,4224]{1,0:T(8,128)(2,1)} %pack.1.refs_2_.refs_8_), channel_id=1, source_target_pairs={{0,0},{1,1},{2,2},{3,3},{4,8},{5,9},{6,10},{7,11},{8,4},{9,5},{10,... | collective-permute-start | bytes 1622024 | tf_op jit(solution)/shard_map/ppermute | solution.py:439
  4.6 18.6 %collective-permute-start.3 = (bf16[64,4224]{1,0:T(8,128)(2,1)}, bf16[64,4224]{1,0:T(8,128)(2,1)S(1)}, u32[]{:S(2)}, u32[]{:S(2)}) collective-permute-start(bf16[64,4224]{1,0:T(8,128)(2,1)} %pack.1.refs_2_.refs_8_), channel_id=1, source_target_pairs={{0,4},{1,5},{2,6},{3,7},{4,0},{5,1},{6,2},{7,3},{8,12},{9,13},{10,... | collective-permute-start | bytes 1622024 | tf_op jit(solution)/shard_map/ppermute | solution.py:439
  23.3 13.6 %collective-permute-start.5 = (bf16[64,4224]{1,0:T(8,128)(2,1)S(1)}, bf16[64,4224]{1,0:T(8,128)(2,1)S(1)}, u32[]{:S(2)}, u32[]{:S(2)}) collective-permute-start(bf16[64,4224]{1,0:T(8,128)(2,1)S(1)} %collective-permute-done.3.refs_3_.refs_2_), channel_id=1, source_target_pairs={{0,0},{1,1},{2,2},{3,3},{4,8},{5,9},{6,10},{7,11},{8,4},{9,5},{10,... | collective-permute-start | bytes 1622024 | tf_op jit(solution)/shard_map/ppermute | solution.py:439
  24.1 12.8 %collective-permute-start.6 = (bf16[64,4224]{1,0:T(8,128)(2,1)S(1)}, bf16[64,4224]{1,0:T(8,128)(2,1)S(1)}, u32[]{:S(2)}, u32[]{:S(2)}) collective-permute-start(bf16[64,4224]{1,0:T(8,128)(2,1)S(1)} %collective-permute-done.4.refs_3_.refs_4_.refs_6_), channel_id=1, source_target_pairs={{0,4},{1,5},{2,6},{3,7},{4,0},{5,1},{6,2},{7,3},{8,12},{9,13},{10,... | collective-permute-start | bytes 1622024 | tf_op jit(solution)/shard_map/ppermute | solution.py:439
  31.0 12.0 %collective-permute-start.9 = (bf16[64,2048]{1,0:T(8,128)(2,1)}, bf16[64,2048]{1,0:T(8,128)(2,1)}, u32[]{:S(2)}, u32[]{:S(2)}) collective-permute-start(bf16[64,2048]{1,0:T(8,128)(2,1)} %get-tuple-element.130), channel_id=1, source_target_pairs={{0,2},{1,3},{2,0},{3,1},{4,6},{5,7},{6,4},{7,5},{8,10},{9,11},{10,... | collective-permute-start | bytes 786440 | tf_op jit(solution)/shard_map/ppermute | solution.py:489
  43.0 21.6 %collective-permute-start.14 = (bf16[1,2048,768]{2,1,0:T(8,128)(2,1)}, bf16[1,2048,768]{2,1,0:T(8,128)(2,1)}, u32[]{:S(2)}, u32[]{:S(2)}) collective-permute-start(bf16[1,2048,768]{2,1,0:T(8,128)(2,1)} %pad_maximum_fusion), channel_id=1, source_target_pairs={{0,16},{16,0},{1,17},{17,1},{2,18},{18,2},{3,19},{19,3},{4,20},{20... | collective-permute-start | bytes 9437192 | tf_op jit(solution)/shard_map/ppermute | solution.py:502
  43.0 14.7 %collective-permute-start.7 = (bf16[64,4224]{1,0:T(8,128)(2,1)S(1)}, bf16[64,4224]{1,0:T(8,128)(2,1)S(1)}, u32[]{:S(2)}, u32[]{:S(2)}) collective-permute-start(bf16[64,4224]{1,0:T(8,128)(2,1)S(1)} %collective-permute-done.5.refs_2_.refs_4_), channel_id=1, source_target_pairs={{0,4},{1,5},{2,6},{3,7},{4,0},{5,1},{6,2},{7,3},{8,12},{9,13},{10,... | collective-permute-start | bytes 1622024 | tf_op jit(solution)/shard_map/ppermute | solution.py:439
  43.4 19.3 %collective-permute-start.11 = (bf16[96,2048]{1,0:T(8,128)(2,1)}, bf16[96,2048]{1,0:T(8,128)(2,1)S(1)}, u32[]{:S(2)}, u32[]{:S(2)}) collective-permute-start(bf16[96,2048]{1,0:T(8,128)(2,1)} %get-tuple-element.145), channel_id=1, source_target_pairs={{0,1},{1,0},{2,3},{3,2},{4,5},{5,4},{6,7},{7,6},{8,9},{9,8},{10,11... | collective-permute-start | bytes 1179656 | tf_op jit(solution)/shard_map/ppermute | solution.py:489
  45.0 19.5 %collective-permute-start.12 = (bf16[96,2048]{1,0:T(8,128)(2,1)}, bf16[96,2048]{1,0:T(8,128)(2,1)S(1)}, u32[]{:S(2)}, u32[]{:S(2)}) collective-permute-start(bf16[96,2048]{1,0:T(8,128)(2,1)} %get-tuple-element.146), channel_id=1, source_target_pairs={{0,2},{1,3},{2,0},{3,1},{4,6},{5,7},{6,4},{7,5},{8,10},{9,11},{10,... | collective-permute-start | bytes 1179656 | tf_op jit(solution)/shard_map/ppermute | solution.py:489
  46.4 18.2 %collective-permute-start.13 = (bf16[96,2048]{1,0:T(8,128)(2,1)}, bf16[96,2048]{1,0:T(8,128)(2,1)S(1)}, u32[]{:S(2)}, u32[]{:S(2)}) collective-permute-start(bf16[96,2048]{1,0:T(8,128)(2,1)} %get-tuple-element.147), channel_id=1, source_target_pairs={{0,3},{1,2},{2,1},{3,0},{4,7},{5,6},{6,5},{7,4},{8,11},{9,10},{10,... | collective-permute-start | bytes 1179656 | tf_op jit(solution)/shard_map/ppermute | solution.py:489
  64.7 18.9 %collective-permute-start.16 = (bf16[96,2048]{1,0:T(8,128)(2,1)}, bf16[96,2048]{1,0:T(8,128)(2,1)S(1)}, u32[]{:S(2)}, u32[]{:S(2)}) collective-permute-start(bf16[96,2048]{1,0:T(8,128)(2,1)} %get-tuple-element.163), channel_id=1, source_target_pairs={{0,1},{1,0},{2,3},{3,2},{4,5},{5,4},{6,7},{7,6},{8,9},{9,8},{10,11... | collective-permute-start | bytes 1179656 | tf_op jit(solution)/shard_map/ppermute | solution.py:489
  65.7 19.4 %collective-permute-start.17 = (bf16[96,2048]{1,0:T(8,128)(2,1)}, bf16[96,2048]{1,0:T(8,128)(2,1)S(1)}, u32[]{:S(2)}, u32[]{:S(2)}) collective-permute-start(bf16[96,2048]{1,0:T(8,128)(2,1)} %get-tuple-element.164), channel_id=1, source_target_pairs={{0,2},{1,3},{2,0},{3,1},{4,6},{5,7},{6,4},{7,5},{8,10},{9,11},{10,... | collective-permute-start | bytes 1179656 | tf_op jit(solution)/shard_map/ppermute | solution.py:489
  66.6 19.2 %collective-permute-start.18 = (bf16[96,2048]{1,0:T(8,128)(2,1)}, bf16[96,2048]{1,0:T(8,128)(2,1)S(1)}, u32[]{:S(2)}, u32[]{:S(2)}) collective-permute-start(bf16[96,2048]{1,0:T(8,128)(2,1)} %get-tuple-element.165), channel_id=1, source_target_pairs={{0,3},{1,2},{2,1},{3,0},{4,7},{5,6},{6,5},{7,4},{8,11},{9,10},{10,... | collective-permute-start | bytes 1179656 | tf_op jit(solution)/shard_map/ppermute | solution.py:489
  81.6 17.8 %collective-permute-start.19 = (bf16[96,2176]{1,0:T(8,128)(2,1)}, bf16[96,2176]{1,0:T(8,128)(2,1)S(1)}, u32[]{:S(2)}, u32[]{:S(2)}) collective-permute-start(bf16[96,2176]{1,0:T(8,128)(2,1)} %get-tuple-element.178), channel_id=1, source_target_pairs={{0,1},{1,0},{2,3},{3,2},{4,5},{5,4},{6,7},{7,6},{8,9},{9,8},{10,11... | collective-permute-start | bytes 1253384 | tf_op jit(solution)/shard_map/ppermute | solution.py:489
  82.6 17.8 %collective-permute-start.20 = (bf16[96,2176]{1,0:T(8,128)(2,1)}, bf16[96,2176]{1,0:T(8,128)(2,1)S(1)}, u32[]{:S(2)}, u32[]{:S(2)}) collective-permute-start(bf16[96,2176]{1,0:T(8,128)(2,1)} %get-tuple-element.179), channel_id=1, source_target_pairs={{0,2},{1,3},{2,0},{3,1},{4,6},{5,7},{6,4},{7,5},{8,10},{9,11},{10,... | collective-permute-start | bytes 1253384 | tf_op jit(solution)/shard_map/ppermute | solution.py:489
  83.5 20.6 %collective-permute-start.21 = (bf16[96,2176]{1,0:T(8,128)(2,1)}, bf16[96,2176]{1,0:T(8,128)(2,1)S(1)}, u32[]{:S(2)}, u32[]{:S(2)}) collective-permute-start(bf16[96,2176]{1,0:T(8,128)(2,1)} %get-tuple-element.180), channel_id=1, source_target_pairs={{0,3},{1,2},{2,1},{3,0},{4,7},{5,6},{6,5},{7,4},{8,11},{9,10},{10,... | collective-permute-start | bytes 1253384 | tf_op jit(solution)/shard_map/ppermute | solution.py:489
  96.8 16.1 %collective-permute-start.22 = (bf16[48,2176]{1,0:T(8,128)(2,1)}, bf16[48,2176]{1,0:T(8,128)(2,1)S(1)}, u32[]{:S(2)}, u32[]{:S(2)}) collective-permute-start(bf16[48,2176]{1,0:T(8,128)(2,1)} %get-tuple-element.186), channel_id=1, source_target_pairs={{0,1},{1,0},{2,3},{3,2},{4,5},{5,4},{6,7},{7,6},{8,9},{9,8},{10,11... | collective-permute-start | bytes 626696 | tf_op jit(solution)/shard_map/ppermute | solution.py:489
  97.9 15.1 %collective-permute-start.23 = (bf16[48,2176]{1,0:T(8,128)(2,1)}, bf16[48,2176]{1,0:T(8,128)(2,1)S(1)}, u32[]{:S(2)}, u32[]{:S(2)}) collective-permute-start(bf16[48,2176]{1,0:T(8,128)(2,1)} %get-tuple-element.187), channel_id=1, source_target_pairs={{0,2},{1,3},{2,0},{3,1},{4,6},{5,7},{6,4},{7,5},{8,10},{9,11},{10,... | collective-permute-start | bytes 626696 | tf_op jit(solution)/shard_map/ppermute | solution.py:489
  99.3 13.7 %collective-permute-start.24 = (bf16[48,2176]{1,0:T(8,128)(2,1)}, bf16[48,2176]{1,0:T(8,128)(2,1)S(1)}, u32[]{:S(2)}, u32[]{:S(2)}) collective-permute-start(bf16[48,2176]{1,0:T(8,128)(2,1)} %get-tuple-element.188), channel_id=1, source_target_pairs={{0,3},{1,2},{2,1},{3,0},{4,7},{5,6},{6,5},{7,4},{8,11},{9,10},{10,... | collective-permute-start | bytes 626696 | tf_op jit(solution)/shard_map/ppermute | solution.py:489
  113.8 20.1 %collective-permute-start.29 = (bf16[1,2048,384]{2,1,0:T(8,128)(2,1)}, bf16[1,2048,384]{2,1,0:T(8,128)(2,1)S(1)}, u32[]{:S(2)}, u32[]{:S(2)}) collective-permute-start(bf16[1,2048,384]{2,1,0:T(8,128)(2,1)} %get-tuple-element.204), channel_id=1, source_target_pairs={{0,16},{16,0},{1,17},{17,1},{2,18},{18,2},{3,19},{19,3},{4,20},{20... | collective-permute-start | bytes 4718600 | tf_op jit(solution)/shard_map/ppermute | solution.py:584
  113.8 20.1 %collective-permute-start.30 = (bf16[1,384,2048]{2,1,0:T(8,128)(2,1)}, bf16[1,384,2048]{2,1,0:T(8,128)(2,1)S(1)}, u32[]{:S(2)}, u32[]{:S(2)}) collective-permute-start(bf16[1,384,2048]{2,1,0:T(8,128)(2,1)} %get-tuple-element.205), channel_id=1, source_target_pairs={{0,16},{16,0},{1,17},{17,1},{2,18},{18,2},{3,19},{19,3},{4,20},{20... | collective-permute-start | bytes 4718600 | tf_op jit(solution)/shard_map/ppermute | solution.py:584
  114.3 19.6 %collective-permute-start.28 = (bf16[1,2048,384]{2,1,0:T(8,128)(2,1)}, bf16[1,2048,384]{2,1,0:T(8,128)(2,1)}, u32[]{:S(2)}, u32[]{:S(2)}) collective-permute-start(bf16[1,2048,384]{2,1,0:T(8,128)(2,1)} %get-tuple-element.197.refs_17_), channel_id=1, source_target_pairs={{0,16},{16,0},{1,17},{17,1},{2,18},{18,2},{3,19},{19,3},{4,20},{20... | collective-permute-start | bytes 4718600 | tf_op jit(solution)/shard_map/ppermute | solution.py:584
  130.9 15.4 %collective-permute-start.27 = (bf16[64,2176]{1,0:T(8,128)(2,1)}, bf16[64,2176]{1,0:T(8,128)(2,1)S(1)}, u32[]{:S(2)}, u32[]{:S(2)}) collective-permute-start(bf16[64,2176]{1,0:T(8,128)(2,1)} %add.5), channel_id=1, source_target_pairs={{0,8},{1,9},{2,10},{3,11},{4,12},{5,13},{6,14},{7,15},{8,0},{9,1},... | collective-permute-start | bytes 835592 | tf_op jit(solution)/shard_map/ppermute | solution.py:589
  132.4 13.8 %collective-permute-start.26 = (bf16[64,2176]{1,0:T(8,128)(2,1)}, bf16[64,2176]{1,0:T(8,128)(2,1)S(1)}, u32[]{:S(2)}, u32[]{:S(2)}) collective-permute-start(bf16[64,2176]{1,0:T(8,128)(2,1)} %get-tuple-element.201), channel_id=1, source_target_pairs={{0,4},{1,5},{2,6},{3,7},{4,0},{5,1},{6,2},{7,3},{8,12},{9,13},{10,... | collective-permute-start | bytes 835592 | tf_op jit(solution)/shard_map/ppermute | solution.py:589
  (34 other events, 194.7 us)

commit v10 on v9

--- a/solution.py
+++ b/solution.py
@@ -22,7 +22,7 @@
 NT = (((1,), (1,)), ((), ()))
 
 
-def params(megabytes=60):
+def params(megabytes=64):
     return pltpu.CompilerParams(vmem_limit_bytes=megabytes << 20)
 
 
@@ -384,10 +384,6 @@
         outs[i][...] = sums[i * tok : (i + 1) * tok]
 
 
-def add_kernel(a_ref, b_ref, o_ref):
-    o_ref[...] = (a_ref[...].astype(F32) + b_ref[...].astype(F32)).astype(BF)
-
-
 def home_kernel(plan, count, *refs):
     parts = refs[:count]
     routes_ref, comb_ref, _, tok_o, comb_o = refs[count:]
@@ -592,13 +588,8 @@
                 continue
             if bit == 1:
                 sums[1], sent = lax.optimization_barrier((sums[1], sent))
-            sums[r - bit] = pl.pallas_call(
-                add_kernel,
-                out_shape=shape((tok, width + LANES), BF),
-                in_specs=[VMEM] * 2,
-                out_specs=VMEM,
-                name="add",
-            )(sums[r - bit], sent)
+            total = sums[r - bit].astype(F32) + sent.astype(F32)
+            sums[r - bit] = total.astype(BF)
         bit *= 2
     grads = weight_grads(True, theirs)
     home = [sums[0]] + came

time: 150 us -> 154 us (1.027)
  local copies, waits for them, and re-layouts: 8.45 us -> 1.2 us
  starting transfers between devices: 35.9 us -> 41.9 us
  waiting for transfers between devices: 34.7 us -> 39.6 us
  other arithmetic: 3.33 us -> 5.54 us
  Pallas kernels: 66 us -> 64.1 us
    unnamed x54 -> x0, local copies, waits for them, and re-layouts: 7.25 us -> none
    ppermute x5, starting transfers between devices: 10.1 us -> 15 us  [hop(): blocks[i] = lax.ppermute(before, 'expert', plan.exchange(r, chain))]
    ppermute x18, waiting for transfers between devices: 13.7 us -> 16 us  [cross(): lax.ppermute(arrays[d], 'expert', plan.across(d))]
    pallas_call x1 -> x0, Pallas kernels: 1.79 us -> none  [on_device(): pl.pallas_call(add_kernel, out_shape=shape((tok, width + LANES), BF), in_...]
    convert_element_type x0 -> x1, other arithmetic: none -> 1.72 us  [on_device(): sums[r - bit] = total.astype(BF)]
    ppermute x3, waiting for transfers between devices: 9.95 us -> 11.5 us  [on_device(): sent = lax.ppermute(sums[r], 'expert', plan.flip(bit))]
  transfers between devices with their start and end apart: 31 -> 31, of which waited for: 10 -> 16; matrix products, arithmetic and copies ran while one was open for 3% -> 4% of each run, Pallas kernels for 41% -> 39%
where the time goes in v10:
time: 154 us; the launch traced here: 153 us
  Pallas kernels  64.1 us (42%)
  starting transfers between devices  41.9 us (27%)
  waiting for transfers between devices  39.6 us (26%)
  other arithmetic  5.54 us (4%)
    pallas_call x2, Pallas kernels, expert(): pl.pallas_call(functools.partial(expert_kernel, plan, g), out_shape=[shap...  23.3 us
    ppermute x18, starting transfers between devices, cross(): lax.ppermute(arrays[d], 'expert', plan.across(d))  21.4 us
    pallas_call x2, Pallas kernels, weight_grads(): pl.pallas_call(functools.partial(weight_kernel, plan, own, len(extra)), o...  17.3 us
    ppermute x18, waiting for transfers between devices, cross(): lax.ppermute(arrays[d], 'expert', plan.across(d))  16 us
    ppermute x5, starting transfers between devices, hop(): blocks[i] = lax.ppermute(before, 'expert', plan.exchange(r, chain))  15 us
    pallas_call x4, Pallas kernels, compact(): pl.pallas_call(functools.partial(compact_kernel, plan, c), out_shape=[sha...  14.4 us
    ppermute x5, waiting for transfers between devices, hop(): blocks[i] = lax.ppermute(before, 'expert', plan.exchange(r, chain))  11.9 us
    ppermute x3, waiting for transfers between devices, on_device(): sent = lax.ppermute(sums[r], 'expert', plan.flip(bit))  11.5 us
  transfers between devices with their start and end apart: 31, of which 16 were waited for; matrix products, arithmetic and copies ran while one was open for 4% of the time, Pallas kernels for 39%

profile of v10, /device:TPU:0, one launch (start us, length us, event | category | flops | bytes accessed | tf_op | source)
XLA Modules:
  0.0 153.2 jit_solution(11395462826237604953)
XLA Ops:
  0.6 2.1 %pack.1.refs_2_.refs_8_ = bf16[64,4224]{1,0:T(8,128)(2,1)} custom-call(bf16[64,2048]{1,0:T(8,128)(2,1)} %tok_ref.1, bf16[64,2048]{1,0:T(8,128)(2,1)} %up_ref.1, s32[8,64]{1,0:T(8,128)} %bitcast.5, bf16[8,64]{1,0:T(8,128)(2,1)} %bitcast.7), custom_call_target="tpu_custom_call" | custom-call | flops 1000000 | bytes 1081344 | tf_op jit(solution)/shard_map/pack/pallas_call | solution.py:417
  2.8 5.8 %collective-permute-start.4 = (bf16[64,4224]{1,0:T(8,128)(2,1)}, bf16[64,4224]{1,0:T(8,128)(2,1)}, u32[]{:S(2)}, u32[]{:S(2)}) collective-permute-start(bf16[64,4224]{1,0:T(8,128)(2,1)} %pack.1.refs_2_.refs_8_), channel_id=1, source_target_pairs={{0,0},{1,1},{2,2},{3,3},{4,8},{5,9},{6,10},{7,11},{8,4},{9,5},{10,... | collective-permute-start | bytes 1622024 | tf_op jit(solution)/shard_map/ppermute | solution.py:435
  10.5 3.0 %compact.4 = (bf16[32,2048]{1,0:T(8,128)(2,1)}, bf16[32,2048]{1,0:T(8,128)(2,1)}, bf16[32,2048]{1,0:T(8,128)(2,1)}, bf16[32,2048]{1,0:T(8,128)(2,1)}) custom-call(s32[15]{0:T(128)} %dynamic-slice_bitcast_fusion.refs_0_, s32[1,64]{1,0:T(1,128)} %constant.21.clone.refs_1_, bf16[64,4224]{1,0:T(8,128)(2,1)} %pack.1.refs_2_.refs_8_), custom_call_target="tpu_custom_call" | custom-call | flops 33554432 | bytes 540672 | tf_op jit(solution)/shard_map/compact/pallas_call | solution.py:444
  13.5 2.3 %collective-permute-start = (bf16[32,2048]{1,0:T(8,128)(2,1)}, bf16[32,2048]{1,0:T(8,128)(2,1)}, u32[]{:S(2)}, u32[]{:S(2)}) collective-permute-start(bf16[32,2048]{1,0:T(8,128)(2,1)} %get-tuple-element.109), channel_id=1, source_target_pairs={{0,1},{1,0},{2,3},{3,2},{4,5},{5,4},{6,7},{7,6},{8,9},{9,8},{10,11... | collective-permute-start | bytes 393224 | tf_op jit(solution)/shard_map/ppermute | solution.py:485
  17.3 2.7 %collective-permute-done.refs_2_.refs_1_ = bf16[32,2048]{1,0:T(8,128)(2,1)} collective-permute-done((bf16[32,2048]{1,0:T(8,128)(2,1)}, bf16[32,2048]{1,0:T(8,128)(2,1)}, u32[]{:S(2)}, u32[]{:S(2)}) %collective-permute-start) | collective-permute-done | bytes 131104 | tf_op jit(solution)/shard_map/ppermute | solution.py:485
  20.0 3.9 %collective-permute-done.1.refs_3_.refs_2_ = bf16[32,2048]{1,0:T(8,128)(2,1)} collective-permute-done((bf16[32,2048]{1,0:T(8,128)(2,1)}, bf16[32,2048]{1,0:T(8,128)(2,1)}, u32[]{:S(2)}, u32[]{:S(2)}) %collective-permute-start.1) | collective-permute-done | bytes 131104 | tf_op jit(solution)/shard_map/ppermute | solution.py:485
  23.9 5.8 %collective-permute-start.5 = (bf16[64,4224]{1,0:T(8,128)(2,1)}, bf16[64,4224]{1,0:T(8,128)(2,1)}, u32[]{:S(2)}, u32[]{:S(2)}) collective-permute-start(bf16[64,4224]{1,0:T(8,128)(2,1)} %collective-permute-done.3.refs_3_.refs_2_), channel_id=1, source_target_pairs={{0,0},{1,1},{2,2},{3,3},{4,8},{5,9},{6,10},{7,11},{8,4},{9,5},{10,... | collective-permute-start | bytes 1622024 | tf_op jit(solution)/shard_map/ppermute | solution.py:435
  30.6 3.4 %compact.5 = (bf16[64,2048]{1,0:T(8,128)(2,1)}, bf16[64,2048]{1,0:T(8,128)(2,1)}, bf16[64,2048]{1,0:T(8,128)(2,1)}, bf16[64,2048]{1,0:T(8,128)(2,1)}) custom-call(s32[15]{0:T(128)} %dynamic-slice_bitcast_fusion.refs_0_, s32[1,128]{1,0:T(1,128)} %constant.22.clone.refs_1_, bf16[64,4224]{1,0:T(8,128)(2,1)} %pack.1.refs_2_.refs_8_, ...), custom_call_target="tpu_custom_call" | custom-call | flops 134217728 | bytes 1081344 | tf_op jit(solution)/shard_map/compact/pallas_call | solution.py:444
  37.6 3.8 %pad_maximum_fusion = bf16[1,2048,768]{2,1,0:T(8,128)(2,1)} fusion(bf16[1,2048,384]{2,1,0:T(8,128)(2,1)} %refs_6_.1, bf16[1,2048,384]{2,1,0:T(8,128)(2,1)} %refs_5_.1), kind=kLoop, calls=%fused_computation | loop fusion | flops 6291456 | bytes 6291456 | tf_op jit(solution)/shard_map/concatenate | solution.py:427
  41.4 2.1 %collective-permute-done.6.refs_4_.refs_5_.refs_7_ = bf16[64,4224]{1,0:T(8,128)(2,1)} collective-permute-done((bf16[64,4224]{1,0:T(8,128)(2,1)}, bf16[64,4224]{1,0:T(8,128)(2,1)}, u32[]{:S(2)}, u32[]{:S(2)}) %collective-permute-start.6) | collective-permute-done | bytes 540704 | tf_op jit(solution)/shard_map/ppermute | solution.py:435
  43.5 3.9 %compact.6 = (bf16[96,2048]{1,0:T(8,128)(2,1)}, bf16[96,2048]{1,0:T(8,128)(2,1)}, bf16[96,2048]{1,0:T(8,128)(2,1)}, bf16[96,2048]{1,0:T(8,128)(2,1)}) custom-call(s32[15]{0:T(128)} %dynamic-slice_bitcast_fusion.refs_0_, s32[1,192]{1,0:T(1,128)} %constant.23.clone.refs_1_, bf16[64,4224]{1,0:T(8,128)(2,1)} %collective-permute-done.3.refs_3_.refs_2_, ...), custom_call_target="tpu_custom_call" | custom-call | flops 301989888 | bytes 1622016 | tf_op jit(solution)/shard_map/compact/pallas_call | solution.py:444
  53.2 9.8 %collective-permute-done.7.refs_3_.refs_5_ = bf16[64,4224]{1,0:T(8,128)(2,1)} collective-permute-done((bf16[64,4224]{1,0:T(8,128)(2,1)}, bf16[64,4224]{1,0:T(8,128)(2,1)}, u32[]{:S(2)}, u32[]{:S(2)}) %collective-permute-start.7) | collective-permute-done | bytes 540704 | tf_op jit(solution)/shard_map/ppermute | solution.py:435
  63.0 4.1 %compact.7 = (bf16[96,2048]{1,0:T(8,128)(2,1)}, bf16[96,2048]{1,0:T(8,128)(2,1)}, bf16[96,2048]{1,0:T(8,128)(2,1)}, bf16[96,2048]{1,0:T(8,128)(2,1)}) custom-call(s32[15]{0:T(128)} %dynamic-slice_bitcast_fusion.refs_0_, s32[1,192]{1,0:T(1,128)} %constant.24.clone.refs_1_, bf16[64,4224]{1,0:T(8,128)(2,1)} %collective-permute-done.5.refs_2_.refs_4_, ...), custom_call_target="tpu_custom_call" | custom-call | flops 402653184 | bytes 2162688 | tf_op jit(solution)/shard_map/compact/pallas_call | solution.py:444
  67.1 1.9 %collective-permute-done.12.refs_11_.refs_10_ = bf16[96,2048]{1,0:T(8,128)(2,1)} collective-permute-done((bf16[96,2048]{1,0:T(8,128)(2,1)}, bf16[96,2048]{1,0:T(8,128)(2,1)}, u32[]{:S(2)}, u32[]{:S(2)}) %collective-permute-start.12) | collective-permute-done | bytes 393248 | tf_op jit(solution)/shard_map/ppermute | solution.py:485
  74.4 13.1 %expert.2 = (bf16[384,768]{1,0:T(8,128)(2,1)}, bf16[384,768]{1,0:T(8,128)(2,1)}, bf16[384,768]{1,0:T(8,128)(2,1)}, bf16[96,2176]{1,0:T(8,128)(2,1)}, bf16[96,217...) custom-call(s32[15]{0:T(128)} %dynamic-slice_bitcast_fusion.refs_0_, ...), custom_call_target="tpu_custom_call" | custom-call | flops 6039797760 | bytes 9437184 | tf_op jit(solution)/shard_map/expert/pallas_call | solution.py:463
  91.5 10.2 %expert.3 = (bf16[192,768]{1,0:T(8,128)(2,1)}, bf16[192,768]{1,0:T(8,128)(2,1)}, bf16[192,768]{1,0:T(8,128)(2,1)}, bf16[48,2176]{1,0:T(8,128)(2,1)}, bf16[48,217...) custom-call(s32[15]{0:T(128)} %dynamic-slice_bitcast_fusion.refs_0_, ...), custom_call_target="tpu_custom_call" | custom-call | flops 3019898880 | bytes 9437184 | tf_op jit(solution)/shard_map/expert/pallas_call | solution.py:463
  105.3 3.9 %collective-permute-done.20.refs_23_.refs_11_ = bf16[96,2176]{1,0:T(8,128)(2,1)} collective-permute-done((bf16[96,2176]{1,0:T(8,128)(2,1)}, bf16[96,2176]{1,0:T(8,128)(2,1)}, u32[]{:S(2)}, u32[]{:S(2)}) %collective-permute-start.20) | collective-permute-done | bytes 417824 | tf_op jit(solution)/shard_map/ppermute | solution.py:485
  109.6 8.1 %weight_grads.2 = (bf16[1,2048,384]{2,1,0:T(8,128)(2,1)}, bf16[1,2048,384]{2,1,0:T(8,128)(2,1)}, bf16[1,384,2048]{2,1,0:T(8,128)(2,1)}) custom-call(bf16[32,2048]{1,0:T(8,128)(2,1)} %get-tuple-element.124.refs_1_.refs_0_, bf16[32,2048]{1,0:T(8,128)(2,1)} %collective-permute-done.refs_2_.refs_1_, bf16[32,2048]{1,0:T(8,128)(2,1)} %collective-permute-done.1.refs_3_.refs_2_, ...), custom_call_target="tpu_custom_call" | custom-call | flops 2717908992 | bytes 6488064 | tf_op jit(solution)/shard_map/weight_grads/pallas_call | solution.py:527
  118.9 4.7 %spread.1 = (bf16[64,2176]{1,0:T(8,128)(2,1)}, bf16[64,2176]{1,0:T(8,128)(2,1)}, bf16[64,2176]{1,0:T(8,128)(2,1)}, bf16[64,2176]{1,0:T(8,128)(2,1)}) custom-call(s32[15]{0:T(128)} %dynamic-slice_bitcast_fusion.refs_0_, s32[1,576]{1,0:T(1,128)} %constant.25.clone.refs_1_, bf16[64,4224]{1,0:T(8,128)(2,1)} %pack.1.refs_2_.refs_8_, ...), custom_call_target="tpu_custom_call" | custom-call | flops 603979776 | bytes 2359296 | tf_op jit(solution)/shard_map/spread/pallas_call | solution.py:554
  124.3 8.6 %collective-permute-done.25 = bf16[64,2176]{1,0:T(8,128)(2,1)S(1)} collective-permute-done((bf16[64,2176]{1,0:T(8,128)(2,1)}, bf16[64,2176]{1,0:T(8,128)(2,1)S(1)}, u32[]{:S(2)}, u32[]{:S(2)}) %collective-permute-start.25) | collective-permute-done | bytes 278560 | tf_op jit(solution)/shard_map/ppermute | solution.py:585
  134.6 2.8 %collective-permute-start.27 = (bf16[64,2176]{1,0:T(8,128)(2,1)}, bf16[64,2176]{1,0:T(8,128)(2,1)}, u32[]{:S(2)}, u32[]{:S(2)}) collective-permute-start(bf16[64,2176]{1,0:T(8,128)(2,1)} %add_convert_fusion), channel_id=1, source_target_pairs={{0,8},{1,9},{2,10},{3,11},{4,12},{5,13},{6,14},{7,15},{8,0},{9,1},... | collective-permute-start | bytes 835592 | tf_op jit(solution)/shard_map/ppermute | solution.py:585
  138.8 9.2 %weight_grads.3 = (bf16[1,2048,384]{2,1,0:T(8,128)(2,1)}, bf16[1,2048,384]{2,1,0:T(8,128)(2,1)}, bf16[1,384,2048]{2,1,0:T(8,128)(2,1)}) custom-call(bf16[32,2048]{1,0:T(8,128)(2,1)} %get-tuple-element.124.refs_1_.refs_0_, bf16[32,2048]{1,0:T(8,128)(2,1)} %collective-permute-done.refs_2_.refs_1_, bf16[32,2048]{1,0:T(8,128)(2,1)} %collective-permute-done.1.refs_3_.refs_2_, ...), custom_call_target="tpu_custom_call" | custom-call | flops 2717908992 | bytes 6488064 | tf_op jit(solution)/shard_map/weight_grads/pallas_call | solution.py:527
  148.0 2.4 %collective-permute-done.27.refs_2_ = bf16[64,2176]{1,0:T(8,128)(2,1)} collective-permute-done((bf16[64,2176]{1,0:T(8,128)(2,1)}, bf16[64,2176]{1,0:T(8,128)(2,1)}, u32[]{:S(2)}, u32[]{:S(2)}) %collective-permute-start.27) | collective-permute-done | bytes 278560 | tf_op jit(solution)/shard_map/ppermute | solution.py:585
  151.0 2.2 %home.1 = (bf16[64,2048]{1,0:T(8,128)(2,1)}, bf16[8,64]{1,0:T(8,128)(2,1)}) custom-call(bf16[64,2176]{1,0:T(8,128)(2,1)} %get-tuple-element.198.refs_0_, bf16[64,2176]{1,0:T(8,128)(2,1)} %collective-permute-done.26.refs_1_, bf16[64,2176]{1,0:T(8,128)(2,1)} %collective-permute-done.27.refs_2_, s32[8,64]{1,0:T(8,128)} %bitcast.6, bf16[8,64]{1,0:T(8,128)(2,1)} %bitcast.8, ...), custom_call_target="tpu_custom_call" | custom-call | flops 1000000 | bytes 1310720 | tf_op jit(solution)/shard_map/home/pallas_call | solution.py:596
  (52 shorter events, 32.6 us)
Async XLA Ops:
  2.8 21.1 %collective-permute-start.4 = (bf16[64,4224]{1,0:T(8,128)(2,1)}, bf16[64,4224]{1,0:T(8,128)(2,1)}, u32[]{:S(2)}, u32[]{:S(2)}) collective-permute-start(bf16[64,4224]{1,0:T(8,128)(2,1)} %pack.1.refs_2_.refs_8_), channel_id=1, source_target_pairs={{0,0},{1,1},{2,2},{3,3},{4,8},{5,9},{6,10},{7,11},{8,4},{9,5},{10,... | collective-permute-start | bytes 1622024 | tf_op jit(solution)/shard_map/ppermute | solution.py:435
  8.6 15.3 %collective-permute-start.3 = (bf16[64,4224]{1,0:T(8,128)(2,1)}, bf16[64,4224]{1,0:T(8,128)(2,1)}, u32[]{:S(2)}, u32[]{:S(2)}) collective-permute-start(bf16[64,4224]{1,0:T(8,128)(2,1)} %pack.1.refs_2_.refs_8_), channel_id=1, source_target_pairs={{0,4},{1,5},{2,6},{3,7},{4,0},{5,1},{6,2},{7,3},{8,12},{9,13},{10,... | collective-permute-start | bytes 1622024 | tf_op jit(solution)/shard_map/ppermute | solution.py:435
  23.9 17.5 %collective-permute-start.5 = (bf16[64,4224]{1,0:T(8,128)(2,1)}, bf16[64,4224]{1,0:T(8,128)(2,1)}, u32[]{:S(2)}, u32[]{:S(2)}) collective-permute-start(bf16[64,4224]{1,0:T(8,128)(2,1)} %collective-permute-done.3.refs_3_.refs_2_), channel_id=1, source_target_pairs={{0,0},{1,1},{2,2},{3,3},{4,8},{5,9},{6,10},{7,11},{8,4},{9,5},{10,... | collective-permute-start | bytes 1622024 | tf_op jit(solution)/shard_map/ppermute | solution.py:435
  29.7 13.8 %collective-permute-start.6 = (bf16[64,4224]{1,0:T(8,128)(2,1)}, bf16[64,4224]{1,0:T(8,128)(2,1)}, u32[]{:S(2)}, u32[]{:S(2)}) collective-permute-start(bf16[64,4224]{1,0:T(8,128)(2,1)} %collective-permute-done.4.refs_3_.refs_4_.refs_6_), channel_id=1, source_target_pairs={{0,4},{1,5},{2,6},{3,7},{4,0},{5,1},{6,2},{7,3},{8,12},{9,13},{10,... | collective-permute-start | bytes 1622024 | tf_op jit(solution)/shard_map/ppermute | solution.py:435
  34.0 13.4 %collective-permute-start.8 = (bf16[64,2048]{1,0:T(8,128)(2,1)}, bf16[64,2048]{1,0:T(8,128)(2,1)}, u32[]{:S(2)}, u32[]{:S(2)}) collective-permute-start(bf16[64,2048]{1,0:T(8,128)(2,1)} %get-tuple-element.129), channel_id=1, source_target_pairs={{0,1},{1,0},{2,3},{3,2},{4,5},{5,4},{6,7},{7,6},{8,9},{9,8},{10,11... | collective-permute-start | bytes 786440 | tf_op jit(solution)/shard_map/ppermute | solution.py:485
  48.0 22.7 %collective-permute-start.14 = (bf16[1,2048,768]{2,1,0:T(8,128)(2,1)}, bf16[1,2048,768]{2,1,0:T(8,128)(2,1)}, u32[]{:S(2)}, u32[]{:S(2)}) collective-permute-start(bf16[1,2048,768]{2,1,0:T(8,128)(2,1)} %pad_maximum_fusion), channel_id=1, source_target_pairs={{0,16},{16,0},{1,17},{17,1},{2,18},{18,2},{3,19},{19,3},{4,20},{20... | collective-permute-start | bytes 9437192 | tf_op jit(solution)/shard_map/ppermute | solution.py:498
  48.0 15.0 %collective-permute-start.7 = (bf16[64,4224]{1,0:T(8,128)(2,1)}, bf16[64,4224]{1,0:T(8,128)(2,1)}, u32[]{:S(2)}, u32[]{:S(2)}) collective-permute-start(bf16[64,4224]{1,0:T(8,128)(2,1)} %collective-permute-done.5.refs_2_.refs_4_), channel_id=1, source_target_pairs={{0,4},{1,5},{2,6},{3,7},{4,0},{5,1},{6,2},{7,3},{8,12},{9,13},{10,... | collective-permute-start | bytes 1622024 | tf_op jit(solution)/shard_map/ppermute | solution.py:435
  49.7 17.4 %collective-permute-start.11 = (bf16[96,2048]{1,0:T(8,128)(2,1)}, bf16[96,2048]{1,0:T(8,128)(2,1)}, u32[]{:S(2)}, u32[]{:S(2)}) collective-permute-start(bf16[96,2048]{1,0:T(8,128)(2,1)} %get-tuple-element.145), channel_id=1, source_target_pairs={{0,1},{1,0},{2,3},{3,2},{4,5},{5,4},{6,7},{7,6},{8,9},{9,8},{10,11... | collective-permute-start | bytes 1179656 | tf_op jit(solution)/shard_map/ppermute | solution.py:485
  50.9 18.1 %collective-permute-start.12 = (bf16[96,2048]{1,0:T(8,128)(2,1)}, bf16[96,2048]{1,0:T(8,128)(2,1)}, u32[]{:S(2)}, u32[]{:S(2)}) collective-permute-start(bf16[96,2048]{1,0:T(8,128)(2,1)} %get-tuple-element.146), channel_id=1, source_target_pairs={{0,2},{1,3},{2,0},{3,1},{4,6},{5,7},{6,4},{7,5},{8,10},{9,11},{10,... | collective-permute-start | bytes 1179656 | tf_op jit(solution)/shard_map/ppermute | solution.py:485
  51.8 18.9 %collective-permute-start.13 = (bf16[96,2048]{1,0:T(8,128)(2,1)}, bf16[96,2048]{1,0:T(8,128)(2,1)}, u32[]{:S(2)}, u32[]{:S(2)}) collective-permute-start(bf16[96,2048]{1,0:T(8,128)(2,1)} %get-tuple-element.147), channel_id=1, source_target_pairs={{0,3},{1,2},{2,1},{3,0},{4,7},{5,6},{6,5},{7,4},{8,11},{9,10},{10,... | collective-permute-start | bytes 1179656 | tf_op jit(solution)/shard_map/ppermute | solution.py:485
  70.7 19.2 %collective-permute-start.16 = (bf16[96,2048]{1,0:T(8,128)(2,1)}, bf16[96,2048]{1,0:T(8,128)(2,1)}, u32[]{:S(2)}, u32[]{:S(2)}) collective-permute-start(bf16[96,2048]{1,0:T(8,128)(2,1)} %get-tuple-element.163), channel_id=1, source_target_pairs={{0,1},{1,0},{2,3},{3,2},{4,5},{5,4},{6,7},{7,6},{8,9},{9,8},{10,11... | collective-permute-start | bytes 1179656 | tf_op jit(solution)/shard_map/ppermute | solution.py:485
  71.5 19.9 %collective-permute-start.17 = (bf16[96,2048]{1,0:T(8,128)(2,1)}, bf16[96,2048]{1,0:T(8,128)(2,1)}, u32[]{:S(2)}, u32[]{:S(2)}) collective-permute-start(bf16[96,2048]{1,0:T(8,128)(2,1)} %get-tuple-element.164), channel_id=1, source_target_pairs={{0,2},{1,3},{2,0},{3,1},{4,6},{5,7},{6,4},{7,5},{8,10},{9,11},{10,... | collective-permute-start | bytes 1179656 | tf_op jit(solution)/shard_map/ppermute | solution.py:485
  73.0 18.5 %collective-permute-start.18 = (bf16[96,2048]{1,0:T(8,128)(2,1)}, bf16[96,2048]{1,0:T(8,128)(2,1)}, u32[]{:S(2)}, u32[]{:S(2)}) collective-permute-start(bf16[96,2048]{1,0:T(8,128)(2,1)} %get-tuple-element.165), channel_id=1, source_target_pairs={{0,3},{1,2},{2,1},{3,0},{4,7},{5,6},{6,5},{7,4},{8,11},{9,10},{10,... | collective-permute-start | bytes 1179656 | tf_op jit(solution)/shard_map/ppermute | solution.py:485
  87.5 16.3 %collective-permute-start.19 = (bf16[96,2176]{1,0:T(8,128)(2,1)}, bf16[96,2176]{1,0:T(8,128)(2,1)}, u32[]{:S(2)}, u32[]{:S(2)}) collective-permute-start(bf16[96,2176]{1,0:T(8,128)(2,1)} %get-tuple-element.178), channel_id=1, source_target_pairs={{0,1},{1,0},{2,3},{3,2},{4,5},{5,4},{6,7},{7,6},{8,9},{9,8},{10,11... | collective-permute-start | bytes 1253384 | tf_op jit(solution)/shard_map/ppermute | solution.py:485
  88.4 20.8 %collective-permute-start.20 = (bf16[96,2176]{1,0:T(8,128)(2,1)}, bf16[96,2176]{1,0:T(8,128)(2,1)}, u32[]{:S(2)}, u32[]{:S(2)}) collective-permute-start(bf16[96,2176]{1,0:T(8,128)(2,1)} %get-tuple-element.179), channel_id=1, source_target_pairs={{0,2},{1,3},{2,0},{3,1},{4,6},{5,7},{6,4},{7,5},{8,10},{9,11},{10,... | collective-permute-start | bytes 1253384 | tf_op jit(solution)/shard_map/ppermute | solution.py:485
  89.9 19.7 %collective-permute-start.21 = (bf16[96,2176]{1,0:T(8,128)(2,1)}, bf16[96,2176]{1,0:T(8,128)(2,1)}, u32[]{:S(2)}, u32[]{:S(2)}) collective-permute-start(bf16[96,2176]{1,0:T(8,128)(2,1)} %get-tuple-element.180), channel_id=1, source_target_pairs={{0,3},{1,2},{2,1},{3,0},{4,7},{5,6},{6,5},{7,4},{8,11},{9,10},{10,... | collective-permute-start | bytes 1253384 | tf_op jit(solution)/shard_map/ppermute | solution.py:485
  101.7 16.0 %collective-permute-start.22 = (bf16[48,2176]{1,0:T(8,128)(2,1)}, bf16[48,2176]{1,0:T(8,128)(2,1)}, u32[]{:S(2)}, u32[]{:S(2)}) collective-permute-start(bf16[48,2176]{1,0:T(8,128)(2,1)} %get-tuple-element.186), channel_id=1, source_target_pairs={{0,1},{1,0},{2,3},{3,2},{4,5},{5,4},{6,7},{7,6},{8,9},{9,8},{10,11... | collective-permute-start | bytes 626696 | tf_op jit(solution)/shard_map/ppermute | solution.py:485
  103.2 15.1 %collective-permute-start.23 = (bf16[48,2176]{1,0:T(8,128)(2,1)}, bf16[48,2176]{1,0:T(8,128)(2,1)}, u32[]{:S(2)}, u32[]{:S(2)}) collective-permute-start(bf16[48,2176]{1,0:T(8,128)(2,1)} %get-tuple-element.187), channel_id=1, source_target_pairs={{0,2},{1,3},{2,0},{3,1},{4,6},{5,7},{6,4},{7,5},{8,10},{9,11},{10,... | collective-permute-start | bytes 626696 | tf_op jit(solution)/shard_map/ppermute | solution.py:485
  103.9 14.5 %collective-permute-start.24 = (bf16[48,2176]{1,0:T(8,128)(2,1)}, bf16[48,2176]{1,0:T(8,128)(2,1)}, u32[]{:S(2)}, u32[]{:S(2)}) collective-permute-start(bf16[48,2176]{1,0:T(8,128)(2,1)} %get-tuple-element.188), channel_id=1, source_target_pairs={{0,3},{1,2},{2,1},{3,0},{4,7},{5,6},{6,5},{7,4},{8,11},{9,10},{10,... | collective-permute-start | bytes 626696 | tf_op jit(solution)/shard_map/ppermute | solution.py:485
  118.3 20.5 %collective-permute-start.29 = (bf16[1,2048,384]{2,1,0:T(8,128)(2,1)}, bf16[1,2048,384]{2,1,0:T(8,128)(2,1)}, u32[]{:S(2)}, u32[]{:S(2)}) collective-permute-start(bf16[1,2048,384]{2,1,0:T(8,128)(2,1)} %get-tuple-element.204), channel_id=1, source_target_pairs={{0,16},{16,0},{1,17},{17,1},{2,18},{18,2},{3,19},{19,3},{4,20},{20... | collective-permute-start | bytes 4718600 | tf_op jit(solution)/shard_map/ppermute | solution.py:580
  118.4 20.4 %collective-permute-start.30 = (bf16[1,384,2048]{2,1,0:T(8,128)(2,1)}, bf16[1,384,2048]{2,1,0:T(8,128)(2,1)}, u32[]{:S(2)}, u32[]{:S(2)}) collective-permute-start(bf16[1,384,2048]{2,1,0:T(8,128)(2,1)} %get-tuple-element.205), channel_id=1, source_target_pairs={{0,16},{16,0},{1,17},{17,1},{2,18},{18,2},{3,19},{19,3},{4,20},{20... | collective-permute-start | bytes 4718600 | tf_op jit(solution)/shard_map/ppermute | solution.py:580
  118.8 20.0 %collective-permute-start.28 = (bf16[1,2048,384]{2,1,0:T(8,128)(2,1)}, bf16[1,2048,384]{2,1,0:T(8,128)(2,1)}, u32[]{:S(2)}, u32[]{:S(2)}) collective-permute-start(bf16[1,2048,384]{2,1,0:T(8,128)(2,1)} %get-tuple-element.197.refs_17_), channel_id=1, source_target_pairs={{0,16},{16,0},{1,17},{17,1},{2,18},{18,2},{3,19},{19,3},{4,20},{20... | collective-permute-start | bytes 4718600 | tf_op jit(solution)/shard_map/ppermute | solution.py:580
  134.6 15.8 %collective-permute-start.27 = (bf16[64,2176]{1,0:T(8,128)(2,1)}, bf16[64,2176]{1,0:T(8,128)(2,1)}, u32[]{:S(2)}, u32[]{:S(2)}) collective-permute-start(bf16[64,2176]{1,0:T(8,128)(2,1)} %add_convert_fusion), channel_id=1, source_target_pairs={{0,8},{1,9},{2,10},{3,11},{4,12},{5,13},{6,14},{7,15},{8,0},{9,1},... | collective-permute-start | bytes 835592 | tf_op jit(solution)/shard_map/ppermute | solution.py:585
  137.5 13.5 %collective-permute-start.26 = (bf16[64,2176]{1,0:T(8,128)(2,1)}, bf16[64,2176]{1,0:T(8,128)(2,1)}, u32[]{:S(2)}, u32[]{:S(2)}) collective-permute-start(bf16[64,2176]{1,0:T(8,128)(2,1)} %get-tuple-element.201), channel_id=1, source_target_pairs={{0,4},{1,5},{2,6},{3,7},{4,0},{5,1},{6,2},{7,3},{8,12},{9,13},{10,... | collective-permute-start | bytes 835592 | tf_op jit(solution)/shard_map/ppermute | solution.py:585
  (7 other events, 58.3 us)

commit v11 on v10

--- a/solution.py
+++ b/solution.py
@@ -22,7 +22,7 @@
 NT = (((1,), (1,)), ((), ()))
 
 
-def params(megabytes=64):
+def params(megabytes=60):
     return pltpu.CompilerParams(vmem_limit_bytes=megabytes << 20)
 
 
@@ -54,6 +54,10 @@
         self.sizes = [b - a for a, b in self.spans]
         self.cands = 2 * self.outer - 1
         self.use = [self.used(*c) for c in self.chunks]
+        middle, end = width // 2, width + LANES
+        self.halves = [(0, 0, end), (1, 0, end)] + [
+            (r, a, b) for r in range(2, outer) for a, b in ((0, middle), (middle, end))
+        ]
         needed = set().union(*self.use)
         self.last = [
             max(i for i in needed if 0 < i < outer),
@@ -356,7 +360,8 @@
     blocks = refs[2 : 2 + plan.cands]
     at = 2 + plan.cands
     backs = refs[at : at + groups * inner]
-    outs = refs[-5 - len(homes) : -5]
+    outs = list(refs[at + groups * inner : -5])
+    outs = outs[len(outs) - len(plan.halves) :]
     held, metas, pick_s, sems, meta_sems = refs[-5:]
     copies, later, start = [], [], 0
     for i, b in enumerate(blocks):
@@ -380,22 +385,27 @@
     for c in later:
         c.wait()
     sums = jnp.dot(pick_s[...], held[...], preferred_element_type=F32).astype(BF)
-    for i in range(len(homes)):
-        outs[i][...] = sums[i * tok : (i + 1) * tok]
+    for o, (r, a, b) in zip(outs, plan.halves):
+        o[...] = sums[r * tok : (r + 1) * tok, a:b]
 
 
 def home_kernel(plan, count, *refs):
     parts = refs[:count]
     routes_ref, comb_ref, _, tok_o, comb_o = refs[count:]
     width, tok = plan.width, plan.tok
-    total = parts[0][...].astype(F32)
-    for p in parts[1:]:
-        total += p[...].astype(F32)
-    tok_o[...] = total[:, :width].astype(BF)
+    middle = width // 2
+    total = parts[0][...].astype(F32) + parts[1][...].astype(F32)
+    low, high = total[:, :middle], total[:, middle:]
+    for p in parts[2::2]:
+        low += p[...].astype(F32)
+    for p in parts[3::2]:
+        high += p[...].astype(F32)
+    tok_o[:, :middle] = low.astype(BF)
+    tok_o[:, middle:] = high[:, :middle].astype(BF)
     row = lax.broadcasted_iota(jnp.int32, (LANES, LANES), 0)
     col = lax.broadcasted_iota(jnp.int32, (LANES, LANES), 1)
     same = jnp.where(row == col, 1.0, 0.0).astype(BF)
-    found = total[:, width:].astype(BF)
+    found = high[:, width - middle :].astype(BF)
     found = lax.dot_general(same, found, NT, preferred_element_type=F32)
     kind = lax.broadcasted_iota(jnp.int32, (LANES, tok), 0)
     out = []
@@ -553,9 +563,9 @@
         slots = inner * sum(plan.sizes[:groups])
         return pl.pallas_call(
             functools.partial(spread_kernel, plan, homes, groups),
-            out_shape=[shape((tok, width + LANES), BF)] * len(homes),
+            out_shape=[shape((tok, b - a), BF) for _, a, b in plan.halves],
             in_specs=[SMEM, VMEM] + [ANY] * (plan.cands + groups * inner + len(extra)),
-            out_specs=[VMEM] * len(homes),
+            out_specs=[VMEM] * len(plan.halves),
             scratch_shapes=[
                 pltpu.VMEM((slots, width + LANES), BF),
                 pltpu.VMEM((plan.cands, tok, LANES), BF),
@@ -578,21 +588,26 @@
     backs = backs + cross(more[3:])
     mine, backs = lax.optimization_barrier((mine, backs))
     theirs = [lax.ppermute(w, "dp", swap) for w in mine]
-    sums = dict(enumerate(spread(list(range(outer)), 2, [mine[0]])))
-    came, bit = [], 1
+    cut = spread(list(range(outer)), 2, [mine[0]])
+    sums = {(r, a): part for (r, a, b), part in zip(plan.halves, cut)}
+    came, bit, starts = [], 1, (0, width // 2)
     while bit < outer:
         for r in range(outer - bit, 0, -2 * bit):
-            sent = lax.ppermute(sums[r], "expert", plan.flip(bit))
-            if r == bit:
-                came.append(sent)
+            if r == 1:
+                came.append(lax.ppermute(sums[1, 0], "expert", plan.flip(1)))
                 continue
-            if bit == 1:
-                sums[1], sent = lax.optimization_barrier((sums[1], sent))
-            total = sums[r - bit].astype(F32) + sent.astype(F32)
-            sums[r - bit] = total.astype(BF)
+            for a in starts:
+                sent = lax.ppermute(sums[r, a], "expert", plan.flip(bit))
+                if r == bit:
+                    came.append(sent)
+                    continue
+                if bit == 1:
+                    sums[1, 0], sent = lax.optimization_barrier((sums[1, 0], sent))
+                total = sums[r - bit, a].astype(F32) + sent.astype(F32)
+                sums[r - bit, a] = total.astype(BF)
         bit *= 2
     grads = weight_grads(True, theirs)
-    home = [sums[0]] + came
+    home = [sums[0, 0]] + came
     grad_tokens, grad_combine = pl.pallas_call(
         functools.partial(home_kernel, plan, len(home)),
         out_shape=[shape((tok, width), BF), shape((plan.top, tok), BF)],

time: 154 us -> 146 us (0.948)
  waiting for transfers between devices: 39.6 us -> 29.4 us
  local copies, waits for them, and re-layouts: 1.2 us -> 7.33 us
  starting transfers between devices: 41.9 us -> 38.6 us
    ppermute x3 -> x5, waiting for transfers between devices: 11.5 us -> 4.73 us  [the longest x4 4.73 us: on_device(): sent = lax.ppermute(sums[r, a], 'expert', plan.flip(bit))]
    unnamed x0 -> x54, local copies, waits for them, and re-layouts: none -> 6.13 us
    ppermute x5, starting transfers between devices: 15 us -> 10 us  [hop(): blocks[i] = lax.ppermute(before, 'expert', plan.exchange(r, chain))]
    ppermute x18, waiting for transfers between devices: 16 us -> 13.7 us  [cross(): lax.ppermute(arrays[d], 'expert', plan.across(d))]
    ppermute x3 -> x5, starting transfers between devices: 4.89 us -> 6.71 us  [the longest x4 5.51 us: on_device(): sent = lax.ppermute(sums[r, a], 'expert', plan.flip(bit))]
  transfers between devices with their start and end apart: 31 -> 33, of which waited for: 16 -> 10; matrix products, arithmetic and copies ran while one was open for 4% -> 4% of each run, Pallas kernels for 39% -> 41%
where the time goes in v11:
time: 146 us
  Pallas kernels  64.3 us (44%)
  starting transfers between devices  38.6 us (26%)
  waiting for transfers between devices  29.4 us (20%)
  local copies, waits for them, and re-layouts  7.33 us (5%)
  other arithmetic  5.23 us (4%)
    pallas_call x2, Pallas kernels, expert(): pl.pallas_call(functools.partial(expert_kernel, plan, g), out_shape=[shap...  23.3 us
    ppermute x18, starting transfers between devices, cross(): lax.ppermute(arrays[d], 'expert', plan.across(d))  21.3 us
    pallas_call x2, Pallas kernels, weight_grads(): pl.pallas_call(functools.partial(weight_kernel, plan, own, len(extra)), o...  17.3 us
    pallas_call x4, Pallas kernels, compact(): pl.pallas_call(functools.partial(compact_kernel, plan, c), out_shape=[sha...  14.4 us
    ppermute x18, waiting for transfers between devices, cross(): lax.ppermute(arrays[d], 'expert', plan.across(d))  13.7 us
    ppermute x5, waiting for transfers between devices, hop(): blocks[i] = lax.ppermute(before, 'expert', plan.exchange(r, chain))  10.8 us
    ppermute x5, starting transfers between devices, hop(): blocks[i] = lax.ppermute(before, 'expert', plan.exchange(r, chain))  10 us
    unnamed x54, local copies, waits for them, and re-layouts  6.13 us
  transfers between devices with their start and end apart: 33, of which 10 were waited for; matrix products, arithmetic and copies ran while one was open for 4% of the time, Pallas kernels for 41%

profile of v11, /device:TPU:0, one launch (start us, length us, event | category | flops | bytes accessed | tf_op | source)
XLA Modules:
  0.0 145.9 jit_solution(16038818359535726520)
XLA Ops:
  0.6 2.3 %pack.1.refs_2_.refs_8_ = bf16[64,4224]{1,0:T(8,128)(2,1)} custom-call(bf16[64,2048]{1,0:T(8,128)(2,1)} %tok_ref.1, bf16[64,2048]{1,0:T(8,128)(2,1)} %up_ref.1, s32[8,64]{1,0:T(8,128)} %bitcast.5, bf16[8,64]{1,0:T(8,128)(2,1)} %bitcast.7), custom_call_target="tpu_custom_call" | custom-call | flops 1000000 | bytes 1081344 | tf_op jit(solution)/shard_map/pack/pallas_call | solution.py:427
  2.9 1.7 %collective-permute-start.4 = (bf16[64,4224]{1,0:T(8,128)(2,1)}, bf16[64,4224]{1,0:T(8,128)(2,1)S(1)}, u32[]{:S(2)}, u32[]{:S(2)}) collective-permute-start(bf16[64,4224]{1,0:T(8,128)(2,1)} %pack.1.refs_2_.refs_8_), channel_id=1, source_target_pairs={{0,0},{1,1},{2,2},{3,3},{4,8},{5,9},{6,10},{7,11},{8,4},{9,5},{10,... | collective-permute-start | bytes 1622024 | tf_op jit(solution)/shard_map/ppermute | solution.py:445
  4.6 4.9 %collective-permute-start.3 = (bf16[64,4224]{1,0:T(8,128)(2,1)}, bf16[64,4224]{1,0:T(8,128)(2,1)S(1)}, u32[]{:S(2)}, u32[]{:S(2)}) collective-permute-start(bf16[64,4224]{1,0:T(8,128)(2,1)} %pack.1.refs_2_.refs_8_), channel_id=1, source_target_pairs={{0,4},{1,5},{2,6},{3,7},{4,0},{5,1},{6,2},{7,3},{8,12},{9,13},{10,... | collective-permute-start | bytes 1622024 | tf_op jit(solution)/shard_map/ppermute | solution.py:445
  10.7 3.0 %compact.4 = (bf16[32,2048]{1,0:T(8,128)(2,1)}, bf16[32,2048]{1,0:T(8,128)(2,1)}, bf16[32,2048]{1,0:T(8,128)(2,1)}, bf16[32,2048]{1,0:T(8,128)(2,1)}) custom-call(s32[15]{0:T(128)} %dynamic-slice_bitcast_fusion.refs_0_, s32[1,64]{1,0:T(1,128)} %constant.21.clone.refs_1_, bf16[64,4224]{1,0:T(8,128)(2,1)} %pack.1.refs_2_.refs_8_), custom_call_target="tpu_custom_call" | custom-call | flops 33554432 | bytes 540672 | tf_op jit(solution)/shard_map/compact/pallas_call | solution.py:454
  17.2 2.4 %collective-permute-done.refs_2_.refs_1_ = bf16[32,2048]{1,0:T(8,128)(2,1)S(1)} collective-permute-done((bf16[32,2048]{1,0:T(8,128)(2,1)}, bf16[32,2048]{1,0:T(8,128)(2,1)S(1)}, u32[]{:S(2)}, u32[]{:S(2)}) %collective-permute-start) | collective-permute-done | bytes 131104 | tf_op jit(solution)/shard_map/ppermute | solution.py:495
  19.7 3.5 %collective-permute-done.1.refs_3_.refs_2_ = bf16[32,2048]{1,0:T(8,128)(2,1)S(1)} collective-permute-done((bf16[32,2048]{1,0:T(8,128)(2,1)}, bf16[32,2048]{1,0:T(8,128)(2,1)S(1)}, u32[]{:S(2)}, u32[]{:S(2)}) %collective-permute-start.1) | collective-permute-done | bytes 131104 | tf_op jit(solution)/shard_map/ppermute | solution.py:495
  24.2 2.4 %collective-permute-start.6 = (bf16[64,4224]{1,0:T(8,128)(2,1)S(1)}, bf16[64,4224]{1,0:T(8,128)(2,1)S(1)}, u32[]{:S(2)}, u32[]{:S(2)}) collective-permute-start(bf16[64,4224]{1,0:T(8,128)(2,1)S(1)} %collective-permute-done.4.refs_3_.refs_4_.refs_6_), channel_id=1, source_target_pairs={{0,4},{1,5},{2,6},{3,7},{4,0},{5,1},{6,2},{7,3},{8,12},{9,13},{10,... | collective-permute-start | bytes 1622024 | tf_op jit(solution)/shard_map/ppermute | solution.py:445
  26.6 3.4 %compact.5 = (bf16[64,2048]{1,0:T(8,128)(2,1)}, bf16[64,2048]{1,0:T(8,128)(2,1)}, bf16[64,2048]{1,0:T(8,128)(2,1)}, bf16[64,2048]{1,0:T(8,128)(2,1)}) custom-call(s32[15]{0:T(128)} %dynamic-slice_bitcast_fusion.refs_0_, s32[1,128]{1,0:T(1,128)} %constant.22.clone.refs_1_, bf16[64,4224]{1,0:T(8,128)(2,1)} %pack.1.refs_2_.refs_8_, bf16[64,4224]{1,0:T(8,128)(2,1)} %copy-done.2), custom_call_target="tpu_custom_call" | custom-call | flops 134217728 | bytes 1081344 | tf_op jit(solution)/shard_map/compact/pallas_call | solution.py:454
  33.5 3.3 %pad_maximum_fusion = bf16[1,2048,768]{2,1,0:T(8,128)(2,1)} fusion(bf16[1,2048,384]{2,1,0:T(8,128)(2,1)} %refs_6_.1, bf16[1,2048,384]{2,1,0:T(8,128)(2,1)S(1)} %copy-done.5), kind=kLoop, calls=%fused_computation | loop fusion | flops 6291456 | bytes 6291456 | tf_op jit(solution)/shard_map/concatenate | solution.py:437
  37.7 3.9 %compact.6 = (bf16[96,2048]{1,0:T(8,128)(2,1)}, bf16[96,2048]{1,0:T(8,128)(2,1)}, bf16[96,2048]{1,0:T(8,128)(2,1)}, bf16[96,2048]{1,0:T(8,128)(2,1)}) custom-call(s32[15]{0:T(128)} %dynamic-slice_bitcast_fusion.refs_0_, s32[1,192]{1,0:T(1,128)} %constant.23.clone.refs_1_, bf16[64,4224]{1,0:T(8,128)(2,1)} %copy-done.2, bf16[64,4224]{1,0:T(8,128)(2,1)} %copy-done, ...), custom_call_target="tpu_custom_call" | custom-call | flops 301989888 | bytes 1622016 | tf_op jit(solution)/shard_map/compact/pallas_call | solution.py:454
  43.4 1.7 %collective-permute-start.11 = (bf16[96,2048]{1,0:T(8,128)(2,1)}, bf16[96,2048]{1,0:T(8,128)(2,1)S(1)}, u32[]{:S(2)}, u32[]{:S(2)}) collective-permute-start(bf16[96,2048]{1,0:T(8,128)(2,1)} %get-tuple-element.149), channel_id=1, source_target_pairs={{0,1},{1,0},{2,3},{3,2},{4,5},{5,4},{6,7},{7,6},{8,9},{9,8},{10,11... | collective-permute-start | bytes 1179656 | tf_op jit(solution)/shard_map/ppermute | solution.py:495
  46.9 10.8 %collective-permute-done.7.refs_3_.refs_5_ = bf16[64,4224]{1,0:T(8,128)(2,1)S(1)} collective-permute-done((bf16[64,4224]{1,0:T(8,128)(2,1)S(1)}, bf16[64,4224]{1,0:T(8,128)(2,1)S(1)}, u32[]{:S(2)}, u32[]{:S(2)}) %collective-permute-start.7) | collective-permute-done | bytes 540704 | tf_op jit(solution)/shard_map/ppermute | solution.py:445
  58.5 4.1 %compact.7 = (bf16[96,2048]{1,0:T(8,128)(2,1)}, bf16[96,2048]{1,0:T(8,128)(2,1)}, bf16[96,2048]{1,0:T(8,128)(2,1)}, bf16[96,2048]{1,0:T(8,128)(2,1)}) custom-call(s32[15]{0:T(128)} %dynamic-slice_bitcast_fusion.refs_0_, s32[1,192]{1,0:T(1,128)} %constant.24.clone.refs_1_, bf16[64,4224]{1,0:T(8,128)(2,1)} %copy-done.3, bf16[64,4224]{1,0:T(8,128)(2,1)} %copy-done.4, ...), custom_call_target="tpu_custom_call" | custom-call | flops 402653184 | bytes 2162688 | tf_op jit(solution)/shard_map/compact/pallas_call | solution.py:454
  62.7 1.9 %collective-permute-done.12.refs_11_.refs_10_ = bf16[96,2048]{1,0:T(8,128)(2,1)S(1)} collective-permute-done((bf16[96,2048]{1,0:T(8,128)(2,1)}, bf16[96,2048]{1,0:T(8,128)(2,1)S(1)}, u32[]{:S(2)}, u32[]{:S(2)}) %collective-permute-start.12) | collective-permute-done | bytes 393248 | tf_op jit(solution)/shard_map/ppermute | solution.py:495
  68.5 13.1 %expert.2 = (bf16[384,768]{1,0:T(8,128)(2,1)}, bf16[384,768]{1,0:T(8,128)(2,1)}, bf16[384,768]{1,0:T(8,128)(2,1)}, bf16[96,2176]{1,0:T(8,128)(2,1)}, bf16[96,217...) custom-call(s32[15]{0:T(128)} %dynamic-slice_bitcast_fusion.refs_0_, ...), custom_call_target="tpu_custom_call" | custom-call | flops 6039797760 | bytes 9437184 | tf_op jit(solution)/shard_map/expert/pallas_call | solution.py:473
  83.5 1.6 %collective-permute-start.21 = (bf16[96,2176]{1,0:T(8,128)(2,1)}, bf16[96,2176]{1,0:T(8,128)(2,1)S(1)}, u32[]{:S(2)}, u32[]{:S(2)}) collective-permute-start(bf16[96,2176]{1,0:T(8,128)(2,1)} %get-tuple-element.184), channel_id=1, source_target_pairs={{0,3},{1,2},{2,1},{3,0},{4,7},{5,6},{6,5},{7,4},{8,11},{9,10},{10,... | collective-permute-start | bytes 1253384 | tf_op jit(solution)/shard_map/ppermute | solution.py:495
  86.6 10.2 %expert.3 = (bf16[192,768]{1,0:T(8,128)(2,1)}, bf16[192,768]{1,0:T(8,128)(2,1)}, bf16[192,768]{1,0:T(8,128)(2,1)}, bf16[48,2176]{1,0:T(8,128)(2,1)}, bf16[48,217...) custom-call(s32[15]{0:T(128)} %dynamic-slice_bitcast_fusion.refs_0_, ...), custom_call_target="tpu_custom_call" | custom-call | flops 3019898880 | bytes 9437184 | tf_op jit(solution)/shard_map/expert/pallas_call | solution.py:473
  100.4 3.7 %collective-permute-done.21.refs_24_.refs_12_ = bf16[96,2176]{1,0:T(8,128)(2,1)S(1)} collective-permute-done((bf16[96,2176]{1,0:T(8,128)(2,1)}, bf16[96,2176]{1,0:T(8,128)(2,1)S(1)}, u32[]{:S(2)}, u32[]{:S(2)}) %collective-permute-start.21) | collective-permute-done | bytes 417824 | tf_op jit(solution)/shard_map/ppermute | solution.py:495
  104.9 8.1 %weight_grads.2 = (bf16[1,2048,384]{2,1,0:T(8,128)(2,1)}, bf16[1,2048,384]{2,1,0:T(8,128)(2,1)}, bf16[1,384,2048]{2,1,0:T(8,128)(2,1)}) custom-call(bf16[32,2048]{1,0:T(8,128)(2,1)} %get-tuple-element.128.refs_1_.refs_0_, bf16[32,2048]{1,0:T(8,128)(2,1)} %copy-done.23, bf16[32,2048]{1,0:T(8,128)(2,1)} %copy-done.24, bf16[32,2048]{1,0:T(8,128)(2,1)} %copy-done.25, ...), custom_call_target="tpu_custom_call" | custom-call | flops 2717908992 | bytes 6488064 | tf_op jit(solution)/shard_map/weight_grads/pallas_call | solution.py:537
  114.3 4.8 %spread.1 = (bf16[64,2176]{1,0:T(8,128)(2,1)}, bf16[64,2176]{1,0:T(8,128)(2,1)}, bf16[64,1024]{1,0:T(8,128)(2,1)}, bf16[64,1152]{1,0:T(8,128)(2,1)}, bf16[64,1024]{1,0:T(8,128)(2,1)}, /*index=5*/bf16[64,1152]{1,0:T(8,128)(2,1)}) custom-call(s32[15]{0:T(128)} %dynamic-slice_bitcast_fusion.refs_0_, s32[1,576]{1,0:T(1,128)} %constant.25.clone.refs_1_, ...), custom_call_target="tpu_custom_call" | custom-call | flops 603979776 | bytes 2359296 | tf_op jit(solution)/shard_map/spread/pallas_call | solution.py:564
  121.2 4.5 %collective-permute-done.25 = bf16[64,1024]{1,0:T(8,128)(2,1)S(1)} collective-permute-done((bf16[64,1024]{1,0:T(8,128)(2,1)}, bf16[64,1024]{1,0:T(8,128)(2,1)S(1)}, u32[]{:S(2)}, u32[]{:S(2)}) %collective-permute-start.25) | collective-permute-done | bytes 131104 | tf_op jit(solution)/shard_map/ppermute | solution.py:600
  130.6 1.8 %collective-permute-start.29 = (bf16[64,1152]{1,0:T(8,128)(2,1)S(1)}, bf16[64,1152]{1,0:T(8,128)(2,1)S(1)}, u32[]{:S(2)}, u32[]{:S(2)}) collective-permute-start(bf16[64,1152]{1,0:T(8,128)(2,1)S(1)} %add_convert_fusion), channel_id=1, source_target_pairs={{0,8},{1,9},{2,10},{3,11},{4,12},{5,13},{6,14},{7,15},{8,0},{9,1},... | collective-permute-start | bytes 442376 | tf_op jit(solution)/shard_map/ppermute | solution.py:600
  133.6 9.2 %weight_grads.3 = (bf16[1,2048,384]{2,1,0:T(8,128)(2,1)}, bf16[1,2048,384]{2,1,0:T(8,128)(2,1)}, bf16[1,384,2048]{2,1,0:T(8,128)(2,1)}) custom-call(bf16[32,2048]{1,0:T(8,128)(2,1)} %get-tuple-element.128.refs_1_.refs_0_, bf16[32,2048]{1,0:T(8,128)(2,1)} %copy-done.23, bf16[32,2048]{1,0:T(8,128)(2,1)} %copy-done.24, bf16[32,2048]{1,0:T(8,128)(2,1)} %copy-done.25, ...), custom_call_target="tpu_custom_call" | custom-call | flops 2717908992 | bytes 6488064 | tf_op jit(solution)/shard_map/weight_grads/pallas_call | solution.py:537
  143.7 2.2 %home.1 = (bf16[64,2048]{1,0:T(8,128)(2,1)}, bf16[8,64]{1,0:T(8,128)(2,1)}) custom-call(bf16[64,2176]{1,0:T(8,128)(2,1)} %get-tuple-element.202.refs_0_, bf16[64,2176]{1,0:T(8,128)(2,1)} %copy-done.17, bf16[64,1024]{1,0:T(8,128)(2,1)} %copy-done.26, bf16[64,1152]{1,0:T(8,128)(2,1)} %copy-done.22, s32[8,64]{1,0:T(8,128)} %bitcast.6, bf16[8,64]{1,0:T(8,128)(2,1)} %bitcast.8, ...), custom_call_target="tpu_custom_call" | custom-call | flops 1000000 | bytes 1310720 | tf_op jit(solution)/shard_map/home/pallas_call | solution.py:611
  (111 shorter events, 36.3 us)
Async XLA Ops:
  2.9 20.3 %collective-permute-start.4 = (bf16[64,4224]{1,0:T(8,128)(2,1)}, bf16[64,4224]{1,0:T(8,128)(2,1)S(1)}, u32[]{:S(2)}, u32[]{:S(2)}) collective-permute-start(bf16[64,4224]{1,0:T(8,128)(2,1)} %pack.1.refs_2_.refs_8_), channel_id=1, source_target_pairs={{0,0},{1,1},{2,2},{3,3},{4,8},{5,9},{6,10},{7,11},{8,4},{9,5},{10,... | collective-permute-start | bytes 1622024 | tf_op jit(solution)/shard_map/ppermute | solution.py:445
  4.6 18.6 %collective-permute-start.3 = (bf16[64,4224]{1,0:T(8,128)(2,1)}, bf16[64,4224]{1,0:T(8,128)(2,1)S(1)}, u32[]{:S(2)}, u32[]{:S(2)}) collective-permute-start(bf16[64,4224]{1,0:T(8,128)(2,1)} %pack.1.refs_2_.refs_8_), channel_id=1, source_target_pairs={{0,4},{1,5},{2,6},{3,7},{4,0},{5,1},{6,2},{7,3},{8,12},{9,13},{10,... | collective-permute-start | bytes 1622024 | tf_op jit(solution)/shard_map/ppermute | solution.py:445
  23.3 13.6 %collective-permute-start.5 = (bf16[64,4224]{1,0:T(8,128)(2,1)S(1)}, bf16[64,4224]{1,0:T(8,128)(2,1)S(1)}, u32[]{:S(2)}, u32[]{:S(2)}) collective-permute-start(bf16[64,4224]{1,0:T(8,128)(2,1)S(1)} %collective-permute-done.3.refs_3_.refs_2_), channel_id=1, source_target_pairs={{0,0},{1,1},{2,2},{3,3},{4,8},{5,9},{6,10},{7,11},{8,4},{9,5},{10,... | collective-permute-start | bytes 1622024 | tf_op jit(solution)/shard_map/ppermute | solution.py:445
  24.2 12.7 %collective-permute-start.6 = (bf16[64,4224]{1,0:T(8,128)(2,1)S(1)}, bf16[64,4224]{1,0:T(8,128)(2,1)S(1)}, u32[]{:S(2)}, u32[]{:S(2)}) collective-permute-start(bf16[64,4224]{1,0:T(8,128)(2,1)S(1)} %collective-permute-done.4.refs_3_.refs_4_.refs_6_), channel_id=1, source_target_pairs={{0,4},{1,5},{2,6},{3,7},{4,0},{5,1},{6,2},{7,3},{8,12},{9,13},{10,... | collective-permute-start | bytes 1622024 | tf_op jit(solution)/shard_map/ppermute | solution.py:445
  43.0 21.6 %collective-permute-start.14 = (bf16[1,2048,768]{2,1,0:T(8,128)(2,1)}, bf16[1,2048,768]{2,1,0:T(8,128)(2,1)}, u32[]{:S(2)}, u32[]{:S(2)}) collective-permute-start(bf16[1,2048,768]{2,1,0:T(8,128)(2,1)} %pad_maximum_fusion), channel_id=1, source_target_pairs={{0,16},{16,0},{1,17},{17,1},{2,18},{18,2},{3,19},{19,3},{4,20},{20... | collective-permute-start | bytes 9437192 | tf_op jit(solution)/shard_map/ppermute | solution.py:508
  43.0 14.7 %collective-permute-start.7 = (bf16[64,4224]{1,0:T(8,128)(2,1)S(1)}, bf16[64,4224]{1,0:T(8,128)(2,1)S(1)}, u32[]{:S(2)}, u32[]{:S(2)}) collective-permute-start(bf16[64,4224]{1,0:T(8,128)(2,1)S(1)} %collective-permute-done.5.refs_2_.refs_4_), channel_id=1, source_target_pairs={{0,4},{1,5},{2,6},{3,7},{4,0},{5,1},{6,2},{7,3},{8,12},{9,13},{10,... | collective-permute-start | bytes 1622024 | tf_op jit(solution)/shard_map/ppermute | solution.py:445
  43.4 19.3 %collective-permute-start.11 = (bf16[96,2048]{1,0:T(8,128)(2,1)}, bf16[96,2048]{1,0:T(8,128)(2,1)S(1)}, u32[]{:S(2)}, u32[]{:S(2)}) collective-permute-start(bf16[96,2048]{1,0:T(8,128)(2,1)} %get-tuple-element.149), channel_id=1, source_target_pairs={{0,1},{1,0},{2,3},{3,2},{4,5},{5,4},{6,7},{7,6},{8,9},{9,8},{10,11... | collective-permute-start | bytes 1179656 | tf_op jit(solution)/shard_map/ppermute | solution.py:495
  45.1 19.5 %collective-permute-start.12 = (bf16[96,2048]{1,0:T(8,128)(2,1)}, bf16[96,2048]{1,0:T(8,128)(2,1)S(1)}, u32[]{:S(2)}, u32[]{:S(2)}) collective-permute-start(bf16[96,2048]{1,0:T(8,128)(2,1)} %get-tuple-element.150), channel_id=1, source_target_pairs={{0,2},{1,3},{2,0},{3,1},{4,6},{5,7},{6,4},{7,5},{8,10},{9,11},{10,... | collective-permute-start | bytes 1179656 | tf_op jit(solution)/shard_map/ppermute | solution.py:495
  46.4 18.2 %collective-permute-start.13 = (bf16[96,2048]{1,0:T(8,128)(2,1)}, bf16[96,2048]{1,0:T(8,128)(2,1)S(1)}, u32[]{:S(2)}, u32[]{:S(2)}) collective-permute-start(bf16[96,2048]{1,0:T(8,128)(2,1)} %get-tuple-element.151), channel_id=1, source_target_pairs={{0,3},{1,2},{2,1},{3,0},{4,7},{5,6},{6,5},{7,4},{8,11},{9,10},{10,... | collective-permute-start | bytes 1179656 | tf_op jit(solution)/shard_map/ppermute | solution.py:495
  64.7 18.8 %collective-permute-start.16 = (bf16[96,2048]{1,0:T(8,128)(2,1)}, bf16[96,2048]{1,0:T(8,128)(2,1)S(1)}, u32[]{:S(2)}, u32[]{:S(2)}) collective-permute-start(bf16[96,2048]{1,0:T(8,128)(2,1)} %get-tuple-element.167), channel_id=1, source_target_pairs={{0,1},{1,0},{2,3},{3,2},{4,5},{5,4},{6,7},{7,6},{8,9},{9,8},{10,11... | collective-permute-start | bytes 1179656 | tf_op jit(solution)/shard_map/ppermute | solution.py:495
  65.8 19.4 %collective-permute-start.17 = (bf16[96,2048]{1,0:T(8,128)(2,1)}, bf16[96,2048]{1,0:T(8,128)(2,1)S(1)}, u32[]{:S(2)}, u32[]{:S(2)}) collective-permute-start(bf16[96,2048]{1,0:T(8,128)(2,1)} %get-tuple-element.168), channel_id=1, source_target_pairs={{0,2},{1,3},{2,0},{3,1},{4,6},{5,7},{6,4},{7,5},{8,10},{9,11},{10,... | collective-permute-start | bytes 1179656 | tf_op jit(solution)/shard_map/ppermute | solution.py:495
  66.6 19.2 %collective-permute-start.18 = (bf16[96,2048]{1,0:T(8,128)(2,1)}, bf16[96,2048]{1,0:T(8,128)(2,1)S(1)}, u32[]{:S(2)}, u32[]{:S(2)}) collective-permute-start(bf16[96,2048]{1,0:T(8,128)(2,1)} %get-tuple-element.169), channel_id=1, source_target_pairs={{0,3},{1,2},{2,1},{3,0},{4,7},{5,6},{6,5},{7,4},{8,11},{9,10},{10,... | collective-permute-start | bytes 1179656 | tf_op jit(solution)/shard_map/ppermute | solution.py:495
  81.6 17.8 %collective-permute-start.19 = (bf16[96,2176]{1,0:T(8,128)(2,1)}, bf16[96,2176]{1,0:T(8,128)(2,1)S(1)}, u32[]{:S(2)}, u32[]{:S(2)}) collective-permute-start(bf16[96,2176]{1,0:T(8,128)(2,1)} %get-tuple-element.182), channel_id=1, source_target_pairs={{0,1},{1,0},{2,3},{3,2},{4,5},{5,4},{6,7},{7,6},{8,9},{9,8},{10,11... | collective-permute-start | bytes 1253384 | tf_op jit(solution)/shard_map/ppermute | solution.py:495
  82.7 17.8 %collective-permute-start.20 = (bf16[96,2176]{1,0:T(8,128)(2,1)}, bf16[96,2176]{1,0:T(8,128)(2,1)S(1)}, u32[]{:S(2)}, u32[]{:S(2)}) collective-permute-start(bf16[96,2176]{1,0:T(8,128)(2,1)} %get-tuple-element.183), channel_id=1, source_target_pairs={{0,2},{1,3},{2,0},{3,1},{4,6},{5,7},{6,4},{7,5},{8,10},{9,11},{10,... | collective-permute-start | bytes 1253384 | tf_op jit(solution)/shard_map/ppermute | solution.py:495
  83.5 20.6 %collective-permute-start.21 = (bf16[96,2176]{1,0:T(8,128)(2,1)}, bf16[96,2176]{1,0:T(8,128)(2,1)S(1)}, u32[]{:S(2)}, u32[]{:S(2)}) collective-permute-start(bf16[96,2176]{1,0:T(8,128)(2,1)} %get-tuple-element.184), channel_id=1, source_target_pairs={{0,3},{1,2},{2,1},{3,0},{4,7},{5,6},{6,5},{7,4},{8,11},{9,10},{10,... | collective-permute-start | bytes 1253384 | tf_op jit(solution)/shard_map/ppermute | solution.py:495
  96.9 16.1 %collective-permute-start.22 = (bf16[48,2176]{1,0:T(8,128)(2,1)}, bf16[48,2176]{1,0:T(8,128)(2,1)S(1)}, u32[]{:S(2)}, u32[]{:S(2)}) collective-permute-start(bf16[48,2176]{1,0:T(8,128)(2,1)} %get-tuple-element.190), channel_id=1, source_target_pairs={{0,1},{1,0},{2,3},{3,2},{4,5},{5,4},{6,7},{7,6},{8,9},{9,8},{10,11... | collective-permute-start | bytes 626696 | tf_op jit(solution)/shard_map/ppermute | solution.py:495
  97.9 15.1 %collective-permute-start.23 = (bf16[48,2176]{1,0:T(8,128)(2,1)}, bf16[48,2176]{1,0:T(8,128)(2,1)S(1)}, u32[]{:S(2)}, u32[]{:S(2)}) collective-permute-start(bf16[48,2176]{1,0:T(8,128)(2,1)} %get-tuple-element.191), channel_id=1, source_target_pairs={{0,2},{1,3},{2,0},{3,1},{4,6},{5,7},{6,4},{7,5},{8,10},{9,11},{10,... | collective-permute-start | bytes 626696 | tf_op jit(solution)/shard_map/ppermute | solution.py:495
  99.4 13.7 %collective-permute-start.24 = (bf16[48,2176]{1,0:T(8,128)(2,1)}, bf16[48,2176]{1,0:T(8,128)(2,1)S(1)}, u32[]{:S(2)}, u32[]{:S(2)}) collective-permute-start(bf16[48,2176]{1,0:T(8,128)(2,1)} %get-tuple-element.192), channel_id=1, source_target_pairs={{0,3},{1,2},{2,1},{3,0},{4,7},{5,6},{6,5},{7,4},{8,11},{9,10},{10,... | collective-permute-start | bytes 626696 | tf_op jit(solution)/shard_map/ppermute | solution.py:495
  113.8 16.8 %collective-permute-start.31 = (bf16[1,2048,384]{2,1,0:T(8,128)(2,1)}, bf16[1,2048,384]{2,1,0:T(8,128)(2,1)S(1)}, u32[]{:S(2)}, u32[]{:S(2)}) collective-permute-start(bf16[1,2048,384]{2,1,0:T(8,128)(2,1)} %get-tuple-element.212), channel_id=1, source_target_pairs={{0,16},{16,0},{1,17},{17,1},{2,18},{18,2},{3,19},{19,3},{4,20},{20... | collective-permute-start | bytes 4718600 | tf_op jit(solution)/shard_map/ppermute | solution.py:590
  113.8 18.6 %collective-permute-start.32 = (bf16[1,384,2048]{2,1,0:T(8,128)(2,1)}, bf16[1,384,2048]{2,1,0:T(8,128)(2,1)S(1)}, u32[]{:S(2)}, u32[]{:S(2)}) collective-permute-start(bf16[1,384,2048]{2,1,0:T(8,128)(2,1)} %get-tuple-element.213), channel_id=1, source_target_pairs={{0,16},{16,0},{1,17},{17,1},{2,18},{18,2},{3,19},{19,3},{4,20},{20... | collective-permute-start | bytes 4718600 | tf_op jit(solution)/shard_map/ppermute | solution.py:590
  114.3 18.1 %collective-permute-start.30 = (bf16[1,2048,384]{2,1,0:T(8,128)(2,1)}, bf16[1,2048,384]{2,1,0:T(8,128)(2,1)}, u32[]{:S(2)}, u32[]{:S(2)}) collective-permute-start(bf16[1,2048,384]{2,1,0:T(8,128)(2,1)} %get-tuple-element.201.refs_17_), channel_id=1, source_target_pairs={{0,16},{16,0},{1,17},{17,1},{2,18},{18,2},{3,19},{19,3},{4,20},{20... | collective-permute-start | bytes 4718600 | tf_op jit(solution)/shard_map/ppermute | solution.py:590
  126.6 16.2 %collective-permute-start.28 = (bf16[64,1024]{1,0:T(8,128)(2,1)S(1)}, bf16[64,1024]{1,0:T(8,128)(2,1)S(1)}, u32[]{:S(2)}, u32[]{:S(2)}) collective-permute-start(bf16[64,1024]{1,0:T(8,128)(2,1)S(1)} %add_convert_fusion.1), channel_id=1, source_target_pairs={{0,8},{1,9},{2,10},{3,11},{4,12},{5,13},{6,14},{7,15},{8,0},{9,1},... | collective-permute-start | bytes 393224 | tf_op jit(solution)/shard_map/ppermute | solution.py:600
  128.5 14.4 %collective-permute-start.27 = (bf16[64,2176]{1,0:T(8,128)(2,1)}, bf16[64,2176]{1,0:T(8,128)(2,1)S(1)}, u32[]{:S(2)}, u32[]{:S(2)}) collective-permute-start(bf16[64,2176]{1,0:T(8,128)(2,1)} %get-tuple-element.207), channel_id=1, source_target_pairs={{0,4},{1,5},{2,6},{3,7},{4,0},{5,1},{6,2},{7,3},{8,12},{9,13},{10,... | collective-permute-start | bytes 835592 | tf_op jit(solution)/shard_map/ppermute | solution.py:597
  130.6 12.2 %collective-permute-start.29 = (bf16[64,1152]{1,0:T(8,128)(2,1)S(1)}, bf16[64,1152]{1,0:T(8,128)(2,1)S(1)}, u32[]{:S(2)}, u32[]{:S(2)}) collective-permute-start(bf16[64,1152]{1,0:T(8,128)(2,1)S(1)} %add_convert_fusion), channel_id=1, source_target_pairs={{0,8},{1,9},{2,10},{3,11},{4,12},{5,13},{6,14},{7,15},{8,0},{9,1},... | collective-permute-start | bytes 442376 | tf_op jit(solution)/shard_map/ppermute | solution.py:600
  (36 other events, 212.0 us)

commit v12 on v11

--- a/solution.py
+++ b/solution.py
@@ -554,7 +554,7 @@
                 pltpu.SemaphoreType.DMA((8,)),
                 *(grad_scratch if own else []),
             ],
-            compiler_params=params(),
+            compiler_params=params(64 if own else 60),
             cost_estimate=cost(6 * count * part * width, 4 * count * (width + hidden)),
             name="weight_grads",
         )(*got, *mids, *extra)

time: 146 us -> 145 us (level)
  local copies, waits for them, and re-layouts: 7.33 us -> 4.74 us
    unnamed x54 -> x44, local copies, waits for them, and re-layouts: 6.13 us -> 3.54 us
  transfers between devices with their start and end apart: 33 -> 33, of which waited for: 10 -> 10; matrix products, arithmetic and copies ran while one was open for 4% -> 5% of each run, Pallas kernels for 41% -> 42%
where the time goes in v12:
time: 145 us; the launch traced here: 144 us
  Pallas kernels  64.3 us (44%)
  starting transfers between devices  38 us (26%)
  waiting for transfers between devices  29.4 us (20%)
  other arithmetic  6.55 us (5%)
  local copies, waits for them, and re-layouts  4.74 us (3%)
    pallas_call x2, Pallas kernels, expert(): pl.pallas_call(functools.partial(expert_kernel, plan, g), out_shape=[shap...  23.4 us
    ppermute x18, starting transfers between devices, cross(): lax.ppermute(arrays[d], 'expert', plan.across(d))  21.3 us
    pallas_call x2, Pallas kernels, weight_grads(): pl.pallas_call(functools.partial(weight_kernel, plan, own, len(extra)), o...  17.3 us
    pallas_call x4, Pallas kernels, compact(): pl.pallas_call(functools.partial(compact_kernel, plan, c), out_shape=[sha...  14.4 us
    ppermute x18, waiting for transfers between devices, cross(): lax.ppermute(arrays[d], 'expert', plan.across(d))  13.7 us
    ppermute x5, waiting for transfers between devices, hop(): blocks[i] = lax.ppermute(before, 'expert', plan.exchange(r, chain))  10.8 us
    ppermute x5, starting transfers between devices, hop(): blocks[i] = lax.ppermute(before, 'expert', plan.exchange(r, chain))  10.1 us
    pallas_call x1, Pallas kernels, spread(): pl.pallas_call(functools.partial(spread_kernel, plan, homes, groups), out...  4.75 us
  transfers between devices with their start and end apart: 33, of which 10 were waited for; matrix products, arithmetic and copies ran while one was open for 5% of the time, Pallas kernels for 42%

profile of v12, /device:TPU:0, one launch (start us, length us, event | category | flops | bytes accessed | tf_op | source)
XLA Modules:
  0.0 143.9 jit_solution(9271379550596684875)
XLA Ops:
  0.6 2.2 %pack.1.refs_2_.refs_8_ = bf16[64,4224]{1,0:T(8,128)(2,1)} custom-call(bf16[64,2048]{1,0:T(8,128)(2,1)} %tok_ref.1, bf16[64,2048]{1,0:T(8,128)(2,1)} %up_ref.1, s32[8,64]{1,0:T(8,128)} %bitcast.5, bf16[8,64]{1,0:T(8,128)(2,1)} %bitcast.7), custom_call_target="tpu_custom_call" | custom-call | flops 1000000 | bytes 1081344 | tf_op jit(solution)/shard_map/pack/pallas_call | solution.py:427
  2.9 1.7 %collective-permute-start.4 = (bf16[64,4224]{1,0:T(8,128)(2,1)}, bf16[64,4224]{1,0:T(8,128)(2,1)S(1)}, u32[]{:S(2)}, u32[]{:S(2)}) collective-permute-start(bf16[64,4224]{1,0:T(8,128)(2,1)} %pack.1.refs_2_.refs_8_), channel_id=1, source_target_pairs={{0,0},{1,1},{2,2},{3,3},{4,8},{5,9},{6,10},{7,11},{8,4},{9,5},{10,... | collective-permute-start | bytes 1622024 | tf_op jit(solution)/shard_map/ppermute | solution.py:445
  4.6 4.9 %collective-permute-start.3 = (bf16[64,4224]{1,0:T(8,128)(2,1)}, bf16[64,4224]{1,0:T(8,128)(2,1)S(1)}, u32[]{:S(2)}, u32[]{:S(2)}) collective-permute-start(bf16[64,4224]{1,0:T(8,128)(2,1)} %pack.1.refs_2_.refs_8_), channel_id=1, source_target_pairs={{0,4},{1,5},{2,6},{3,7},{4,0},{5,1},{6,2},{7,3},{8,12},{9,13},{10,... | collective-permute-start | bytes 1622024 | tf_op jit(solution)/shard_map/ppermute | solution.py:445
  10.6 3.0 %compact.4 = (bf16[32,2048]{1,0:T(8,128)(2,1)}, bf16[32,2048]{1,0:T(8,128)(2,1)}, bf16[32,2048]{1,0:T(8,128)(2,1)}, bf16[32,2048]{1,0:T(8,128)(2,1)}) custom-call(s32[15]{0:T(128)} %dynamic-slice_bitcast_fusion.refs_0_, s32[1,64]{1,0:T(1,128)} %constant.21.clone.refs_1_, bf16[64,4224]{1,0:T(8,128)(2,1)} %pack.1.refs_2_.refs_8_), custom_call_target="tpu_custom_call" | custom-call | flops 33554432 | bytes 540672 | tf_op jit(solution)/shard_map/compact/pallas_call | solution.py:454
  17.2 2.4 %collective-permute-done.refs_2_.refs_1_ = bf16[32,2048]{1,0:T(8,128)(2,1)S(1)} collective-permute-done((bf16[32,2048]{1,0:T(8,128)(2,1)}, bf16[32,2048]{1,0:T(8,128)(2,1)S(1)}, u32[]{:S(2)}, u32[]{:S(2)}) %collective-permute-start) | collective-permute-done | bytes 131104 | tf_op jit(solution)/shard_map/ppermute | solution.py:495
  19.6 3.5 %collective-permute-done.1.refs_3_.refs_2_ = bf16[32,2048]{1,0:T(8,128)(2,1)S(1)} collective-permute-done((bf16[32,2048]{1,0:T(8,128)(2,1)}, bf16[32,2048]{1,0:T(8,128)(2,1)S(1)}, u32[]{:S(2)}, u32[]{:S(2)}) %collective-permute-start.1) | collective-permute-done | bytes 131104 | tf_op jit(solution)/shard_map/ppermute | solution.py:495
  24.1 2.4 %collective-permute-start.6 = (bf16[64,4224]{1,0:T(8,128)(2,1)S(1)}, bf16[64,4224]{1,0:T(8,128)(2,1)S(1)}, u32[]{:S(2)}, u32[]{:S(2)}) collective-permute-start(bf16[64,4224]{1,0:T(8,128)(2,1)S(1)} %collective-permute-done.4.refs_3_.refs_4_.refs_6_), channel_id=1, source_target_pairs={{0,4},{1,5},{2,6},{3,7},{4,0},{5,1},{6,2},{7,3},{8,12},{9,13},{10,... | collective-permute-start | bytes 1622024 | tf_op jit(solution)/shard_map/ppermute | solution.py:445
  26.6 3.4 %compact.5 = (bf16[64,2048]{1,0:T(8,128)(2,1)}, bf16[64,2048]{1,0:T(8,128)(2,1)}, bf16[64,2048]{1,0:T(8,128)(2,1)}, bf16[64,2048]{1,0:T(8,128)(2,1)}) custom-call(s32[15]{0:T(128)} %dynamic-slice_bitcast_fusion.refs_0_, s32[1,128]{1,0:T(1,128)} %constant.22.clone.refs_1_, bf16[64,4224]{1,0:T(8,128)(2,1)} %pack.1.refs_2_.refs_8_, bf16[64,4224]{1,0:T(8,128)(2,1)} %copy-done.2), custom_call_target="tpu_custom_call" | custom-call | flops 134217728 | bytes 1081344 | tf_op jit(solution)/shard_map/compact/pallas_call | solution.py:454
  33.5 3.3 %pad_maximum_fusion = bf16[1,2048,768]{2,1,0:T(8,128)(2,1)} fusion(bf16[1,2048,384]{2,1,0:T(8,128)(2,1)} %refs_6_.1, bf16[1,2048,384]{2,1,0:T(8,128)(2,1)S(1)} %copy-done.5), kind=kLoop, calls=%fused_computation | loop fusion | flops 6291456 | bytes 6291456 | tf_op jit(solution)/shard_map/concatenate | solution.py:437
  37.7 3.9 %compact.6 = (bf16[96,2048]{1,0:T(8,128)(2,1)}, bf16[96,2048]{1,0:T(8,128)(2,1)}, bf16[96,2048]{1,0:T(8,128)(2,1)}, bf16[96,2048]{1,0:T(8,128)(2,1)}) custom-call(s32[15]{0:T(128)} %dynamic-slice_bitcast_fusion.refs_0_, s32[1,192]{1,0:T(1,128)} %constant.23.clone.refs_1_, bf16[64,4224]{1,0:T(8,128)(2,1)} %copy-done.2, bf16[64,4224]{1,0:T(8,128)(2,1)} %copy-done, ...), custom_call_target="tpu_custom_call" | custom-call | flops 301989888 | bytes 1622016 | tf_op jit(solution)/shard_map/compact/pallas_call | solution.py:454
  43.4 1.6 %collective-permute-start.11 = (bf16[96,2048]{1,0:T(8,128)(2,1)}, bf16[96,2048]{1,0:T(8,128)(2,1)S(1)}, u32[]{:S(2)}, u32[]{:S(2)}) collective-permute-start(bf16[96,2048]{1,0:T(8,128)(2,1)} %get-tuple-element.149), channel_id=1, source_target_pairs={{0,1},{1,0},{2,3},{3,2},{4,5},{5,4},{6,7},{7,6},{8,9},{9,8},{10,11... | collective-permute-start | bytes 1179656 | tf_op jit(solution)/shard_map/ppermute | solution.py:495
  46.9 10.8 %collective-permute-done.7.refs_3_.refs_5_ = bf16[64,4224]{1,0:T(8,128)(2,1)S(1)} collective-permute-done((bf16[64,4224]{1,0:T(8,128)(2,1)S(1)}, bf16[64,4224]{1,0:T(8,128)(2,1)S(1)}, u32[]{:S(2)}, u32[]{:S(2)}) %collective-permute-start.7) | collective-permute-done | bytes 540704 | tf_op jit(solution)/shard_map/ppermute | solution.py:445
  58.5 4.1 %compact.7 = (bf16[96,2048]{1,0:T(8,128)(2,1)}, bf16[96,2048]{1,0:T(8,128)(2,1)}, bf16[96,2048]{1,0:T(8,128)(2,1)}, bf16[96,2048]{1,0:T(8,128)(2,1)}) custom-call(s32[15]{0:T(128)} %dynamic-slice_bitcast_fusion.refs_0_, s32[1,192]{1,0:T(1,128)} %constant.24.clone.refs_1_, bf16[64,4224]{1,0:T(8,128)(2,1)} %copy-done.3, bf16[64,4224]{1,0:T(8,128)(2,1)} %copy-done.4, ...), custom_call_target="tpu_custom_call" | custom-call | flops 402653184 | bytes 2162688 | tf_op jit(solution)/shard_map/compact/pallas_call | solution.py:454
  62.7 1.9 %collective-permute-done.12.refs_11_.refs_10_ = bf16[96,2048]{1,0:T(8,128)(2,1)S(1)} collective-permute-done((bf16[96,2048]{1,0:T(8,128)(2,1)}, bf16[96,2048]{1,0:T(8,128)(2,1)S(1)}, u32[]{:S(2)}, u32[]{:S(2)}) %collective-permute-start.12) | collective-permute-done | bytes 393248 | tf_op jit(solution)/shard_map/ppermute | solution.py:495
  68.4 13.1 %expert.2 = (bf16[384,768]{1,0:T(8,128)(2,1)}, bf16[384,768]{1,0:T(8,128)(2,1)}, bf16[384,768]{1,0:T(8,128)(2,1)}, bf16[96,2176]{1,0:T(8,128)(2,1)}, bf16[96,217...) custom-call(s32[15]{0:T(128)} %dynamic-slice_bitcast_fusion.refs_0_, ...), custom_call_target="tpu_custom_call" | custom-call | flops 6039797760 | bytes 9437184 | tf_op jit(solution)/shard_map/expert/pallas_call | solution.py:473
  86.6 10.2 %expert.3 = (bf16[192,768]{1,0:T(8,128)(2,1)}, bf16[192,768]{1,0:T(8,128)(2,1)}, bf16[192,768]{1,0:T(8,128)(2,1)}, bf16[48,2176]{1,0:T(8,128)(2,1)}, bf16[48,217...) custom-call(s32[15]{0:T(128)} %dynamic-slice_bitcast_fusion.refs_0_, ...), custom_call_target="tpu_custom_call" | custom-call | flops 3019898880 | bytes 9437184 | tf_op jit(solution)/shard_map/expert/pallas_call | solution.py:473
  100.4 3.7 %collective-permute-done.21.refs_24_.refs_12_ = bf16[96,2176]{1,0:T(8,128)(2,1)S(1)} collective-permute-done((bf16[96,2176]{1,0:T(8,128)(2,1)}, bf16[96,2176]{1,0:T(8,128)(2,1)S(1)}, u32[]{:S(2)}, u32[]{:S(2)}) %collective-permute-start.21) | collective-permute-done | bytes 417824 | tf_op jit(solution)/shard_map/ppermute | solution.py:495
  104.9 8.1 %weight_grads.2 = (bf16[1,2048,384]{2,1,0:T(8,128)(2,1)}, bf16[1,2048,384]{2,1,0:T(8,128)(2,1)}, bf16[1,384,2048]{2,1,0:T(8,128)(2,1)}) custom-call(bf16[32,2048]{1,0:T(8,128)(2,1)} %get-tuple-element.128.refs_1_.refs_0_, bf16[32,2048]{1,0:T(8,128)(2,1)} %copy-done.19, bf16[32,2048]{1,0:T(8,128)(2,1)} %copy-done.20, bf16[32,2048]{1,0:T(8,128)(2,1)} %copy-done.21, ...), custom_call_target="tpu_custom_call" | custom-call | flops 2717908992 | bytes 6488064 | tf_op jit(solution)/shard_map/weight_grads/pallas_call | solution.py:537
  113.9 4.7 %spread.1 = (bf16[64,2176]{1,0:T(8,128)(2,1)}, bf16[64,2176]{1,0:T(8,128)(2,1)}, bf16[64,1024]{1,0:T(8,128)(2,1)}, bf16[64,1152]{1,0:T(8,128)(2,1)}, bf16[64,1024]{1,0:T(8,128)(2,1)}, /*index=5*/bf16[64,1152]{1,0:T(8,128)(2,1)}) custom-call(s32[15]{0:T(128)} %dynamic-slice_bitcast_fusion.refs_0_, s32[1,576]{1,0:T(1,128)} %constant.25.clone.refs_1_, ...), custom_call_target="tpu_custom_call" | custom-call | flops 603979776 | bytes 2359296 | tf_op jit(solution)/shard_map/spread/pallas_call | solution.py:564
  120.7 4.5 %collective-permute-done.25 = bf16[64,1024]{1,0:T(8,128)(2,1)S(1)} collective-permute-done((bf16[64,1024]{1,0:T(8,128)(2,1)}, bf16[64,1024]{1,0:T(8,128)(2,1)S(1)}, u32[]{:S(2)}, u32[]{:S(2)}) %collective-permute-start.25) | collective-permute-done | bytes 131104 | tf_op jit(solution)/shard_map/ppermute | solution.py:600
  125.2 1.6 %add_convert_fusion.1 = bf16[64,1024]{1,0:T(8,128)(2,1)} fusion(bf16[64,1024]{1,0:T(8,128)(2,1)S(1)} %collective-permute-done.25, bf16[64,1024]{1,0:T(8,128)(2,1)} %get-tuple-element.208), kind=kLoop, calls=%fused_computation.2 | loop fusion | flops 262144 | bytes 393216 | tf_op jit(solution)/shard_map/convert_element_type | solution.py:607
  129.8 1.6 %add_convert_fusion = bf16[64,1152]{1,0:T(8,128)(2,1)} fusion(bf16[64,1152]{1,0:T(8,128)(2,1)S(1)} %collective-permute-done.26, bf16[64,1152]{1,0:T(8,128)(2,1)} %get-tuple-element.210), kind=kLoop, calls=%fused_computation.1 | loop fusion | flops 294912 | bytes 442368 | tf_op jit(solution)/shard_map/convert_element_type | solution.py:607
  132.4 9.2 %weight_grads.3 = (bf16[1,2048,384]{2,1,0:T(8,128)(2,1)}, bf16[1,2048,384]{2,1,0:T(8,128)(2,1)}, bf16[1,384,2048]{2,1,0:T(8,128)(2,1)}) custom-call(bf16[32,2048]{1,0:T(8,128)(2,1)} %get-tuple-element.128.refs_1_.refs_0_, bf16[32,2048]{1,0:T(8,128)(2,1)} %copy-done.19, bf16[32,2048]{1,0:T(8,128)(2,1)} %copy-done.20, bf16[32,2048]{1,0:T(8,128)(2,1)} %copy-done.21, ...), custom_call_target="tpu_custom_call" | custom-call | flops 2717908992 | bytes 6488064 | tf_op jit(solution)/shard_map/weight_grads/pallas_call | solution.py:537
  141.7 2.2 %home.1 = (bf16[64,2048]{1,0:T(8,128)(2,1)}, bf16[8,64]{1,0:T(8,128)(2,1)}) custom-call(bf16[64,2176]{1,0:T(8,128)(2,1)} %get-tuple-element.202.refs_0_, bf16[64,2176]{1,0:T(8,128)(2,1)} %collective-permute-done.27.refs_1_, bf16[64,1024]{1,0:T(8,128)(2,1)} %collective-permute-done.28.refs_2_, bf16[64,1152]{1,0:T(8,128)(2,1)} %collective-permute-done.29.refs_3_, ...), custom_call_target="tpu_custom_call" | custom-call | flops 1000000 | bytes 1310720 | tf_op jit(solution)/shard_map/home/pallas_call | solution.py:611
  (101 shorter events, 34.6 us)
Async XLA Ops:
  2.9 20.3 %collective-permute-start.4 = (bf16[64,4224]{1,0:T(8,128)(2,1)}, bf16[64,4224]{1,0:T(8,128)(2,1)S(1)}, u32[]{:S(2)}, u32[]{:S(2)}) collective-permute-start(bf16[64,4224]{1,0:T(8,128)(2,1)} %pack.1.refs_2_.refs_8_), channel_id=1, source_target_pairs={{0,0},{1,1},{2,2},{3,3},{4,8},{5,9},{6,10},{7,11},{8,4},{9,5},{10,... | collective-permute-start | bytes 1622024 | tf_op jit(solution)/shard_map/ppermute | solution.py:445
  4.6 18.6 %collective-permute-start.3 = (bf16[64,4224]{1,0:T(8,128)(2,1)}, bf16[64,4224]{1,0:T(8,128)(2,1)S(1)}, u32[]{:S(2)}, u32[]{:S(2)}) collective-permute-start(bf16[64,4224]{1,0:T(8,128)(2,1)} %pack.1.refs_2_.refs_8_), channel_id=1, source_target_pairs={{0,4},{1,5},{2,6},{3,7},{4,0},{5,1},{6,2},{7,3},{8,12},{9,13},{10,... | collective-permute-start | bytes 1622024 | tf_op jit(solution)/shard_map/ppermute | solution.py:445
  23.2 13.6 %collective-permute-start.5 = (bf16[64,4224]{1,0:T(8,128)(2,1)S(1)}, bf16[64,4224]{1,0:T(8,128)(2,1)S(1)}, u32[]{:S(2)}, u32[]{:S(2)}) collective-permute-start(bf16[64,4224]{1,0:T(8,128)(2,1)S(1)} %collective-permute-done.3.refs_3_.refs_2_), channel_id=1, source_target_pairs={{0,0},{1,1},{2,2},{3,3},{4,8},{5,9},{6,10},{7,11},{8,4},{9,5},{10,... | collective-permute-start | bytes 1622024 | tf_op jit(solution)/shard_map/ppermute | solution.py:445
  24.1 12.8 %collective-permute-start.6 = (bf16[64,4224]{1,0:T(8,128)(2,1)S(1)}, bf16[64,4224]{1,0:T(8,128)(2,1)S(1)}, u32[]{:S(2)}, u32[]{:S(2)}) collective-permute-start(bf16[64,4224]{1,0:T(8,128)(2,1)S(1)} %collective-permute-done.4.refs_3_.refs_4_.refs_6_), channel_id=1, source_target_pairs={{0,4},{1,5},{2,6},{3,7},{4,0},{5,1},{6,2},{7,3},{8,12},{9,13},{10,... | collective-permute-start | bytes 1622024 | tf_op jit(solution)/shard_map/ppermute | solution.py:445
  31.0 12.0 %collective-permute-start.9 = (bf16[64,2048]{1,0:T(8,128)(2,1)}, bf16[64,2048]{1,0:T(8,128)(2,1)}, u32[]{:S(2)}, u32[]{:S(2)}) collective-permute-start(bf16[64,2048]{1,0:T(8,128)(2,1)} %get-tuple-element.134), channel_id=1, source_target_pairs={{0,2},{1,3},{2,0},{3,1},{4,6},{5,7},{6,4},{7,5},{8,10},{9,11},{10,... | collective-permute-start | bytes 786440 | tf_op jit(solution)/shard_map/ppermute | solution.py:495
  43.0 21.6 %collective-permute-start.14 = (bf16[1,2048,768]{2,1,0:T(8,128)(2,1)}, bf16[1,2048,768]{2,1,0:T(8,128)(2,1)}, u32[]{:S(2)}, u32[]{:S(2)}) collective-permute-start(bf16[1,2048,768]{2,1,0:T(8,128)(2,1)} %pad_maximum_fusion), channel_id=1, source_target_pairs={{0,16},{16,0},{1,17},{17,1},{2,18},{18,2},{3,19},{19,3},{4,20},{20... | collective-permute-start | bytes 9437192 | tf_op jit(solution)/shard_map/ppermute | solution.py:508
  43.0 14.7 %collective-permute-start.7 = (bf16[64,4224]{1,0:T(8,128)(2,1)S(1)}, bf16[64,4224]{1,0:T(8,128)(2,1)S(1)}, u32[]{:S(2)}, u32[]{:S(2)}) collective-permute-start(bf16[64,4224]{1,0:T(8,128)(2,1)S(1)} %collective-permute-done.5.refs_2_.refs_4_), channel_id=1, source_target_pairs={{0,4},{1,5},{2,6},{3,7},{4,0},{5,1},{6,2},{7,3},{8,12},{9,13},{10,... | collective-permute-start | bytes 1622024 | tf_op jit(solution)/shard_map/ppermute | solution.py:445
  43.4 19.3 %collective-permute-start.11 = (bf16[96,2048]{1,0:T(8,128)(2,1)}, bf16[96,2048]{1,0:T(8,128)(2,1)S(1)}, u32[]{:S(2)}, u32[]{:S(2)}) collective-permute-start(bf16[96,2048]{1,0:T(8,128)(2,1)} %get-tuple-element.149), channel_id=1, source_target_pairs={{0,1},{1,0},{2,3},{3,2},{4,5},{5,4},{6,7},{7,6},{8,9},{9,8},{10,11... | collective-permute-start | bytes 1179656 | tf_op jit(solution)/shard_map/ppermute | solution.py:495
  45.0 19.5 %collective-permute-start.12 = (bf16[96,2048]{1,0:T(8,128)(2,1)}, bf16[96,2048]{1,0:T(8,128)(2,1)S(1)}, u32[]{:S(2)}, u32[]{:S(2)}) collective-permute-start(bf16[96,2048]{1,0:T(8,128)(2,1)} %get-tuple-element.150), channel_id=1, source_target_pairs={{0,2},{1,3},{2,0},{3,1},{4,6},{5,7},{6,4},{7,5},{8,10},{9,11},{10,... | collective-permute-start | bytes 1179656 | tf_op jit(solution)/shard_map/ppermute | solution.py:495
  46.4 18.2 %collective-permute-start.13 = (bf16[96,2048]{1,0:T(8,128)(2,1)}, bf16[96,2048]{1,0:T(8,128)(2,1)S(1)}, u32[]{:S(2)}, u32[]{:S(2)}) collective-permute-start(bf16[96,2048]{1,0:T(8,128)(2,1)} %get-tuple-element.151), channel_id=1, source_target_pairs={{0,3},{1,2},{2,1},{3,0},{4,7},{5,6},{6,5},{7,4},{8,11},{9,10},{10,... | collective-permute-start | bytes 1179656 | tf_op jit(solution)/shard_map/ppermute | solution.py:495
  64.7 18.9 %collective-permute-start.16 = (bf16[96,2048]{1,0:T(8,128)(2,1)}, bf16[96,2048]{1,0:T(8,128)(2,1)S(1)}, u32[]{:S(2)}, u32[]{:S(2)}) collective-permute-start(bf16[96,2048]{1,0:T(8,128)(2,1)} %get-tuple-element.167), channel_id=1, source_target_pairs={{0,1},{1,0},{2,3},{3,2},{4,5},{5,4},{6,7},{7,6},{8,9},{9,8},{10,11... | collective-permute-start | bytes 1179656 | tf_op jit(solution)/shard_map/ppermute | solution.py:495
  65.7 19.4 %collective-permute-start.17 = (bf16[96,2048]{1,0:T(8,128)(2,1)}, bf16[96,2048]{1,0:T(8,128)(2,1)S(1)}, u32[]{:S(2)}, u32[]{:S(2)}) collective-permute-start(bf16[96,2048]{1,0:T(8,128)(2,1)} %get-tuple-element.168), channel_id=1, source_target_pairs={{0,2},{1,3},{2,0},{3,1},{4,6},{5,7},{6,4},{7,5},{8,10},{9,11},{10,... | collective-permute-start | bytes 1179656 | tf_op jit(solution)/shard_map/ppermute | solution.py:495
  66.6 19.2 %collective-permute-start.18 = (bf16[96,2048]{1,0:T(8,128)(2,1)}, bf16[96,2048]{1,0:T(8,128)(2,1)S(1)}, u32[]{:S(2)}, u32[]{:S(2)}) collective-permute-start(bf16[96,2048]{1,0:T(8,128)(2,1)} %get-tuple-element.169), channel_id=1, source_target_pairs={{0,3},{1,2},{2,1},{3,0},{4,7},{5,6},{6,5},{7,4},{8,11},{9,10},{10,... | collective-permute-start | bytes 1179656 | tf_op jit(solution)/shard_map/ppermute | solution.py:495
  81.6 17.8 %collective-permute-start.19 = (bf16[96,2176]{1,0:T(8,128)(2,1)}, bf16[96,2176]{1,0:T(8,128)(2,1)S(1)}, u32[]{:S(2)}, u32[]{:S(2)}) collective-permute-start(bf16[96,2176]{1,0:T(8,128)(2,1)} %get-tuple-element.182), channel_id=1, source_target_pairs={{0,1},{1,0},{2,3},{3,2},{4,5},{5,4},{6,7},{7,6},{8,9},{9,8},{10,11... | collective-permute-start | bytes 1253384 | tf_op jit(solution)/shard_map/ppermute | solution.py:495
  82.6 17.8 %collective-permute-start.20 = (bf16[96,2176]{1,0:T(8,128)(2,1)}, bf16[96,2176]{1,0:T(8,128)(2,1)S(1)}, u32[]{:S(2)}, u32[]{:S(2)}) collective-permute-start(bf16[96,2176]{1,0:T(8,128)(2,1)} %get-tuple-element.183), channel_id=1, source_target_pairs={{0,2},{1,3},{2,0},{3,1},{4,6},{5,7},{6,4},{7,5},{8,10},{9,11},{10,... | collective-permute-start | bytes 1253384 | tf_op jit(solution)/shard_map/ppermute | solution.py:495
  83.5 20.6 %collective-permute-start.21 = (bf16[96,2176]{1,0:T(8,128)(2,1)}, bf16[96,2176]{1,0:T(8,128)(2,1)S(1)}, u32[]{:S(2)}, u32[]{:S(2)}) collective-permute-start(bf16[96,2176]{1,0:T(8,128)(2,1)} %get-tuple-element.184), channel_id=1, source_target_pairs={{0,3},{1,2},{2,1},{3,0},{4,7},{5,6},{6,5},{7,4},{8,11},{9,10},{10,... | collective-permute-start | bytes 1253384 | tf_op jit(solution)/shard_map/ppermute | solution.py:495
  96.8 16.2 %collective-permute-start.22 = (bf16[48,2176]{1,0:T(8,128)(2,1)}, bf16[48,2176]{1,0:T(8,128)(2,1)S(1)}, u32[]{:S(2)}, u32[]{:S(2)}) collective-permute-start(bf16[48,2176]{1,0:T(8,128)(2,1)} %get-tuple-element.190), channel_id=1, source_target_pairs={{0,1},{1,0},{2,3},{3,2},{4,5},{5,4},{6,7},{7,6},{8,9},{9,8},{10,11... | collective-permute-start | bytes 626696 | tf_op jit(solution)/shard_map/ppermute | solution.py:495
  97.9 15.1 %collective-permute-start.23 = (bf16[48,2176]{1,0:T(8,128)(2,1)}, bf16[48,2176]{1,0:T(8,128)(2,1)S(1)}, u32[]{:S(2)}, u32[]{:S(2)}) collective-permute-start(bf16[48,2176]{1,0:T(8,128)(2,1)} %get-tuple-element.191), channel_id=1, source_target_pairs={{0,2},{1,3},{2,0},{3,1},{4,6},{5,7},{6,4},{7,5},{8,10},{9,11},{10,... | collective-permute-start | bytes 626696 | tf_op jit(solution)/shard_map/ppermute | solution.py:495
  99.4 13.7 %collective-permute-start.24 = (bf16[48,2176]{1,0:T(8,128)(2,1)}, bf16[48,2176]{1,0:T(8,128)(2,1)S(1)}, u32[]{:S(2)}, u32[]{:S(2)}) collective-permute-start(bf16[48,2176]{1,0:T(8,128)(2,1)} %get-tuple-element.192), channel_id=1, source_target_pairs={{0,3},{1,2},{2,1},{3,0},{4,7},{5,6},{6,5},{7,4},{8,11},{9,10},{10,... | collective-permute-start | bytes 626696 | tf_op jit(solution)/shard_map/ppermute | solution.py:495
  113.1 18.3 %collective-permute-start.31 = (bf16[1,2048,384]{2,1,0:T(8,128)(2,1)}, bf16[1,2048,384]{2,1,0:T(8,128)(2,1)}, u32[]{:S(2)}, u32[]{:S(2)}) collective-permute-start(bf16[1,2048,384]{2,1,0:T(8,128)(2,1)} %get-tuple-element.212), channel_id=1, source_target_pairs={{0,16},{16,0},{1,17},{17,1},{2,18},{18,2},{3,19},{19,3},{4,20},{20... | collective-permute-start | bytes 4718600 | tf_op jit(solution)/shard_map/ppermute | solution.py:590
  113.1 19.2 %collective-permute-start.32 = (bf16[1,384,2048]{2,1,0:T(8,128)(2,1)}, bf16[1,384,2048]{2,1,0:T(8,128)(2,1)}, u32[]{:S(2)}, u32[]{:S(2)}) collective-permute-start(bf16[1,384,2048]{2,1,0:T(8,128)(2,1)} %get-tuple-element.213), channel_id=1, source_target_pairs={{0,16},{16,0},{1,17},{17,1},{2,18},{18,2},{3,19},{19,3},{4,20},{20... | collective-permute-start | bytes 4718600 | tf_op jit(solution)/shard_map/ppermute | solution.py:590
  113.6 18.7 %collective-permute-start.30 = (bf16[1,2048,384]{2,1,0:T(8,128)(2,1)}, bf16[1,2048,384]{2,1,0:T(8,128)(2,1)}, u32[]{:S(2)}, u32[]{:S(2)}) collective-permute-start(bf16[1,2048,384]{2,1,0:T(8,128)(2,1)} %get-tuple-element.201.refs_17_), channel_id=1, source_target_pairs={{0,16},{16,0},{1,17},{17,1},{2,18},{18,2},{3,19},{19,3},{4,20},{20... | collective-permute-start | bytes 4718600 | tf_op jit(solution)/shard_map/ppermute | solution.py:590
  126.8 14.7 %collective-permute-start.28 = (bf16[64,1024]{1,0:T(8,128)(2,1)}, bf16[64,1024]{1,0:T(8,128)(2,1)}, u32[]{:S(2)}, u32[]{:S(2)}) collective-permute-start(bf16[64,1024]{1,0:T(8,128)(2,1)} %add_convert_fusion.1), channel_id=1, source_target_pairs={{0,8},{1,9},{2,10},{3,11},{4,12},{5,13},{6,14},{7,15},{8,0},{9,1},... | collective-permute-start | bytes 393224 | tf_op jit(solution)/shard_map/ppermute | solution.py:600
  128.4 13.3 %collective-permute-start.27 = (bf16[64,2176]{1,0:T(8,128)(2,1)}, bf16[64,2176]{1,0:T(8,128)(2,1)}, u32[]{:S(2)}, u32[]{:S(2)}) collective-permute-start(bf16[64,2176]{1,0:T(8,128)(2,1)} %get-tuple-element.207), channel_id=1, source_target_pairs={{0,4},{1,5},{2,6},{3,7},{4,0},{5,1},{6,2},{7,3},{8,12},{9,13},{10,... | collective-permute-start | bytes 835592 | tf_op jit(solution)/shard_map/ppermute | solution.py:597
  (31 other events, 205.5 us)

commit v13 on v12

--- a/solution.py
+++ b/solution.py
@@ -554,7 +554,7 @@
                 pltpu.SemaphoreType.DMA((8,)),
                 *(grad_scratch if own else []),
             ],
-            compiler_params=params(64 if own else 60),
+            compiler_params=params(64),
             cost_estimate=cost(6 * count * part * width, 4 * count * (width + hidden)),
             name="weight_grads",
         )(*got, *mids, *extra)

time: 145 us -> 144 us (level)
    unnamed x44 -> x32, local copies, waits for them, and re-layouts: 3.54 us -> 2.59 us
  transfers between devices with their start and end apart: 33 -> 33, of which waited for: 10 -> 11; matrix products, arithmetic and copies ran while one was open for 5% -> 5% of each run, Pallas kernels for 42% -> 42%
where the time goes in v13:
time: 144 us
  Pallas kernels  64.2 us (45%)
  starting transfers between devices  38.2 us (27%)
  waiting for transfers between devices  29.9 us (21%)
  other arithmetic  6.51 us (5%)
  local copies, waits for them, and re-layouts  3.79 us (3%)
    pallas_call x2, Pallas kernels, expert(): pl.pallas_call(functools.partial(expert_kernel, plan, g), out_shape=[shap...  23.4 us
    ppermute x18, starting transfers between devices, cross(): lax.ppermute(arrays[d], 'expert', plan.across(d))  21.3 us
    pallas_call x2, Pallas kernels, weight_grads(): pl.pallas_call(functools.partial(weight_kernel, plan, own, len(extra)), o...  17.3 us
    pallas_call x4, Pallas kernels, compact(): pl.pallas_call(functools.partial(compact_kernel, plan, c), out_shape=[sha...  14.4 us
    ppermute x18, waiting for transfers between devices, cross(): lax.ppermute(arrays[d], 'expert', plan.across(d))  14.1 us
    ppermute x5, waiting for transfers between devices, hop(): blocks[i] = lax.ppermute(before, 'expert', plan.exchange(r, chain))  10.8 us
    ppermute x5, starting transfers between devices, hop(): blocks[i] = lax.ppermute(before, 'expert', plan.exchange(r, chain))  10.1 us
    ppermute x4, starting transfers between devices, on_device(): sent = lax.ppermute(sums[r, a], 'expert', plan.flip(bit))  5.1 us
  transfers between devices with their start and end apart: 33, of which 11 were waited for; matrix products, arithmetic and copies ran while one was open for 5% of the time, Pallas kernels for 42%

profile of v13, /device:TPU:0, one launch (start us, length us, event | category | flops | bytes accessed | tf_op | source)
XLA Modules:
  0.0 143.5 jit_solution(12506102511871848811)
XLA Ops:
  0.6 2.2 %pack.1.refs_2_.refs_8_ = bf16[64,4224]{1,0:T(8,128)(2,1)} custom-call(bf16[64,2048]{1,0:T(8,128)(2,1)} %tok_ref.1, bf16[64,2048]{1,0:T(8,128)(2,1)} %up_ref.1, s32[8,64]{1,0:T(8,128)} %bitcast.5, bf16[8,64]{1,0:T(8,128)(2,1)} %bitcast.7), custom_call_target="tpu_custom_call" | custom-call | flops 1000000 | bytes 1081344 | tf_op jit(solution)/shard_map/pack/pallas_call | solution.py:427
  2.9 1.7 %collective-permute-start.4 = (bf16[64,4224]{1,0:T(8,128)(2,1)}, bf16[64,4224]{1,0:T(8,128)(2,1)S(1)}, u32[]{:S(2)}, u32[]{:S(2)}) collective-permute-start(bf16[64,4224]{1,0:T(8,128)(2,1)} %pack.1.refs_2_.refs_8_), channel_id=1, source_target_pairs={{0,0},{1,1},{2,2},{3,3},{4,8},{5,9},{6,10},{7,11},{8,4},{9,5},{10,... | collective-permute-start | bytes 1622024 | tf_op jit(solution)/shard_map/ppermute | solution.py:445
  4.6 4.9 %collective-permute-start.3 = (bf16[64,4224]{1,0:T(8,128)(2,1)}, bf16[64,4224]{1,0:T(8,128)(2,1)S(1)}, u32[]{:S(2)}, u32[]{:S(2)}) collective-permute-start(bf16[64,4224]{1,0:T(8,128)(2,1)} %pack.1.refs_2_.refs_8_), channel_id=1, source_target_pairs={{0,4},{1,5},{2,6},{3,7},{4,0},{5,1},{6,2},{7,3},{8,12},{9,13},{10,... | collective-permute-start | bytes 1622024 | tf_op jit(solution)/shard_map/ppermute | solution.py:445
  10.6 3.0 %compact.4 = (bf16[32,2048]{1,0:T(8,128)(2,1)}, bf16[32,2048]{1,0:T(8,128)(2,1)}, bf16[32,2048]{1,0:T(8,128)(2,1)}, bf16[32,2048]{1,0:T(8,128)(2,1)}) custom-call(s32[15]{0:T(128)} %dynamic-slice_bitcast_fusion.refs_0_, s32[1,64]{1,0:T(1,128)} %constant.21.clone.refs_1_, bf16[64,4224]{1,0:T(8,128)(2,1)} %pack.1.refs_2_.refs_8_), custom_call_target="tpu_custom_call" | custom-call | flops 33554432 | bytes 540672 | tf_op jit(solution)/shard_map/compact/pallas_call | solution.py:454
  17.2 2.4 %collective-permute-done.refs_2_.refs_1_ = bf16[32,2048]{1,0:T(8,128)(2,1)S(1)} collective-permute-done((bf16[32,2048]{1,0:T(8,128)(2,1)}, bf16[32,2048]{1,0:T(8,128)(2,1)S(1)}, u32[]{:S(2)}, u32[]{:S(2)}) %collective-permute-start) | collective-permute-done | bytes 131104 | tf_op jit(solution)/shard_map/ppermute | solution.py:495
  19.6 3.5 %collective-permute-done.1.refs_3_.refs_2_ = bf16[32,2048]{1,0:T(8,128)(2,1)S(1)} collective-permute-done((bf16[32,2048]{1,0:T(8,128)(2,1)}, bf16[32,2048]{1,0:T(8,128)(2,1)S(1)}, u32[]{:S(2)}, u32[]{:S(2)}) %collective-permute-start.1) | collective-permute-done | bytes 131104 | tf_op jit(solution)/shard_map/ppermute | solution.py:495
  24.1 2.4 %collective-permute-start.6 = (bf16[64,4224]{1,0:T(8,128)(2,1)S(1)}, bf16[64,4224]{1,0:T(8,128)(2,1)S(1)}, u32[]{:S(2)}, u32[]{:S(2)}) collective-permute-start(bf16[64,4224]{1,0:T(8,128)(2,1)S(1)} %collective-permute-done.4.refs_3_.refs_4_.refs_6_), channel_id=1, source_target_pairs={{0,4},{1,5},{2,6},{3,7},{4,0},{5,1},{6,2},{7,3},{8,12},{9,13},{10,... | collective-permute-start | bytes 1622024 | tf_op jit(solution)/shard_map/ppermute | solution.py:445
  26.5 3.4 %compact.5 = (bf16[64,2048]{1,0:T(8,128)(2,1)}, bf16[64,2048]{1,0:T(8,128)(2,1)}, bf16[64,2048]{1,0:T(8,128)(2,1)}, bf16[64,2048]{1,0:T(8,128)(2,1)}) custom-call(s32[15]{0:T(128)} %dynamic-slice_bitcast_fusion.refs_0_, s32[1,128]{1,0:T(1,128)} %constant.22.clone.refs_1_, bf16[64,4224]{1,0:T(8,128)(2,1)} %pack.1.refs_2_.refs_8_, bf16[64,4224]{1,0:T(8,128)(2,1)} %copy-done.2), custom_call_target="tpu_custom_call" | custom-call | flops 134217728 | bytes 1081344 | tf_op jit(solution)/shard_map/compact/pallas_call | solution.py:454
  33.5 3.3 %pad_maximum_fusion = bf16[1,2048,768]{2,1,0:T(8,128)(2,1)} fusion(bf16[1,2048,384]{2,1,0:T(8,128)(2,1)} %refs_6_.1, bf16[1,2048,384]{2,1,0:T(8,128)(2,1)S(1)} %copy-done.5), kind=kLoop, calls=%fused_computation | loop fusion | flops 6291456 | bytes 6291456 | tf_op jit(solution)/shard_map/concatenate | solution.py:437
  37.7 3.9 %compact.6 = (bf16[96,2048]{1,0:T(8,128)(2,1)}, bf16[96,2048]{1,0:T(8,128)(2,1)}, bf16[96,2048]{1,0:T(8,128)(2,1)}, bf16[96,2048]{1,0:T(8,128)(2,1)}) custom-call(s32[15]{0:T(128)} %dynamic-slice_bitcast_fusion.refs_0_, s32[1,192]{1,0:T(1,128)} %constant.23.clone.refs_1_, bf16[64,4224]{1,0:T(8,128)(2,1)} %copy-done.2, bf16[64,4224]{1,0:T(8,128)(2,1)} %copy-done, ...), custom_call_target="tpu_custom_call" | custom-call | flops 301989888 | bytes 1622016 | tf_op jit(solution)/shard_map/compact/pallas_call | solution.py:454
  43.4 1.7 %collective-permute-start.11 = (bf16[96,2048]{1,0:T(8,128)(2,1)}, bf16[96,2048]{1,0:T(8,128)(2,1)S(1)}, u32[]{:S(2)}, u32[]{:S(2)}) collective-permute-start(bf16[96,2048]{1,0:T(8,128)(2,1)} %get-tuple-element.149), channel_id=1, source_target_pairs={{0,1},{1,0},{2,3},{3,2},{4,5},{5,4},{6,7},{7,6},{8,9},{9,8},{10,11... | collective-permute-start | bytes 1179656 | tf_op jit(solution)/shard_map/ppermute | solution.py:495
  46.9 10.8 %collective-permute-done.7.refs_3_.refs_5_ = bf16[64,4224]{1,0:T(8,128)(2,1)S(1)} collective-permute-done((bf16[64,4224]{1,0:T(8,128)(2,1)S(1)}, bf16[64,4224]{1,0:T(8,128)(2,1)S(1)}, u32[]{:S(2)}, u32[]{:S(2)}) %collective-permute-start.7) | collective-permute-done | bytes 540704 | tf_op jit(solution)/shard_map/ppermute | solution.py:445
  58.5 4.1 %compact.7 = (bf16[96,2048]{1,0:T(8,128)(2,1)}, bf16[96,2048]{1,0:T(8,128)(2,1)}, bf16[96,2048]{1,0:T(8,128)(2,1)}, bf16[96,2048]{1,0:T(8,128)(2,1)}) custom-call(s32[15]{0:T(128)} %dynamic-slice_bitcast_fusion.refs_0_, s32[1,192]{1,0:T(1,128)} %constant.24.clone.refs_1_, bf16[64,4224]{1,0:T(8,128)(2,1)} %copy-done.3, bf16[64,4224]{1,0:T(8,128)(2,1)} %copy-done.4, ...), custom_call_target="tpu_custom_call" | custom-call | flops 402653184 | bytes 2162688 | tf_op jit(solution)/shard_map/compact/pallas_call | solution.py:454
  62.6 1.9 %collective-permute-done.12.refs_11_.refs_10_ = bf16[96,2048]{1,0:T(8,128)(2,1)S(1)} collective-permute-done((bf16[96,2048]{1,0:T(8,128)(2,1)}, bf16[96,2048]{1,0:T(8,128)(2,1)S(1)}, u32[]{:S(2)}, u32[]{:S(2)}) %collective-permute-start.12) | collective-permute-done | bytes 393248 | tf_op jit(solution)/shard_map/ppermute | solution.py:495
  68.4 13.1 %expert.2 = (bf16[384,768]{1,0:T(8,128)(2,1)}, bf16[384,768]{1,0:T(8,128)(2,1)}, bf16[384,768]{1,0:T(8,128)(2,1)}, bf16[96,2176]{1,0:T(8,128)(2,1)}, bf16[96,217...) custom-call(s32[15]{0:T(128)} %dynamic-slice_bitcast_fusion.refs_0_, ...), custom_call_target="tpu_custom_call" | custom-call | flops 6039797760 | bytes 9437184 | tf_op jit(solution)/shard_map/expert/pallas_call | solution.py:473
  86.6 10.2 %expert.3 = (bf16[192,768]{1,0:T(8,128)(2,1)}, bf16[192,768]{1,0:T(8,128)(2,1)}, bf16[192,768]{1,0:T(8,128)(2,1)}, bf16[48,2176]{1,0:T(8,128)(2,1)}, bf16[48,217...) custom-call(s32[15]{0:T(128)} %dynamic-slice_bitcast_fusion.refs_0_, ...), custom_call_target="tpu_custom_call" | custom-call | flops 3019898880 | bytes 9437184 | tf_op jit(solution)/shard_map/expert/pallas_call | solution.py:473
  100.4 3.8 %collective-permute-done.21.refs_24_.refs_12_ = bf16[96,2176]{1,0:T(8,128)(2,1)} collective-permute-done((bf16[96,2176]{1,0:T(8,128)(2,1)}, bf16[96,2176]{1,0:T(8,128)(2,1)}, u32[]{:S(2)}, u32[]{:S(2)}) %collective-permute-start.21) | collective-permute-done | bytes 417824 | tf_op jit(solution)/shard_map/ppermute | solution.py:495
  104.2 8.1 %weight_grads.2 = (bf16[1,2048,384]{2,1,0:T(8,128)(2,1)}, bf16[1,2048,384]{2,1,0:T(8,128)(2,1)}, bf16[1,384,2048]{2,1,0:T(8,128)(2,1)}) custom-call(bf16[32,2048]{1,0:T(8,128)(2,1)} %get-tuple-element.128.refs_1_.refs_0_, bf16[32,2048]{1,0:T(8,128)(2,1)} %copy-done.13, bf16[32,2048]{1,0:T(8,128)(2,1)} %copy-done.14, bf16[32,2048]{1,0:T(8,128)(2,1)} %copy-done.15, ...), custom_call_target="tpu_custom_call" | custom-call | flops 2717908992 | bytes 6488064 | tf_op jit(solution)/shard_map/weight_grads/pallas_call | solution.py:537
  113.2 4.7 %spread.1 = (bf16[64,2176]{1,0:T(8,128)(2,1)}, bf16[64,2176]{1,0:T(8,128)(2,1)}, bf16[64,1024]{1,0:T(8,128)(2,1)}, bf16[64,1152]{1,0:T(8,128)(2,1)}, bf16[64,1024]{1,0:T(8,128)(2,1)}, /*index=5*/bf16[64,1152]{1,0:T(8,128)(2,1)}) custom-call(s32[15]{0:T(128)} %dynamic-slice_bitcast_fusion.refs_0_, s32[1,576]{1,0:T(1,128)} %constant.25.clone.refs_1_, ...), custom_call_target="tpu_custom_call" | custom-call | flops 603979776 | bytes 2359296 | tf_op jit(solution)/shard_map/spread/pallas_call | solution.py:564
  120.0 4.5 %collective-permute-done.25 = bf16[64,1024]{1,0:T(8,128)(2,1)S(1)} collective-permute-done((bf16[64,1024]{1,0:T(8,128)(2,1)}, bf16[64,1024]{1,0:T(8,128)(2,1)S(1)}, u32[]{:S(2)}, u32[]{:S(2)}) %collective-permute-start.25) | collective-permute-done | bytes 131104 | tf_op jit(solution)/shard_map/ppermute | solution.py:600
  126.1 1.8 %collective-permute-start.28 = (bf16[64,1024]{1,0:T(8,128)(2,1)}, bf16[64,1024]{1,0:T(8,128)(2,1)}, u32[]{:S(2)}, u32[]{:S(2)}) collective-permute-start(bf16[64,1024]{1,0:T(8,128)(2,1)} %add_convert_fusion.1), channel_id=1, source_target_pairs={{0,8},{1,9},{2,10},{3,11},{4,12},{5,13},{6,14},{7,15},{8,0},{9,1},... | collective-permute-start | bytes 393224 | tf_op jit(solution)/shard_map/ppermute | solution.py:600
  129.0 1.6 %add_convert_fusion = bf16[64,1152]{1,0:T(8,128)(2,1)} fusion(bf16[64,1152]{1,0:T(8,128)(2,1)S(1)} %collective-permute-done.26, bf16[64,1152]{1,0:T(8,128)(2,1)} %get-tuple-element.210), kind=kLoop, calls=%fused_computation.1 | loop fusion | flops 294912 | bytes 442368 | tf_op jit(solution)/shard_map/convert_element_type | solution.py:607
  131.8 9.2 %weight_grads.3 = (bf16[1,2048,384]{2,1,0:T(8,128)(2,1)}, bf16[1,2048,384]{2,1,0:T(8,128)(2,1)}, bf16[1,384,2048]{2,1,0:T(8,128)(2,1)}) custom-call(bf16[32,2048]{1,0:T(8,128)(2,1)} %get-tuple-element.128.refs_1_.refs_0_, bf16[32,2048]{1,0:T(8,128)(2,1)} %copy-done.13, bf16[32,2048]{1,0:T(8,128)(2,1)} %copy-done.14, bf16[32,2048]{1,0:T(8,128)(2,1)} %copy-done.15, ...), custom_call_target="tpu_custom_call" | custom-call | flops 2717908992 | bytes 6488064 | tf_op jit(solution)/shard_map/weight_grads/pallas_call | solution.py:537
  141.3 2.2 %home.1 = (bf16[64,2048]{1,0:T(8,128)(2,1)}, bf16[8,64]{1,0:T(8,128)(2,1)}) custom-call(bf16[64,2176]{1,0:T(8,128)(2,1)} %get-tuple-element.202.refs_0_, bf16[64,2176]{1,0:T(8,128)(2,1)} %collective-permute-done.27.refs_1_, bf16[64,1024]{1,0:T(8,128)(2,1)} %collective-permute-done.28.refs_2_, bf16[64,1152]{1,0:T(8,128)(2,1)} %collective-permute-done.29.refs_3_, ...), custom_call_target="tpu_custom_call" | custom-call | flops 1000000 | bytes 1310720 | tf_op jit(solution)/shard_map/home/pallas_call | solution.py:611
  (89 shorter events, 33.9 us)
Async XLA Ops:
  2.9 20.3 %collective-permute-start.4 = (bf16[64,4224]{1,0:T(8,128)(2,1)}, bf16[64,4224]{1,0:T(8,128)(2,1)S(1)}, u32[]{:S(2)}, u32[]{:S(2)}) collective-permute-start(bf16[64,4224]{1,0:T(8,128)(2,1)} %pack.1.refs_2_.refs_8_), channel_id=1, source_target_pairs={{0,0},{1,1},{2,2},{3,3},{4,8},{5,9},{6,10},{7,11},{8,4},{9,5},{10,... | collective-permute-start | bytes 1622024 | tf_op jit(solution)/shard_map/ppermute | solution.py:445
  4.6 18.6 %collective-permute-start.3 = (bf16[64,4224]{1,0:T(8,128)(2,1)}, bf16[64,4224]{1,0:T(8,128)(2,1)S(1)}, u32[]{:S(2)}, u32[]{:S(2)}) collective-permute-start(bf16[64,4224]{1,0:T(8,128)(2,1)} %pack.1.refs_2_.refs_8_), channel_id=1, source_target_pairs={{0,4},{1,5},{2,6},{3,7},{4,0},{5,1},{6,2},{7,3},{8,12},{9,13},{10,... | collective-permute-start | bytes 1622024 | tf_op jit(solution)/shard_map/ppermute | solution.py:445
  23.2 13.6 %collective-permute-start.5 = (bf16[64,4224]{1,0:T(8,128)(2,1)S(1)}, bf16[64,4224]{1,0:T(8,128)(2,1)S(1)}, u32[]{:S(2)}, u32[]{:S(2)}) collective-permute-start(bf16[64,4224]{1,0:T(8,128)(2,1)S(1)} %collective-permute-done.3.refs_3_.refs_2_), channel_id=1, source_target_pairs={{0,0},{1,1},{2,2},{3,3},{4,8},{5,9},{6,10},{7,11},{8,4},{9,5},{10,... | collective-permute-start | bytes 1622024 | tf_op jit(solution)/shard_map/ppermute | solution.py:445
  24.1 12.8 %collective-permute-start.6 = (bf16[64,4224]{1,0:T(8,128)(2,1)S(1)}, bf16[64,4224]{1,0:T(8,128)(2,1)S(1)}, u32[]{:S(2)}, u32[]{:S(2)}) collective-permute-start(bf16[64,4224]{1,0:T(8,128)(2,1)S(1)} %collective-permute-done.4.refs_3_.refs_4_.refs_6_), channel_id=1, source_target_pairs={{0,4},{1,5},{2,6},{3,7},{4,0},{5,1},{6,2},{7,3},{8,12},{9,13},{10,... | collective-permute-start | bytes 1622024 | tf_op jit(solution)/shard_map/ppermute | solution.py:445
  31.0 12.0 %collective-permute-start.9 = (bf16[64,2048]{1,0:T(8,128)(2,1)}, bf16[64,2048]{1,0:T(8,128)(2,1)}, u32[]{:S(2)}, u32[]{:S(2)}) collective-permute-start(bf16[64,2048]{1,0:T(8,128)(2,1)} %get-tuple-element.134), channel_id=1, source_target_pairs={{0,2},{1,3},{2,0},{3,1},{4,6},{5,7},{6,4},{7,5},{8,10},{9,11},{10,... | collective-permute-start | bytes 786440 | tf_op jit(solution)/shard_map/ppermute | solution.py:495
  43.0 21.6 %collective-permute-start.14 = (bf16[1,2048,768]{2,1,0:T(8,128)(2,1)}, bf16[1,2048,768]{2,1,0:T(8,128)(2,1)}, u32[]{:S(2)}, u32[]{:S(2)}) collective-permute-start(bf16[1,2048,768]{2,1,0:T(8,128)(2,1)} %pad_maximum_fusion), channel_id=1, source_target_pairs={{0,16},{16,0},{1,17},{17,1},{2,18},{18,2},{3,19},{19,3},{4,20},{20... | collective-permute-start | bytes 9437192 | tf_op jit(solution)/shard_map/ppermute | solution.py:508
  43.0 14.7 %collective-permute-start.7 = (bf16[64,4224]{1,0:T(8,128)(2,1)S(1)}, bf16[64,4224]{1,0:T(8,128)(2,1)S(1)}, u32[]{:S(2)}, u32[]{:S(2)}) collective-permute-start(bf16[64,4224]{1,0:T(8,128)(2,1)S(1)} %collective-permute-done.5.refs_2_.refs_4_), channel_id=1, source_target_pairs={{0,4},{1,5},{2,6},{3,7},{4,0},{5,1},{6,2},{7,3},{8,12},{9,13},{10,... | collective-permute-start | bytes 1622024 | tf_op jit(solution)/shard_map/ppermute | solution.py:445
  43.4 19.3 %collective-permute-start.11 = (bf16[96,2048]{1,0:T(8,128)(2,1)}, bf16[96,2048]{1,0:T(8,128)(2,1)S(1)}, u32[]{:S(2)}, u32[]{:S(2)}) collective-permute-start(bf16[96,2048]{1,0:T(8,128)(2,1)} %get-tuple-element.149), channel_id=1, source_target_pairs={{0,1},{1,0},{2,3},{3,2},{4,5},{5,4},{6,7},{7,6},{8,9},{9,8},{10,11... | collective-permute-start | bytes 1179656 | tf_op jit(solution)/shard_map/ppermute | solution.py:495
  45.0 19.5 %collective-permute-start.12 = (bf16[96,2048]{1,0:T(8,128)(2,1)}, bf16[96,2048]{1,0:T(8,128)(2,1)S(1)}, u32[]{:S(2)}, u32[]{:S(2)}) collective-permute-start(bf16[96,2048]{1,0:T(8,128)(2,1)} %get-tuple-element.150), channel_id=1, source_target_pairs={{0,2},{1,3},{2,0},{3,1},{4,6},{5,7},{6,4},{7,5},{8,10},{9,11},{10,... | collective-permute-start | bytes 1179656 | tf_op jit(solution)/shard_map/ppermute | solution.py:495
  46.4 18.2 %collective-permute-start.13 = (bf16[96,2048]{1,0:T(8,128)(2,1)}, bf16[96,2048]{1,0:T(8,128)(2,1)S(1)}, u32[]{:S(2)}, u32[]{:S(2)}) collective-permute-start(bf16[96,2048]{1,0:T(8,128)(2,1)} %get-tuple-element.151), channel_id=1, source_target_pairs={{0,3},{1,2},{2,1},{3,0},{4,7},{5,6},{6,5},{7,4},{8,11},{9,10},{10,... | collective-permute-start | bytes 1179656 | tf_op jit(solution)/shard_map/ppermute | solution.py:495
  64.7 18.9 %collective-permute-start.16 = (bf16[96,2048]{1,0:T(8,128)(2,1)}, bf16[96,2048]{1,0:T(8,128)(2,1)S(1)}, u32[]{:S(2)}, u32[]{:S(2)}) collective-permute-start(bf16[96,2048]{1,0:T(8,128)(2,1)} %get-tuple-element.167), channel_id=1, source_target_pairs={{0,1},{1,0},{2,3},{3,2},{4,5},{5,4},{6,7},{7,6},{8,9},{9,8},{10,11... | collective-permute-start | bytes 1179656 | tf_op jit(solution)/shard_map/ppermute | solution.py:495
  65.7 19.4 %collective-permute-start.17 = (bf16[96,2048]{1,0:T(8,128)(2,1)}, bf16[96,2048]{1,0:T(8,128)(2,1)S(1)}, u32[]{:S(2)}, u32[]{:S(2)}) collective-permute-start(bf16[96,2048]{1,0:T(8,128)(2,1)} %get-tuple-element.168), channel_id=1, source_target_pairs={{0,2},{1,3},{2,0},{3,1},{4,6},{5,7},{6,4},{7,5},{8,10},{9,11},{10,... | collective-permute-start | bytes 1179656 | tf_op jit(solution)/shard_map/ppermute | solution.py:495
  66.6 19.2 %collective-permute-start.18 = (bf16[96,2048]{1,0:T(8,128)(2,1)}, bf16[96,2048]{1,0:T(8,128)(2,1)S(1)}, u32[]{:S(2)}, u32[]{:S(2)}) collective-permute-start(bf16[96,2048]{1,0:T(8,128)(2,1)} %get-tuple-element.169), channel_id=1, source_target_pairs={{0,3},{1,2},{2,1},{3,0},{4,7},{5,6},{6,5},{7,4},{8,11},{9,10},{10,... | collective-permute-start | bytes 1179656 | tf_op jit(solution)/shard_map/ppermute | solution.py:495
  81.6 17.8 %collective-permute-start.19 = (bf16[96,2176]{1,0:T(8,128)(2,1)}, bf16[96,2176]{1,0:T(8,128)(2,1)}, u32[]{:S(2)}, u32[]{:S(2)}) collective-permute-start(bf16[96,2176]{1,0:T(8,128)(2,1)} %get-tuple-element.182), channel_id=1, source_target_pairs={{0,1},{1,0},{2,3},{3,2},{4,5},{5,4},{6,7},{7,6},{8,9},{9,8},{10,11... | collective-permute-start | bytes 1253384 | tf_op jit(solution)/shard_map/ppermute | solution.py:495
  82.6 17.8 %collective-permute-start.20 = (bf16[96,2176]{1,0:T(8,128)(2,1)}, bf16[96,2176]{1,0:T(8,128)(2,1)}, u32[]{:S(2)}, u32[]{:S(2)}) collective-permute-start(bf16[96,2176]{1,0:T(8,128)(2,1)} %get-tuple-element.183), channel_id=1, source_target_pairs={{0,2},{1,3},{2,0},{3,1},{4,6},{5,7},{6,4},{7,5},{8,10},{9,11},{10,... | collective-permute-start | bytes 1253384 | tf_op jit(solution)/shard_map/ppermute | solution.py:495
  83.5 20.7 %collective-permute-start.21 = (bf16[96,2176]{1,0:T(8,128)(2,1)}, bf16[96,2176]{1,0:T(8,128)(2,1)}, u32[]{:S(2)}, u32[]{:S(2)}) collective-permute-start(bf16[96,2176]{1,0:T(8,128)(2,1)} %get-tuple-element.184), channel_id=1, source_target_pairs={{0,3},{1,2},{2,1},{3,0},{4,7},{5,6},{6,5},{7,4},{8,11},{9,10},{10,... | collective-permute-start | bytes 1253384 | tf_op jit(solution)/shard_map/ppermute | solution.py:495
  96.8 15.5 %collective-permute-start.22 = (bf16[48,2176]{1,0:T(8,128)(2,1)}, bf16[48,2176]{1,0:T(8,128)(2,1)}, u32[]{:S(2)}, u32[]{:S(2)}) collective-permute-start(bf16[48,2176]{1,0:T(8,128)(2,1)} %get-tuple-element.190), channel_id=1, source_target_pairs={{0,1},{1,0},{2,3},{3,2},{4,5},{5,4},{6,7},{7,6},{8,9},{9,8},{10,11... | collective-permute-start | bytes 626696 | tf_op jit(solution)/shard_map/ppermute | solution.py:495
  97.9 14.4 %collective-permute-start.23 = (bf16[48,2176]{1,0:T(8,128)(2,1)}, bf16[48,2176]{1,0:T(8,128)(2,1)}, u32[]{:S(2)}, u32[]{:S(2)}) collective-permute-start(bf16[48,2176]{1,0:T(8,128)(2,1)} %get-tuple-element.191), channel_id=1, source_target_pairs={{0,2},{1,3},{2,0},{3,1},{4,6},{5,7},{6,4},{7,5},{8,10},{9,11},{10,... | collective-permute-start | bytes 626696 | tf_op jit(solution)/shard_map/ppermute | solution.py:495
  99.4 13.3 %collective-permute-start.24 = (bf16[48,2176]{1,0:T(8,128)(2,1)}, bf16[48,2176]{1,0:T(8,128)(2,1)}, u32[]{:S(2)}, u32[]{:S(2)}) collective-permute-start(bf16[48,2176]{1,0:T(8,128)(2,1)} %get-tuple-element.192), channel_id=1, source_target_pairs={{0,3},{1,2},{2,1},{3,0},{4,7},{5,6},{6,5},{7,4},{8,11},{9,10},{10,... | collective-permute-start | bytes 626696 | tf_op jit(solution)/shard_map/ppermute | solution.py:495
  112.6 18.0 %collective-permute-start.31 = (bf16[1,2048,384]{2,1,0:T(8,128)(2,1)}, bf16[1,2048,384]{2,1,0:T(8,128)(2,1)}, u32[]{:S(2)}, u32[]{:S(2)}) collective-permute-start(bf16[1,2048,384]{2,1,0:T(8,128)(2,1)} %get-tuple-element.212), channel_id=1, source_target_pairs={{0,16},{16,0},{1,17},{17,1},{2,18},{18,2},{3,19},{19,3},{4,20},{20... | collective-permute-start | bytes 4718600 | tf_op jit(solution)/shard_map/ppermute | solution.py:590
  112.6 19.2 %collective-permute-start.32 = (bf16[1,384,2048]{2,1,0:T(8,128)(2,1)}, bf16[1,384,2048]{2,1,0:T(8,128)(2,1)}, u32[]{:S(2)}, u32[]{:S(2)}) collective-permute-start(bf16[1,384,2048]{2,1,0:T(8,128)(2,1)} %get-tuple-element.213), channel_id=1, source_target_pairs={{0,16},{16,0},{1,17},{17,1},{2,18},{18,2},{3,19},{19,3},{4,20},{20... | collective-permute-start | bytes 4718600 | tf_op jit(solution)/shard_map/ppermute | solution.py:590
  113.1 18.7 %collective-permute-start.30 = (bf16[1,2048,384]{2,1,0:T(8,128)(2,1)}, bf16[1,2048,384]{2,1,0:T(8,128)(2,1)}, u32[]{:S(2)}, u32[]{:S(2)}) collective-permute-start(bf16[1,2048,384]{2,1,0:T(8,128)(2,1)} %get-tuple-element.201.refs_17_), channel_id=1, source_target_pairs={{0,16},{16,0},{1,17},{17,1},{2,18},{18,2},{3,19},{19,3},{4,20},{20... | collective-permute-start | bytes 4718600 | tf_op jit(solution)/shard_map/ppermute | solution.py:590
  126.1 15.0 %collective-permute-start.28 = (bf16[64,1024]{1,0:T(8,128)(2,1)}, bf16[64,1024]{1,0:T(8,128)(2,1)}, u32[]{:S(2)}, u32[]{:S(2)}) collective-permute-start(bf16[64,1024]{1,0:T(8,128)(2,1)} %add_convert_fusion.1), channel_id=1, source_target_pairs={{0,8},{1,9},{2,10},{3,11},{4,12},{5,13},{6,14},{7,15},{8,0},{9,1},... | collective-permute-start | bytes 393224 | tf_op jit(solution)/shard_map/ppermute | solution.py:600
  127.9 13.4 %collective-permute-start.27 = (bf16[64,2176]{1,0:T(8,128)(2,1)}, bf16[64,2176]{1,0:T(8,128)(2,1)}, u32[]{:S(2)}, u32[]{:S(2)}) collective-permute-start(bf16[64,2176]{1,0:T(8,128)(2,1)} %get-tuple-element.207), channel_id=1, source_target_pairs={{0,4},{1,5},{2,6},{3,7},{4,0},{5,1},{6,2},{7,3},{8,12},{9,13},{10,... | collective-permute-start | bytes 835592 | tf_op jit(solution)/shard_map/ppermute | solution.py:597
  (25 other events, 194.2 us)
